TPU v7x, 512 devices: a whole 4x8x8 slice. The times are simulated.
512 devices in a mesh: gx: 16 (over x_hi, y), gy: 4 (over x_lo, core), gz: 8 (over z).
Axes of the slice: x: 4 (x_hi: 2, x_lo: 2; x = x_hi * 2 + x_lo), y: 8, z: 8, core: 2. Of those that a mesh axis runs over, the one named last changes fastest.
Arguments:
- efield: float32 [3, 32, 2048, 512], P(None, 'gz', 'gx', 'gy'), may hold values from -6 to 6
- density: float32 [32, 2048, 512], P('gz', 'gx', 'gy'), may hold values from 0.5 to 2
- mobility_prev: float32 [32, 2048, 512], P('gz', 'gx', 'gy'), may hold values from 0.5 to 2
- thermal_prev: float32 [32, 2048, 512], P('gz', 'gx', 'gy'), may hold values from 0 to 2
- owner: int32 [8, 16, 4, 512, 1], P('gz', 'gx', 'gy'), may hold values from 0 to 63; in each aligned block of 512 rows (0 to 511, 512 to 1023, ..., all dimensions but the last counted through in order) at most 16 rows name the same one
- block: int32 [8, 16, 4, 512], P('gz', 'gx', 'gy'), may hold values from 0 to 511
- live: int32 [8, 16, 4, 512], P('gz', 'gx', 'gy'), may hold values from 1 to 128
- material: int32 [8, 16, 4, 512], P('gz', 'gx', 'gy'), may hold values from 0 to 7
- mat_conductivity: float32 [8], replicated, may hold values from 0.5 to 5
- mat_softening: float32 [8], replicated, may hold values from 0.1 to 0.8
- mat_capacity: float32 [8], replicated, may hold values from 0.01 to 0.1
Outputs:
- thermal: float32 [32, 2048, 512], P('gz', 'gx', 'gy')
- mobility: float32 [32, 2048, 512], P('gz', 'gx', 'gy')
- ionization: float32 [32, 2048, 512], P('gz', 'gx', 'gy')
Inputs may be any that keep to these rules, and one draw needn't show every extreme that they name: Among the rows of one device, at most 16 name the same owner; some device reaches 16.
All inputs are finite; a program needn't handle non-finite values.
Results may differ from a plain program's by a relative error of at most 0.0001.
Values sent between devices are 32-bit elements; how exact they have to be, the bound alone decides.
No kernel may reach another device: no remote copies, remote signals or barrier semaphores. Data moves between devices by JAX's collectives and lax.ppermute only.
A program may use at most 64 MiB of HBM per device.

v0:
```python
import jax
import jax.numpy as jnp
from jax import lax
from jax.sharding import PartitionSpec as P

SWEEPS = 6


def with_halo(cells, sides, width):
    for axis, dim in sides:
        count = lax.axis_size(axis)
        ends = count - 1
        head = lax.slice_in_dim(cells, 0, width, axis=dim)
        tail = lax.slice_in_dim(cells, cells.shape[dim] - width, cells.shape[dim], axis=dim)
        cells = jnp.concatenate(
            [
                lax.ppermute(tail, axis, [(i, (i + 1) % count) for i in range(ends)]),
                cells,
                lax.ppermute(head, axis, [((i + 1) % count, i) for i in range(ends)]),
            ],
            axis=dim,
        )
    return cells


def neighbours(padded):
    return [
        padded[2:, 1:-1, 1:-1],
        padded[:-2, 1:-1, 1:-1],
        padded[1:-1, 2:, 1:-1],
        padded[1:-1, :-2, 1:-1],
        padded[1:-1, 1:-1, 2:],
        padded[1:-1, 1:-1, :-2],
    ]


def send_heat(outgoing, labels):
    peers, slots, width = outgoing.shape
    received, ids = (
        lax.all_to_all(outgoing, ("gx", "gy"), split_axis=0, concat_axis=0, tiled=True),
        lax.all_to_all(labels, ("gx", "gy"), split_axis=0, concat_axis=0, tiled=True),
    )
    return (received.reshape(peers * slots, width), ids.reshape(peers * slots))


def send_back(replies):
    peers, slots, width = replies.shape
    returned = lax.all_to_all(replies, ("gx", "gy"), split_axis=0, concat_axis=0, tiled=True)
    return returned.reshape(peers * slots, width)


def per_device(
    efield,
    density,
    mobility_prev,
    thermal_prev,
    owner,
    block,
    live,
    material,
    mat_conductivity,
    mat_softening,
    mat_capacity,
):
    layers, xcells, width = density.shape
    nrows = layers * xcells
    across = lax.axis_size("gx")
    along = lax.axis_size("gy")
    peers = across * along
    slots = max(2, 2 * nrows // peers)
    esq = efield[0] * efield[0] + efield[1] * efield[1] + efield[2] * efield[2]
    heat = 0.2 * density * mobility_prev * esq
    column = lax.broadcasted_iota(jnp.int32, (layers, xcells, width), 2)
    heat = jnp.where(column < live.reshape(layers, xcells, 1), heat, jnp.float32(0.0))
    heat_rows = heat.reshape(nrows, width)
    owners = owner.reshape(nrows)
    targets = block.reshape(nrows)
    member = (owners[:, None] == jnp.arange(peers, dtype=jnp.int32)[None, :]).astype(jnp.int32)
    earlier = jnp.cumsum(member, axis=0) - member
    position = jnp.sum(earlier * member, axis=1)
    destination = owners * slots + position
    nblocks = material.size
    outgoing = jnp.zeros((peers * slots, width), jnp.float32).at[destination].set(heat_rows)
    labels = jnp.full((peers * slots,), nblocks, jnp.int32).at[destination].set(targets)
    received, ids = send_heat(outgoing.reshape(peers, slots, width), labels.reshape(peers, slots))
    picks = (jnp.arange(nblocks, dtype=jnp.int32)[:, None] == ids[None, :]).astype(jnp.float32)
    source_rows = jnp.dot(
        picks, received, precision=lax.Precision.HIGHEST, preferred_element_type=jnp.float32
    )
    tlayers, txcells, _ = thermal_prev.shape
    source = source_rows.reshape(tlayers, txcells, width)
    choose = (
        material.reshape(tlayers, txcells, 1, 1)
        == jnp.arange(mat_conductivity.shape[0], dtype=jnp.int32)
    ).astype(jnp.float32)
    k_base = jnp.sum(choose * mat_conductivity, -1)
    k_soft = jnp.sum(choose * mat_softening, -1)
    capf = jnp.sum(choose * mat_capacity, -1)
    cond = k_base / (1.0 + k_soft * thermal_prev)
    rhs = capf * thermal_prev + source
    cond_padded = with_halo(cond, (("gx", 1), ("gy", 2), ("gz", 0)), 1)
    fixed_weights = [0.5 * (cond + n) for n in neighbours(cond_padded)]
    fixed_diag = capf + sum(fixed_weights)

    def residual_of(x):
        padded = with_halo(x, (("gx", 1), ("gy", 2), ("gz", 0)), 1)
        applied = capf * x + sum((w * (x - n) for w, n in zip(fixed_weights, neighbours(padded))))
        return (rhs - applied, fixed_diag)

    theta = 1.01
    delta = 0.99
    sigma = theta / delta
    x = thermal_prev
    r, diag = residual_of(x)
    d = r / (theta * diag)
    x = x + d
    rho = 1.0 / sigma
    for sweep in range(SWEEPS - 1):
        r, diag = residual_of(x)
        rho_new = 1.0 / (2.0 * sigma - rho)
        d = rho_new * rho * d + 2.0 * rho_new / delta * r / diag
        x = x + d
        rho = rho_new
    thermal_rows = x.reshape(nblocks, width)
    valid = (ids < nblocks).astype(jnp.float32)
    replies = jnp.take(thermal_rows, jnp.minimum(ids, nblocks - 1), axis=0) * valid[:, None]
    returned = send_back(replies.reshape(peers, slots, width))
    back = returned[destination].reshape(layers, xcells, width)
    mobility = mobility_prev * jnp.exp(-0.7 * back)
    ionization = jnp.exp(-2.0 * (1.0 + 0.3 * back) / jnp.sqrt(esq + 1.0))
    return (x, mobility, ionization)


def solution(mesh):
    placed = (
        P(None, "gz", "gx", "gy"),
        P("gz", "gx", "gy"),
        P("gz", "gx", "gy"),
        P("gz", "gx", "gy"),
        P("gz", "gx", "gy", None, None),
        P("gz", "gx", "gy", None),
        P("gz", "gx", "gy", None),
        P("gz", "gx", "gy", None),
        P(),
        P(),
        P(),
    )
    return jax.shard_map(
        per_device,
        mesh=mesh,
        in_specs=placed,
        out_specs=(P("gz", "gx", "gy"), P("gz", "gx", "gy"), P("gz", "gx", "gy")),
        check_vma=False,
    )
```

profile of v0, /device:TPU:1, one launch (start us, length us, event | category | flops | bytes accessed | tf_op | source)
XLA Modules:
  0.0 272.9 jit_solution(2815567943467667347)
XLA Ops:
  1.6 4.0 %collective-permute-start.5 = (f32[4,1,128]{2,1,0:T(1,128)S(1)}, f32[4,1,128]{2,1,0:T(1,128)S(1)}, u32[]{:S(2)}, u32[]{:S(2)}) collective-permute-start(f32[4,1,128]{2,1,0:T(1,128)S(1)} %get-tuple-element.64), channel_id=1, source_target_pairs={{0,32},{32,64},{64,96},{96,128},{128,160},{160,192},{192,224},{224... | collective-permute-start | bytes 6152 | tf_op jit(solution)/shard_map/ppermute | solution.py:17
  10.6 2.6 scatter_custom_fusion
  13.9 13.4 %all-to-all-start = ((s32[64,1,16]{2,1,0:T(1,128)}), s32[64,1,16]{2,1,0:T(1,128)S(1)}, u32[]{:S(2)}, u32[]{:S(2)}) async-start(s32[64,1,16]{2,1,0:T(1,128)} %bitcast.8), calls=%async_computation | async-start | bytes 65536 | tf_op jit(solution)/shard_map/all_to_all | solution.py:41
  28.9 4.0 %collective-permute-start = (f32[4,1,128]{2,1,0:T(1,128)S(1)}, f32[4,1,128]{2,1,0:T(1,128)S(1)}, u32[]{:S(2)}, u32[]{:S(2)}) collective-permute-start(f32[4,1,128]{2,1,0:T(1,128)S(1)} %get-tuple-element.63), channel_id=1, source_target_pairs={{0,32},{32,64},{64,96},{96,128},{128,160},{160,192},{192,224},{224... | collective-permute-start | bytes 6152 | tf_op jit(solution)/shard_map/ppermute | solution.py:17
  34.6 2.5 scatter_custom_fusion.1
  37.1 11.0 %all-to-all-start.1 = ((f32[64,16,128]{2,1,0:T(8,128)}), f32[64,16,128]{2,1,0:T(8,128)S(1)}, u32[]{:S(2)}, u32[]{:S(2)}) async-start(f32[64,16,128]{2,1,0:T(8,128)} %bitcast.12), calls=%async_computation.1 | async-start | bytes 1048576 | tf_op jit(solution)/shard_map/all_to_all | solution.py:40
  48.2 3.5 %collective-permute-start.2 = (f32[4,130,1]{2,1,0:T(8,128)S(1)}, f32[4,130,1]{2,1,0:T(8,128)S(1)}, u32[]{:S(2)}, u32[]{:S(2)}) collective-permute-start(f32[4,130,1]{2,1,0:T(8,128)S(1)} %get-tuple-element.46), channel_id=1, source_target_pairs={{0,8},{8,16},{16,24},{1,9},{9,17},{17,25},{2,10},{10,18},{18,26},{... | collective-permute-start | bytes 6248 | tf_op jit(solution)/shard_map/ppermute | solution.py:17
  51.8 1.9 collective-permute-start.3
  53.9 1.9 collective-permute-start.8
  55.8 3.6 %collective-permute-start.7 = (f32[4,130,1]{2,1,0:T(8,128)S(1)}, f32[4,130,1]{2,1,0:T(8,128)S(1)}, u32[]{:S(2)}, u32[]{:S(2)}) collective-permute-start(f32[4,130,1]{2,1,0:T(8,128)S(1)} %get-tuple-element.49), channel_id=1, source_target_pairs={{0,8},{8,16},{16,24},{1,9},{9,17},{17,25},{2,10},{10,18},{18,26},{... | collective-permute-start | bytes 6248 | tf_op jit(solution)/shard_map/ppermute | solution.py:17
  59.5 2.7 collective-permute-done.3
  63.0 4.6 %collective-permute-start.10 = (f32[1,130,130]{2,1,0:T(8,128)}, f32[1,130,130]{2,1,0:T(8,128)}, u32[]{:S(2)}, u32[]{:S(2)}) collective-permute-start(f32[1,130,130]{2,1,0:T(8,128)} %get-tuple-element.32), channel_id=1, source_target_pairs={{0,1},{1,2},{2,3},{3,4},{4,5},{5,6},{6,7},{8,9},{9,10},{10,11},{11... | collective-permute-start | bytes 202808 | tf_op jit(solution)/shard_map/ppermute | solution.py:17
  71.2 4.6 %collective-permute-start.11 = (f32[1,130,130]{2,1,0:T(8,128)}, f32[1,130,130]{2,1,0:T(8,128)S(1)}, u32[]{:S(2)}, u32[]{:S(2)}) collective-permute-start(f32[1,130,130]{2,1,0:T(8,128)} %get-tuple-element.35), channel_id=1, source_target_pairs={{0,1},{1,2},{2,3},{3,4},{4,5},{5,6},{6,7},{8,9},{9,10},{10,11},{11... | collective-permute-start | bytes 202808 | tf_op jit(solution)/shard_map/ppermute | solution.py:17
  78.8 4.0 %fusion.171 = (f32[4,128,128]{2,1,0:T(8,128)S(1)}, f32[4,128,128]{2,1,0:T(8,128)S(1)}, f32[4,128,128]{2,1,0:T(8,128)S(1)}, f32[4,128,128]{2,1,0:T(8,128)S(1)}, f...) fusion(f32[4,128,128]{2,1,0:T(8,128)S(1)} %copy-done.2, ...), kind=kOutput, calls=%fused_computation.365 | convolution fusion | flops 810942464 | bytes 3178688 | tf_op jit(solution)/shard_map/dot_general | solution.py:87
  82.9 2.6 collective-permute-start.12
  86.8 3.3 %collective-permute-done.13 = f32[4,1,128]{2,1,0:T(1,128)S(1)} collective-permute-done((f32[4,1,128]{2,1,0:T(1,128)S(1)}, f32[4,1,128]{2,1,0:T(1,128)S(1)}, u32[]{:S(2)}, u32[]{:S(2)}) %collective-permute-start.13) | collective-permute-done | bytes 2080 | tf_op jit(solution)/shard_map/ppermute | solution.py:19
  90.3 1.9 collective-permute-start.15
  92.2 4.0 %collective-permute-start.14 = (f32[4,130,1]{2,1,0:T(8,128)S(1)}, f32[4,130,1]{2,1,0:T(8,128)S(1)}, u32[]{:S(2)}, u32[]{:S(2)}) collective-permute-start(f32[4,130,1]{2,1,0:T(8,128)S(1)} %get-tuple-element.45), channel_id=1, source_target_pairs={{0,8},{8,16},{16,24},{1,9},{9,17},{17,25},{2,10},{10,18},{18,26},{... | collective-permute-start | bytes 6248 | tf_op jit(solution)/shard_map/ppermute | solution.py:17
  96.2 2.3 collective-permute-done.15
  101.2 4.6 %collective-permute-start.17 = (f32[1,130,130]{2,1,0:T(8,128)S(1)}, f32[1,130,130]{2,1,0:T(8,128)S(1)}, u32[]{:S(2)}, u32[]{:S(2)}) collective-permute-start(f32[1,130,130]{2,1,0:T(8,128)S(1)} %get-tuple-element.31), channel_id=1, source_target_pairs={{0,1},{1,2},{2,3},{3,4},{4,5},{5,6},{6,7},{8,9},{9,10},{10,11},{11... | collective-permute-start | bytes 202808 | tf_op jit(solution)/shard_map/ppermute | solution.py:17
  108.5 3.6 %collective-permute-start.18 = (f32[4,1,128]{2,1,0:T(1,128)S(1)}, f32[4,1,128]{2,1,0:T(1,128)S(1)}, u32[]{:S(2)}, u32[]{:S(2)}) collective-permute-start(f32[4,1,128]{2,1,0:T(1,128)S(1)} %get-tuple-element.58), channel_id=1, source_target_pairs={{0,32},{32,64},{64,96},{96,128},{128,160},{160,192},{192,224},{224... | collective-permute-start | bytes 6152 | tf_op jit(solution)/shard_map/ppermute | solution.py:17
  113.5 3.1 %collective-permute-done.19 = f32[4,1,128]{2,1,0:T(1,128)S(1)} collective-permute-done((f32[4,1,128]{2,1,0:T(1,128)S(1)}, f32[4,1,128]{2,1,0:T(1,128)S(1)}, u32[]{:S(2)}, u32[]{:S(2)}) %collective-permute-start.19) | collective-permute-done | bytes 2080 | tf_op jit(solution)/shard_map/ppermute | solution.py:19
  116.7 1.9 collective-permute-start.21
  118.7 6.6 %collective-permute-start.20 = (f32[4,130,1]{2,1,0:T(8,128)S(1)}, f32[4,130,1]{2,1,0:T(8,128)S(1)}, u32[]{:S(2)}, u32[]{:S(2)}) collective-permute-start(f32[4,130,1]{2,1,0:T(8,128)S(1)} %get-tuple-element.43), channel_id=1, source_target_pairs={{0,8},{8,16},{16,24},{1,9},{9,17},{17,25},{2,10},{10,18},{18,26},{... | collective-permute-start | bytes 6248 | tf_op jit(solution)/shard_map/ppermute | solution.py:17
  125.3 2.3 collective-permute-done.21
  130.2 5.6 %collective-permute-start.23 = (f32[1,130,130]{2,1,0:T(8,128)S(1)}, f32[1,130,130]{2,1,0:T(8,128)S(1)}, u32[]{:S(2)}, u32[]{:S(2)}) collective-permute-start(f32[1,130,130]{2,1,0:T(8,128)S(1)} %get-tuple-element.29), channel_id=1, source_target_pairs={{0,1},{1,2},{2,3},{3,4},{4,5},{5,6},{6,7},{8,9},{9,10},{10,11},{11... | collective-permute-start | bytes 202808 | tf_op jit(solution)/shard_map/ppermute | solution.py:17
  138.5 4.7 %collective-permute-start.24 = (f32[4,1,128]{2,1,0:T(1,128)S(1)}, f32[4,1,128]{2,1,0:T(1,128)S(1)}, u32[]{:S(2)}, u32[]{:S(2)}) collective-permute-start(f32[4,1,128]{2,1,0:T(1,128)S(1)} %get-tuple-element.56), channel_id=1, source_target_pairs={{0,32},{32,64},{64,96},{96,128},{128,160},{160,192},{192,224},{224... | collective-permute-start | bytes 6152 | tf_op jit(solution)/shard_map/ppermute | solution.py:17
  144.5 3.3 %collective-permute-done.25 = f32[4,1,128]{2,1,0:T(1,128)S(1)} collective-permute-done((f32[4,1,128]{2,1,0:T(1,128)S(1)}, f32[4,1,128]{2,1,0:T(1,128)S(1)}, u32[]{:S(2)}, u32[]{:S(2)}) %collective-permute-start.25) | collective-permute-done | bytes 2080 | tf_op jit(solution)/shard_map/ppermute | solution.py:19
  147.9 1.9 collective-permute-start.27
  149.9 6.4 %collective-permute-start.26 = (f32[4,130,1]{2,1,0:T(8,128)S(1)}, f32[4,130,1]{2,1,0:T(8,128)S(1)}, u32[]{:S(2)}, u32[]{:S(2)}) collective-permute-start(f32[4,130,1]{2,1,0:T(8,128)S(1)} %get-tuple-element.41), channel_id=1, source_target_pairs={{0,8},{8,16},{16,24},{1,9},{9,17},{17,25},{2,10},{10,18},{18,26},{... | collective-permute-start | bytes 6248 | tf_op jit(solution)/shard_map/ppermute | solution.py:17
  156.3 2.3 collective-permute-done.27
  161.4 5.5 %collective-permute-start.29 = (f32[1,130,130]{2,1,0:T(8,128)S(1)}, f32[1,130,130]{2,1,0:T(8,128)S(1)}, u32[]{:S(2)}, u32[]{:S(2)}) collective-permute-start(f32[1,130,130]{2,1,0:T(8,128)S(1)} %get-tuple-element.27), channel_id=1, source_target_pairs={{0,1},{1,2},{2,3},{3,4},{4,5},{5,6},{6,7},{8,9},{9,10},{10,11},{11... | collective-permute-start | bytes 202808 | tf_op jit(solution)/shard_map/ppermute | solution.py:17
  167.2 1.7 collective-permute-done.29
  169.6 3.6 %collective-permute-start.30 = (f32[4,1,128]{2,1,0:T(1,128)S(1)}, f32[4,1,128]{2,1,0:T(1,128)S(1)}, u32[]{:S(2)}, u32[]{:S(2)}) collective-permute-start(f32[4,1,128]{2,1,0:T(1,128)S(1)} %get-tuple-element.54), channel_id=1, source_target_pairs={{0,32},{32,64},{64,96},{96,128},{128,160},{160,192},{192,224},{224... | collective-permute-start | bytes 6152 | tf_op jit(solution)/shard_map/ppermute | solution.py:17
  174.5 3.0 %collective-permute-done.31 = f32[4,1,128]{2,1,0:T(1,128)S(1)} collective-permute-done((f32[4,1,128]{2,1,0:T(1,128)S(1)}, f32[4,1,128]{2,1,0:T(1,128)S(1)}, u32[]{:S(2)}, u32[]{:S(2)}) %collective-permute-start.31) | collective-permute-done | bytes 2080 | tf_op jit(solution)/shard_map/ppermute | solution.py:19
  177.7 1.9 collective-permute-start.33
  179.6 6.7 %collective-permute-start.32 = (f32[4,130,1]{2,1,0:T(8,128)S(1)}, f32[4,130,1]{2,1,0:T(8,128)S(1)}, u32[]{:S(2)}, u32[]{:S(2)}) collective-permute-start(f32[4,130,1]{2,1,0:T(8,128)S(1)} %get-tuple-element.39), channel_id=1, source_target_pairs={{0,8},{8,16},{16,24},{1,9},{9,17},{17,25},{2,10},{10,18},{18,26},{... | collective-permute-start | bytes 6248 | tf_op jit(solution)/shard_map/ppermute | solution.py:17
  186.3 2.3 collective-permute-done.33
  191.3 5.8 %collective-permute-start.35 = (f32[1,130,130]{2,1,0:T(8,128)S(1)}, f32[1,130,130]{2,1,0:T(8,128)S(1)}, u32[]{:S(2)}, u32[]{:S(2)}) collective-permute-start(f32[1,130,130]{2,1,0:T(8,128)S(1)} %get-tuple-element.25), channel_id=1, source_target_pairs={{0,1},{1,2},{2,3},{3,4},{4,5},{5,6},{6,7},{8,9},{9,10},{10,11},{11... | collective-permute-start | bytes 202808 | tf_op jit(solution)/shard_map/ppermute | solution.py:17
  199.8 2.9 %collective-permute-start.36 = (f32[4,1,128]{2,1,0:T(1,128)S(1)}, f32[4,1,128]{2,1,0:T(1,128)S(1)}, u32[]{:S(2)}, u32[]{:S(2)}) collective-permute-start(f32[4,1,128]{2,1,0:T(1,128)S(1)} %get-tuple-element.52), channel_id=1, source_target_pairs={{0,32},{32,64},{64,96},{96,128},{128,160},{160,192},{192,224},{224... | collective-permute-start | bytes 6152 | tf_op jit(solution)/shard_map/ppermute | solution.py:17
  204.6 2.3 collective-permute-done.37
  207.1 1.9 collective-permute-start.39
  209.1 6.7 %collective-permute-start.38 = (f32[4,130,1]{2,1,0:T(8,128)S(1)}, f32[4,130,1]{2,1,0:T(8,128)S(1)}, u32[]{:S(2)}, u32[]{:S(2)}) collective-permute-start(f32[4,130,1]{2,1,0:T(8,128)S(1)} %get-tuple-element.37), channel_id=1, source_target_pairs={{0,8},{8,16},{16,24},{1,9},{9,17},{17,25},{2,10},{10,18},{18,26},{... | collective-permute-start | bytes 6248 | tf_op jit(solution)/shard_map/ppermute | solution.py:17
  215.8 2.3 collective-permute-done.39
  220.7 5.9 %collective-permute-start.41 = (f32[1,130,130]{2,1,0:T(8,128)S(1)}, f32[1,130,130]{2,1,0:T(8,128)S(1)}, u32[]{:S(2)}, u32[]{:S(2)}) collective-permute-start(f32[1,130,130]{2,1,0:T(8,128)S(1)} %get-tuple-element.23), channel_id=1, source_target_pairs={{0,1},{1,2},{2,3},{3,4},{4,5},{5,6},{6,7},{8,9},{9,10},{10,11},{11... | collective-permute-start | bytes 202808 | tf_op jit(solution)/shard_map/ppermute | solution.py:17
  229.3 2.8 %gather_fusion = f32[1024,128]{1,0:T(8,128)S(1)} fusion(f32[512,128]{1,0:T(8,128)S(1)} %bitcast.58, s32[1024]{0:T(1024)S(1)} %broadcast_clamp_fusion), kind=kCustom, calls=%fused_computation | custom fusion | bytes 1052672 | tf_op jit(solution)/shard_map/jit(_take)/gather | solution.py:126
  233.3 19.0 %all-to-all-start.2 = ((f32[64,16,128]{2,1,0:T(8,128)}), f32[64,16,128]{2,1,0:T(8,128)S(1)}, u32[]{:S(2)}, u32[]{:S(2)}) async-start(f32[64,16,128]{2,1,0:T(8,128)} %select_multiply_fusion), calls=%async_computation.2 | async-start | bytes 1048576 | tf_op jit(solution)/shard_map/all_to_all | solution.py:48
  252.3 18.0 %all-to-all-done.2 = f32[64,16,128]{2,1,0:T(8,128)S(1)} async-done(((f32[64,16,128]{2,1,0:T(8,128)}), f32[64,16,128]{2,1,0:T(8,128)S(1)}, u32[]{:S(2)}, u32[]{:S(2)}) %all-to-all-start.2) | async-done | bytes 524320 | tf_op jit(solution)/shard_map/all_to_all | solution.py:48
  (143 shorter events, 54.2 us)
Async XLA Ops:
  0.7 32.2 %copy-start.3 = (f32[4,128,128]{2,1,0:T(8,128)S(1)}, f32[4,128,128]{2,1,0:T(8,128)}, u32[]{:S(2)}) copy-start(f32[4,128,128]{2,1,0:T(8,128)} %param.13) | copy-start | bytes 786436
  0.7 32.2 %copy-start.1 = (f32[3,4,128,128]{3,2,1,0:T(8,128)S(1)}, f32[3,4,128,128]{3,2,1,0:T(8,128)}, u32[]{:S(2)}) copy-start(f32[3,4,128,128]{3,2,1,0:T(8,128)} %param.11) | copy-start | bytes 2359300
  0.7 32.2 %copy-start.12 = (s32[1,1,1,512]{3,2,1,0:T(1,128)S(1)}, s32[1,1,1,512]{3,2,1,0:T(1,128)}, u32[]{:S(2)}) copy-start(s32[1,1,1,512]{3,2,1,0:T(1,128)} %param.17) | copy-start | bytes 6148
  1.6 52.1 %collective-permute-start.5 = (f32[4,1,128]{2,1,0:T(1,128)S(1)}, f32[4,1,128]{2,1,0:T(1,128)S(1)}, u32[]{:S(2)}, u32[]{:S(2)}) collective-permute-start(f32[4,1,128]{2,1,0:T(1,128)S(1)} %get-tuple-element.64), channel_id=1, source_target_pairs={{0,32},{32,64},{64,96},{96,128},{128,160},{160,192},{192,224},{224... | collective-permute-start | bytes 6152 | tf_op jit(solution)/shard_map/ppermute | solution.py:17
  5.6 48.1 %collective-permute-start.6 = (f32[4,1,128]{2,1,0:T(1,128)S(1)}, f32[4,1,128]{2,1,0:T(1,128)S(1)}, u32[]{:S(2)}, u32[]{:S(2)}) collective-permute-start(f32[4,1,128]{2,1,0:T(1,128)S(1)} %get-tuple-element.65), channel_id=1, source_target_pairs={{32,0},{64,32},{96,64},{128,96},{160,128},{192,160},{224,192},{256... | collective-permute-start | bytes 6152 | tf_op jit(solution)/shard_map/ppermute | solution.py:19
  13.9 23.3 %all-to-all-start = ((s32[64,1,16]{2,1,0:T(1,128)}), s32[64,1,16]{2,1,0:T(1,128)S(1)}, u32[]{:S(2)}, u32[]{:S(2)}) async-start(s32[64,1,16]{2,1,0:T(1,128)} %bitcast.8), calls=%async_computation | async-start | bytes 65536 | tf_op jit(solution)/shard_map/all_to_all | solution.py:41
  27.6 9.5 %collective-permute-start.1 = (f32[4,1,128]{2,1,0:T(1,128)S(1)}, f32[4,1,128]{2,1,0:T(1,128)S(1)}, u32[]{:S(2)}, u32[]{:S(2)}) collective-permute-start(f32[4,1,128]{2,1,0:T(1,128)S(1)} %get-tuple-element.62), channel_id=1, source_target_pairs={{32,0},{64,32},{96,64},{128,96},{160,128},{192,160},{224,192},{256... | collective-permute-start | bytes 6152 | tf_op jit(solution)/shard_map/ppermute | solution.py:19
  28.9 8.2 %collective-permute-start = (f32[4,1,128]{2,1,0:T(1,128)S(1)}, f32[4,1,128]{2,1,0:T(1,128)S(1)}, u32[]{:S(2)}, u32[]{:S(2)}) collective-permute-start(f32[4,1,128]{2,1,0:T(1,128)S(1)} %get-tuple-element.63), channel_id=1, source_target_pairs={{0,32},{32,64},{64,96},{96,128},{128,160},{160,192},{192,224},{224... | collective-permute-start | bytes 6152 | tf_op jit(solution)/shard_map/ppermute | solution.py:17
  37.1 41.1 %all-to-all-start.1 = ((f32[64,16,128]{2,1,0:T(8,128)}), f32[64,16,128]{2,1,0:T(8,128)S(1)}, u32[]{:S(2)}, u32[]{:S(2)}) async-start(f32[64,16,128]{2,1,0:T(8,128)} %bitcast.12), calls=%async_computation.1 | async-start | bytes 1048576 | tf_op jit(solution)/shard_map/all_to_all | solution.py:40
  48.2 11.3 %collective-permute-start.2 = (f32[4,130,1]{2,1,0:T(8,128)S(1)}, f32[4,130,1]{2,1,0:T(8,128)S(1)}, u32[]{:S(2)}, u32[]{:S(2)}) collective-permute-start(f32[4,130,1]{2,1,0:T(8,128)S(1)} %get-tuple-element.46), channel_id=1, source_target_pairs={{0,8},{8,16},{16,24},{1,9},{9,17},{17,25},{2,10},{10,18},{18,26},{... | collective-permute-start | bytes 6248 | tf_op jit(solution)/shard_map/ppermute | solution.py:17
  51.8 10.4 %collective-permute-start.3 = (f32[4,130,1]{2,1,0:T(8,128)S(1)}, f32[4,130,1]{2,1,0:T(8,128)S(1)}, u32[]{:S(2)}, u32[]{:S(2)}) collective-permute-start(f32[4,130,1]{2,1,0:T(8,128)S(1)} %get-tuple-element.47), channel_id=1, source_target_pairs={{8,0},{16,8},{24,16},{9,1},{17,9},{25,17},{10,2},{18,10},{26,18},{... | collective-permute-start | bytes 6248 | tf_op jit(solution)/shard_map/ppermute | solution.py:19
  53.9 15.0 %collective-permute-start.8 = (f32[4,130,1]{2,1,0:T(8,128)S(1)}, f32[4,130,1]{2,1,0:T(8,128)S(1)}, u32[]{:S(2)}, u32[]{:S(2)}) collective-permute-start(f32[4,130,1]{2,1,0:T(8,128)S(1)} %get-tuple-element.48), channel_id=1, source_target_pairs={{8,0},{16,8},{24,16},{9,1},{17,9},{25,17},{10,2},{18,10},{26,18},{... | collective-permute-start | bytes 6248 | tf_op jit(solution)/shard_map/ppermute | solution.py:19
  55.8 13.1 %collective-permute-start.7 = (f32[4,130,1]{2,1,0:T(8,128)S(1)}, f32[4,130,1]{2,1,0:T(8,128)S(1)}, u32[]{:S(2)}, u32[]{:S(2)}) collective-permute-start(f32[4,130,1]{2,1,0:T(8,128)S(1)} %get-tuple-element.49), channel_id=1, source_target_pairs={{0,8},{8,16},{16,24},{1,9},{9,17},{17,25},{2,10},{10,18},{18,26},{... | collective-permute-start | bytes 6248 | tf_op jit(solution)/shard_map/ppermute | solution.py:17
  63.0 14.9 %collective-permute-start.10 = (f32[1,130,130]{2,1,0:T(8,128)}, f32[1,130,130]{2,1,0:T(8,128)}, u32[]{:S(2)}, u32[]{:S(2)}) collective-permute-start(f32[1,130,130]{2,1,0:T(8,128)} %get-tuple-element.32), channel_id=1, source_target_pairs={{0,1},{1,2},{2,3},{3,4},{4,5},{5,6},{6,7},{8,9},{9,10},{10,11},{11... | collective-permute-start | bytes 202808 | tf_op jit(solution)/shard_map/ppermute | solution.py:17
  67.7 10.2 %collective-permute-start.4 = (f32[1,130,130]{2,1,0:T(8,128)S(1)}, f32[1,130,130]{2,1,0:T(8,128)}, u32[]{:S(2)}, u32[]{:S(2)}) collective-permute-start(f32[1,130,130]{2,1,0:T(8,128)S(1)} %get-tuple-element.33), channel_id=1, source_target_pairs={{1,0},{2,1},{3,2},{4,3},{5,4},{6,5},{7,6},{9,8},{10,9},{11,10},{12... | collective-permute-start | bytes 202808 | tf_op jit(solution)/shard_map/ppermute | solution.py:19
  69.9 8.0 %collective-permute-start.9 = (f32[1,130,130]{2,1,0:T(8,128)}, f32[1,130,130]{2,1,0:T(8,128)S(1)}, u32[]{:S(2)}, u32[]{:S(2)}) collective-permute-start(f32[1,130,130]{2,1,0:T(8,128)} %get-tuple-element.34), channel_id=1, source_target_pairs={{1,0},{2,1},{3,2},{4,3},{5,4},{6,5},{7,6},{9,8},{10,9},{11,10},{12... | collective-permute-start | bytes 202808 | tf_op jit(solution)/shard_map/ppermute | solution.py:19
  71.2 7.0 %collective-permute-start.11 = (f32[1,130,130]{2,1,0:T(8,128)}, f32[1,130,130]{2,1,0:T(8,128)S(1)}, u32[]{:S(2)}, u32[]{:S(2)}) collective-permute-start(f32[1,130,130]{2,1,0:T(8,128)} %get-tuple-element.35), channel_id=1, source_target_pairs={{0,1},{1,2},{2,3},{3,4},{4,5},{5,6},{6,7},{8,9},{9,10},{10,11},{11... | collective-permute-start | bytes 202808 | tf_op jit(solution)/shard_map/ppermute | solution.py:17
  82.9 3.9 %collective-permute-start.12 = (f32[4,1,128]{2,1,0:T(1,128)S(1)}, f32[4,1,128]{2,1,0:T(1,128)S(1)}, u32[]{:S(2)}, u32[]{:S(2)}) collective-permute-start(f32[4,1,128]{2,1,0:T(1,128)S(1)} %get-tuple-element.60), channel_id=1, source_target_pairs={{0,32},{32,64},{64,96},{96,128},{128,160},{160,192},{192,224},{224... | collective-permute-start | bytes 6152 | tf_op jit(solution)/shard_map/ppermute | solution.py:17
  85.5 4.6 %collective-permute-start.13 = (f32[4,1,128]{2,1,0:T(1,128)S(1)}, f32[4,1,128]{2,1,0:T(1,128)S(1)}, u32[]{:S(2)}, u32[]{:S(2)}) collective-permute-start(f32[4,1,128]{2,1,0:T(1,128)S(1)} %get-tuple-element.61), channel_id=1, source_target_pairs={{32,0},{64,32},{96,64},{128,96},{160,128},{192,160},{224,192},{256... | collective-permute-start | bytes 6152 | tf_op jit(solution)/shard_map/ppermute | solution.py:19
  90.3 8.2 %collective-permute-start.15 = (f32[4,130,1]{2,1,0:T(8,128)S(1)}, f32[4,130,1]{2,1,0:T(8,128)S(1)}, u32[]{:S(2)}, u32[]{:S(2)}) collective-permute-start(f32[4,130,1]{2,1,0:T(8,128)S(1)} %get-tuple-element.44), channel_id=1, source_target_pairs={{8,0},{16,8},{24,16},{9,1},{17,9},{25,17},{10,2},{18,10},{26,18},{... | collective-permute-start | bytes 6248 | tf_op jit(solution)/shard_map/ppermute | solution.py:19
  92.2 7.5 %collective-permute-start.14 = (f32[4,130,1]{2,1,0:T(8,128)S(1)}, f32[4,130,1]{2,1,0:T(8,128)S(1)}, u32[]{:S(2)}, u32[]{:S(2)}) collective-permute-start(f32[4,130,1]{2,1,0:T(8,128)S(1)} %get-tuple-element.45), channel_id=1, source_target_pairs={{0,8},{8,16},{16,24},{1,9},{9,17},{17,25},{2,10},{10,18},{18,26},{... | collective-permute-start | bytes 6248 | tf_op jit(solution)/shard_map/ppermute | solution.py:17
  99.9 6.4 %collective-permute-start.16 = (f32[1,130,130]{2,1,0:T(8,128)S(1)}, f32[1,130,130]{2,1,0:T(8,128)S(1)}, u32[]{:S(2)}, u32[]{:S(2)}) collective-permute-start(f32[1,130,130]{2,1,0:T(8,128)S(1)} %get-tuple-element.30), channel_id=1, source_target_pairs={{1,0},{2,1},{3,2},{4,3},{5,4},{6,5},{7,6},{9,8},{10,9},{11,10},{12... | collective-permute-start | bytes 202808 | tf_op jit(solution)/shard_map/ppermute | solution.py:19
  101.2 6.6 %collective-permute-start.17 = (f32[1,130,130]{2,1,0:T(8,128)S(1)}, f32[1,130,130]{2,1,0:T(8,128)S(1)}, u32[]{:S(2)}, u32[]{:S(2)}) collective-permute-start(f32[1,130,130]{2,1,0:T(8,128)S(1)} %get-tuple-element.31), channel_id=1, source_target_pairs={{0,1},{1,2},{2,3},{3,4},{4,5},{5,6},{6,7},{8,9},{9,10},{10,11},{11... | collective-permute-start | bytes 202808 | tf_op jit(solution)/shard_map/ppermute | solution.py:17
  108.5 4.9 %collective-permute-start.18 = (f32[4,1,128]{2,1,0:T(1,128)S(1)}, f32[4,1,128]{2,1,0:T(1,128)S(1)}, u32[]{:S(2)}, u32[]{:S(2)}) collective-permute-start(f32[4,1,128]{2,1,0:T(1,128)S(1)} %get-tuple-element.58), channel_id=1, source_target_pairs={{0,32},{32,64},{64,96},{96,128},{128,160},{160,192},{192,224},{224... | collective-permute-start | bytes 6152 | tf_op jit(solution)/shard_map/ppermute | solution.py:17
  112.1 4.4 %collective-permute-start.19 = (f32[4,1,128]{2,1,0:T(1,128)S(1)}, f32[4,1,128]{2,1,0:T(1,128)S(1)}, u32[]{:S(2)}, u32[]{:S(2)}) collective-permute-start(f32[4,1,128]{2,1,0:T(1,128)S(1)} %get-tuple-element.59), channel_id=1, source_target_pairs={{32,0},{64,32},{96,64},{128,96},{160,128},{192,160},{224,192},{256... | collective-permute-start | bytes 6152 | tf_op jit(solution)/shard_map/ppermute | solution.py:19
  116.7 10.8 %collective-permute-start.21 = (f32[4,130,1]{2,1,0:T(8,128)S(1)}, f32[4,130,1]{2,1,0:T(8,128)S(1)}, u32[]{:S(2)}, u32[]{:S(2)}) collective-permute-start(f32[4,130,1]{2,1,0:T(8,128)S(1)} %get-tuple-element.42), channel_id=1, source_target_pairs={{8,0},{16,8},{24,16},{9,1},{17,9},{25,17},{10,2},{18,10},{26,18},{... | collective-permute-start | bytes 6248 | tf_op jit(solution)/shard_map/ppermute | solution.py:19
  118.7 10.1 %collective-permute-start.20 = (f32[4,130,1]{2,1,0:T(8,128)S(1)}, f32[4,130,1]{2,1,0:T(8,128)S(1)}, u32[]{:S(2)}, u32[]{:S(2)}) collective-permute-start(f32[4,130,1]{2,1,0:T(8,128)S(1)} %get-tuple-element.43), channel_id=1, source_target_pairs={{0,8},{8,16},{16,24},{1,9},{9,17},{17,25},{2,10},{10,18},{18,26},{... | collective-permute-start | bytes 6248 | tf_op jit(solution)/shard_map/ppermute | solution.py:17
  128.9 7.4 %collective-permute-start.22 = (f32[1,130,130]{2,1,0:T(8,128)S(1)}, f32[1,130,130]{2,1,0:T(8,128)S(1)}, u32[]{:S(2)}, u32[]{:S(2)}) collective-permute-start(f32[1,130,130]{2,1,0:T(8,128)S(1)} %get-tuple-element.28), channel_id=1, source_target_pairs={{1,0},{2,1},{3,2},{4,3},{5,4},{6,5},{7,6},{9,8},{10,9},{11,10},{12... | collective-permute-start | bytes 202808 | tf_op jit(solution)/shard_map/ppermute | solution.py:19
  130.2 7.6 %collective-permute-start.23 = (f32[1,130,130]{2,1,0:T(8,128)S(1)}, f32[1,130,130]{2,1,0:T(8,128)S(1)}, u32[]{:S(2)}, u32[]{:S(2)}) collective-permute-start(f32[1,130,130]{2,1,0:T(8,128)S(1)} %get-tuple-element.29), channel_id=1, source_target_pairs={{0,1},{1,2},{2,3},{3,4},{4,5},{5,6},{6,7},{8,9},{9,10},{10,11},{11... | collective-permute-start | bytes 202808 | tf_op jit(solution)/shard_map/ppermute | solution.py:17
  138.5 6.0 %collective-permute-start.24 = (f32[4,1,128]{2,1,0:T(1,128)S(1)}, f32[4,1,128]{2,1,0:T(1,128)S(1)}, u32[]{:S(2)}, u32[]{:S(2)}) collective-permute-start(f32[4,1,128]{2,1,0:T(1,128)S(1)} %get-tuple-element.56), channel_id=1, source_target_pairs={{0,32},{32,64},{64,96},{96,128},{128,160},{160,192},{192,224},{224... | collective-permute-start | bytes 6152 | tf_op jit(solution)/shard_map/ppermute | solution.py:17
  143.1 4.6 %collective-permute-start.25 = (f32[4,1,128]{2,1,0:T(1,128)S(1)}, f32[4,1,128]{2,1,0:T(1,128)S(1)}, u32[]{:S(2)}, u32[]{:S(2)}) collective-permute-start(f32[4,1,128]{2,1,0:T(1,128)S(1)} %get-tuple-element.57), channel_id=1, source_target_pairs={{32,0},{64,32},{96,64},{128,96},{160,128},{192,160},{224,192},{256... | collective-permute-start | bytes 6152 | tf_op jit(solution)/shard_map/ppermute | solution.py:19
  147.9 10.6 %collective-permute-start.27 = (f32[4,130,1]{2,1,0:T(8,128)S(1)}, f32[4,130,1]{2,1,0:T(8,128)S(1)}, u32[]{:S(2)}, u32[]{:S(2)}) collective-permute-start(f32[4,130,1]{2,1,0:T(8,128)S(1)} %get-tuple-element.40), channel_id=1, source_target_pairs={{8,0},{16,8},{24,16},{9,1},{17,9},{25,17},{10,2},{18,10},{26,18},{... | collective-permute-start | bytes 6248 | tf_op jit(solution)/shard_map/ppermute | solution.py:19
  149.9 9.9 %collective-permute-start.26 = (f32[4,130,1]{2,1,0:T(8,128)S(1)}, f32[4,130,1]{2,1,0:T(8,128)S(1)}, u32[]{:S(2)}, u32[]{:S(2)}) collective-permute-start(f32[4,130,1]{2,1,0:T(8,128)S(1)} %get-tuple-element.41), channel_id=1, source_target_pairs={{0,8},{8,16},{16,24},{1,9},{9,17},{17,25},{2,10},{10,18},{18,26},{... | collective-permute-start | bytes 6248 | tf_op jit(solution)/shard_map/ppermute | solution.py:17
  159.9 7.3 %collective-permute-start.28 = (f32[1,130,130]{2,1,0:T(8,128)S(1)}, f32[1,130,130]{2,1,0:T(8,128)S(1)}, u32[]{:S(2)}, u32[]{:S(2)}) collective-permute-start(f32[1,130,130]{2,1,0:T(8,128)S(1)} %get-tuple-element.26), channel_id=1, source_target_pairs={{1,0},{2,1},{3,2},{4,3},{5,4},{6,5},{7,6},{9,8},{10,9},{11,10},{12... | collective-permute-start | bytes 202808 | tf_op jit(solution)/shard_map/ppermute | solution.py:19
  161.4 7.5 %collective-permute-start.29 = (f32[1,130,130]{2,1,0:T(8,128)S(1)}, f32[1,130,130]{2,1,0:T(8,128)S(1)}, u32[]{:S(2)}, u32[]{:S(2)}) collective-permute-start(f32[1,130,130]{2,1,0:T(8,128)S(1)} %get-tuple-element.27), channel_id=1, source_target_pairs={{0,1},{1,2},{2,3},{3,4},{4,5},{5,6},{6,7},{8,9},{9,10},{10,11},{11... | collective-permute-start | bytes 202808 | tf_op jit(solution)/shard_map/ppermute | solution.py:17
  169.6 4.9 %collective-permute-start.30 = (f32[4,1,128]{2,1,0:T(1,128)S(1)}, f32[4,1,128]{2,1,0:T(1,128)S(1)}, u32[]{:S(2)}, u32[]{:S(2)}) collective-permute-start(f32[4,1,128]{2,1,0:T(1,128)S(1)} %get-tuple-element.54), channel_id=1, source_target_pairs={{0,32},{32,64},{64,96},{96,128},{128,160},{160,192},{192,224},{224... | collective-permute-start | bytes 6152 | tf_op jit(solution)/shard_map/ppermute | solution.py:17
  173.2 4.3 %collective-permute-start.31 = (f32[4,1,128]{2,1,0:T(1,128)S(1)}, f32[4,1,128]{2,1,0:T(1,128)S(1)}, u32[]{:S(2)}, u32[]{:S(2)}) collective-permute-start(f32[4,1,128]{2,1,0:T(1,128)S(1)} %get-tuple-element.55), channel_id=1, source_target_pairs={{32,0},{64,32},{96,64},{128,96},{160,128},{192,160},{224,192},{256... | collective-permute-start | bytes 6152 | tf_op jit(solution)/shard_map/ppermute | solution.py:19
  177.7 10.9 %collective-permute-start.33 = (f32[4,130,1]{2,1,0:T(8,128)S(1)}, f32[4,130,1]{2,1,0:T(8,128)S(1)}, u32[]{:S(2)}, u32[]{:S(2)}) collective-permute-start(f32[4,130,1]{2,1,0:T(8,128)S(1)} %get-tuple-element.38), channel_id=1, source_target_pairs={{8,0},{16,8},{24,16},{9,1},{17,9},{25,17},{10,2},{18,10},{26,18},{... | collective-permute-start | bytes 6248 | tf_op jit(solution)/shard_map/ppermute | solution.py:19
  179.6 10.2 %collective-permute-start.32 = (f32[4,130,1]{2,1,0:T(8,128)S(1)}, f32[4,130,1]{2,1,0:T(8,128)S(1)}, u32[]{:S(2)}, u32[]{:S(2)}) collective-permute-start(f32[4,130,1]{2,1,0:T(8,128)S(1)} %get-tuple-element.39), channel_id=1, source_target_pairs={{0,8},{8,16},{16,24},{1,9},{9,17},{17,25},{2,10},{10,18},{18,26},{... | collective-permute-start | bytes 6248 | tf_op jit(solution)/shard_map/ppermute | solution.py:17
  190.0 7.6 %collective-permute-start.34 = (f32[1,130,130]{2,1,0:T(8,128)S(1)}, f32[1,130,130]{2,1,0:T(8,128)S(1)}, u32[]{:S(2)}, u32[]{:S(2)}) collective-permute-start(f32[1,130,130]{2,1,0:T(8,128)S(1)} %get-tuple-element.24), channel_id=1, source_target_pairs={{1,0},{2,1},{3,2},{4,3},{5,4},{6,5},{7,6},{9,8},{10,9},{11,10},{12... | collective-permute-start | bytes 202808 | tf_op jit(solution)/shard_map/ppermute | solution.py:19
  191.3 7.8 %collective-permute-start.35 = (f32[1,130,130]{2,1,0:T(8,128)S(1)}, f32[1,130,130]{2,1,0:T(8,128)S(1)}, u32[]{:S(2)}, u32[]{:S(2)}) collective-permute-start(f32[1,130,130]{2,1,0:T(8,128)S(1)} %get-tuple-element.25), channel_id=1, source_target_pairs={{0,1},{1,2},{2,3},{3,4},{4,5},{5,6},{6,7},{8,9},{9,10},{10,11},{11... | collective-permute-start | bytes 202808 | tf_op jit(solution)/shard_map/ppermute | solution.py:17
  199.8 4.9 %collective-permute-start.36 = (f32[4,1,128]{2,1,0:T(1,128)S(1)}, f32[4,1,128]{2,1,0:T(1,128)S(1)}, u32[]{:S(2)}, u32[]{:S(2)}) collective-permute-start(f32[4,1,128]{2,1,0:T(1,128)S(1)} %get-tuple-element.52), channel_id=1, source_target_pairs={{0,32},{32,64},{64,96},{96,128},{128,160},{160,192},{192,224},{224... | collective-permute-start | bytes 6152 | tf_op jit(solution)/shard_map/ppermute | solution.py:17
  202.6 4.3 %collective-permute-start.37 = (f32[4,1,128]{2,1,0:T(1,128)S(1)}, f32[4,1,128]{2,1,0:T(1,128)S(1)}, u32[]{:S(2)}, u32[]{:S(2)}) collective-permute-start(f32[4,1,128]{2,1,0:T(1,128)S(1)} %get-tuple-element.53), channel_id=1, source_target_pairs={{32,0},{64,32},{96,64},{128,96},{160,128},{192,160},{224,192},{256... | collective-permute-start | bytes 6152 | tf_op jit(solution)/shard_map/ppermute | solution.py:19
  207.1 10.9 %collective-permute-start.39 = (f32[4,130,1]{2,1,0:T(8,128)S(1)}, f32[4,130,1]{2,1,0:T(8,128)S(1)}, u32[]{:S(2)}, u32[]{:S(2)}) collective-permute-start(f32[4,130,1]{2,1,0:T(8,128)S(1)} %get-tuple-element.36), channel_id=1, source_target_pairs={{8,0},{16,8},{24,16},{9,1},{17,9},{25,17},{10,2},{18,10},{26,18},{... | collective-permute-start | bytes 6248 | tf_op jit(solution)/shard_map/ppermute | solution.py:19
  209.1 10.2 %collective-permute-start.38 = (f32[4,130,1]{2,1,0:T(8,128)S(1)}, f32[4,130,1]{2,1,0:T(8,128)S(1)}, u32[]{:S(2)}, u32[]{:S(2)}) collective-permute-start(f32[4,130,1]{2,1,0:T(8,128)S(1)} %get-tuple-element.37), channel_id=1, source_target_pairs={{0,8},{8,16},{16,24},{1,9},{9,17},{17,25},{2,10},{10,18},{18,26},{... | collective-permute-start | bytes 6248 | tf_op jit(solution)/shard_map/ppermute | solution.py:17
  219.4 7.7 %collective-permute-start.40 = (f32[1,130,130]{2,1,0:T(8,128)S(1)}, f32[1,130,130]{2,1,0:T(8,128)S(1)}, u32[]{:S(2)}, u32[]{:S(2)}) collective-permute-start(f32[1,130,130]{2,1,0:T(8,128)S(1)} %get-tuple-element.22), channel_id=1, source_target_pairs={{1,0},{2,1},{3,2},{4,3},{5,4},{6,5},{7,6},{9,8},{10,9},{11,10},{12... | collective-permute-start | bytes 202808 | tf_op jit(solution)/shard_map/ppermute | solution.py:19
  220.7 7.9 %collective-permute-start.41 = (f32[1,130,130]{2,1,0:T(8,128)S(1)}, f32[1,130,130]{2,1,0:T(8,128)S(1)}, u32[]{:S(2)}, u32[]{:S(2)}) collective-permute-start(f32[1,130,130]{2,1,0:T(8,128)S(1)} %get-tuple-element.23), channel_id=1, source_target_pairs={{0,1},{1,2},{2,3},{3,4},{4,5},{5,6},{6,7},{8,9},{9,10},{10,11},{11... | collective-permute-start | bytes 202808 | tf_op jit(solution)/shard_map/ppermute | solution.py:17
  233.3 37.0 %all-to-all-start.2 = ((f32[64,16,128]{2,1,0:T(8,128)}), f32[64,16,128]{2,1,0:T(8,128)S(1)}, u32[]{:S(2)}, u32[]{:S(2)}) async-start(f32[64,16,128]{2,1,0:T(8,128)} %select_multiply_fusion), calls=%async_computation.2 | async-start | bytes 1048576 | tf_op jit(solution)/shard_map/all_to_all | solution.py:48
  (16 other events, 234.9 us)
where the time goes:
time: 278 us; the launch traced here: 273 us
  starting transfers between devices  175 us (63%)
  waiting for transfers between devices  63.3 us (23%)
  other arithmetic  15.7 us (6%)
  local copies, waits for them, and re-layouts  13.7 us (5%)
  matrix products  4.01 us (1%)
    ppermute x21, starting transfers between devices, with_halo(): lax.ppermute(tail, axis, [(i, (i + 1) % count) for i in range(ends)])  99.7 us
    ppermute x21, starting transfers between devices, with_halo(): lax.ppermute(head, axis, [((i + 1) % count, i) for i in range(ends)])  31.7 us
    ppermute x21, waiting for transfers between devices, with_halo(): lax.ppermute(head, axis, [((i + 1) % count, i) for i in range(ends)])  31.5 us
    all_to_all x1, starting transfers between devices, send_back(): lax.all_to_all(replies, ('gx', 'gy'), split_axis=0, concat_axis=0, tiled=...  19 us
    all_to_all x1, waiting for transfers between devices, send_back(): lax.all_to_all(replies, ('gx', 'gy'), split_axis=0, concat_axis=0, tiled=...  18 us
    ppermute x21, waiting for transfers between devices, with_halo(): lax.ppermute(tail, axis, [(i, (i + 1) % count) for i in range(ends)])  13.9 us
    all_to_all x1, starting transfers between devices, send_heat(): lax.all_to_all(labels, ('gx', 'gy'), split_axis=0, concat_axis=0, tiled=T...  13.4 us
    all_to_all x1, starting transfers between devices, send_heat(): lax.all_to_all(outgoing, ('gx', 'gy'), split_axis=0, concat_axis=0, tiled...  11 us
  transfers between devices with their start and end apart: 45, of which 28 were waited for; matrix products, arithmetic and copies ran while one was open for 6% of the time, Pallas kernels for 0%

commit v1 on v0

--- a/solution.py
+++ b/solution.py
@@ -75,9 +75,9 @@
     heat_rows = heat.reshape(nrows, width)
     owners = owner.reshape(nrows)
     targets = block.reshape(nrows)
-    member = (owners[:, None] == jnp.arange(peers, dtype=jnp.int32)[None, :]).astype(jnp.int32)
-    earlier = jnp.cumsum(member, axis=0) - member
-    position = jnp.sum(earlier * member, axis=1)
+    order = jnp.arange(nrows, dtype=jnp.int32)
+    earlier = (owners[:, None] == owners[None, :]) & (order[None, :] < order[:, None])
+    position = jnp.sum(earlier.astype(jnp.int32), axis=1)
     destination = owners * slots + position
     nblocks = material.size
     outgoing = jnp.zeros((peers * slots, width), jnp.float32).at[destination].set(heat_rows)

time: 278 us -> 277 us (level)
  transfers between devices with their start and end apart: 45 -> 45, of which waited for: 28 -> 27; matrix products, arithmetic and copies ran while one was open for 6% -> 5% of each run, Pallas kernels for 0% -> 0%
where the time goes in v1:
time: 277 us; the launch traced here: 272 us
  starting transfers between devices  174 us (63%)
  waiting for transfers between devices  63.7 us (23%)
  other arithmetic  14.5 us (5%)
  local copies, waits for them, and re-layouts  14.4 us (5%)
  matrix products  4 us (1%)
    ppermute x21, starting transfers between devices, with_halo(): lax.ppermute(tail, axis, [(i, (i + 1) % count) for i in range(ends)])  99.1 us
    ppermute x21, waiting for transfers between devices, with_halo(): lax.ppermute(head, axis, [((i + 1) % count, i) for i in range(ends)])  32.3 us
    ppermute x21, starting transfers between devices, with_halo(): lax.ppermute(head, axis, [((i + 1) % count, i) for i in range(ends)])  31.5 us
    all_to_all x1, starting transfers between devices, send_back(): lax.all_to_all(replies, ('gx', 'gy'), split_axis=0, concat_axis=0, tiled=...  19 us
    all_to_all x1, waiting for transfers between devices, send_back(): lax.all_to_all(replies, ('gx', 'gy'), split_axis=0, concat_axis=0, tiled=...  18 us
    ppermute x21, waiting for transfers between devices, with_halo(): lax.ppermute(tail, axis, [(i, (i + 1) % count) for i in range(ends)])  13.4 us
    all_to_all x1, starting transfers between devices, send_heat(): lax.all_to_all(labels, ('gx', 'gy'), split_axis=0, concat_axis=0, tiled=T...  13.4 us
    all_to_all x1, starting transfers between devices, send_heat(): lax.all_to_all(outgoing, ('gx', 'gy'), split_axis=0, concat_axis=0, tiled...  11 us
  transfers between devices with their start and end apart: 45, of which 27 were waited for; matrix products, arithmetic and copies ran while one was open for 5% of the time, Pallas kernels for 0%

profile of v1, /device:TPU:1, one launch (start us, length us, event | category | flops | bytes accessed | tf_op | source)
XLA Modules:
  0.0 272.1 jit_solution(12853593905723033028)
XLA Ops:
  1.4 4.0 %collective-permute-start.5 = (f32[4,1,128]{2,1,0:T(1,128)S(1)}, f32[4,1,128]{2,1,0:T(1,128)S(1)}, u32[]{:S(2)}, u32[]{:S(2)}) collective-permute-start(f32[4,1,128]{2,1,0:T(1,128)S(1)} %get-tuple-element.64), channel_id=1, source_target_pairs={{0,32},{32,64},{64,96},{96,128},{128,160},{160,192},{192,224},{224... | collective-permute-start | bytes 6152 | tf_op jit(solution)/shard_map/ppermute | solution.py:17
  8.5 2.6 scatter_custom_fusion
  11.8 13.4 %all-to-all-start = ((s32[64,1,16]{2,1,0:T(1,128)}), s32[64,1,16]{2,1,0:T(1,128)S(1)}, u32[]{:S(2)}, u32[]{:S(2)}) async-start(s32[64,1,16]{2,1,0:T(1,128)} %bitcast.6), calls=%async_computation | async-start | bytes 65536 | tf_op jit(solution)/shard_map/all_to_all | solution.py:41
  29.0 4.0 %collective-permute-start = (f32[4,1,128]{2,1,0:T(1,128)S(1)}, f32[4,1,128]{2,1,0:T(1,128)S(1)}, u32[]{:S(2)}, u32[]{:S(2)}) collective-permute-start(f32[4,1,128]{2,1,0:T(1,128)S(1)} %get-tuple-element.63), channel_id=1, source_target_pairs={{0,32},{32,64},{64,96},{96,128},{128,160},{160,192},{192,224},{224... | collective-permute-start | bytes 6152 | tf_op jit(solution)/shard_map/ppermute | solution.py:17
  34.9 2.5 scatter_custom_fusion.1
  37.4 11.0 %all-to-all-start.1 = ((f32[64,16,128]{2,1,0:T(8,128)}), f32[64,16,128]{2,1,0:T(8,128)S(1)}, u32[]{:S(2)}, u32[]{:S(2)}) async-start(f32[64,16,128]{2,1,0:T(8,128)} %bitcast.10), calls=%async_computation.1 | async-start | bytes 1048576 | tf_op jit(solution)/shard_map/all_to_all | solution.py:40
  48.5 3.5 %collective-permute-start.2 = (f32[4,130,1]{2,1,0:T(8,128)S(1)}, f32[4,130,1]{2,1,0:T(8,128)S(1)}, u32[]{:S(2)}, u32[]{:S(2)}) collective-permute-start(f32[4,130,1]{2,1,0:T(8,128)S(1)} %get-tuple-element.46), channel_id=1, source_target_pairs={{0,8},{8,16},{16,24},{1,9},{9,17},{17,25},{2,10},{10,18},{18,26},{... | collective-permute-start | bytes 6248 | tf_op jit(solution)/shard_map/ppermute | solution.py:17
  52.1 1.9 collective-permute-start.3
  54.2 1.9 collective-permute-start.8
  56.2 3.6 %collective-permute-start.7 = (f32[4,130,1]{2,1,0:T(8,128)S(1)}, f32[4,130,1]{2,1,0:T(8,128)S(1)}, u32[]{:S(2)}, u32[]{:S(2)}) collective-permute-start(f32[4,130,1]{2,1,0:T(8,128)S(1)} %get-tuple-element.49), channel_id=1, source_target_pairs={{0,8},{8,16},{16,24},{1,9},{9,17},{17,25},{2,10},{10,18},{18,26},{... | collective-permute-start | bytes 6248 | tf_op jit(solution)/shard_map/ppermute | solution.py:17
  59.8 2.7 collective-permute-done.3
  62.7 4.0 %collective-permute-start.10 = (f32[1,130,130]{2,1,0:T(8,128)S(1)}, f32[1,130,130]{2,1,0:T(8,128)S(1)}, u32[]{:S(2)}, u32[]{:S(2)}) collective-permute-start(f32[1,130,130]{2,1,0:T(8,128)S(1)} %get-tuple-element.32), channel_id=1, source_target_pairs={{0,1},{1,2},{2,3},{3,4},{4,5},{5,6},{6,7},{8,9},{9,10},{10,11},{11... | collective-permute-start | bytes 202808 | tf_op jit(solution)/shard_map/ppermute | solution.py:17
  69.6 5.9 %collective-permute-start.11 = (f32[1,130,130]{2,1,0:T(8,128)S(1)}, f32[1,130,130]{2,1,0:T(8,128)}, u32[]{:S(2)}, u32[]{:S(2)}) collective-permute-start(f32[1,130,130]{2,1,0:T(8,128)S(1)} %get-tuple-element.35), channel_id=1, source_target_pairs={{0,1},{1,2},{2,3},{3,4},{4,5},{5,6},{6,7},{8,9},{9,10},{10,11},{11... | collective-permute-start | bytes 202808 | tf_op jit(solution)/shard_map/ppermute | solution.py:17
  78.2 4.0 %fusion.168 = (f32[4,128,128]{2,1,0:T(8,128)S(1)}, f32[4,128,128]{2,1,0:T(8,128)S(1)}, f32[4,128,128]{2,1,0:T(8,128)S(1)}, f32[4,128,128]{2,1,0:T(8,128)S(1)}, f...) fusion(f32[4,128,128]{2,1,0:T(8,128)S(1)} %copy-done.2, ...), kind=kOutput, calls=%fused_computation.359 | convolution fusion | flops 810942464 | bytes 3178688 | tf_op jit(solution)/shard_map/dot_general | solution.py:87
  82.2 2.6 collective-permute-start.12
  86.2 3.3 %collective-permute-done.13 = f32[4,1,128]{2,1,0:T(1,128)S(1)} collective-permute-done((f32[4,1,128]{2,1,0:T(1,128)S(1)}, f32[4,1,128]{2,1,0:T(1,128)S(1)}, u32[]{:S(2)}, u32[]{:S(2)}) %collective-permute-start.13) | collective-permute-done | bytes 2080 | tf_op jit(solution)/shard_map/ppermute | solution.py:19
  89.7 1.9 collective-permute-start.15
  91.6 3.6 %collective-permute-start.14 = (f32[4,130,1]{2,1,0:T(8,128)S(1)}, f32[4,130,1]{2,1,0:T(8,128)S(1)}, u32[]{:S(2)}, u32[]{:S(2)}) collective-permute-start(f32[4,130,1]{2,1,0:T(8,128)S(1)} %get-tuple-element.45), channel_id=1, source_target_pairs={{0,8},{8,16},{16,24},{1,9},{9,17},{17,25},{2,10},{10,18},{18,26},{... | collective-permute-start | bytes 6248 | tf_op jit(solution)/shard_map/ppermute | solution.py:17
  95.2 2.3 collective-permute-done.15
  100.2 4.0 %collective-permute-start.17 = (f32[1,130,130]{2,1,0:T(8,128)S(1)}, f32[1,130,130]{2,1,0:T(8,128)S(1)}, u32[]{:S(2)}, u32[]{:S(2)}) collective-permute-start(f32[1,130,130]{2,1,0:T(8,128)S(1)} %get-tuple-element.31), channel_id=1, source_target_pairs={{0,1},{1,2},{2,3},{3,4},{4,5},{5,6},{6,7},{8,9},{9,10},{10,11},{11... | collective-permute-start | bytes 202808 | tf_op jit(solution)/shard_map/ppermute | solution.py:17
  104.7 1.5 collective-permute-done.17
  106.9 3.4 %collective-permute-start.18 = (f32[4,1,128]{2,1,0:T(1,128)S(1)}, f32[4,1,128]{2,1,0:T(1,128)S(1)}, u32[]{:S(2)}, u32[]{:S(2)}) collective-permute-start(f32[4,1,128]{2,1,0:T(1,128)S(1)} %get-tuple-element.58), channel_id=1, source_target_pairs={{0,32},{32,64},{64,96},{96,128},{128,160},{160,192},{192,224},{224... | collective-permute-start | bytes 6152 | tf_op jit(solution)/shard_map/ppermute | solution.py:17
  111.5 3.4 %collective-permute-done.19 = f32[4,1,128]{2,1,0:T(1,128)S(1)} collective-permute-done((f32[4,1,128]{2,1,0:T(1,128)S(1)}, f32[4,1,128]{2,1,0:T(1,128)S(1)}, u32[]{:S(2)}, u32[]{:S(2)}) %collective-permute-start.19) | collective-permute-done | bytes 2080 | tf_op jit(solution)/shard_map/ppermute | solution.py:19
  115.1 1.9 collective-permute-start.21
  117.0 6.7 %collective-permute-start.20 = (f32[4,130,1]{2,1,0:T(8,128)S(1)}, f32[4,130,1]{2,1,0:T(8,128)S(1)}, u32[]{:S(2)}, u32[]{:S(2)}) collective-permute-start(f32[4,130,1]{2,1,0:T(8,128)S(1)} %get-tuple-element.43), channel_id=1, source_target_pairs={{0,8},{8,16},{16,24},{1,9},{9,17},{17,25},{2,10},{10,18},{18,26},{... | collective-permute-start | bytes 6248 | tf_op jit(solution)/shard_map/ppermute | solution.py:17
  123.7 2.3 collective-permute-done.21
  128.7 5.6 %collective-permute-start.23 = (f32[1,130,130]{2,1,0:T(8,128)S(1)}, f32[1,130,130]{2,1,0:T(8,128)S(1)}, u32[]{:S(2)}, u32[]{:S(2)}) collective-permute-start(f32[1,130,130]{2,1,0:T(8,128)S(1)} %get-tuple-element.29), channel_id=1, source_target_pairs={{0,1},{1,2},{2,3},{3,4},{4,5},{5,6},{6,7},{8,9},{9,10},{10,11},{11... | collective-permute-start | bytes 202808 | tf_op jit(solution)/shard_map/ppermute | solution.py:17
  136.9 4.6 %collective-permute-start.24 = (f32[4,1,128]{2,1,0:T(1,128)S(1)}, f32[4,1,128]{2,1,0:T(1,128)S(1)}, u32[]{:S(2)}, u32[]{:S(2)}) collective-permute-start(f32[4,1,128]{2,1,0:T(1,128)S(1)} %get-tuple-element.56), channel_id=1, source_target_pairs={{0,32},{32,64},{64,96},{96,128},{128,160},{160,192},{192,224},{224... | collective-permute-start | bytes 6152 | tf_op jit(solution)/shard_map/ppermute | solution.py:17
  142.8 3.3 %collective-permute-done.25 = f32[4,1,128]{2,1,0:T(1,128)S(1)} collective-permute-done((f32[4,1,128]{2,1,0:T(1,128)S(1)}, f32[4,1,128]{2,1,0:T(1,128)S(1)}, u32[]{:S(2)}, u32[]{:S(2)}) %collective-permute-start.25) | collective-permute-done | bytes 2080 | tf_op jit(solution)/shard_map/ppermute | solution.py:19
  146.3 1.9 collective-permute-start.27
  148.2 6.4 %collective-permute-start.26 = (f32[4,130,1]{2,1,0:T(8,128)S(1)}, f32[4,130,1]{2,1,0:T(8,128)S(1)}, u32[]{:S(2)}, u32[]{:S(2)}) collective-permute-start(f32[4,130,1]{2,1,0:T(8,128)S(1)} %get-tuple-element.41), channel_id=1, source_target_pairs={{0,8},{8,16},{16,24},{1,9},{9,17},{17,25},{2,10},{10,18},{18,26},{... | collective-permute-start | bytes 6248 | tf_op jit(solution)/shard_map/ppermute | solution.py:17
  154.6 2.3 collective-permute-done.27
  159.5 5.5 %collective-permute-start.29 = (f32[1,130,130]{2,1,0:T(8,128)S(1)}, f32[1,130,130]{2,1,0:T(8,128)S(1)}, u32[]{:S(2)}, u32[]{:S(2)}) collective-permute-start(f32[1,130,130]{2,1,0:T(8,128)S(1)} %get-tuple-element.27), channel_id=1, source_target_pairs={{0,1},{1,2},{2,3},{3,4},{4,5},{5,6},{6,7},{8,9},{9,10},{10,11},{11... | collective-permute-start | bytes 202808 | tf_op jit(solution)/shard_map/ppermute | solution.py:17
  167.5 3.6 %collective-permute-start.30 = (f32[4,1,128]{2,1,0:T(1,128)S(1)}, f32[4,1,128]{2,1,0:T(1,128)S(1)}, u32[]{:S(2)}, u32[]{:S(2)}) collective-permute-start(f32[4,1,128]{2,1,0:T(1,128)S(1)} %get-tuple-element.54), channel_id=1, source_target_pairs={{0,32},{32,64},{64,96},{96,128},{128,160},{160,192},{192,224},{224... | collective-permute-start | bytes 6152 | tf_op jit(solution)/shard_map/ppermute | solution.py:17
  172.5 3.0 %collective-permute-done.31 = f32[4,1,128]{2,1,0:T(1,128)S(1)} collective-permute-done((f32[4,1,128]{2,1,0:T(1,128)S(1)}, f32[4,1,128]{2,1,0:T(1,128)S(1)}, u32[]{:S(2)}, u32[]{:S(2)}) %collective-permute-start.31) | collective-permute-done | bytes 2080 | tf_op jit(solution)/shard_map/ppermute | solution.py:19
  175.7 1.9 collective-permute-start.33
  177.6 6.7 %collective-permute-start.32 = (f32[4,130,1]{2,1,0:T(8,128)S(1)}, f32[4,130,1]{2,1,0:T(8,128)S(1)}, u32[]{:S(2)}, u32[]{:S(2)}) collective-permute-start(f32[4,130,1]{2,1,0:T(8,128)S(1)} %get-tuple-element.39), channel_id=1, source_target_pairs={{0,8},{8,16},{16,24},{1,9},{9,17},{17,25},{2,10},{10,18},{18,26},{... | collective-permute-start | bytes 6248 | tf_op jit(solution)/shard_map/ppermute | solution.py:17
  184.3 2.3 collective-permute-done.33
  189.3 5.9 %collective-permute-start.35 = (f32[1,130,130]{2,1,0:T(8,128)S(1)}, f32[1,130,130]{2,1,0:T(8,128)S(1)}, u32[]{:S(2)}, u32[]{:S(2)}) collective-permute-start(f32[1,130,130]{2,1,0:T(8,128)S(1)} %get-tuple-element.25), channel_id=1, source_target_pairs={{0,1},{1,2},{2,3},{3,4},{4,5},{5,6},{6,7},{8,9},{9,10},{10,11},{11... | collective-permute-start | bytes 202808 | tf_op jit(solution)/shard_map/ppermute | solution.py:17
  197.9 2.9 %collective-permute-start.36 = (f32[4,1,128]{2,1,0:T(1,128)S(1)}, f32[4,1,128]{2,1,0:T(1,128)S(1)}, u32[]{:S(2)}, u32[]{:S(2)}) collective-permute-start(f32[4,1,128]{2,1,0:T(1,128)S(1)} %get-tuple-element.52), channel_id=1, source_target_pairs={{0,32},{32,64},{64,96},{96,128},{128,160},{160,192},{192,224},{224... | collective-permute-start | bytes 6152 | tf_op jit(solution)/shard_map/ppermute | solution.py:17
  202.1 2.9 %collective-permute-done.37 = f32[4,1,128]{2,1,0:T(1,128)S(1)} collective-permute-done((f32[4,1,128]{2,1,0:T(1,128)S(1)}, f32[4,1,128]{2,1,0:T(1,128)S(1)}, u32[]{:S(2)}, u32[]{:S(2)}) %collective-permute-start.37) | collective-permute-done | bytes 2080 | tf_op jit(solution)/shard_map/ppermute | solution.py:19
  205.2 1.9 collective-permute-start.39
  207.2 6.7 %collective-permute-start.38 = (f32[4,130,1]{2,1,0:T(8,128)S(1)}, f32[4,130,1]{2,1,0:T(8,128)S(1)}, u32[]{:S(2)}, u32[]{:S(2)}) collective-permute-start(f32[4,130,1]{2,1,0:T(8,128)S(1)} %get-tuple-element.37), channel_id=1, source_target_pairs={{0,8},{8,16},{16,24},{1,9},{9,17},{17,25},{2,10},{10,18},{18,26},{... | collective-permute-start | bytes 6248 | tf_op jit(solution)/shard_map/ppermute | solution.py:17
  213.9 2.3 collective-permute-done.39
  218.8 5.9 %collective-permute-start.41 = (f32[1,130,130]{2,1,0:T(8,128)S(1)}, f32[1,130,130]{2,1,0:T(8,128)S(1)}, u32[]{:S(2)}, u32[]{:S(2)}) collective-permute-start(f32[1,130,130]{2,1,0:T(8,128)S(1)} %get-tuple-element.23), channel_id=1, source_target_pairs={{0,1},{1,2},{2,3},{3,4},{4,5},{5,6},{6,7},{8,9},{9,10},{10,11},{11... | collective-permute-start | bytes 202808 | tf_op jit(solution)/shard_map/ppermute | solution.py:17
  227.4 2.8 %gather_fusion = f32[1024,128]{1,0:T(8,128)S(1)} fusion(f32[512,128]{1,0:T(8,128)S(1)} %bitcast.38, s32[1024]{0:T(1024)S(1)} %broadcast_clamp_fusion), kind=kCustom, calls=%fused_computation | custom fusion | bytes 1052672 | tf_op jit(solution)/shard_map/jit(_take)/gather | solution.py:126
  231.4 19.0 %all-to-all-start.2 = ((f32[64,16,128]{2,1,0:T(8,128)}), f32[64,16,128]{2,1,0:T(8,128)S(1)}, u32[]{:S(2)}, u32[]{:S(2)}) async-start(f32[64,16,128]{2,1,0:T(8,128)} %select_multiply_fusion), calls=%async_computation.2 | async-start | bytes 1048576 | tf_op jit(solution)/shard_map/all_to_all | solution.py:48
  250.4 18.0 %all-to-all-done.2 = f32[64,16,128]{2,1,0:T(8,128)S(1)} async-done(((f32[64,16,128]{2,1,0:T(8,128)}), f32[64,16,128]{2,1,0:T(8,128)S(1)}, u32[]{:S(2)}, u32[]{:S(2)}) %all-to-all-start.2) | async-done | bytes 524320 | tf_op jit(solution)/shard_map/all_to_all | solution.py:48
  (134 shorter events, 53.2 us)
Async XLA Ops:
  0.6 32.4 %copy-start.3 = (f32[4,128,128]{2,1,0:T(8,128)S(1)}, f32[4,128,128]{2,1,0:T(8,128)}, u32[]{:S(2)}) copy-start(f32[4,128,128]{2,1,0:T(8,128)} %param.13) | copy-start | bytes 786436
  0.6 32.4 %copy-start.5 = (f32[4,128,128]{2,1,0:T(8,128)S(1)}, f32[4,128,128]{2,1,0:T(8,128)}, u32[]{:S(2)}) copy-start(f32[4,128,128]{2,1,0:T(8,128)} %param.12) | copy-start | bytes 786436
  1.4 52.6 %collective-permute-start.5 = (f32[4,1,128]{2,1,0:T(1,128)S(1)}, f32[4,1,128]{2,1,0:T(1,128)S(1)}, u32[]{:S(2)}, u32[]{:S(2)}) collective-permute-start(f32[4,1,128]{2,1,0:T(1,128)S(1)} %get-tuple-element.64), channel_id=1, source_target_pairs={{0,32},{32,64},{64,96},{96,128},{128,160},{160,192},{192,224},{224... | collective-permute-start | bytes 6152 | tf_op jit(solution)/shard_map/ppermute | solution.py:17
  5.5 48.6 %collective-permute-start.6 = (f32[4,1,128]{2,1,0:T(1,128)S(1)}, f32[4,1,128]{2,1,0:T(1,128)S(1)}, u32[]{:S(2)}, u32[]{:S(2)}) collective-permute-start(f32[4,1,128]{2,1,0:T(1,128)S(1)} %get-tuple-element.65), channel_id=1, source_target_pairs={{32,0},{64,32},{96,64},{128,96},{160,128},{192,160},{224,192},{256... | collective-permute-start | bytes 6152 | tf_op jit(solution)/shard_map/ppermute | solution.py:19
  8.5 26.4 %copy-start.13 = (s32[512,1]{0,1:T(1,128)}, s32[512,1]{0,1:T(1,128)S(1)}, u32[]{:S(2)}) copy-start(s32[512,1]{0,1:T(1,128)S(1)} %compare_select_fusion.2) | copy-start | bytes 6148
  11.8 25.7 %all-to-all-start = ((s32[64,1,16]{2,1,0:T(1,128)}), s32[64,1,16]{2,1,0:T(1,128)S(1)}, u32[]{:S(2)}, u32[]{:S(2)}) async-start(s32[64,1,16]{2,1,0:T(1,128)} %bitcast.6), calls=%async_computation | async-start | bytes 65536 | tf_op jit(solution)/shard_map/all_to_all | solution.py:41
  27.7 9.7 %collective-permute-start.1 = (f32[4,1,128]{2,1,0:T(1,128)S(1)}, f32[4,1,128]{2,1,0:T(1,128)S(1)}, u32[]{:S(2)}, u32[]{:S(2)}) collective-permute-start(f32[4,1,128]{2,1,0:T(1,128)S(1)} %get-tuple-element.62), channel_id=1, source_target_pairs={{32,0},{64,32},{96,64},{128,96},{160,128},{192,160},{224,192},{256... | collective-permute-start | bytes 6152 | tf_op jit(solution)/shard_map/ppermute | solution.py:19
  29.0 8.4 %collective-permute-start = (f32[4,1,128]{2,1,0:T(1,128)S(1)}, f32[4,1,128]{2,1,0:T(1,128)S(1)}, u32[]{:S(2)}, u32[]{:S(2)}) collective-permute-start(f32[4,1,128]{2,1,0:T(1,128)S(1)} %get-tuple-element.63), channel_id=1, source_target_pairs={{0,32},{32,64},{64,96},{96,128},{128,160},{160,192},{192,224},{224... | collective-permute-start | bytes 6152 | tf_op jit(solution)/shard_map/ppermute | solution.py:17
  37.4 40.1 %all-to-all-start.1 = ((f32[64,16,128]{2,1,0:T(8,128)}), f32[64,16,128]{2,1,0:T(8,128)S(1)}, u32[]{:S(2)}, u32[]{:S(2)}) async-start(f32[64,16,128]{2,1,0:T(8,128)} %bitcast.10), calls=%async_computation.1 | async-start | bytes 1048576 | tf_op jit(solution)/shard_map/all_to_all | solution.py:40
  48.5 11.3 %collective-permute-start.2 = (f32[4,130,1]{2,1,0:T(8,128)S(1)}, f32[4,130,1]{2,1,0:T(8,128)S(1)}, u32[]{:S(2)}, u32[]{:S(2)}) collective-permute-start(f32[4,130,1]{2,1,0:T(8,128)S(1)} %get-tuple-element.46), channel_id=1, source_target_pairs={{0,8},{8,16},{16,24},{1,9},{9,17},{17,25},{2,10},{10,18},{18,26},{... | collective-permute-start | bytes 6248 | tf_op jit(solution)/shard_map/ppermute | solution.py:17
  52.1 10.4 %collective-permute-start.3 = (f32[4,130,1]{2,1,0:T(8,128)S(1)}, f32[4,130,1]{2,1,0:T(8,128)S(1)}, u32[]{:S(2)}, u32[]{:S(2)}) collective-permute-start(f32[4,130,1]{2,1,0:T(8,128)S(1)} %get-tuple-element.47), channel_id=1, source_target_pairs={{8,0},{16,8},{24,16},{9,1},{17,9},{25,17},{10,2},{18,10},{26,18},{... | collective-permute-start | bytes 6248 | tf_op jit(solution)/shard_map/ppermute | solution.py:19
  54.2 13.8 %collective-permute-start.8 = (f32[4,130,1]{2,1,0:T(8,128)S(1)}, f32[4,130,1]{2,1,0:T(8,128)S(1)}, u32[]{:S(2)}, u32[]{:S(2)}) collective-permute-start(f32[4,130,1]{2,1,0:T(8,128)S(1)} %get-tuple-element.48), channel_id=1, source_target_pairs={{8,0},{16,8},{24,16},{9,1},{17,9},{25,17},{10,2},{18,10},{26,18},{... | collective-permute-start | bytes 6248 | tf_op jit(solution)/shard_map/ppermute | solution.py:19
  56.2 11.9 %collective-permute-start.7 = (f32[4,130,1]{2,1,0:T(8,128)S(1)}, f32[4,130,1]{2,1,0:T(8,128)S(1)}, u32[]{:S(2)}, u32[]{:S(2)}) collective-permute-start(f32[4,130,1]{2,1,0:T(8,128)S(1)} %get-tuple-element.49), channel_id=1, source_target_pairs={{0,8},{8,16},{16,24},{1,9},{9,17},{17,25},{2,10},{10,18},{18,26},{... | collective-permute-start | bytes 6248 | tf_op jit(solution)/shard_map/ppermute | solution.py:17
  62.7 14.8 %collective-permute-start.10 = (f32[1,130,130]{2,1,0:T(8,128)S(1)}, f32[1,130,130]{2,1,0:T(8,128)S(1)}, u32[]{:S(2)}, u32[]{:S(2)}) collective-permute-start(f32[1,130,130]{2,1,0:T(8,128)S(1)} %get-tuple-element.32), channel_id=1, source_target_pairs={{0,1},{1,2},{2,3},{3,4},{4,5},{5,6},{6,7},{8,9},{9,10},{10,11},{11... | collective-permute-start | bytes 202808 | tf_op jit(solution)/shard_map/ppermute | solution.py:17
  66.7 10.8 %collective-permute-start.4 = (f32[1,130,130]{2,1,0:T(8,128)S(1)}, f32[1,130,130]{2,1,0:T(8,128)S(1)}, u32[]{:S(2)}, u32[]{:S(2)}) collective-permute-start(f32[1,130,130]{2,1,0:T(8,128)S(1)} %get-tuple-element.33), channel_id=1, source_target_pairs={{1,0},{2,1},{3,2},{4,3},{5,4},{6,5},{7,6},{9,8},{10,9},{11,10},{12... | collective-permute-start | bytes 202808 | tf_op jit(solution)/shard_map/ppermute | solution.py:19
  68.3 9.2 %collective-permute-start.9 = (f32[1,130,130]{2,1,0:T(8,128)S(1)}, f32[1,130,130]{2,1,0:T(8,128)}, u32[]{:S(2)}, u32[]{:S(2)}) collective-permute-start(f32[1,130,130]{2,1,0:T(8,128)S(1)} %get-tuple-element.34), channel_id=1, source_target_pairs={{1,0},{2,1},{3,2},{4,3},{5,4},{6,5},{7,6},{9,8},{10,9},{11,10},{12... | collective-permute-start | bytes 202808 | tf_op jit(solution)/shard_map/ppermute | solution.py:19
  69.6 8.0 %collective-permute-start.11 = (f32[1,130,130]{2,1,0:T(8,128)S(1)}, f32[1,130,130]{2,1,0:T(8,128)}, u32[]{:S(2)}, u32[]{:S(2)}) collective-permute-start(f32[1,130,130]{2,1,0:T(8,128)S(1)} %get-tuple-element.35), channel_id=1, source_target_pairs={{0,1},{1,2},{2,3},{3,4},{4,5},{5,6},{6,7},{8,9},{9,10},{10,11},{11... | collective-permute-start | bytes 202808 | tf_op jit(solution)/shard_map/ppermute | solution.py:17
  82.2 3.9 %collective-permute-start.12 = (f32[4,1,128]{2,1,0:T(1,128)S(1)}, f32[4,1,128]{2,1,0:T(1,128)S(1)}, u32[]{:S(2)}, u32[]{:S(2)}) collective-permute-start(f32[4,1,128]{2,1,0:T(1,128)S(1)} %get-tuple-element.60), channel_id=1, source_target_pairs={{0,32},{32,64},{64,96},{96,128},{128,160},{160,192},{192,224},{224... | collective-permute-start | bytes 6152 | tf_op jit(solution)/shard_map/ppermute | solution.py:17
  84.9 4.6 %collective-permute-start.13 = (f32[4,1,128]{2,1,0:T(1,128)S(1)}, f32[4,1,128]{2,1,0:T(1,128)S(1)}, u32[]{:S(2)}, u32[]{:S(2)}) collective-permute-start(f32[4,1,128]{2,1,0:T(1,128)S(1)} %get-tuple-element.61), channel_id=1, source_target_pairs={{32,0},{64,32},{96,64},{128,96},{160,128},{192,160},{224,192},{256... | collective-permute-start | bytes 6152 | tf_op jit(solution)/shard_map/ppermute | solution.py:19
  89.7 7.9 %collective-permute-start.15 = (f32[4,130,1]{2,1,0:T(8,128)S(1)}, f32[4,130,1]{2,1,0:T(8,128)S(1)}, u32[]{:S(2)}, u32[]{:S(2)}) collective-permute-start(f32[4,130,1]{2,1,0:T(8,128)S(1)} %get-tuple-element.44), channel_id=1, source_target_pairs={{8,0},{16,8},{24,16},{9,1},{17,9},{25,17},{10,2},{18,10},{26,18},{... | collective-permute-start | bytes 6248 | tf_op jit(solution)/shard_map/ppermute | solution.py:19
  91.6 7.1 %collective-permute-start.14 = (f32[4,130,1]{2,1,0:T(8,128)S(1)}, f32[4,130,1]{2,1,0:T(8,128)S(1)}, u32[]{:S(2)}, u32[]{:S(2)}) collective-permute-start(f32[4,130,1]{2,1,0:T(8,128)S(1)} %get-tuple-element.45), channel_id=1, source_target_pairs={{0,8},{8,16},{16,24},{1,9},{9,17},{17,25},{2,10},{10,18},{18,26},{... | collective-permute-start | bytes 6248 | tf_op jit(solution)/shard_map/ppermute | solution.py:17
  98.9 5.8 %collective-permute-start.16 = (f32[1,130,130]{2,1,0:T(8,128)S(1)}, f32[1,130,130]{2,1,0:T(8,128)S(1)}, u32[]{:S(2)}, u32[]{:S(2)}) collective-permute-start(f32[1,130,130]{2,1,0:T(8,128)S(1)} %get-tuple-element.30), channel_id=1, source_target_pairs={{1,0},{2,1},{3,2},{4,3},{5,4},{6,5},{7,6},{9,8},{10,9},{11,10},{12... | collective-permute-start | bytes 202808 | tf_op jit(solution)/shard_map/ppermute | solution.py:19
  100.2 6.0 %collective-permute-start.17 = (f32[1,130,130]{2,1,0:T(8,128)S(1)}, f32[1,130,130]{2,1,0:T(8,128)S(1)}, u32[]{:S(2)}, u32[]{:S(2)}) collective-permute-start(f32[1,130,130]{2,1,0:T(8,128)S(1)} %get-tuple-element.31), channel_id=1, source_target_pairs={{0,1},{1,2},{2,3},{3,4},{4,5},{5,6},{6,7},{8,9},{9,10},{10,11},{11... | collective-permute-start | bytes 202808 | tf_op jit(solution)/shard_map/ppermute | solution.py:17
  106.9 4.7 %collective-permute-start.18 = (f32[4,1,128]{2,1,0:T(1,128)S(1)}, f32[4,1,128]{2,1,0:T(1,128)S(1)}, u32[]{:S(2)}, u32[]{:S(2)}) collective-permute-start(f32[4,1,128]{2,1,0:T(1,128)S(1)} %get-tuple-element.58), channel_id=1, source_target_pairs={{0,32},{32,64},{64,96},{96,128},{128,160},{160,192},{192,224},{224... | collective-permute-start | bytes 6152 | tf_op jit(solution)/shard_map/ppermute | solution.py:17
  110.2 4.7 %collective-permute-start.19 = (f32[4,1,128]{2,1,0:T(1,128)S(1)}, f32[4,1,128]{2,1,0:T(1,128)S(1)}, u32[]{:S(2)}, u32[]{:S(2)}) collective-permute-start(f32[4,1,128]{2,1,0:T(1,128)S(1)} %get-tuple-element.59), channel_id=1, source_target_pairs={{32,0},{64,32},{96,64},{128,96},{160,128},{192,160},{224,192},{256... | collective-permute-start | bytes 6152 | tf_op jit(solution)/shard_map/ppermute | solution.py:19
  115.1 10.9 %collective-permute-start.21 = (f32[4,130,1]{2,1,0:T(8,128)S(1)}, f32[4,130,1]{2,1,0:T(8,128)S(1)}, u32[]{:S(2)}, u32[]{:S(2)}) collective-permute-start(f32[4,130,1]{2,1,0:T(8,128)S(1)} %get-tuple-element.42), channel_id=1, source_target_pairs={{8,0},{16,8},{24,16},{9,1},{17,9},{25,17},{10,2},{18,10},{26,18},{... | collective-permute-start | bytes 6248 | tf_op jit(solution)/shard_map/ppermute | solution.py:19
  117.0 10.2 %collective-permute-start.20 = (f32[4,130,1]{2,1,0:T(8,128)S(1)}, f32[4,130,1]{2,1,0:T(8,128)S(1)}, u32[]{:S(2)}, u32[]{:S(2)}) collective-permute-start(f32[4,130,1]{2,1,0:T(8,128)S(1)} %get-tuple-element.43), channel_id=1, source_target_pairs={{0,8},{8,16},{16,24},{1,9},{9,17},{17,25},{2,10},{10,18},{18,26},{... | collective-permute-start | bytes 6248 | tf_op jit(solution)/shard_map/ppermute | solution.py:17
  127.4 7.4 %collective-permute-start.22 = (f32[1,130,130]{2,1,0:T(8,128)S(1)}, f32[1,130,130]{2,1,0:T(8,128)S(1)}, u32[]{:S(2)}, u32[]{:S(2)}) collective-permute-start(f32[1,130,130]{2,1,0:T(8,128)S(1)} %get-tuple-element.28), channel_id=1, source_target_pairs={{1,0},{2,1},{3,2},{4,3},{5,4},{6,5},{7,6},{9,8},{10,9},{11,10},{12... | collective-permute-start | bytes 202808 | tf_op jit(solution)/shard_map/ppermute | solution.py:19
  128.7 7.6 %collective-permute-start.23 = (f32[1,130,130]{2,1,0:T(8,128)S(1)}, f32[1,130,130]{2,1,0:T(8,128)S(1)}, u32[]{:S(2)}, u32[]{:S(2)}) collective-permute-start(f32[1,130,130]{2,1,0:T(8,128)S(1)} %get-tuple-element.29), channel_id=1, source_target_pairs={{0,1},{1,2},{2,3},{3,4},{4,5},{5,6},{6,7},{8,9},{9,10},{10,11},{11... | collective-permute-start | bytes 202808 | tf_op jit(solution)/shard_map/ppermute | solution.py:17
  136.9 5.9 %collective-permute-start.24 = (f32[4,1,128]{2,1,0:T(1,128)S(1)}, f32[4,1,128]{2,1,0:T(1,128)S(1)}, u32[]{:S(2)}, u32[]{:S(2)}) collective-permute-start(f32[4,1,128]{2,1,0:T(1,128)S(1)} %get-tuple-element.56), channel_id=1, source_target_pairs={{0,32},{32,64},{64,96},{96,128},{128,160},{160,192},{192,224},{224... | collective-permute-start | bytes 6152 | tf_op jit(solution)/shard_map/ppermute | solution.py:17
  141.5 4.6 %collective-permute-start.25 = (f32[4,1,128]{2,1,0:T(1,128)S(1)}, f32[4,1,128]{2,1,0:T(1,128)S(1)}, u32[]{:S(2)}, u32[]{:S(2)}) collective-permute-start(f32[4,1,128]{2,1,0:T(1,128)S(1)} %get-tuple-element.57), channel_id=1, source_target_pairs={{32,0},{64,32},{96,64},{128,96},{160,128},{192,160},{224,192},{256... | collective-permute-start | bytes 6152 | tf_op jit(solution)/shard_map/ppermute | solution.py:19
  146.3 10.6 %collective-permute-start.27 = (f32[4,130,1]{2,1,0:T(8,128)S(1)}, f32[4,130,1]{2,1,0:T(8,128)S(1)}, u32[]{:S(2)}, u32[]{:S(2)}) collective-permute-start(f32[4,130,1]{2,1,0:T(8,128)S(1)} %get-tuple-element.40), channel_id=1, source_target_pairs={{8,0},{16,8},{24,16},{9,1},{17,9},{25,17},{10,2},{18,10},{26,18},{... | collective-permute-start | bytes 6248 | tf_op jit(solution)/shard_map/ppermute | solution.py:19
  148.2 9.9 %collective-permute-start.26 = (f32[4,130,1]{2,1,0:T(8,128)S(1)}, f32[4,130,1]{2,1,0:T(8,128)S(1)}, u32[]{:S(2)}, u32[]{:S(2)}) collective-permute-start(f32[4,130,1]{2,1,0:T(8,128)S(1)} %get-tuple-element.41), channel_id=1, source_target_pairs={{0,8},{8,16},{16,24},{1,9},{9,17},{17,25},{2,10},{10,18},{18,26},{... | collective-permute-start | bytes 6248 | tf_op jit(solution)/shard_map/ppermute | solution.py:17
  158.2 7.1 %collective-permute-start.28 = (f32[1,130,130]{2,1,0:T(8,128)S(1)}, f32[1,130,130]{2,1,0:T(8,128)S(1)}, u32[]{:S(2)}, u32[]{:S(2)}) collective-permute-start(f32[1,130,130]{2,1,0:T(8,128)S(1)} %get-tuple-element.26), channel_id=1, source_target_pairs={{1,0},{2,1},{3,2},{4,3},{5,4},{6,5},{7,6},{9,8},{10,9},{11,10},{12... | collective-permute-start | bytes 202808 | tf_op jit(solution)/shard_map/ppermute | solution.py:19
  159.5 7.3 %collective-permute-start.29 = (f32[1,130,130]{2,1,0:T(8,128)S(1)}, f32[1,130,130]{2,1,0:T(8,128)S(1)}, u32[]{:S(2)}, u32[]{:S(2)}) collective-permute-start(f32[1,130,130]{2,1,0:T(8,128)S(1)} %get-tuple-element.27), channel_id=1, source_target_pairs={{0,1},{1,2},{2,3},{3,4},{4,5},{5,6},{6,7},{8,9},{9,10},{10,11},{11... | collective-permute-start | bytes 202808 | tf_op jit(solution)/shard_map/ppermute | solution.py:17
  167.5 4.9 %collective-permute-start.30 = (f32[4,1,128]{2,1,0:T(1,128)S(1)}, f32[4,1,128]{2,1,0:T(1,128)S(1)}, u32[]{:S(2)}, u32[]{:S(2)}) collective-permute-start(f32[4,1,128]{2,1,0:T(1,128)S(1)} %get-tuple-element.54), channel_id=1, source_target_pairs={{0,32},{32,64},{64,96},{96,128},{128,160},{160,192},{192,224},{224... | collective-permute-start | bytes 6152 | tf_op jit(solution)/shard_map/ppermute | solution.py:17
  171.2 4.3 %collective-permute-start.31 = (f32[4,1,128]{2,1,0:T(1,128)S(1)}, f32[4,1,128]{2,1,0:T(1,128)S(1)}, u32[]{:S(2)}, u32[]{:S(2)}) collective-permute-start(f32[4,1,128]{2,1,0:T(1,128)S(1)} %get-tuple-element.55), channel_id=1, source_target_pairs={{32,0},{64,32},{96,64},{128,96},{160,128},{192,160},{224,192},{256... | collective-permute-start | bytes 6152 | tf_op jit(solution)/shard_map/ppermute | solution.py:19
  175.7 10.9 %collective-permute-start.33 = (f32[4,130,1]{2,1,0:T(8,128)S(1)}, f32[4,130,1]{2,1,0:T(8,128)S(1)}, u32[]{:S(2)}, u32[]{:S(2)}) collective-permute-start(f32[4,130,1]{2,1,0:T(8,128)S(1)} %get-tuple-element.38), channel_id=1, source_target_pairs={{8,0},{16,8},{24,16},{9,1},{17,9},{25,17},{10,2},{18,10},{26,18},{... | collective-permute-start | bytes 6248 | tf_op jit(solution)/shard_map/ppermute | solution.py:19
  177.6 10.2 %collective-permute-start.32 = (f32[4,130,1]{2,1,0:T(8,128)S(1)}, f32[4,130,1]{2,1,0:T(8,128)S(1)}, u32[]{:S(2)}, u32[]{:S(2)}) collective-permute-start(f32[4,130,1]{2,1,0:T(8,128)S(1)} %get-tuple-element.39), channel_id=1, source_target_pairs={{0,8},{8,16},{16,24},{1,9},{9,17},{17,25},{2,10},{10,18},{18,26},{... | collective-permute-start | bytes 6248 | tf_op jit(solution)/shard_map/ppermute | solution.py:17
  188.0 7.7 %collective-permute-start.34 = (f32[1,130,130]{2,1,0:T(8,128)S(1)}, f32[1,130,130]{2,1,0:T(8,128)S(1)}, u32[]{:S(2)}, u32[]{:S(2)}) collective-permute-start(f32[1,130,130]{2,1,0:T(8,128)S(1)} %get-tuple-element.24), channel_id=1, source_target_pairs={{1,0},{2,1},{3,2},{4,3},{5,4},{6,5},{7,6},{9,8},{10,9},{11,10},{12... | collective-permute-start | bytes 202808 | tf_op jit(solution)/shard_map/ppermute | solution.py:19
  189.3 7.9 %collective-permute-start.35 = (f32[1,130,130]{2,1,0:T(8,128)S(1)}, f32[1,130,130]{2,1,0:T(8,128)S(1)}, u32[]{:S(2)}, u32[]{:S(2)}) collective-permute-start(f32[1,130,130]{2,1,0:T(8,128)S(1)} %get-tuple-element.25), channel_id=1, source_target_pairs={{0,1},{1,2},{2,3},{3,4},{4,5},{5,6},{6,7},{8,9},{9,10},{10,11},{11... | collective-permute-start | bytes 202808 | tf_op jit(solution)/shard_map/ppermute | solution.py:17
  197.9 4.3 %collective-permute-start.36 = (f32[4,1,128]{2,1,0:T(1,128)S(1)}, f32[4,1,128]{2,1,0:T(1,128)S(1)}, u32[]{:S(2)}, u32[]{:S(2)}) collective-permute-start(f32[4,1,128]{2,1,0:T(1,128)S(1)} %get-tuple-element.52), channel_id=1, source_target_pairs={{0,32},{32,64},{64,96},{96,128},{128,160},{160,192},{192,224},{224... | collective-permute-start | bytes 6152 | tf_op jit(solution)/shard_map/ppermute | solution.py:17
  200.7 4.3 %collective-permute-start.37 = (f32[4,1,128]{2,1,0:T(1,128)S(1)}, f32[4,1,128]{2,1,0:T(1,128)S(1)}, u32[]{:S(2)}, u32[]{:S(2)}) collective-permute-start(f32[4,1,128]{2,1,0:T(1,128)S(1)} %get-tuple-element.53), channel_id=1, source_target_pairs={{32,0},{64,32},{96,64},{128,96},{160,128},{192,160},{224,192},{256... | collective-permute-start | bytes 6152 | tf_op jit(solution)/shard_map/ppermute | solution.py:19
  205.2 10.9 %collective-permute-start.39 = (f32[4,130,1]{2,1,0:T(8,128)S(1)}, f32[4,130,1]{2,1,0:T(8,128)S(1)}, u32[]{:S(2)}, u32[]{:S(2)}) collective-permute-start(f32[4,130,1]{2,1,0:T(8,128)S(1)} %get-tuple-element.36), channel_id=1, source_target_pairs={{8,0},{16,8},{24,16},{9,1},{17,9},{25,17},{10,2},{18,10},{26,18},{... | collective-permute-start | bytes 6248 | tf_op jit(solution)/shard_map/ppermute | solution.py:19
  207.2 10.2 %collective-permute-start.38 = (f32[4,130,1]{2,1,0:T(8,128)S(1)}, f32[4,130,1]{2,1,0:T(8,128)S(1)}, u32[]{:S(2)}, u32[]{:S(2)}) collective-permute-start(f32[4,130,1]{2,1,0:T(8,128)S(1)} %get-tuple-element.37), channel_id=1, source_target_pairs={{0,8},{8,16},{16,24},{1,9},{9,17},{17,25},{2,10},{10,18},{18,26},{... | collective-permute-start | bytes 6248 | tf_op jit(solution)/shard_map/ppermute | solution.py:17
  217.5 7.7 %collective-permute-start.40 = (f32[1,130,130]{2,1,0:T(8,128)S(1)}, f32[1,130,130]{2,1,0:T(8,128)S(1)}, u32[]{:S(2)}, u32[]{:S(2)}) collective-permute-start(f32[1,130,130]{2,1,0:T(8,128)S(1)} %get-tuple-element.22), channel_id=1, source_target_pairs={{1,0},{2,1},{3,2},{4,3},{5,4},{6,5},{7,6},{9,8},{10,9},{11,10},{12... | collective-permute-start | bytes 202808 | tf_op jit(solution)/shard_map/ppermute | solution.py:19
  218.8 7.9 %collective-permute-start.41 = (f32[1,130,130]{2,1,0:T(8,128)S(1)}, f32[1,130,130]{2,1,0:T(8,128)S(1)}, u32[]{:S(2)}, u32[]{:S(2)}) collective-permute-start(f32[1,130,130]{2,1,0:T(8,128)S(1)} %get-tuple-element.23), channel_id=1, source_target_pairs={{0,1},{1,2},{2,3},{3,4},{4,5},{5,6},{6,7},{8,9},{9,10},{10,11},{11... | collective-permute-start | bytes 202808 | tf_op jit(solution)/shard_map/ppermute | solution.py:17
  231.4 37.0 %all-to-all-start.2 = ((f32[64,16,128]{2,1,0:T(8,128)}), f32[64,16,128]{2,1,0:T(8,128)S(1)}, u32[]{:S(2)}, u32[]{:S(2)}) async-start(f32[64,16,128]{2,1,0:T(8,128)} %select_multiply_fusion), calls=%async_computation.2 | async-start | bytes 1048576 | tf_op jit(solution)/shard_map/all_to_all | solution.py:48
  (14 other events, 167.6 us)

commit v2 on v1

v2 whole, which is shorter than its diff:
```python
import functools

import jax
import jax.numpy as jnp
from jax import lax
from jax.experimental import pallas as pl
from jax.experimental.pallas import tpu as pltpu
from jax.sharding import PartitionSpec as P

SWEEPS = 6
THETA = 1.01
DELTA = 0.99
LANES = 128
EDGE = 8
F32 = jnp.float32
BF16 = jnp.bfloat16
I32 = jnp.int32


def steps():
    sigma = THETA / DELTA
    rho = 1.0 / sigma
    found = [(0.0, 1.0 / THETA)]
    for _ in range(SWEEPS - 1):
        rho_new = 1.0 / (2.0 * sigma - rho)
        found.append((rho_new * rho, 2.0 * rho_new / DELTA))
        rho = rho_new
    return found


def iota(shape, dim):
    return lax.broadcasted_iota(I32, shape, dim)


def dot(a, b, ca, cb):
    return lax.dot_general(a, b, (((ca,), (cb,)), ((), ())), preferred_element_type=F32)


def parts(v):
    high = v.astype(BF16)
    return high, (v - high.astype(F32)).astype(BF16)


def pick_rows(hot, rows):
    high, low = parts(rows)
    got = dot(hot, jnp.concatenate([high, low], axis=1), 1, 0)
    width = rows.shape[1]
    return got[:, :width] + got[:, width:]


def column(row):
    same = iota((LANES, LANES), 0) == iota((LANES, LANES), 1)
    found = []
    for at in range(0, row.shape[1], LANES):
        piece = jnp.broadcast_to(row[:, at : at + LANES], (LANES, LANES))
        found.append(jnp.sum(jnp.where(same, piece, 0), axis=1, keepdims=True))
    return jnp.concatenate(found, axis=0)


def hot_of(cond):
    return jnp.where(cond, F32(1.0), F32(0.0)).astype(BF16)


def edge_lanes():
    r, y = iota((2 * EDGE, LANES), 0), iota((2 * EDGE, LANES), 1)
    return hot_of(y == jnp.where(r < EDGE, r, r + LANES - 2 * EDGE))


def call(kernel, outs, ins, name, scratch=(), limit=32, flops=0, smem=()):
    bytes_of = lambda a: a.size * a.dtype.itemsize
    return pl.pallas_call(
        kernel,
        out_shape=[jax.ShapeDtypeStruct(s, t) for s, t in outs],
        in_specs=[
            pl.BlockSpec(memory_space=pltpu.SMEM if i in smem else pltpu.VMEM)
            for i in range(len(ins))
        ],
        out_specs=[pl.BlockSpec(memory_space=pltpu.VMEM) for _ in outs],
        scratch_shapes=list(scratch),
        compiler_params=pltpu.CompilerParams(vmem_limit_bytes=limit << 20),
        cost_estimate=pl.CostEstimate(
            flops=flops,
            bytes_accessed=sum(bytes_of(a) for a in ins)
            + sum(jax.ShapeDtypeStruct(s, t).size * 4 for s, t in outs),
            transcendentals=0,
        ),
        name=name,
    )(*ins)


def dispatch_kernel(peers, slots, ef, den, mob, owner, block, live, out):
    n = owner.shape[1]
    esq = ef[0] * ef[0] + ef[1] * ef[1] + ef[2] * ef[2]
    heat = 0.2 * den[...] * mob[...] * esq
    heat = jnp.where(iota(heat.shape, 1) < column(live[...]), heat, F32(0.0))
    own = owner[...]
    own_col = column(own)
    pos = jnp.zeros((1, n), I32)
    for at in range(0, n, LANES):
        r = iota((LANES, n), 0) + at
        earlier = (own_col[at : at + LANES] == own) & (r < iota((LANES, n), 1))
        pos = pos + jnp.sum(jnp.where(earlier, 1, 0), axis=0, keepdims=True)
    dest = own * (slots + 1) + pos
    hot = hot_of(iota((peers * (slots + 1), n), 0) == dest)
    out[...] = pick_rows(hot, heat)
    named = hot_of(iota((peers, n), 0) == own)
    at_slot = iota((LANES, n), 0) == pos
    code = block[...] + 1
    high = jnp.where(at_slot, code // 32, 0).astype(F32).astype(BF16)
    low = jnp.where(at_slot, code % 32, 0).astype(F32).astype(BF16)
    out[pl.ds(slots, peers, stride=slots + 1), :] = dot(named, high, 1, 1) * 32.0 + dot(named, low, 1, 1)


def after_kernel(slots, ef, owner, gain, dest):
    n = owner.shape[1]
    esq = ef[0] * ef[0] + ef[1] * ef[1] + ef[2] * ef[2]
    gain[...] = -2.0 * lax.rsqrt(esq + 1.0)
    own = owner[...]
    own_col = column(own)
    for at in range(0, n, LANES):
        r = iota((LANES, n), 0) + at
        piece = own_col[at : at + LANES]
        earlier = (piece == own) & (iota((LANES, n), 1) < r)
        pos = jnp.sum(jnp.where(earlier, 1, 0), axis=1, keepdims=True)
        dest[pl.ds(at, LANES), :] = jnp.broadcast_to(piece * slots + pos, (LANES, LANES))


def labels_of(received, peers, slots):
    got = received[pl.ds(slots, peers, stride=slots + 1), :]
    high = jnp.floor(got * (1.0 / 32.0))
    return high.astype(BF16), (got - 32.0 * high).astype(BF16)


def combine_kernel(peers, slots, far, received, source, first, last):
    n = source.shape[0]
    total = received.shape[0]
    high, low = labels_of(received, peers, slots)
    j = iota((LANES, total), 1)
    spread = hot_of(iota((LANES, total), 0) == j - (slots + 1) * lax.div(j, slots + 1))
    named = dot(high, spread, 1, 0) * 32.0 + dot(low, spread, 1, 0)
    mine = iota((peers, total), 0) == lax.div(iota((peers, total), 1), slots + 1)
    ids = jnp.sum(jnp.where(mine, named, 0.0), axis=0, keepdims=True).astype(I32)
    picks = hot_of(iota((n, total), 0) + 1 == ids)
    source[...] = pick_rows(picks, received[...])
    rows = far * (n // 4)
    first[...] = source[pl.ds(0, rows), :]
    last[...] = source[pl.ds(n - rows, rows), :]


def ids_kernel(peers, slots, received, ids):
    total = peers * slots
    high, low = labels_of(received, peers, slots)
    own = hot_of(lax.div(iota((total, peers), 0), slots) == iota((total, peers), 1))
    named = dot(own, high, 1, 0) * 32.0 + dot(own, low, 1, 0)
    i = iota((total, LANES), 0)
    mine = iota((total, LANES), 1) == i - slots * lax.div(i, slots)
    found = jnp.sum(jnp.where(mine, named, 0.0), axis=1, keepdims=True) - 1.0
    ids[...] = jnp.broadcast_to(found, (total, LANES)).astype(I32)


def start_z_kernel(far, x0, material, near, up, down):
    layers, xcells = material.shape
    n = layers * xcells
    mat = (material[...] + 1).astype(F32)
    rows = far * xcells
    zeros = lambda k: jnp.zeros((k, LANES), F32)
    near[pl.ds(0, n), :] = x0[...]
    near[pl.ds(n, EDGE), :] = jnp.concatenate([mat, zeros(EDGE - layers)], axis=0)
    up[pl.ds(0, rows), :] = x0[pl.ds(n - rows, rows), :]
    up[pl.ds(rows, EDGE), :] = jnp.concatenate([mat[layers - far :], zeros(EDGE - far)], axis=0)
    down[pl.ds(0, rows), :] = x0[pl.ds(0, rows), :]
    down[pl.ds(rows, EDGE), :] = jnp.concatenate([mat[:far], zeros(EDGE - far)], axis=0)


def layers_of(far, pieces):
    low2, low, own, high, high2 = pieces
    found = [(low2, k) for k in range(far)]
    for ref in (low, own, high):
        found += [(ref, k) for k in range(4)]
    return found + [(high2, k) for k in range(far)]


def start_x_kernel(far, low2, low, own, high, high2, xz, mats, xlow, xhigh):
    found = layers_of(far, (low2, low, own, high, high2))
    count = len(found)
    for k, (ref, at) in enumerate(found):
        piece = ref[pl.ds(at * LANES, LANES), :]
        xz[k] = piece
        xlow[pl.ds(k * EDGE, EDGE), :] = piece[:EDGE]
        xhigh[pl.ds(k * EDGE, EDGE), :] = piece[LANES - EDGE :]
        tail = ref.shape[0] - EDGE
        mats[pl.ds(k, 1), :] = ref[pl.ds(tail + at, 1), :]
    xlow[pl.ds(count * EDGE, count), :] = mats[...]
    xhigh[pl.ds(count * EDGE, count), :] = mats[...]


def start_y_kernel(xz, mats, after, before, xm, around, ylow, yhigh):
    count = xz.shape[0]
    for k in range(count):
        xm[k, pl.ds(0, LANES)] = xz[k]
        xm[k, pl.ds(LANES, EDGE)] = after[pl.ds(k * EDGE, EDGE), :]
        xm[k, pl.ds(LANES + EDGE, EDGE)] = before[pl.ds(k * EDGE, EDGE), :]
    around[pl.ds(0, count), :] = mats[...]
    around[pl.ds(count, count), :] = after[pl.ds(count * EDGE, count), :]
    around[pl.ds(2 * count, count), :] = before[pl.ds(count * EDGE, count), :]
    total = count * xm.shape[1]
    high, low = parts(xm[...].reshape(total, LANES))
    edges = edge_lanes()
    sides = dot(edges, high, 1, 1) + dot(edges, low, 1, 1)
    ylow[:, pl.ds(0, total)] = sides[:EDGE]
    yhigh[:, pl.ds(0, total)] = sides[EDGE:]
    for b in range(3 * count // EDGE):
        block = around[pl.ds(b * EDGE, EDGE), :]
        ylow[:, pl.ds(total + b * LANES, LANES)] = block
        yhigh[:, pl.ds(total + b * LANES, LANES)] = block


def turned(v, by, axis):
    return pltpu.roll(v, by % v.shape[axis], axis)


def east(m, s):
    last = iota(m.shape, 1) == LANES - 1
    rm, rs = turned(m, -1, 1), turned(s, -1, 1)
    return jnp.where(last, rs, rm), jnp.where(last, rm, rs)


def west(m, s):
    first = iota(m.shape, 1) == 0
    rm, rs = turned(m, 1, 1), turned(s, 1, 1)
    return jnp.where(first, rs, rm), jnp.where(first, rm, rs)


def weights_kernel(xm, around, left, right, base, soft, heat, xs, wz, wx, wy, inv, b0, cond, capf, flip):
    count, rows, _ = xm.shape
    total = count * rows
    edges = edge_lanes()
    high, low = parts(jnp.concatenate([right[:, :total], left[:, :total]], axis=0))
    xs[...] = (dot(high, edges, 0, 0) + dot(low, edges, 0, 0)).reshape(count, rows, LANES)
    depth = 3 * count

    def table(mat, values):
        found = jnp.zeros(mat.shape, F32)
        for m in range(values.shape[0]):
            found = jnp.where(mat == F32(m + 1), values[m], found)
        return found

    def unpacked(ref):
        return jnp.concatenate(
            [ref[:, pl.ds(total + b * LANES, LANES)] for b in range(depth // EDGE)], axis=0
        )

    pad = jnp.zeros((LANES - depth, LANES), F32)
    for i, mat in enumerate((around[...], unpacked(left), unpacked(right))):
        for j, values in enumerate((base, soft, heat)):
            flip[i, j] = jnp.transpose(jnp.concatenate([table(mat, values), pad], axis=0))

    def col(i, j, k):
        own = flip[i, j, :, pl.ds(k, 1)]
        after = flip[i, j, pl.ds(0, EDGE), pl.ds(count + k, 1)]
        before = flip[i, j, pl.ds(LANES - EDGE, EDGE), pl.ds(2 * count + k, 1)]
        return jnp.broadcast_to(jnp.concatenate([own, after, before], axis=0), (rows, LANES))

    hither = iota((rows, LANES), 1) < LANES // 2
    for k in range(count):
        cond[0, k] = col(0, 0, k) / (1.0 + col(0, 1, k) * xm[k])
        capf[0, k] = col(0, 2, k)
        side = [jnp.where(hither, col(2, j, k), col(1, j, k)) for j in range(3)]
        cond[1, k] = side[0] / (1.0 + side[1] * xs[k])
        capf[1, k] = side[2]

    wz[0, 0] = 0.5 * (cond[0, 0] + cond[0, 1])
    wz[0, 1] = 0.5 * (cond[1, 0] + cond[1, 1])

    @pl.loop(0, count - 2)
    def _(j):
        k = j + 1
        c = (cond[0, k], cond[1, k])
        e = east(*c)
        wyy = tuple(0.5 * (c[t] + e[t]) for t in range(2))
        w = west(*wyy)
        for t in range(2):
            up = 0.5 * (c[t] + cond[t, k + 1])
            wz[k, t] = up
            wxx = 0.5 * (c[t] + turned(c[t], -1, 0))
            wx[j, t] = wxx
            wy[j, t] = wyy[t]
            cf = capf[t, k]
            diag = cf + up + wz[j, t] + wxx + turned(wxx, 1, 0) + wyy[t] + w[t]
            i = jnp.where(cf > 0.0, 1.0 / diag, 0.0)
            inv[j, t] = i
            x = xm[k] if t == 0 else xs[k]
            b0[j, t] = cf * x * i


def source_x_kernel(far, low2, low, own, high, high2, xlow, xhigh):
    for k, (ref, at) in enumerate(layers_of(far, (low2, low, own, high, high2))):
        xlow[pl.ds(k * EDGE, EDGE), :] = ref[pl.ds(at * LANES, EDGE), :]
        xhigh[pl.ds(k * EDGE, EDGE), :] = ref[pl.ds((at + 1) * LANES - EDGE, EDGE), :]


def lay(found, after, before, put):
    for k, (ref, at) in enumerate(found):
        put(k, 0, LANES, ref[pl.ds(at * LANES, LANES), :])
        put(k, LANES, EDGE, after[pl.ds(k * EDGE, EDGE), :])
        put(k, LANES + EDGE, EDGE, before[pl.ds(k * EDGE, EDGE), :])


def source_y_kernel(far, low2, low, own, high, high2, after, before, ylow, yhigh, full):
    rows = LANES + 2 * EDGE

    def put(k, at, size, piece):
        full[pl.ds(k * rows + at, size), :] = piece

    lay(layers_of(far, (low2, low, own, high, high2)), after, before, put)
    big, small = parts(full[...])
    edges = edge_lanes()
    sides = dot(edges, big, 1, 1) + dot(edges, small, 1, 1)
    ylow[...] = sides[:EDGE]
    yhigh[...] = sides[EDGE:]


def sweep_kernel(far, xm, xs, wz, wx, wy, inv, b0, low2, low, own, high, high2, after, before, left, right, ids,
                 out, replies, b, d, xa, xb):
    count, rows, _ = xm.shape
    inner = count - 2

    def put(k, at, size, piece):
        part = pl.ds(at, size)
        b[k, 0, part] = b0[k, 0, part] + piece * inv[k, 0, part]

    lay(layers_of(far, (low2, low, own, high, high2)), after, before, put)
    edges = edge_lanes()
    big, small = parts(jnp.concatenate([right[...], left[...]], axis=0))
    side = dot(big, edges, 0, 0) + dot(small, edges, 0, 0)
    for k in range(inner):
        b[k, 1] = b0[k, 1] + side[k * rows : (k + 1) * rows] * inv[k, 1]

    for s, (keep, add) in enumerate(steps()):
        if s == 0:
            load = lambda k, t: xm[k] if t == 0 else xs[k]
        else:
            load = lambda k, t, src=(xa if s % 2 else xb): src[k, t]
        into = xb if s % 2 else xa

        @pl.loop(1 + s, count - 1 - s)
        def _(k):
            j = k - 1
            x = (load(k, 0), load(k, 1))
            e, w = east(*x), west(*x)
            we = (wy[j, 0], wy[j, 1])
            ww = west(*we)
            for t in range(2):
                wxx = wx[j, t]
                near = wz[k, t] * load(k + 1, t) + wz[k - 1, t] * load(k - 1, t)
                near += wxx * turned(x[t], -1, 0) + turned(wxx, 1, 0) * turned(x[t], 1, 0)
                near += we[t] * e[t] + ww[t] * w[t]
                step = add * (b[j, t] - x[t] + inv[j, t] * near)
                if s > 0:
                    step = step + keep * d[j, t]
                if s < SWEEPS - 1:
                    d[j, t] = step
                into[k, t] = x[t] + step

    final = xb if SWEEPS % 2 == 0 else xa
    for k in range(4):
        out[pl.ds(k * LANES, LANES), :] = final[SWEEPS + k, 0, pl.ds(0, LANES)]
    n = out.shape[0]
    name = ids[...]
    hot = jnp.concatenate([hot_of(name == iota(name.shape, 1) + at) for at in range(0, n, LANES)], axis=1)
    replies[...] = pick_rows(hot, out[...])


def final_kernel(returned, dest, gain, mob, mobility, ionization):
    total = returned.shape[0]
    name = dest[...]
    hot = jnp.concatenate([hot_of(name == iota(name.shape, 1) + at) for at in range(0, total, LANES)], axis=1)
    back = pick_rows(hot, returned[...])
    mobility[...] = mob[...] * jnp.exp(-0.7 * back)
    ionization[...] = jnp.exp(gain[...] * (1.0 + 0.3 * back))


def shifted(v, axis, by):
    count = lax.axis_size(axis)
    pairs = [(i, i + by) for i in range(count) if 0 <= i + by < count]
    return lax.ppermute(v, axis, pairs) if pairs else jnp.zeros_like(v)


def exchanged(v):
    lines = v.reshape(v.shape[0], 1, v.shape[1])
    return lax.all_to_all(lines, ("gx", "gy"), split_axis=0, concat_axis=0, tiled=True).reshape(v.shape)


def per_device(
    efield, density, mobility_prev, thermal_prev, owner, block, live, material,
    mat_conductivity, mat_softening, mat_capacity,
):
    layers, xcells, width = density.shape
    n = layers * xcells
    peers = lax.axis_size("gx") * lax.axis_size("gy")
    slots = max(2, 2 * n // peers)
    line = peers * (slots + 1)
    flat = lambda a: a.reshape(n, width)
    ef = efield.reshape(3, n, width)
    den, mob, x0 = flat(density), flat(mobility_prev), flat(thermal_prev)
    own, blk, liv = owner.reshape(1, n), block.reshape(1, n), live.reshape(1, n)
    mat = material.reshape(layers, xcells)
    sized = lambda *s: (s, F32)

    [sent] = call(functools.partial(dispatch_kernel, peers, slots), [sized(line, width)],
                  [ef, den, mob, own, blk, liv], "dispatch", flops=10**8)
    received = exchanged(sent)

    far = SWEEPS - layers
    count = layers + 2 * SWEEPS
    rows = xcells + 2 * EDGE
    near, up, down = call(
        functools.partial(start_z_kernel, far),
        [sized(n + EDGE, width), sized(far * xcells + EDGE, width), sized(far * xcells + EDGE, width)],
        [x0, mat], "start_z")
    low, high = shifted(near, "gz", 1), shifted(near, "gz", -1)
    low2, high2 = shifted(up, "gz", 2), shifted(down, "gz", -2)
    xz, mats, xlow, xhigh = call(
        functools.partial(start_x_kernel, far),
        [sized(count, xcells, width), sized(count, width)] + [sized(count * (EDGE + 1), width)] * 2,
        [low2, low, near, high, high2], "start_x")
    before, after = shifted(xhigh, "gx", 1), shifted(xlow, "gx", -1)
    long = count * rows + 3 * count * LANES // EDGE
    xm, around, ylow, yhigh = call(
        start_y_kernel,
        [sized(count, rows, width), sized(3 * count, width), sized(EDGE, long), sized(EDGE, long)],
        [xz, mats, after, before], "start_y")
    left, right = shifted(yhigh, "gy", 1), shifted(ylow, "gy", -1)
    pair = lambda k: sized(k, 2, rows, width)
    xs, wz, wx, wy, inv, b0 = call(
        weights_kernel,
        [sized(count, rows, width), pair(count - 1)] + [pair(count - 2)] * 4,
        [xm, around, left, right, mat_conductivity, mat_softening, mat_capacity], "weights",
        scratch=[pltpu.VMEM((2, count, rows, width), F32)] * 2 + [pltpu.VMEM((3, 3, LANES, LANES), F32)],
        limit=56, flops=10**7, smem=(4, 5, 6))
    gain, dest = call(functools.partial(after_kernel, slots), [sized(n, width), ((n, LANES), I32)], [ef, own], "gain")

    received, inv, gain, dest = lax.optimization_barrier((received, inv, gain, dest))
    far -= 1
    source, first, last = call(
        functools.partial(combine_kernel, peers, slots, far),
        [sized(n, width)] + [sized(far * xcells, width)] * 2, [received], "combine", flops=10**8)
    [ids] = call(functools.partial(ids_kernel, peers, slots), [((peers * slots, LANES), I32)], [received], "ids")
    low, high = shifted(source, "gz", 1), shifted(source, "gz", -1)
    low2, high2 = shifted(last, "gz", 2), shifted(first, "gz", -2)
    around_z = [low2, low, source, high, high2]
    inner = count - 2
    xlow, xhigh = call(functools.partial(source_x_kernel, far), [sized(inner * EDGE, width)] * 2, around_z, "source_x")
    before, after = shifted(xhigh, "gx", 1), shifted(xlow, "gx", -1)
    ylow, yhigh = call(
        functools.partial(source_y_kernel, far), [sized(EDGE, inner * rows)] * 2,
        around_z + [after, before], "source_y", scratch=[pltpu.VMEM((inner * rows, width), F32)])
    left, right = shifted(yhigh, "gy", 1), shifted(ylow, "gy", -1)
    x, replies = call(
        functools.partial(sweep_kernel, far), [sized(n, width), sized(peers * slots, width)],
        [xm, xs, wz, wx, wy, inv, b0] + around_z + [after, before, left, right, ids], "sweeps",
        scratch=[pltpu.VMEM((inner, 2, rows, width), F32)] * 2 + [pltpu.VMEM((count, 2, rows, width), F32)] * 2,
        limit=60, flops=10**8)
    returned = exchanged(replies)
    mobility, ionization = call(final_kernel, [sized(n, width)] * 2, [returned, dest, gain, mob], "finish", flops=10**8)
    shape = density.shape
    return x.reshape(shape), mobility.reshape(shape), ionization.reshape(shape)


def solution(mesh):
    tile = P("gz", "gx", "gy")
    rows = P("gz", "gx", "gy", None)
    placed = (
        P(None, "gz", "gx", "gy"), tile, tile, tile,
        P("gz", "gx", "gy", None, None), rows, rows, rows, P(), P(), P(),
    )
    return jax.shard_map(
        per_device, mesh=mesh, in_specs=placed, out_specs=(tile, tile, tile), check_vma=False
    )
```

time: 277 us -> 176 us (0.64); the launches traced: 272 us -> 174 us
  starting transfers between devices: 174 us -> 62.3 us
  Pallas kernels: 0 us -> 46 us
  waiting for transfers between devices: 63.7 us -> 23.2 us
  blocking collectives: 0 us -> 33.8 us
  other arithmetic: 14.5 us -> 0 us
  local copies, waits for them, and re-layouts: 14.4 us -> 8.12 us
  matrix products: 4 us -> 0 us
    ppermute x42 -> x16, starting transfers between devices: 131 us -> 50.6 us  [shifted(): return lax.ppermute(v, axis, pairs) if pairs else jnp.zeros_like(v)]
    pallas_call x0 -> x12, Pallas kernels: none -> 46 us  [call(): pl.pallas_call(kernel, out_shape=[jax.ShapeDtypeStruct(s, t) for s, t in...]
    all_to_all x0 -> x1, blocking collectives: none -> 33.8 us  [exchanged(): lax.all_to_all(lines, ('gx', 'gy'), split_axis=0, concat_axis=0, tiled=True)]
    all_to_all x3 -> x1, starting transfers between devices: 43.3 us -> 11.8 us  [exchanged(): lax.all_to_all(lines, ('gx', 'gy'), split_axis=0, concat_axis=0, tiled=True)]
    ppermute x42 -> x16, waiting for transfers between devices: 45.7 us -> 23.2 us  [shifted(): return lax.ppermute(v, axis, pairs) if pairs else jnp.zeros_like(v)]
    all_to_all x3 -> x1, waiting for transfers between devices: 18 us -> 0.01 us  [exchanged(): lax.all_to_all(lines, ('gx', 'gy'), split_axis=0, concat_axis=0, tiled=True)]
    unnamed x34 -> x50, local copies, waits for them, and re-layouts: 1.76 us -> 8.12 us
    scatter x2 -> x0, local copies, waits for them, and re-layouts: 5.1 us -> none  [the longest x1 2.6 us: per_device(): jnp.full((peers * slots,), nblocks, jnp.int32).at[destination].set(targets)]
  transfers between devices with their start and end apart: 45 -> 17, of which waited for: 27 -> 7; matrix products, arithmetic and copies ran while one was open for 5% -> 0% of each run, Pallas kernels for 0% -> 12%
where the time goes in v2:
time: 176 us; the launch traced here: 174 us
  starting transfers between devices  62.3 us (35%)
  Pallas kernels  46 us (26%)
  blocking collectives  33.8 us (19%)
  waiting for transfers between devices  23.2 us (13%)
  local copies, waits for them, and re-layouts  8.12 us (5%)
    ppermute x16, starting transfers between devices, shifted(): return lax.ppermute(v, axis, pairs) if pairs else jnp.zeros_like(v)  50.6 us
    pallas_call x12, Pallas kernels, call(): pl.pallas_call(kernel, out_shape=[jax.ShapeDtypeStruct(s, t) for s, t in...  46 us
    all_to_all x1, blocking collectives, exchanged(): lax.all_to_all(lines, ('gx', 'gy'), split_axis=0, concat_axis=0, tiled=True)  33.8 us
    ppermute x16, waiting for transfers between devices, shifted(): return lax.ppermute(v, axis, pairs) if pairs else jnp.zeros_like(v)  23.2 us
    all_to_all x1, starting transfers between devices, exchanged(): lax.all_to_all(lines, ('gx', 'gy'), split_axis=0, concat_axis=0, tiled=True)  11.8 us
    unnamed x50, local copies, waits for them, and re-layouts  8.12 us
  transfers between devices with their start and end apart: 17, of which 7 were waited for; matrix products, arithmetic and copies ran while one was open for 0% of the time, Pallas kernels for 12%

profile of v2, /device:TPU:1, one launch (start us, length us, event | category | flops | bytes accessed | tf_op | source)
XLA Modules:
  0.0 174.5 jit_solution(15413717777390193706)
XLA Ops:
  0.6 0.0 copy-start.1
  0.7 1.1 copy-done.1
  1.8 0.9 copy-done.7
  2.7 0.9 copy-done.12
  3.7 0.7 copy-done.16
  4.4 0.7 copy-done.19
  5.0 0.7 copy-done.20
  5.7 1.9 %dispatch.1 = f32[1088,128]{1,0:T(8,128)} custom-call(f32[3,512,128]{2,1,0:T(8,128)S(1)} %bitcast.21, f32[512,128]{1,0:T(8,128)S(1)} %bitcast.27, f32[512,128]{1,0:T(8,128)S(1)} %bitcast.24, s32[1,512]{1,0:T(1,128)S(1)} %bitcast.28, s32[1,512]{1,0:T(1,128)S(1)} %bitcast.31, s32[1,512]{1,0:T(1,128)S(1)} %bitcast.32), custom_call_target="tpu_custom_call" | custom-call | flops 100000000 | bytes 1873920 | tf_op jit(solution)/shard_map/dispatch/pallas_call | solution.py:71
  7.6 11.8 %all-to-all-start = ((f32[1088,1,128]{2,1,0:T(1,128)}), f32[1088,1,128]{2,1,0:T(1,128)S(1)}, u32[]{:S(2)}, u32[]{:S(2)}) async-start(f32[1088,1,128]{2,1,0:T(1,128)} %bitcast.9), calls=%async_computation | async-start | bytes 1114112 | tf_op jit(solution)/shard_map/all_to_all | solution.py:391
  19.4 1.3 collective-permute-start.2
  20.7 4.6 %collective-permute-start.1 = (f32[520,128]{1,0:T(8,128)S(1)}, f32[520,128]{1,0:T(8,128)S(1)}, u32[]{:S(2)}, u32[]{:S(2)}) collective-permute-start(f32[520,128]{1,0:T(8,128)S(1)} %get-tuple-element.38.own), channel_id=1, source_target_pairs={{0,1},{1,2},{2,3},{3,4},{4,5},{5,6},{6,7},{8,9},{9,10},{10,11},{11... | collective-permute-start | bytes 798728 | tf_op jit(solution)/shard_map/ppermute | solution.py:386
  25.4 5.8 %collective-permute-start = (f32[264,128]{1,0:T(8,128)S(1)}, f32[264,128]{1,0:T(8,128)S(1)}, u32[]{:S(2)}, u32[]{:S(2)}) collective-permute-start(f32[264,128]{1,0:T(8,128)S(1)} %get-tuple-element.37), channel_id=1, source_target_pairs={{0,2},{1,3},{2,4},{3,5},{4,6},{5,7},{8,10},{9,11},{10,12},{11,13},... | collective-permute-start | bytes 405512 | tf_op jit(solution)/shard_map/ppermute | solution.py:386
  31.2 1.3 collective-permute-start.3
  32.5 0.9 collective-permute-done.low2
  33.4 9.6 %collective-permute-done.3.high2 = f32[264,128]{1,0:T(8,128)S(1)} collective-permute-done((f32[264,128]{1,0:T(8,128)S(1)}, f32[264,128]{1,0:T(8,128)S(1)}, u32[]{:S(2)}, u32[]{:S(2)}) %collective-permute-start.3) | collective-permute-done | bytes 135200 | tf_op jit(solution)/shard_map/ppermute | solution.py:386
  43.1 0.1 start_x.1
  43.1 1.3 collective-permute-start.4
  44.4 4.0 %collective-permute-start.5 = (f32[144,128]{1,0:T(8,128)S(1)}, f32[144,128]{1,0:T(8,128)S(1)}, u32[]{:S(2)}, u32[]{:S(2)}) collective-permute-start(f32[144,128]{1,0:T(8,128)S(1)} %get-tuple-element.43), channel_id=1, source_target_pairs={{0,32},{32,64},{64,96},{96,128},{128,160},{160,192},{192,224},{224... | collective-permute-start | bytes 221192 | tf_op jit(solution)/shard_map/ppermute | solution.py:386
  48.4 1.4 collective-permute-done.5.before
  49.8 0.5 start_y.1
  50.3 1.0 copy-done
  51.3 6.3 %collective-permute-start.6 = (f32[8,3072]{1,0:T(8,128)S(1)}, f32[8,3072]{1,0:T(8,128)S(1)}, u32[]{:S(2)}, u32[]{:S(2)}) collective-permute-start(f32[8,3072]{1,0:T(8,128)S(1)} %get-tuple-element.46), channel_id=1, source_target_pairs={{0,8},{8,16},{16,24},{1,9},{9,17},{17,25},{2,10},{10,18},{18,26},{... | collective-permute-start | bytes 294920 | tf_op jit(solution)/shard_map/ppermute | solution.py:386
  57.6 1.9 %collective-permute-start.7 = (f32[8,3072]{1,0:T(8,128)S(1)}, f32[8,3072]{1,0:T(8,128)S(1)}, u32[]{:S(2)}, u32[]{:S(2)}) collective-permute-start(f32[8,3072]{1,0:T(8,128)S(1)} %get-tuple-element.47), channel_id=1, source_target_pairs={{8,0},{16,8},{24,16},{9,1},{17,9},{25,17},{10,2},{18,10},{26,18},{... | collective-permute-start | bytes 294920 | tf_op jit(solution)/shard_map/ppermute | solution.py:386
  59.5 1.0 gain.1
  60.6 2.9 %collective-permute-done.7.right = f32[8,3072]{1,0:T(8,128)S(1)} collective-permute-done((f32[8,3072]{1,0:T(8,128)S(1)}, f32[8,3072]{1,0:T(8,128)S(1)}, u32[]{:S(2)}, u32[]{:S(2)}) %collective-permute-start.7) | collective-permute-done | bytes 98336 | tf_op jit(solution)/shard_map/ppermute | solution.py:386
  63.5 0.6 copy-done.22
  64.2 19.2 %weights.1 = (f32[16,144,128]{2,1,0:T(8,128)}, f32[15,2,144,128]{3,2,1,0:T(8,128)}, f32[14,2,144,128]{3,2,1,0:T(8,128)}, f32[14,2,144,128]{3,2,1,0:T(8,128)}, f3...) custom-call(f32[16,144,128]{2,1,0:T(8,128)} %copy-done, f32[48,128]{1,0:T(8,128)} %copy-done.15, ...), custom_call_target="tpu_custom_call" | custom-call | flops 10000000 | bytes 13049952 | tf_op jit(solution)/shard_map/weights/pallas_call | solution.py:71
  83.3 0.7 combine.1
  84.1 1.3 collective-permute-start.10
  85.4 4.0 %collective-permute-start.9 = (f32[512,128]{1,0:T(8,128)S(1)}, f32[512,128]{1,0:T(8,128)S(1)}, u32[]{:S(2)}, u32[]{:S(2)}) collective-permute-start(f32[512,128]{1,0:T(8,128)S(1)} %get-tuple-element.59.own), channel_id=1, source_target_pairs={{0,1},{1,2},{2,3},{3,4},{4,5},{5,6},{6,7},{8,9},{9,10},{10,11},{11... | collective-permute-start | bytes 786440 | tf_op jit(solution)/shard_map/ppermute | solution.py:386
  89.4 5.3 %collective-permute-start.8 = (f32[128,128]{1,0:T(8,128)S(1)}, f32[128,128]{1,0:T(8,128)S(1)}, u32[]{:S(2)}, u32[]{:S(2)}) collective-permute-start(f32[128,128]{1,0:T(8,128)S(1)} %get-tuple-element.58), channel_id=1, source_target_pairs={{0,2},{1,3},{2,4},{3,5},{4,6},{5,7},{8,10},{9,11},{10,12},{11,13},... | collective-permute-start | bytes 196616 | tf_op jit(solution)/shard_map/ppermute | solution.py:386
  94.7 1.3 collective-permute-start.11
  96.0 0.0 collective-permute-done.8.low2
  96.0 4.6 %collective-permute-done.11.high2 = f32[128,128]{1,0:T(8,128)S(1)} collective-permute-done((f32[128,128]{1,0:T(8,128)S(1)}, f32[128,128]{1,0:T(8,128)S(1)}, u32[]{:S(2)}, u32[]{:S(2)}) %collective-permute-start.11) | collective-permute-done | bytes 65568 | tf_op jit(solution)/shard_map/ppermute | solution.py:386
  100.7 0.0 copy-start.5
  100.7 1.3 collective-permute-start.12
  102.0 4.6 %collective-permute-start.13 = (f32[112,128]{1,0:T(8,128)S(1)}, f32[112,128]{1,0:T(8,128)S(1)}, u32[]{:S(2)}, u32[]{:S(2)}) collective-permute-start(f32[112,128]{1,0:T(8,128)S(1)} %get-tuple-element.62), channel_id=1, source_target_pairs={{0,32},{32,64},{64,96},{96,128},{128,160},{160,192},{192,224},{224... | collective-permute-start | bytes 172040 | tf_op jit(solution)/shard_map/ppermute | solution.py:386
  106.7 1.2 collective-permute-done.13.before
  107.9 0.4 source_y.1
  108.3 4.4 %collective-permute-start.14 = (f32[8,2016]{1,0:T(8,128)S(1)}, f32[8,2016]{1,0:T(8,128)S(1)}, u32[]{:S(2)}, u32[]{:S(2)}) collective-permute-start(f32[8,2016]{1,0:T(8,128)S(1)} %get-tuple-element.63), channel_id=1, source_target_pairs={{0,8},{8,16},{16,24},{1,9},{9,17},{17,25},{2,10},{10,18},{18,26},{... | collective-permute-start | bytes 193544 | tf_op jit(solution)/shard_map/ppermute | solution.py:386
  112.7 1.9 %collective-permute-start.15 = (f32[8,2016]{1,0:T(8,128)S(1)}, f32[8,2016]{1,0:T(8,128)S(1)}, u32[]{:S(2)}, u32[]{:S(2)}) collective-permute-start(f32[8,2016]{1,0:T(8,128)S(1)} %get-tuple-element.64), channel_id=1, source_target_pairs={{8,0},{16,8},{24,16},{9,1},{17,9},{25,17},{10,2},{18,10},{26,18},{... | collective-permute-start | bytes 193544 | tf_op jit(solution)/shard_map/ppermute | solution.py:386
  114.6 0.4 ids.1
  115.0 0.8 copy-done.6
  115.7 2.5 %collective-permute-done.15.right = f32[8,2016]{1,0:T(8,128)S(1)} collective-permute-done((f32[8,2016]{1,0:T(8,128)S(1)}, f32[8,2016]{1,0:T(8,128)S(1)}, u32[]{:S(2)}, u32[]{:S(2)}) %collective-permute-start.15) | collective-permute-done | bytes 64544 | tf_op jit(solution)/shard_map/ppermute | solution.py:386
  118.3 0.5 copy-done.24
  118.9 20.5 %sweeps.1 = (f32[512,128]{1,0:T(8,128)}, f32[1024,128]{1,0:T(8,128)}) custom-call(f32[16,144,128]{2,1,0:T(8,128)} %copy-done, f32[16,144,128]{2,1,0:T(8,128)} %get-tuple-element.48.xs, f32[15,2,144,128]{3,2,1,0:T(8,128)} %get-tuple-element.49.wz, f32[14,2,144,128]{3,2,1,0:T(8,128)} %get-tuple-element.50.wx, f32[14,2,144,128]{3,2,1,0:T(8,128)} %get-tuple-element.51.wy, ...), custom_call_target="tpu_custom_call" | custom-call | flops 100000000 | bytes 15300608 | tf_op jit(solution)/shard_map/sweeps/pallas_call | solution.py:71
  139.4 33.8 %all_to_all.10 = f32[1024,1,128]{2,1,0:T(1,128)S(1)} all-to-all(f32[1024,1,128]{2,1,0:T(1,128)} %bitcast.33), channel_id=1, replica_groups=mesh['gx'=16,'gy'=4,'gz'=8] {'gx','gy'}, dimensions={0} | all-to-all | bytes 1048576 | tf_op jit(solution)/shard_map/all_to_all | solution.py:391
  173.2 1.2 finish.1
  (49 shorter events, 0.1 us)
Async XLA Ops:
  0.6 18.7 %copy-start.18 = (s32[1,1,1,512]{3,2,1,0:T(1,128)S(1)}, s32[1,1,1,512]{3,2,1,0:T(1,128)}, u32[]{:S(2)}) copy-start(s32[1,1,1,512]{3,2,1,0:T(1,128)} %param.18) | copy-start | bytes 6148
  0.6 1.1 copy-start.1
  1.8 0.9 copy-start.7
  2.7 0.9 copy-start.12
  3.7 0.7 copy-start.16
  4.4 0.7 copy-start.19
  5.0 0.7 copy-start.20
  5.7 13.7 %copy-start.11 = (f32[4,128,128]{2,1,0:T(8,128)S(1)}, f32[4,128,128]{2,1,0:T(8,128)}, u32[]{:S(2)}) copy-start(f32[4,128,128]{2,1,0:T(8,128)} %param.14) | copy-start | bytes 786436
  7.6 51.9 %copy-start.2 = (f32[3,4,128,128]{3,2,1,0:T(8,128)S(1)}, f32[3,4,128,128]{3,2,1,0:T(8,128)}, u32[]{:S(2)}) copy-start(f32[3,4,128,128]{3,2,1,0:T(8,128)} %param.11) | copy-start | bytes 2359300
  7.6 51.9 %copy-start.17 = (s32[1,1,1,512,1]{3,4,2,1,0:T(1,128)S(1)}, s32[1,1,1,512,1]{3,4,2,1,0:T(1,128)}, u32[]{:S(2)}) copy-start(s32[1,1,1,512,1]{3,4,2,1,0:T(1,128)} %param.15) | copy-start | bytes 6148
  7.6 75.7 %all-to-all-start = ((f32[1088,1,128]{2,1,0:T(1,128)}), f32[1088,1,128]{2,1,0:T(1,128)S(1)}, u32[]{:S(2)}, u32[]{:S(2)}) async-start(f32[1088,1,128]{2,1,0:T(1,128)} %bitcast.9), calls=%async_computation | async-start | bytes 1114112 | tf_op jit(solution)/shard_map/all_to_all | solution.py:391
  19.4 23.6 %collective-permute-start.2 = (f32[520,128]{1,0:T(8,128)S(1)}, f32[520,128]{1,0:T(8,128)S(1)}, u32[]{:S(2)}, u32[]{:S(2)}) collective-permute-start(f32[520,128]{1,0:T(8,128)S(1)} %get-tuple-element.38.own), channel_id=1, source_target_pairs={{1,0},{2,1},{3,2},{4,3},{5,4},{6,5},{7,6},{9,8},{10,9},{11,10},{12... | collective-permute-start | bytes 798728 | tf_op jit(solution)/shard_map/ppermute | solution.py:386
  20.7 22.3 %collective-permute-start.1 = (f32[520,128]{1,0:T(8,128)S(1)}, f32[520,128]{1,0:T(8,128)S(1)}, u32[]{:S(2)}, u32[]{:S(2)}) collective-permute-start(f32[520,128]{1,0:T(8,128)S(1)} %get-tuple-element.38.own), channel_id=1, source_target_pairs={{0,1},{1,2},{2,3},{3,4},{4,5},{5,6},{6,7},{8,9},{9,10},{10,11},{11... | collective-permute-start | bytes 798728 | tf_op jit(solution)/shard_map/ppermute | solution.py:386
  25.4 8.1 %collective-permute-start = (f32[264,128]{1,0:T(8,128)S(1)}, f32[264,128]{1,0:T(8,128)S(1)}, u32[]{:S(2)}, u32[]{:S(2)}) collective-permute-start(f32[264,128]{1,0:T(8,128)S(1)} %get-tuple-element.37), channel_id=1, source_target_pairs={{0,2},{1,3},{2,4},{3,5},{4,6},{5,7},{8,10},{9,11},{10,12},{11,13},... | collective-permute-start | bytes 405512 | tf_op jit(solution)/shard_map/ppermute | solution.py:386
  31.2 11.9 %collective-permute-start.3 = (f32[264,128]{1,0:T(8,128)S(1)}, f32[264,128]{1,0:T(8,128)S(1)}, u32[]{:S(2)}, u32[]{:S(2)}) collective-permute-start(f32[264,128]{1,0:T(8,128)S(1)} %get-tuple-element.39), channel_id=1, source_target_pairs={{2,0},{3,1},{4,2},{5,3},{6,4},{7,5},{10,8},{11,9},{12,10},{13,11},... | collective-permute-start | bytes 405512 | tf_op jit(solution)/shard_map/ppermute | solution.py:386
  43.1 5.3 %collective-permute-start.4 = (f32[144,128]{1,0:T(8,128)S(1)}, f32[144,128]{1,0:T(8,128)S(1)}, u32[]{:S(2)}, u32[]{:S(2)}) collective-permute-start(f32[144,128]{1,0:T(8,128)S(1)} %get-tuple-element.42), channel_id=1, source_target_pairs={{32,0},{64,32},{96,64},{128,96},{160,128},{192,160},{224,192},{256... | collective-permute-start | bytes 221192 | tf_op jit(solution)/shard_map/ppermute | solution.py:386
  44.4 5.4 %collective-permute-start.5 = (f32[144,128]{1,0:T(8,128)S(1)}, f32[144,128]{1,0:T(8,128)S(1)}, u32[]{:S(2)}, u32[]{:S(2)}) collective-permute-start(f32[144,128]{1,0:T(8,128)S(1)} %get-tuple-element.43), channel_id=1, source_target_pairs={{0,32},{32,64},{64,96},{96,128},{128,160},{160,192},{192,224},{224... | collective-permute-start | bytes 221192 | tf_op jit(solution)/shard_map/ppermute | solution.py:386
  50.3 1.0 copy-start
  51.3 9.2 %copy-start.15 = (f32[48,128]{1,0:T(8,128)}, f32[48,128]{1,0:T(8,128)S(1)}, u32[]{:S(2)}) copy-start(f32[48,128]{1,0:T(8,128)S(1)} %get-tuple-element.45.around) | copy-start | bytes 73732
  51.3 9.2 %collective-permute-start.6 = (f32[8,3072]{1,0:T(8,128)S(1)}, f32[8,3072]{1,0:T(8,128)S(1)}, u32[]{:S(2)}, u32[]{:S(2)}) collective-permute-start(f32[8,3072]{1,0:T(8,128)S(1)} %get-tuple-element.46), channel_id=1, source_target_pairs={{0,8},{8,16},{16,24},{1,9},{9,17},{17,25},{2,10},{10,18},{18,26},{... | collective-permute-start | bytes 294920 | tf_op jit(solution)/shard_map/ppermute | solution.py:386
  57.6 5.9 %collective-permute-start.7 = (f32[8,3072]{1,0:T(8,128)S(1)}, f32[8,3072]{1,0:T(8,128)S(1)}, u32[]{:S(2)}, u32[]{:S(2)}) collective-permute-start(f32[8,3072]{1,0:T(8,128)S(1)} %get-tuple-element.47), channel_id=1, source_target_pairs={{8,0},{16,8},{24,16},{9,1},{17,9},{25,17},{10,2},{18,10},{26,18},{... | collective-permute-start | bytes 294920 | tf_op jit(solution)/shard_map/ppermute | solution.py:386
  60.6 2.9 %copy-start.21 = (f32[8,3072]{1,0:T(8,128)}, f32[8,3072]{1,0:T(8,128)S(1)}, u32[]{:S(2)}) copy-start(f32[8,3072]{1,0:T(8,128)S(1)} %collective-permute-done.6.left) | copy-start | bytes 294916
  63.5 0.6 copy-start.22
  84.1 34.2 %copy-start.3 = (f32[512,128]{1,0:T(8,128)}, f32[512,128]{1,0:T(8,128)S(1)}, u32[]{:S(2)}) copy-start(f32[512,128]{1,0:T(8,128)S(1)} %get-tuple-element.59.own) | copy-start | bytes 786436
  84.1 16.6 %collective-permute-start.10 = (f32[512,128]{1,0:T(8,128)S(1)}, f32[512,128]{1,0:T(8,128)S(1)}, u32[]{:S(2)}, u32[]{:S(2)}) collective-permute-start(f32[512,128]{1,0:T(8,128)S(1)} %get-tuple-element.59.own), channel_id=1, source_target_pairs={{1,0},{2,1},{3,2},{4,3},{5,4},{6,5},{7,6},{9,8},{10,9},{11,10},{12... | collective-permute-start | bytes 786440 | tf_op jit(solution)/shard_map/ppermute | solution.py:386
  85.4 15.3 %collective-permute-start.9 = (f32[512,128]{1,0:T(8,128)S(1)}, f32[512,128]{1,0:T(8,128)S(1)}, u32[]{:S(2)}, u32[]{:S(2)}) collective-permute-start(f32[512,128]{1,0:T(8,128)S(1)} %get-tuple-element.59.own), channel_id=1, source_target_pairs={{0,1},{1,2},{2,3},{3,4},{4,5},{5,6},{6,7},{8,9},{9,10},{10,11},{11... | collective-permute-start | bytes 786440 | tf_op jit(solution)/shard_map/ppermute | solution.py:386
  89.4 6.6 %collective-permute-start.8 = (f32[128,128]{1,0:T(8,128)S(1)}, f32[128,128]{1,0:T(8,128)S(1)}, u32[]{:S(2)}, u32[]{:S(2)}) collective-permute-start(f32[128,128]{1,0:T(8,128)S(1)} %get-tuple-element.58), channel_id=1, source_target_pairs={{0,2},{1,3},{2,4},{3,5},{4,6},{5,7},{8,10},{9,11},{10,12},{11,13},... | collective-permute-start | bytes 196616 | tf_op jit(solution)/shard_map/ppermute | solution.py:386
  94.7 6.0 %collective-permute-start.11 = (f32[128,128]{1,0:T(8,128)S(1)}, f32[128,128]{1,0:T(8,128)S(1)}, u32[]{:S(2)}, u32[]{:S(2)}) collective-permute-start(f32[128,128]{1,0:T(8,128)S(1)} %get-tuple-element.60), channel_id=1, source_target_pairs={{2,0},{3,1},{4,2},{5,3},{6,4},{7,5},{10,8},{11,9},{12,10},{13,11},... | collective-permute-start | bytes 196616 | tf_op jit(solution)/shard_map/ppermute | solution.py:386
  96.0 22.2 %copy-start.9 = (f32[128,128]{1,0:T(8,128)}, f32[128,128]{1,0:T(8,128)S(1)}, u32[]{:S(2)}) copy-start(f32[128,128]{1,0:T(8,128)S(1)} %collective-permute-done.8.low2) | copy-start | bytes 196612
  100.7 17.6 %copy-start.10 = (f32[128,128]{1,0:T(8,128)}, f32[128,128]{1,0:T(8,128)S(1)}, u32[]{:S(2)}) copy-start(f32[128,128]{1,0:T(8,128)S(1)} %collective-permute-done.11.high2) | copy-start | bytes 196612
  100.7 17.6 %copy-start.4 = (f32[512,128]{1,0:T(8,128)}, f32[512,128]{1,0:T(8,128)S(1)}, u32[]{:S(2)}) copy-start(f32[512,128]{1,0:T(8,128)S(1)} %collective-permute-done.10.high) | copy-start | bytes 786436
  100.7 17.6 %copy-start.5 = (f32[512,128]{1,0:T(8,128)}, f32[512,128]{1,0:T(8,128)S(1)}, u32[]{:S(2)}) copy-start(f32[512,128]{1,0:T(8,128)S(1)} %collective-permute-done.9.low) | copy-start | bytes 786436
  100.7 5.9 %collective-permute-start.12 = (f32[112,128]{1,0:T(8,128)S(1)}, f32[112,128]{1,0:T(8,128)S(1)}, u32[]{:S(2)}, u32[]{:S(2)}) collective-permute-start(f32[112,128]{1,0:T(8,128)S(1)} %get-tuple-element.61), channel_id=1, source_target_pairs={{32,0},{64,32},{96,64},{128,96},{160,128},{192,160},{224,192},{256... | collective-permute-start | bytes 172040 | tf_op jit(solution)/shard_map/ppermute | solution.py:386
  102.0 5.9 %collective-permute-start.13 = (f32[112,128]{1,0:T(8,128)S(1)}, f32[112,128]{1,0:T(8,128)S(1)}, u32[]{:S(2)}, u32[]{:S(2)}) collective-permute-start(f32[112,128]{1,0:T(8,128)S(1)} %get-tuple-element.62), channel_id=1, source_target_pairs={{0,32},{32,64},{64,96},{96,128},{128,160},{160,192},{192,224},{224... | collective-permute-start | bytes 172040 | tf_op jit(solution)/shard_map/ppermute | solution.py:386
  106.7 11.6 %copy-start.13 = (f32[112,128]{1,0:T(8,128)}, f32[112,128]{1,0:T(8,128)S(1)}, u32[]{:S(2)}) copy-start(f32[112,128]{1,0:T(8,128)S(1)} %collective-permute-done.12.after) | copy-start | bytes 172036
  107.9 10.4 %copy-start.14 = (f32[112,128]{1,0:T(8,128)}, f32[112,128]{1,0:T(8,128)S(1)}, u32[]{:S(2)}) copy-start(f32[112,128]{1,0:T(8,128)S(1)} %collective-permute-done.13.before) | copy-start | bytes 172036
  108.3 7.5 %collective-permute-start.14 = (f32[8,2016]{1,0:T(8,128)S(1)}, f32[8,2016]{1,0:T(8,128)S(1)}, u32[]{:S(2)}, u32[]{:S(2)}) collective-permute-start(f32[8,2016]{1,0:T(8,128)S(1)} %get-tuple-element.63), channel_id=1, source_target_pairs={{0,8},{8,16},{16,24},{1,9},{9,17},{17,25},{2,10},{10,18},{18,26},{... | collective-permute-start | bytes 193544 | tf_op jit(solution)/shard_map/ppermute | solution.py:386
  112.7 5.6 %collective-permute-start.15 = (f32[8,2016]{1,0:T(8,128)S(1)}, f32[8,2016]{1,0:T(8,128)S(1)}, u32[]{:S(2)}, u32[]{:S(2)}) collective-permute-start(f32[8,2016]{1,0:T(8,128)S(1)} %get-tuple-element.64), channel_id=1, source_target_pairs={{8,0},{16,8},{24,16},{9,1},{17,9},{25,17},{10,2},{18,10},{26,18},{... | collective-permute-start | bytes 193544 | tf_op jit(solution)/shard_map/ppermute | solution.py:386
  115.0 0.8 copy-start.6
  115.7 2.5 %copy-start.23 = (f32[8,2016]{1,0:T(8,128)}, f32[8,2016]{1,0:T(8,128)S(1)}, u32[]{:S(2)}) copy-start(f32[8,2016]{1,0:T(8,128)S(1)} %collective-permute-done.14.left) | copy-start | bytes 193540
  118.2 0.6 copy-start.24
  118.9 54.4 %copy-start.8 = (f32[4,128,128]{2,1,0:T(8,128)S(1)}, f32[4,128,128]{2,1,0:T(8,128)}, u32[]{:S(2)}) copy-start(f32[4,128,128]{2,1,0:T(8,128)} %param.13) | copy-start | bytes 786436

commit v3 on v2

v3 whole, which is shorter than its diff:
```python
import functools

import jax
import jax.numpy as jnp
from jax import lax
from jax.experimental import pallas as pl
from jax.experimental.pallas import tpu as pltpu
from jax.sharding import PartitionSpec as P

SWEEPS = 6
THETA = 1.01
DELTA = 0.99
LANES = 128
EDGE = 8
F32 = jnp.float32
BF16 = jnp.bfloat16
I32 = jnp.int32


def steps():
    sigma = THETA / DELTA
    rho = 1.0 / sigma
    found = [(0.0, 1.0 / THETA)]
    for _ in range(SWEEPS - 1):
        rho_new = 1.0 / (2.0 * sigma - rho)
        found.append((rho_new * rho, 2.0 * rho_new / DELTA))
        rho = rho_new
    return found


def iota(shape, dim):
    return lax.broadcasted_iota(I32, shape, dim)


def dot(a, b, ca, cb):
    return lax.dot_general(a, b, (((ca,), (cb,)), ((), ())), preferred_element_type=F32)


def parts(v):
    high = v.astype(BF16)
    return high, (v - high.astype(F32)).astype(BF16)


def pick_rows(hot, rows):
    high, low = parts(rows)
    got = dot(hot, jnp.concatenate([high, low], axis=1), 1, 0)
    width = rows.shape[1]
    return got[:, :width] + got[:, width:]


def column(row):
    same = iota((LANES, LANES), 0) == iota((LANES, LANES), 1)
    found = []
    for at in range(0, row.shape[1], LANES):
        piece = jnp.broadcast_to(row[:, at : at + LANES], (LANES, LANES))
        found.append(jnp.sum(jnp.where(same, piece, 0), axis=1, keepdims=True))
    return jnp.concatenate(found, axis=0)


def hot_of(cond):
    return jnp.where(cond, F32(1.0), F32(0.0)).astype(BF16)


def edge_lanes():
    r, y = iota((2 * EDGE, LANES), 0), iota((2 * EDGE, LANES), 1)
    return hot_of(y == jnp.where(r < EDGE, r, r + LANES - 2 * EDGE))


def call(kernel, outs, ins, name, scratch=(), limit=32, flops=0, smem=()):
    bytes_of = lambda a: a.size * a.dtype.itemsize
    return pl.pallas_call(
        kernel,
        out_shape=[jax.ShapeDtypeStruct(s, t) for s, t in outs],
        in_specs=[
            pl.BlockSpec(memory_space=pltpu.SMEM if i in smem else pltpu.VMEM)
            for i in range(len(ins))
        ],
        out_specs=[pl.BlockSpec(memory_space=pltpu.VMEM) for _ in outs],
        scratch_shapes=list(scratch),
        compiler_params=pltpu.CompilerParams(vmem_limit_bytes=limit << 20),
        cost_estimate=pl.CostEstimate(
            flops=flops,
            bytes_accessed=sum(bytes_of(a) for a in ins)
            + sum(jax.ShapeDtypeStruct(s, t).size * 4 for s, t in outs),
            transcendentals=0,
        ),
        name=name,
    )(*ins)


def dispatch_kernel(peers, slots, ef, den, mob, owner, block, live, out):
    n = owner.shape[1]
    esq = ef[0] * ef[0] + ef[1] * ef[1] + ef[2] * ef[2]
    heat = 0.2 * den[...] * mob[...] * esq
    heat = jnp.where(iota(heat.shape, 1) < column(live[...]), heat, F32(0.0))
    own = owner[...]
    own_col = column(own)
    pos = jnp.zeros((1, n), I32)
    for at in range(0, n, LANES):
        r = iota((LANES, n), 0) + at
        earlier = (own_col[at : at + LANES] == own) & (r < iota((LANES, n), 1))
        pos = pos + jnp.sum(jnp.where(earlier, 1, 0), axis=0, keepdims=True)
    dest = own * (slots + 1) + pos
    hot = hot_of(iota((peers * (slots + 1), n), 0) == dest)
    out[...] = pick_rows(hot, heat)
    named = hot_of(iota((peers, n), 0) == own)
    at_slot = iota((LANES, n), 0) == pos
    code = block[...] + 1
    high = jnp.where(at_slot, code // 32, 0).astype(F32).astype(BF16)
    low = jnp.where(at_slot, code % 32, 0).astype(F32).astype(BF16)
    out[pl.ds(slots, peers, stride=slots + 1), :] = dot(named, high, 1, 1) * 32.0 + dot(named, low, 1, 1)


def after_kernel(slots, ef, owner, gain, dest):
    n = owner.shape[1]
    esq = ef[0] * ef[0] + ef[1] * ef[1] + ef[2] * ef[2]
    gain[...] = -2.0 * lax.rsqrt(esq + 1.0)
    own = owner[...]
    own_col = column(own)
    for at in range(0, n, LANES):
        r = iota((LANES, n), 0) + at
        piece = own_col[at : at + LANES]
        earlier = (piece == own) & (iota((LANES, n), 1) < r)
        pos = jnp.sum(jnp.where(earlier, 1, 0), axis=1, keepdims=True)
        dest[pl.ds(at, LANES), :] = jnp.broadcast_to(piece * slots + pos, (LANES, LANES))


def labels_of(received, peers, slots):
    got = received[pl.ds(slots, peers, stride=slots + 1), :]
    high = jnp.floor(got * (1.0 / 32.0))
    return high.astype(BF16), (got - 32.0 * high).astype(BF16)


def combine_kernel(peers, slots, far, place, received, source, far_a, far_b):
    n = source.shape[0]
    total = received.shape[0]
    high, low = labels_of(received, peers, slots)
    j = iota((LANES, total), 1)
    spread = hot_of(iota((LANES, total), 0) == j - (slots + 1) * lax.div(j, slots + 1))
    named = dot(high, spread, 1, 0) * 32.0 + dot(low, spread, 1, 0)
    mine = iota((peers, total), 0) == lax.div(iota((peers, total), 1), slots + 1)
    ids = jnp.sum(jnp.where(mine, named, 0.0), axis=0, keepdims=True).astype(I32)
    picks = hot_of(iota((n, total), 0) + 1 == ids)
    source[...] = pick_rows(picks, received[...])
    rows = far * (n // 4)
    first, last = source[pl.ds(0, rows), :], source[pl.ds(n - rows, rows), :]
    even = place[3] == 0
    far_a[...] = jnp.where(even, last, first)
    far_b[...] = jnp.where(even, first, last)


def ids_kernel(peers, slots, received, ids):
    total = peers * slots
    high, low = labels_of(received, peers, slots)
    own = hot_of(lax.div(iota((total, peers), 0), slots) == iota((total, peers), 1))
    named = dot(own, high, 1, 0) * 32.0 + dot(own, low, 1, 0)
    i = iota((total, LANES), 0)
    mine = iota((total, LANES), 1) == i - slots * lax.div(i, slots)
    found = jnp.sum(jnp.where(mine, named, 0.0), axis=1, keepdims=True) - 1.0
    ids[...] = jnp.broadcast_to(found, (total, LANES)).astype(I32)


def start_z_kernel(far, place, x0, material, near, far_a, far_b):
    layers, xcells = material.shape
    n = layers * xcells
    mat = (material[...] + 1).astype(F32)
    rows = far * xcells
    zeros = lambda k: jnp.zeros((k, LANES), F32)
    near[pl.ds(0, n), :] = x0[...]
    near[pl.ds(n, EDGE), :] = jnp.concatenate([mat, zeros(EDGE - layers)], axis=0)
    up, down = x0[pl.ds(n - rows, rows), :], x0[pl.ds(0, rows), :]
    mat_up = jnp.concatenate([mat[layers - far :], zeros(EDGE - far)], axis=0)
    mat_down = jnp.concatenate([mat[:far], zeros(EDGE - far)], axis=0)
    even = place[3] == 0
    far_a[pl.ds(0, rows), :] = jnp.where(even, up, down)
    far_b[pl.ds(0, rows), :] = jnp.where(even, down, up)
    far_a[pl.ds(rows, EDGE), :] = jnp.where(even, mat_up, mat_down)
    far_b[pl.ds(rows, EDGE), :] = jnp.where(even, mat_down, mat_up)


def layer_readers(far, place, far_a, far_b, near_a, near_b, own):
    even, even2 = place[2] == 0, place[3] == 0

    def one(k, ref):
        return lambda at, size: ref[pl.ds(k * LANES + at, size), :]

    def either(k, cond, yes, no):
        return lambda at, size: jnp.where(cond, one(k, yes)(at, size), one(k, no)(at, size))

    found = [either(k, even2, far_b, far_a) for k in range(far)]
    found += [either(k, even, near_b, near_a) for k in range(4)]
    found += [one(k, own) for k in range(4)]
    found += [either(k, even, near_a, near_b) for k in range(4)]
    return found + [either(k, even2, far_a, far_b) for k in range(far)]


def start_x_kernel(far, place, far_a, far_b, near_a, near_b, own, xz, mats, xa, xb):
    readers = layer_readers(far, place, far_a, far_b, near_a, near_b, own)
    count = len(readers)
    even = place[0] == 0
    for k, read in enumerate(readers):
        piece = read(0, LANES)
        xz[k] = piece
        low, high = piece[:EDGE], piece[LANES - EDGE :]
        xa[pl.ds(k * EDGE, EDGE), :] = jnp.where(even, high, low)
        xb[pl.ds(k * EDGE, EDGE), :] = jnp.where(even, low, high)
    tail = [far * LANES] * far + [4 * LANES] * 12 + [far * LANES] * far
    at = list(range(far)) + list(range(4)) * 3 + list(range(far))
    for k, read in enumerate(readers):
        mats[pl.ds(k, 1), :] = read(tail[k] + at[k] - at[k] * LANES, 1)
    xa[pl.ds(count * EDGE, count), :] = mats[...]
    xb[pl.ds(count * EDGE, count), :] = mats[...]


def flat_sides(rows):
    high, low = parts(rows)
    edges = edge_lanes()
    return dot(edges, high, 1, 1) + dot(edges, low, 1, 1)


def start_y_kernel(place, xz, mats, xa, xb, xm, sides, flat_mat, ya, yb):
    count = xz.shape[0]
    even = place[0] == 0
    after, before = jnp.where(even, xa[...], xb[...]), jnp.where(even, xb[...], xa[...])
    blank = jnp.zeros((EDGE, LANES), F32)
    for k in range(count):
        part = slice(k * EDGE, (k + 1) * EDGE)
        xm[k, pl.ds(0, EDGE)] = blank
        xm[k, pl.ds(EDGE, EDGE)] = before[part]
        xm[k, pl.ds(2 * EDGE, LANES)] = xz[k]
        xm[k, pl.ds(LANES + 2 * EDGE, EDGE)] = after[part]
        xm[k, pl.ds(LANES + 3 * EDGE, EDGE)] = blank
    rows = LANES + 2 * EDGE
    total = count * rows
    found = flat_sides(xm[:, EDGE : EDGE + rows].reshape(total, LANES))
    sides[...] = found
    around = jnp.concatenate([before[count * EDGE :], mats[...], after[count * EDGE :]], axis=0)
    q = iota((1, total), 1)
    layer = lax.div(q, rows)
    row = q - layer * rows
    tile = jnp.where(row < EDGE, 0, jnp.where(row < LANES + EDGE, 1, 2))
    lane = row - EDGE + LANES * (1 - tile)
    spread = hot_of(iota((LANES, total), 0) == lane)
    named = dot(around.astype(BF16), spread, 1, 0)
    mine = iota((3 * count, total), 0) == tile * count + layer
    mat = jnp.sum(jnp.where(mine, named, 0.0), axis=0, keepdims=True)
    mat = jnp.where(iota((EDGE, total), 0) == 0, mat, 0.0)
    flat_mat[...] = mat
    even = place[1] == 0
    ya[pl.ds(0, EDGE), :] = jnp.where(even, found[EDGE:], found[:EDGE])
    yb[pl.ds(0, EDGE), :] = jnp.where(even, found[:EDGE], found[EDGE:])
    ya[pl.ds(EDGE, EDGE), :] = mat
    yb[pl.ds(EDGE, EDGE), :] = mat


def three_parts(v):
    high = v.astype(BF16)
    rest = v - high.astype(F32)
    mid = rest.astype(BF16)
    return high, mid, (rest - mid.astype(F32)).astype(BF16)


def ends_of(strip):
    return jnp.concatenate([strip[EDGE - 1 : EDGE], strip[3 * EDGE : 3 * EDGE + 1]], axis=0)


def end_lanes(depth, times):
    r, y = iota((depth, times * LANES), 0), iota((depth, times * LANES), 1)
    first = (r % 2 == 0) & (y == (r // 2) * LANES)
    last = (r % 2 == 1) & (y == (r // 2) * LANES + LANES - 1)
    return hot_of(first | last)


def turned(v, by, axis):
    return pltpu.roll(v, by % v.shape[axis], axis)


def strip_of(sides, before, after):
    return jnp.concatenate([before, sides, after], axis=0)


def weights_kernel(place, base, soft, heat, xm, sides, flat_mat, ya, yb, wz, wx, wy, wyw, inv, b0, strips, cond, cols, ends):
    count, rows = inv.shape[0], inv.shape[1]
    total = count * rows
    even = place[1] == 0
    after, before = jnp.where(even, ya[...], yb[...]), jnp.where(even, yb[...], ya[...])
    mat = jnp.concatenate([flat_mat[0:1], before[EDGE : EDGE + 1], after[EDGE : EDGE + 1]], axis=0)
    tables = []
    for values in (base, soft, heat):
        found = jnp.zeros(mat.shape, F32)
        for m in range(values.shape[0]):
            found = jnp.where(mat == F32(m + 1), values[m], found)
        tables.append(found)
    own = [p for t in tables for p in three_parts(t[0:1])]
    r, y = iota((9, 3 * LANES), 0), iota((9, 3 * LANES), 1)
    cols[...] = dot(jnp.concatenate(own, axis=0), hot_of(lax.div(r, 3) == lax.div(y, LANES)), 0, 0)
    wide = lambda t, i: jnp.broadcast_to(t[i : i + 1], (EDGE, total))
    kb, ks, cf = (jnp.concatenate([wide(t, 1), wide(t, 0), wide(t, 0), wide(t, 2)], axis=0) for t in tables)
    sx = strip_of(sides[...], before[:EDGE], after[:EDGE])
    sc = kb / (1.0 + ks * sx)
    down = lambda by, axis: 0.5 * (sc + turned(sc, by, axis))
    around = [down(rows, 1), down(-rows, 1), down(1, 1), down(-1, 1), down(1, 0), down(-1, 0)]
    diag = cf
    for w in around:
        diag = diag + w
    si = jnp.where(cf > 0.0, 1.0 / diag, 0.0)
    for i, w in enumerate(around):
        strips[i] = w * si
    strips[6] = si
    strips[7] = cf * sx * si
    strips[8] = sx
    got = [dot(p, end_lanes(2, 1), 0, 0) for p in three_parts(ends_of(sc))]
    ends[...] = got[0] + got[1] + got[2]

    piece = 16
    blank = jnp.zeros((EDGE, LANES), F32)

    @pl.loop(0, count)
    def _(k):
        cond[k, pl.ds(0, EDGE)] = blank
        cond[k, pl.ds(rows + EDGE, EDGE)] = blank
        wx[k, pl.ds(0, EDGE)] = blank
        wx[k, pl.ds(rows + EDGE, EDGE)] = blank
        for at in range(0, rows, piece):
            part = pl.ds(pl.multiple_of(k * rows + at, 8), piece)
            x = xm[k, pl.ds(EDGE + at, piece)]
            cond[k, pl.ds(EDGE + at, piece)] = cols[part, 0:LANES] / (1.0 + cols[part, LANES : 2 * LANES] * x)

    first, last = iota((piece, LANES), 1) == 0, iota((piece, LANES), 1) == LANES - 1
    wz[0] = 0.5 * (cond[0, pl.ds(EDGE, rows)] + cond[1, pl.ds(EDGE, rows)])

    @pl.loop(1, count - 1)
    def _(k):
        for at in range(0, rows, piece):
            here = pl.ds(EDGE + at, piece)
            part = pl.ds(pl.multiple_of(k * rows + at, 8), piece)
            to = pl.ds(at, piece)
            c, end = cond[k, here], ends[part, :]
            up = 0.5 * (c + cond[k + 1, here])
            low = 0.5 * (c + cond[k - 1, here])
            right = 0.5 * (c + cond[k, pl.ds(EDGE + at + 1, piece)])
            left = 0.5 * (c + cond[k, pl.ds(EDGE + at - 1, piece)])
            e = 0.5 * (c + jnp.where(last, end, turned(c, -1, 1)))
            w = 0.5 * (c + jnp.where(first, end, turned(c, 1, 1)))
            cf = cols[part, 2 * LANES : 3 * LANES]
            diag = cf + up + low + right + left + e + w
            i = jnp.where(cf > 0.0, 1.0 / diag, 0.0)
            wz[k, to] = up
            wx[k, here] = right
            wy[k, to] = e
            wyw[k, to] = w
            inv[k, to] = i
            b0[k, to] = cf * xm[k, here] * i


def source_x_kernel(far, place, far_a, far_b, near_a, near_b, own, xa, xb):
    even = place[0] == 0
    for k, read in enumerate(layer_readers(far, place, far_a, far_b, near_a, near_b, own)):
        low, high = read(0, EDGE), read(LANES - EDGE, EDGE)
        xa[pl.ds(k * EDGE, EDGE), :] = jnp.where(even, high, low)
        xb[pl.ds(k * EDGE, EDGE), :] = jnp.where(even, low, high)


def source_y_kernel(far, place, far_a, far_b, near_a, near_b, own, xa, xb, full, sides, ya, yb):
    count, rows, _ = full.shape
    even = place[0] == 0
    full[0] = jnp.zeros((rows, LANES), F32)
    full[count - 1] = jnp.zeros((rows, LANES), F32)
    for k, read in enumerate(layer_readers(far, place, far_a, far_b, near_a, near_b, own)):
        a, b = xa[pl.ds(k * EDGE, EDGE), :], xb[pl.ds(k * EDGE, EDGE), :]
        full[k + 1, pl.ds(0, EDGE)] = jnp.where(even, b, a)
        full[k + 1, pl.ds(EDGE, LANES)] = read(0, LANES)
        full[k + 1, pl.ds(EDGE + LANES, EDGE)] = jnp.where(even, a, b)
    found = flat_sides(full[...].reshape(count * rows, LANES))
    sides[...] = found
    even = place[1] == 0
    ya[...] = jnp.where(even, found[EDGE:], found[:EDGE])
    yb[...] = jnp.where(even, found[:EDGE], found[EDGE:])


def sweep_kernel(place, xm, wz, wx, wy, wyw, inv, b0, strips, full, sides, ya, yb, ids, out, replies, b, d, xa, xb, ends):
    count, rows, _ = inv.shape
    total = count * rows
    even = place[1] == 0
    after, before = jnp.where(even, ya[...], yb[...]), jnp.where(even, yb[...], ya[...])
    factors = steps()

    sb = strips[7] + strip_of(sides[...], before, after) * strips[6]
    sx, sd = strips[8], None
    kept = [ends_of(sx)]
    for keep, add in factors[:-1]:
        near = strips[0] * turned(sx, rows, 1) + strips[1] * turned(sx, -rows, 1)
        near += strips[2] * turned(sx, 1, 1) + strips[3] * turned(sx, -1, 1)
        near += strips[4] * turned(sx, 1, 0) + strips[5] * turned(sx, -1, 0)
        step = add * (sb - sx + near)
        sd = step if sd is None else step + keep * sd
        sx = sx + sd
        kept.append(ends_of(sx))
    place_in = end_lanes(2 * SWEEPS, SWEEPS)
    big, small = parts(jnp.concatenate(kept, axis=0))
    ends[...] = dot(big, place_in, 0, 0) + dot(small, place_in, 0, 0)

    piece = 24
    first, last = iota((piece, LANES), 1) == 0, iota((piece, LANES), 1) == LANES - 1
    blank = jnp.zeros((EDGE, LANES), F32)

    @pl.loop(0, count)
    def _(k):
        for ref in (xa, xb):
            ref[k, pl.ds(0, EDGE)] = blank
            ref[k, pl.ds(rows + EDGE, EDGE)] = blank

    for s, (keep, add) in enumerate(factors):
        src, into = (xm if s == 0 else (xa if s % 2 else xb)), (xb if s % 2 else xa)

        @pl.loop(1 + s, count - 1 - s)
        def _(k):
            for at in range(0, rows, piece):
                here, to = pl.ds(EDGE + at, piece), pl.ds(at, piece)
                x = src[k, here]
                end = ends[pl.ds(pl.multiple_of(k * rows + at, 8), piece), s * LANES : (s + 1) * LANES]
                e = jnp.where(last, end, turned(x, -1, 1))
                w = jnp.where(first, end, turned(x, 1, 1))
                near = wz[k, to] * src[k + 1, here] + wz[k - 1, to] * src[k - 1, here]
                near += wx[k, here] * src[k, pl.ds(EDGE + at + 1, piece)]
                near += wx[k, pl.ds(EDGE + at - 1, piece)] * src[k, pl.ds(EDGE + at - 1, piece)]
                near += wy[k, to] * e + wyw[k, to] * w
                if s == 0:
                    rhs = b0[k, to] + full[k, to] * inv[k, to]
                    b[k, to] = rhs
                else:
                    rhs = b[k, to]
                step = add * (rhs - x + inv[k, to] * near)
                if s > 0:
                    step = step + keep * d[k, to]
                if s < SWEEPS - 1:
                    d[k, to] = step
                into[k, here] = x + step

    final = xb if SWEEPS % 2 == 0 else xa
    for k in range(4):
        out[pl.ds(k * LANES, LANES), :] = final[SWEEPS + k, pl.ds(2 * EDGE, LANES)]
    n = out.shape[0]
    name = ids[...]
    hot = jnp.concatenate([hot_of(name == iota(name.shape, 1) + at) for at in range(0, n, LANES)], axis=1)
    replies[...] = pick_rows(hot, out[...])


def final_kernel(returned, dest, gain, mob, mobility, ionization):
    total = returned.shape[0]
    name = dest[...]
    hot = jnp.concatenate([hot_of(name == iota(name.shape, 1) + at) for at in range(0, total, LANES)], axis=1)
    back = pick_rows(hot, returned[...])
    mobility[...] = mob[...] * jnp.exp(-0.7 * back)
    ionization[...] = jnp.exp(gain[...] * (1.0 + 0.3 * back))


def swapped(a, b, axis, apart=1):
    count = lax.axis_size(axis)
    found = []
    for v, odd in ((a, 0), (b, 1)):
        pairs = []
        for i in range(count - apart):
            if (i // apart) % 2 == odd:
                pairs += [(i, i + apart), (i + apart, i)]
        found.append(lax.ppermute(v, axis, pairs) if pairs else jnp.zeros_like(v))
    return found


def exchanged(v):
    lines = v.reshape(v.shape[0], 1, v.shape[1])
    return lax.all_to_all(lines, ("gx", "gy"), split_axis=0, concat_axis=0, tiled=True).reshape(v.shape)


def per_device(
    efield, density, mobility_prev, thermal_prev, owner, block, live, material,
    mat_conductivity, mat_softening, mat_capacity,
):
    layers, xcells, width = density.shape
    n = layers * xcells
    peers = lax.axis_size("gx") * lax.axis_size("gy")
    slots = max(2, 2 * n // peers)
    line = peers * (slots + 1)
    flat = lambda a: a.reshape(n, width)
    ef = efield.reshape(3, n, width)
    den, mob, x0 = flat(density), flat(mobility_prev), flat(thermal_prev)
    own, blk, liv = owner.reshape(1, n), block.reshape(1, n), live.reshape(1, n)
    mat = material.reshape(layers, xcells)
    sized = lambda *s: (s, F32)

    [sent] = call(functools.partial(dispatch_kernel, peers, slots), [sized(line, width)],
                  [ef, den, mob, own, blk, liv], "dispatch", flops=10**8)
    received = exchanged(sent)

    spot = [lax.axis_index(a) for a in ("gx", "gy", "gz")]
    place = jnp.stack([spot[0] % 2, spot[1] % 2, spot[2] % 2, spot[2] // 2 % 2])
    far = SWEEPS - layers
    count = layers + 2 * SWEEPS
    rows = xcells + 2 * EDGE
    total = count * rows
    aside = sized(far * xcells + EDGE, width)
    near, far_a, far_b = call(
        functools.partial(start_z_kernel, far), [sized(n + EDGE, width), aside, aside],
        [place, x0, mat], "start_z", smem=(0,))
    far_a, far_b = swapped(far_a, far_b, "gz", 2)
    near_a, near_b = swapped(near, near, "gz")
    xz, mats, xa, xb = call(
        functools.partial(start_x_kernel, far),
        [sized(count, xcells, width), sized(count, width)] + [sized(count * (EDGE + 1), width)] * 2,
        [place, far_a, far_b, near_a, near_b, near], "start_x", smem=(0,))
    xa, xb = swapped(xa, xb, "gx")
    tall = sized(count, rows + 2 * EDGE, width)
    xm, sides, flat_mat, ya, yb = call(
        start_y_kernel,
        [tall, sized(2 * EDGE, total), sized(EDGE, total), sized(2 * EDGE, total), sized(2 * EDGE, total)],
        [place, xz, mats, xa, xb], "start_y", smem=(0,))
    ya, yb = swapped(ya, yb, "gy")
    gain, dest = call(functools.partial(after_kernel, slots), [sized(n, width), ((n, LANES), I32)], [ef, own], "gain")
    received, ya, yb, gain, dest = lax.optimization_barrier((received, ya, yb, gain, dest))
    tile = sized(count, rows, width)
    weights = call(
        weights_kernel, [tile, tall, tile, tile, tile, tile, sized(9, 4 * EDGE, total)],
        [place, mat_conductivity, mat_softening, mat_capacity, xm, sides, flat_mat, ya, yb], "weights",
        scratch=[pltpu.VMEM((count, rows + 2 * EDGE, width), F32), pltpu.VMEM((total, 3 * width), F32),
                 pltpu.VMEM((total, width), F32)],
        limit=32, flops=10**9, smem=(0, 1, 2, 3))

    far -= 1
    source, far_a, far_b = call(
        functools.partial(combine_kernel, peers, slots, far),
        [sized(n, width)] + [sized(far * xcells, width)] * 2, [place, received], "combine", flops=10**8, smem=(0,))
    [ids] = call(functools.partial(ids_kernel, peers, slots), [((peers * slots, LANES), I32)], [received], "ids")
    far_a, far_b = swapped(far_a, far_b, "gz", 2)
    near_a, near_b = swapped(source, source, "gz")
    above = [place, far_a, far_b, near_a, near_b, source]
    xa, xb = call(functools.partial(source_x_kernel, far), [sized((count - 2) * EDGE, width)] * 2, above, "source_x", smem=(0,))
    xa, xb = swapped(xa, xb, "gx")
    full, sides, ya, yb = call(
        functools.partial(source_y_kernel, far),
        [tile, sized(2 * EDGE, total), sized(EDGE, total), sized(EDGE, total)], above + [xa, xb], "source_y", smem=(0,))
    ya, yb = swapped(ya, yb, "gy")
    x, replies = call(
        sweep_kernel, [sized(n, width), sized(peers * slots, width)],
        [place, xm] + list(weights) + [full, sides, ya, yb, ids], "sweeps",
        scratch=[pltpu.VMEM((count, rows, width), F32)] * 2 + [pltpu.VMEM((count, rows + 2 * EDGE, width), F32)] * 2
        + [pltpu.VMEM((total, SWEEPS * width), F32)],
        limit=36, flops=10**8, smem=(0,))
    returned = exchanged(replies)
    mobility, ionization = call(final_kernel, [sized(n, width)] * 2, [returned, dest, gain, mob], "finish", flops=10**8)
    shape = density.shape
    return x.reshape(shape), mobility.reshape(shape), ionization.reshape(shape)


def solution(mesh):
    tile = P("gz", "gx", "gy")
    rows = P("gz", "gx", "gy", None)
    placed = (
        P(None, "gz", "gx", "gy"), tile, tile, tile,
        P("gz", "gx", "gy", None, None), rows, rows, rows, P(), P(), P(),
    )
    return jax.shard_map(
        per_device, mesh=mesh, in_specs=placed, out_specs=(tile, tile, tile), check_vma=False
    )
```

time: 176 us -> 146 us (0.83)
  the two profiles are of different devices: /device:TPU:1 before, /device:TPU:131 now
where the time goes in v3:
time: 146 us
  starting transfers between devices  66.5 us (46%)
  blocking collectives  35.7 us (24%)
  Pallas kernels  26.7 us (18%)
  waiting for transfers between devices  10.5 us (7%)
  local copies, waits for them, and re-layouts  5.11 us (4%)
    ppermute x16, starting transfers between devices, swapped(): found.append(lax.ppermute(v, axis, pairs) if pairs else jnp.zeros_like(v))  55.6 us
    all_to_all x1, blocking collectives, exchanged(): lax.all_to_all(lines, ('gx', 'gy'), split_axis=0, concat_axis=0, tiled=True)  35.7 us
    pallas_call x12, Pallas kernels, call(): pl.pallas_call(kernel, out_shape=[jax.ShapeDtypeStruct(s, t) for s, t in...  26.7 us
    all_to_all x1, starting transfers between devices, exchanged(): lax.all_to_all(lines, ('gx', 'gy'), split_axis=0, concat_axis=0, tiled=True)  11 us
    ppermute x16, waiting for transfers between devices, swapped(): found.append(lax.ppermute(v, axis, pairs) if pairs else jnp.zeros_like(v))  10.5 us
    unnamed x28, local copies, waits for them, and re-layouts  5.11 us
  transfers between devices with their start and end apart: 17, of which 6 were waited for; matrix products, arithmetic and copies ran while one was open for 0% of the time, Pallas kernels for 5%

profile of v3, /device:TPU:131, one launch (start us, length us, event | category | flops | bytes accessed | tf_op | source)
XLA Modules:
  0.0 145.6 jit_solution(10333558926328161351)
XLA Ops:
  0.6 0.0 copy-start
  0.6 1.1 copy-done
  1.8 0.9 copy-done.2
  2.7 0.9 copy-done.5
  3.7 0.7 copy-done.6
  4.4 0.7 copy-done.9
  5.0 0.7 copy-done.10
  5.7 1.9 %dispatch.1 = f32[1088,128]{1,0:T(8,128)} custom-call(f32[3,512,128]{2,1,0:T(8,128)S(1)} %bitcast.25, f32[512,128]{1,0:T(8,128)S(1)} %bitcast.32, f32[512,128]{1,0:T(8,128)S(1)} %bitcast.28, s32[1,512]{1,0:T(1,128)S(1)} %bitcast.33, s32[1,512]{1,0:T(1,128)S(1)} %bitcast.36, s32[1,512]{1,0:T(1,128)S(1)} %bitcast.37), custom_call_target="tpu_custom_call" | custom-call | flops 100000000 | bytes 1873920 | tf_op jit(solution)/shard_map/dispatch/pallas_call | solution.py:71
  7.6 11.0 %all-to-all-start = ((f32[1088,1,128]{2,1,0:T(1,128)}), f32[1088,1,128]{2,1,0:T(1,128)S(1)}, u32[]{:S(2)}, u32[]{:S(2)}) async-start(f32[1088,1,128]{2,1,0:T(1,128)} %bitcast.13), calls=%async_computation | async-start | bytes 1114112 | tf_op jit(solution)/shard_map/all_to_all | solution.py:472
  18.6 0.1 pad_add_fusion.place
  18.7 0.6 start_z.1
  19.3 0.0 copy-start.1
  19.3 0.0 copy-start.7
  19.3 2.1 %collective-permute-start.3 = (f32[520,128]{1,0:T(8,128)S(1)}, f32[520,128]{1,0:T(8,128)S(1)}, u32[]{:S(2)}, u32[]{:S(2)}) collective-permute-start(f32[520,128]{1,0:T(8,128)S(1)} %get-tuple-element.44.own), channel_id=1, source_target_pairs={{1,2},{2,1},{3,4},{4,3},{5,6},{6,5},{9,10},{10,9},{11,12},{12,11},... | collective-permute-start | bytes 798728 | tf_op jit(solution)/shard_map/ppermute | solution.py:466
  21.4 7.3 %collective-permute-start.2 = (f32[520,128]{1,0:T(8,128)S(1)}, f32[520,128]{1,0:T(8,128)S(1)}, u32[]{:S(2)}, u32[]{:S(2)}) collective-permute-start(f32[520,128]{1,0:T(8,128)S(1)} %get-tuple-element.44.own), channel_id=1, source_target_pairs={{0,1},{1,0},{2,3},{3,2},{4,5},{5,4},{6,7},{7,6},{8,9},{9,8},{10,11... | collective-permute-start | bytes 798728 | tf_op jit(solution)/shard_map/ppermute | solution.py:466
  28.7 1.9 %collective-permute-start = (f32[264,128]{1,0:T(8,128)S(1)}, f32[264,128]{1,0:T(8,128)S(1)}, u32[]{:S(2)}, u32[]{:S(2)}) collective-permute-start(f32[264,128]{1,0:T(8,128)S(1)} %get-tuple-element.42), channel_id=1, source_target_pairs={{0,2},{2,0},{1,3},{3,1},{4,6},{6,4},{5,7},{7,5},{8,10},{10,8},{9,1... | collective-permute-start | bytes 405512 | tf_op jit(solution)/shard_map/ppermute | solution.py:466
  30.6 4.0 %collective-permute-start.1 = (f32[264,128]{1,0:T(8,128)S(1)}, f32[264,128]{1,0:T(8,128)S(1)}, u32[]{:S(2)}, u32[]{:S(2)}) collective-permute-start(f32[264,128]{1,0:T(8,128)S(1)} %get-tuple-element.43), channel_id=1, source_target_pairs={{2,4},{4,2},{3,5},{5,3},{10,12},{12,10},{11,13},{13,11},{18,20},{2... | collective-permute-start | bytes 405512 | tf_op jit(solution)/shard_map/ppermute | solution.py:466
  34.6 1.1 collective-permute-done.far_a
  35.7 4.0 %collective-permute-done.1.far_b = f32[264,128]{1,0:T(8,128)S(1)} collective-permute-done((f32[264,128]{1,0:T(8,128)S(1)}, f32[264,128]{1,0:T(8,128)S(1)}, u32[]{:S(2)}, u32[]{:S(2)}) %collective-permute-start.1) | collective-permute-done | bytes 135200 | tf_op jit(solution)/shard_map/ppermute | solution.py:466
  39.7 0.6 start_x.1
  40.4 3.1 %collective-permute-start.4 = (f32[144,128]{1,0:T(8,128)S(1)}, f32[144,128]{1,0:T(8,128)S(1)}, u32[]{:S(2)}, u32[]{:S(2)}) collective-permute-start(f32[144,128]{1,0:T(8,128)S(1)} %get-tuple-element.47), channel_id=1, source_target_pairs={{0,32},{32,0},{64,96},{96,64},{128,160},{160,128},{192,224},{224,1... | collective-permute-start | bytes 221192 | tf_op jit(solution)/shard_map/ppermute | solution.py:466
  43.5 0.7 collective-permute-start.5
  44.2 1.3 collective-permute-done.4.xa
  45.5 1.2 start_y.1
  46.6 5.5 %collective-permute-start.6 = (f32[16,2304]{1,0:T(8,128)S(1)}, f32[16,2304]{1,0:T(8,128)S(1)}, u32[]{:S(2)}, u32[]{:S(2)}) collective-permute-start(f32[16,2304]{1,0:T(8,128)S(1)} %get-tuple-element.52), channel_id=1, source_target_pairs={{0,8},{8,0},{16,24},{24,16},{1,9},{9,1},{17,25},{25,17},{2,10},{10... | collective-permute-start | bytes 442376 | tf_op jit(solution)/shard_map/ppermute | solution.py:466
  52.2 0.7 collective-permute-start.7
  52.9 1.0 gain.1
  53.9 1.3 combine.1
  55.2 2.7 %collective-permute-start.11 = (f32[512,128]{1,0:T(8,128)S(1)}, f32[512,128]{1,0:T(8,128)S(1)}, u32[]{:S(2)}, u32[]{:S(2)}) collective-permute-start(f32[512,128]{1,0:T(8,128)S(1)} %get-tuple-element.68.own), channel_id=1, source_target_pairs={{1,2},{2,1},{3,4},{4,3},{5,6},{6,5},{9,10},{10,9},{11,12},{12,11},... | collective-permute-start | bytes 786440 | tf_op jit(solution)/shard_map/ppermute | solution.py:466
  57.9 4.7 %collective-permute-start.10 = (f32[512,128]{1,0:T(8,128)S(1)}, f32[512,128]{1,0:T(8,128)S(1)}, u32[]{:S(2)}, u32[]{:S(2)}) collective-permute-start(f32[512,128]{1,0:T(8,128)S(1)} %get-tuple-element.68.own), channel_id=1, source_target_pairs={{0,1},{1,0},{2,3},{3,2},{4,5},{5,4},{6,7},{7,6},{8,9},{9,8},{10,11... | collective-permute-start | bytes 786440 | tf_op jit(solution)/shard_map/ppermute | solution.py:466
  62.6 1.9 %collective-permute-start.8 = (f32[128,128]{1,0:T(8,128)S(1)}, f32[128,128]{1,0:T(8,128)S(1)}, u32[]{:S(2)}, u32[]{:S(2)}) collective-permute-start(f32[128,128]{1,0:T(8,128)S(1)} %get-tuple-element.66), channel_id=1, source_target_pairs={{0,2},{2,0},{1,3},{3,1},{4,6},{6,4},{5,7},{7,5},{8,10},{10,8},{9,1... | collective-permute-start | bytes 196616 | tf_op jit(solution)/shard_map/ppermute | solution.py:466
  64.5 4.3 %collective-permute-start.9 = (f32[128,128]{1,0:T(8,128)S(1)}, f32[128,128]{1,0:T(8,128)S(1)}, u32[]{:S(2)}, u32[]{:S(2)}) collective-permute-start(f32[128,128]{1,0:T(8,128)S(1)} %get-tuple-element.67), channel_id=1, source_target_pairs={{2,4},{4,2},{3,5},{5,3},{10,12},{12,10},{11,13},{13,11},{18,20},{2... | collective-permute-start | bytes 196616 | tf_op jit(solution)/shard_map/ppermute | solution.py:466
  68.8 0.1 collective-permute-done.8.far_a
  68.9 3.4 %collective-permute-done.9.far_b = f32[128,128]{1,0:T(8,128)S(1)} collective-permute-done((f32[128,128]{1,0:T(8,128)S(1)}, f32[128,128]{1,0:T(8,128)S(1)}, u32[]{:S(2)}, u32[]{:S(2)}) %collective-permute-start.9) | collective-permute-done | bytes 65568 | tf_op jit(solution)/shard_map/ppermute | solution.py:466
  72.4 0.6 source_x.1
  72.9 0.0 copy-start.11
  73.0 0.0 copy-start.13
  73.0 6.1 %collective-permute-start.12 = (f32[112,128]{1,0:T(8,128)S(1)}, f32[112,128]{1,0:T(8,128)S(1)}, u32[]{:S(2)}, u32[]{:S(2)}) collective-permute-start(f32[112,128]{1,0:T(8,128)S(1)} %get-tuple-element.69), channel_id=1, source_target_pairs={{0,32},{32,0},{64,96},{96,64},{128,160},{160,128},{192,224},{224,1... | collective-permute-start | bytes 172040 | tf_op jit(solution)/shard_map/ppermute | solution.py:466
  79.0 0.7 collective-permute-start.13
  79.7 0.4 ids.1
  80.1 0.5 collective-permute-done.12.xa
  80.6 1.0 source_y.1
  81.5 9.2 %collective-permute-start.14 = (f32[8,2304]{1,0:T(8,128)S(1)}, f32[8,2304]{1,0:T(8,128)S(1)}, u32[]{:S(2)}, u32[]{:S(2)}) collective-permute-start(f32[8,2304]{1,0:T(8,128)S(1)} %get-tuple-element.73), channel_id=1, source_target_pairs={{0,8},{8,0},{16,24},{24,16},{1,9},{9,1},{17,25},{25,17},{2,10},{10... | collective-permute-start | bytes 221192 | tf_op jit(solution)/shard_map/ppermute | solution.py:466
  90.8 0.8 collective-permute-start.15
  91.6 4.0 %weights.1 = (f32[16,144,128]{2,1,0:T(8,128)S(1)}, f32[16,160,128]{2,1,0:T(8,128)S(1)}, f32[16,144,128]{2,1,0:T(8,128)S(1)}, f32[16,144,128]{2,1,0:T(8,128)S(1)}...) custom-call(s32[4]{0:T(128)S(1)} %pad_add_fusion.place, f32[8]{0:T(128)S(1)} %copy-done.11, ...), custom_call_target="tpu_custom_call" | custom-call | flops 1000000000 | bytes 11690096 | tf_op jit(solution)/shard_map/weights/pallas_call | solution.py:71
  95.7 13.0 %sweeps.1 = (f32[512,128]{1,0:T(8,128)}, f32[1024,128]{1,0:T(8,128)S(1)}) custom-call(s32[4]{0:T(128)S(1)} %pad_add_fusion.place, f32[16,160,128]{2,1,0:T(8,128)S(1)} %get-tuple-element.49.xm, f32[16,144,128]{2,1,0:T(8,128)S(1)} %get-tuple-element.58.wz, f32[16,160,128]{2,1,0:T(8,128)S(1)} %get-tuple-element.59.wx, ...), custom_call_target="tpu_custom_call" | custom-call | flops 100000000 | bytes 13959184 | tf_op jit(solution)/shard_map/sweeps/pallas_call | solution.py:71
  108.7 35.7 %all_to_all.10 = f32[1024,1,128]{2,1,0:T(1,128)S(1)} all-to-all(f32[1024,1,128]{2,1,0:T(1,128)S(1)} %bitcast.30), channel_id=1, replica_groups=mesh['gx'=16,'gy'=4,'gz'=8] {'gx','gy'}, dimensions={0} | all-to-all | bytes 1048576 | tf_op jit(solution)/shard_map/all_to_all | solution.py:472
  144.4 1.2 finish.1
  (28 shorter events, 0.1 us)
Async XLA Ops:
  0.6 1.1 copy-start
  1.8 0.9 copy-start.2
  2.7 0.9 copy-start.5
  3.7 0.7 copy-start.6
  4.4 0.7 copy-start.9
  5.0 0.7 copy-start.10
  5.7 13.0 %copy-start.4 = (f32[4,128,128]{2,1,0:T(8,128)S(1)}, f32[4,128,128]{2,1,0:T(8,128)}, u32[]{:S(2)}) copy-start(f32[4,128,128]{2,1,0:T(8,128)} %param.14) | copy-start | bytes 786436
  5.7 13.0 %copy-start.8 = (s32[1,1,1,512]{3,2,1,0:T(1,128)S(1)}, s32[1,1,1,512]{3,2,1,0:T(1,128)}, u32[]{:S(2)}) copy-start(s32[1,1,1,512]{3,2,1,0:T(1,128)} %param.18) | copy-start | bytes 6148
  7.6 46.3 %all-to-all-start = ((f32[1088,1,128]{2,1,0:T(1,128)}), f32[1088,1,128]{2,1,0:T(1,128)S(1)}, u32[]{:S(2)}, u32[]{:S(2)}) async-start(f32[1088,1,128]{2,1,0:T(1,128)} %bitcast.13), calls=%async_computation | async-start | bytes 1114112 | tf_op jit(solution)/shard_map/all_to_all | solution.py:472
  19.3 33.6 %copy-start.1 = (f32[3,4,128,128]{3,2,1,0:T(8,128)S(1)}, f32[3,4,128,128]{3,2,1,0:T(8,128)}, u32[]{:S(2)}) copy-start(f32[3,4,128,128]{3,2,1,0:T(8,128)} %param.11) | copy-start | bytes 2359300
  19.3 33.6 %copy-start.7 = (s32[1,1,1,512,1]{3,4,2,1,0:T(1,128)S(1)}, s32[1,1,1,512,1]{3,4,2,1,0:T(1,128)}, u32[]{:S(2)}) copy-start(s32[1,1,1,512,1]{3,4,2,1,0:T(1,128)} %param.15) | copy-start | bytes 6148
  19.3 20.4 %collective-permute-start.3 = (f32[520,128]{1,0:T(8,128)S(1)}, f32[520,128]{1,0:T(8,128)S(1)}, u32[]{:S(2)}, u32[]{:S(2)}) collective-permute-start(f32[520,128]{1,0:T(8,128)S(1)} %get-tuple-element.44.own), channel_id=1, source_target_pairs={{1,2},{2,1},{3,4},{4,3},{5,6},{6,5},{9,10},{10,9},{11,12},{12,11},... | collective-permute-start | bytes 798728 | tf_op jit(solution)/shard_map/ppermute | solution.py:466
  21.4 18.4 %collective-permute-start.2 = (f32[520,128]{1,0:T(8,128)S(1)}, f32[520,128]{1,0:T(8,128)S(1)}, u32[]{:S(2)}, u32[]{:S(2)}) collective-permute-start(f32[520,128]{1,0:T(8,128)S(1)} %get-tuple-element.44.own), channel_id=1, source_target_pairs={{0,1},{1,0},{2,3},{3,2},{4,5},{5,4},{6,7},{7,6},{8,9},{9,8},{10,11... | collective-permute-start | bytes 798728 | tf_op jit(solution)/shard_map/ppermute | solution.py:466
  28.7 7.1 %collective-permute-start = (f32[264,128]{1,0:T(8,128)S(1)}, f32[264,128]{1,0:T(8,128)S(1)}, u32[]{:S(2)}, u32[]{:S(2)}) collective-permute-start(f32[264,128]{1,0:T(8,128)S(1)} %get-tuple-element.42), channel_id=1, source_target_pairs={{0,2},{2,0},{1,3},{3,1},{4,6},{6,4},{5,7},{7,5},{8,10},{10,8},{9,1... | collective-permute-start | bytes 405512 | tf_op jit(solution)/shard_map/ppermute | solution.py:466
  30.6 9.1 %collective-permute-start.1 = (f32[264,128]{1,0:T(8,128)S(1)}, f32[264,128]{1,0:T(8,128)S(1)}, u32[]{:S(2)}, u32[]{:S(2)}) collective-permute-start(f32[264,128]{1,0:T(8,128)S(1)} %get-tuple-element.43), channel_id=1, source_target_pairs={{2,4},{4,2},{3,5},{5,3},{10,12},{12,10},{11,13},{13,11},{18,20},{2... | collective-permute-start | bytes 405512 | tf_op jit(solution)/shard_map/ppermute | solution.py:466
  40.4 5.1 %collective-permute-start.4 = (f32[144,128]{1,0:T(8,128)S(1)}, f32[144,128]{1,0:T(8,128)S(1)}, u32[]{:S(2)}, u32[]{:S(2)}) collective-permute-start(f32[144,128]{1,0:T(8,128)S(1)} %get-tuple-element.47), channel_id=1, source_target_pairs={{0,32},{32,0},{64,96},{96,64},{128,160},{160,128},{192,224},{224,1... | collective-permute-start | bytes 221192 | tf_op jit(solution)/shard_map/ppermute | solution.py:466
  43.5 2.0 %collective-permute-start.5 = (f32[144,128]{1,0:T(8,128)S(1)}, f32[144,128]{1,0:T(8,128)S(1)}, u32[]{:S(2)}, u32[]{:S(2)}) collective-permute-start(f32[144,128]{1,0:T(8,128)S(1)} %get-tuple-element.48), channel_id=1, source_target_pairs={{32,64},{64,32},{96,128},{128,96},{160,192},{192,160},{224,256},{2... | collective-permute-start | bytes 221192 | tf_op jit(solution)/shard_map/ppermute | solution.py:466
  46.6 7.3 %collective-permute-start.6 = (f32[16,2304]{1,0:T(8,128)S(1)}, f32[16,2304]{1,0:T(8,128)S(1)}, u32[]{:S(2)}, u32[]{:S(2)}) collective-permute-start(f32[16,2304]{1,0:T(8,128)S(1)} %get-tuple-element.52), channel_id=1, source_target_pairs={{0,8},{8,0},{16,24},{24,16},{1,9},{9,1},{17,25},{25,17},{2,10},{10... | collective-permute-start | bytes 442376 | tf_op jit(solution)/shard_map/ppermute | solution.py:466
  52.2 1.7 %collective-permute-start.7 = (f32[16,2304]{1,0:T(8,128)S(1)}, f32[16,2304]{1,0:T(8,128)S(1)}, u32[]{:S(2)}, u32[]{:S(2)}) collective-permute-start(f32[16,2304]{1,0:T(8,128)S(1)} %get-tuple-element.53), channel_id=1, source_target_pairs={{8,16},{16,8},{9,17},{17,9},{10,18},{18,10},{11,19},{19,11},{12,20... | collective-permute-start | bytes 442376 | tf_op jit(solution)/shard_map/ppermute | solution.py:466
  55.2 17.1 %collective-permute-start.11 = (f32[512,128]{1,0:T(8,128)S(1)}, f32[512,128]{1,0:T(8,128)S(1)}, u32[]{:S(2)}, u32[]{:S(2)}) collective-permute-start(f32[512,128]{1,0:T(8,128)S(1)} %get-tuple-element.68.own), channel_id=1, source_target_pairs={{1,2},{2,1},{3,4},{4,3},{5,6},{6,5},{9,10},{10,9},{11,12},{12,11},... | collective-permute-start | bytes 786440 | tf_op jit(solution)/shard_map/ppermute | solution.py:466
  57.9 14.5 %collective-permute-start.10 = (f32[512,128]{1,0:T(8,128)S(1)}, f32[512,128]{1,0:T(8,128)S(1)}, u32[]{:S(2)}, u32[]{:S(2)}) collective-permute-start(f32[512,128]{1,0:T(8,128)S(1)} %get-tuple-element.68.own), channel_id=1, source_target_pairs={{0,1},{1,0},{2,3},{3,2},{4,5},{5,4},{6,7},{7,6},{8,9},{9,8},{10,11... | collective-permute-start | bytes 786440 | tf_op jit(solution)/shard_map/ppermute | solution.py:466
  62.6 6.3 %collective-permute-start.8 = (f32[128,128]{1,0:T(8,128)S(1)}, f32[128,128]{1,0:T(8,128)S(1)}, u32[]{:S(2)}, u32[]{:S(2)}) collective-permute-start(f32[128,128]{1,0:T(8,128)S(1)} %get-tuple-element.66), channel_id=1, source_target_pairs={{0,2},{2,0},{1,3},{3,1},{4,6},{6,4},{5,7},{7,5},{8,10},{10,8},{9,1... | collective-permute-start | bytes 196616 | tf_op jit(solution)/shard_map/ppermute | solution.py:466
  64.5 7.8 %collective-permute-start.9 = (f32[128,128]{1,0:T(8,128)S(1)}, f32[128,128]{1,0:T(8,128)S(1)}, u32[]{:S(2)}, u32[]{:S(2)}) collective-permute-start(f32[128,128]{1,0:T(8,128)S(1)} %get-tuple-element.67), channel_id=1, source_target_pairs={{2,4},{4,2},{3,5},{5,3},{10,12},{12,10},{11,13},{13,11},{18,20},{2... | collective-permute-start | bytes 196616 | tf_op jit(solution)/shard_map/ppermute | solution.py:466
  72.9 18.7 %copy-start.11 = (f32[8]{0:T(128)S(1)}, f32[8]{0:T(128)}, u32[]{:S(2)}) copy-start(f32[8]{0:T(128)} %base.1) | copy-start | bytes 100
  72.9 18.7 %copy-start.12 = (f32[8]{0:T(128)S(1)}, f32[8]{0:T(128)}, u32[]{:S(2)}) copy-start(f32[8]{0:T(128)} %soft.1) | copy-start | bytes 100
  73.0 18.7 %copy-start.13 = (f32[8]{0:T(128)S(1)}, f32[8]{0:T(128)}, u32[]{:S(2)}) copy-start(f32[8]{0:T(128)} %heat.1) | copy-start | bytes 100
  73.0 7.6 %collective-permute-start.12 = (f32[112,128]{1,0:T(8,128)S(1)}, f32[112,128]{1,0:T(8,128)S(1)}, u32[]{:S(2)}, u32[]{:S(2)}) collective-permute-start(f32[112,128]{1,0:T(8,128)S(1)} %get-tuple-element.69), channel_id=1, source_target_pairs={{0,32},{32,0},{64,96},{96,64},{128,160},{160,128},{192,224},{224,1... | collective-permute-start | bytes 172040 | tf_op jit(solution)/shard_map/ppermute | solution.py:466
  79.0 1.6 %collective-permute-start.13 = (f32[112,128]{1,0:T(8,128)S(1)}, f32[112,128]{1,0:T(8,128)S(1)}, u32[]{:S(2)}, u32[]{:S(2)}) collective-permute-start(f32[112,128]{1,0:T(8,128)S(1)} %get-tuple-element.70), channel_id=1, source_target_pairs={{32,64},{64,32},{96,128},{128,96},{160,192},{192,160},{224,256},{2... | collective-permute-start | bytes 172040 | tf_op jit(solution)/shard_map/ppermute | solution.py:466
  81.5 14.1 %collective-permute-start.14 = (f32[8,2304]{1,0:T(8,128)S(1)}, f32[8,2304]{1,0:T(8,128)S(1)}, u32[]{:S(2)}, u32[]{:S(2)}) collective-permute-start(f32[8,2304]{1,0:T(8,128)S(1)} %get-tuple-element.73), channel_id=1, source_target_pairs={{0,8},{8,0},{16,24},{24,16},{1,9},{9,1},{17,25},{25,17},{2,10},{10... | collective-permute-start | bytes 221192 | tf_op jit(solution)/shard_map/ppermute | solution.py:466
  90.8 4.9 %collective-permute-start.15 = (f32[8,2304]{1,0:T(8,128)S(1)}, f32[8,2304]{1,0:T(8,128)S(1)}, u32[]{:S(2)}, u32[]{:S(2)}) collective-permute-start(f32[8,2304]{1,0:T(8,128)S(1)} %get-tuple-element.74), channel_id=1, source_target_pairs={{8,16},{16,8},{9,17},{17,9},{10,18},{18,10},{11,19},{19,11},{12,20... | collective-permute-start | bytes 221192 | tf_op jit(solution)/shard_map/ppermute | solution.py:466
  108.7 35.7 %copy-start.3 = (f32[4,128,128]{2,1,0:T(8,128)S(1)}, f32[4,128,128]{2,1,0:T(8,128)}, u32[]{:S(2)}) copy-start(f32[4,128,128]{2,1,0:T(8,128)} %param.13) | copy-start | bytes 786436

commit v4 on v3

--- a/solution.py
+++ b/solution.py
@@ -66,13 +66,13 @@
     return hot_of(y == jnp.where(r < EDGE, r, r + LANES - 2 * EDGE))
 
 
-def call(kernel, outs, ins, name, scratch=(), limit=32, flops=0, smem=()):
+def call(kernel, outs, ins, name, scratch=(), limit=32, flops=0, smem=(), hbm=False):
     bytes_of = lambda a: a.size * a.dtype.itemsize
     return pl.pallas_call(
         kernel,
         out_shape=[jax.ShapeDtypeStruct(s, t) for s, t in outs],
         in_specs=[
-            pl.BlockSpec(memory_space=pltpu.SMEM if i in smem else pltpu.VMEM)
+            pl.BlockSpec(memory_space=pltpu.SMEM if i in smem else pltpu.HBM if hbm else pltpu.VMEM)
             for i in range(len(ins))
         ],
         out_specs=[pl.BlockSpec(memory_space=pltpu.VMEM) for _ in outs],
@@ -88,7 +88,14 @@
     )(*ins)
 
 
-def dispatch_kernel(peers, slots, ef, den, mob, owner, block, live, out):
+def dispatch_kernel(peers, slots, *refs):
+    far, out, near, sems = refs[:6], refs[6], refs[7:13], refs[13]
+    copies = [pltpu.make_async_copy(a, b, sems.at[i]) for i, (a, b) in enumerate(zip(far, near))]
+    for copy in copies:
+        copy.start()
+    for copy in copies:
+        copy.wait()
+    ef, den, mob, owner, block, live = near
     n = owner.shape[1]
     esq = ef[0] * ef[0] + ef[1] * ef[1] + ef[2] * ef[2]
     heat = 0.2 * den[...] * mob[...] * esq
@@ -397,8 +404,8 @@
         sx = sx + sd
         kept.append(ends_of(sx))
     place_in = end_lanes(2 * SWEEPS, SWEEPS)
-    big, small = parts(jnp.concatenate(kept, axis=0))
-    ends[...] = dot(big, place_in, 0, 0) + dot(small, place_in, 0, 0)
+    kept = jnp.concatenate(parts(jnp.concatenate(kept, axis=0)), axis=0)
+    ends[...] = dot(kept, jnp.concatenate([place_in, place_in], axis=0), 0, 0)
 
     piece = 24
     first, last = iota((piece, LANES), 1) == 0, iota((piece, LANES), 1) == LANES - 1
@@ -488,8 +495,10 @@
     mat = material.reshape(layers, xcells)
     sized = lambda *s: (s, F32)
 
-    [sent] = call(functools.partial(dispatch_kernel, peers, slots), [sized(line, width)],
-                  [ef, den, mob, own, blk, liv], "dispatch", flops=10**8)
+    given = [ef, den, mob, own, blk, liv]
+    [sent] = call(
+        functools.partial(dispatch_kernel, peers, slots), [sized(line, width)], given, "dispatch", flops=10**8, hbm=True, limit=60,
+        scratch=[pltpu.VMEM(a.shape, a.dtype) for a in given] + [pltpu.SemaphoreType.DMA((len(given),))])
     received = exchanged(sent)
 
     spot = [lax.axis_index(a) for a in ("gx", "gy", "gz")]
@@ -503,12 +512,14 @@
         functools.partial(start_z_kernel, far), [sized(n + EDGE, width), aside, aside],
         [place, x0, mat], "start_z", smem=(0,))
     far_a, far_b = swapped(far_a, far_b, "gz", 2)
+    near, far_a, far_b = lax.optimization_barrier((near, far_a, far_b))
     near_a, near_b = swapped(near, near, "gz")
     xz, mats, xa, xb = call(
         functools.partial(start_x_kernel, far),
         [sized(count, xcells, width), sized(count, width)] + [sized(count * (EDGE + 1), width)] * 2,
         [place, far_a, far_b, near_a, near_b, near], "start_x", smem=(0,))
     xa, xb = swapped(xa, xb, "gx")
+    received, xa, xb = lax.optimization_barrier((received, xa, xb))
     tall = sized(count, rows + 2 * EDGE, width)
     xm, sides, flat_mat, ya, yb = call(
         start_y_kernel,
@@ -516,7 +527,15 @@
         [place, xz, mats, xa, xb], "start_y", smem=(0,))
     ya, yb = swapped(ya, yb, "gy")
     gain, dest = call(functools.partial(after_kernel, slots), [sized(n, width), ((n, LANES), I32)], [ef, own], "gain")
-    received, ya, yb, gain, dest = lax.optimization_barrier((received, ya, yb, gain, dest))
+    far -= 1
+    source, far_a, far_b = call(
+        functools.partial(combine_kernel, peers, slots, far),
+        [sized(n, width)] + [sized(far * xcells, width)] * 2, [place, received], "combine", flops=10**8, smem=(0,))
+    [ids] = call(functools.partial(ids_kernel, peers, slots), [((peers * slots, LANES), I32)], [received], "ids")
+    far_a, far_b = swapped(far_a, far_b, "gz", 2)
+    source, far_a, far_b = lax.optimization_barrier((source, far_a, far_b))
+    near_a, near_b = swapped(source, source, "gz")
+    near_a, near_b, ya, yb = lax.optimization_barrier((near_a, near_b, ya, yb))
     tile = sized(count, rows, width)
     weights = call(
         weights_kernel, [tile, tall, tile, tile, tile, tile, sized(9, 4 * EDGE, total)],
@@ -524,17 +543,10 @@
         scratch=[pltpu.VMEM((count, rows + 2 * EDGE, width), F32), pltpu.VMEM((total, 3 * width), F32),
                  pltpu.VMEM((total, width), F32)],
         limit=32, flops=10**9, smem=(0, 1, 2, 3))
-
-    far -= 1
-    source, far_a, far_b = call(
-        functools.partial(combine_kernel, peers, slots, far),
-        [sized(n, width)] + [sized(far * xcells, width)] * 2, [place, received], "combine", flops=10**8, smem=(0,))
-    [ids] = call(functools.partial(ids_kernel, peers, slots), [((peers * slots, LANES), I32)], [received], "ids")
-    far_a, far_b = swapped(far_a, far_b, "gz", 2)
-    near_a, near_b = swapped(source, source, "gz")
     above = [place, far_a, far_b, near_a, near_b, source]
     xa, xb = call(functools.partial(source_x_kernel, far), [sized((count - 2) * EDGE, width)] * 2, above, "source_x", smem=(0,))
     xa, xb = swapped(xa, xb, "gx")
+    xa, xb, weights, ids, gain, dest = lax.optimization_barrier((xa, xb, weights, ids, gain, dest))
     full, sides, ya, yb = call(
         functools.partial(source_y_kernel, far),
         [tile, sized(2 * EDGE, total), sized(EDGE, total), sized(EDGE, total)], above + [xa, xb], "source_y", smem=(0,))

time: 146 us -> 151 us (1.034)
  the two profiles are of different devices: /device:TPU:131 before, /device:TPU:1 now
where the time goes in v4:
time: 151 us; the launch traced here: 150 us
  starting transfers between devices  74.2 us (49%)
  blocking collectives  31.3 us (21%)
  Pallas kernels  26.5 us (18%)
  waiting for transfers between devices  17.1 us (11%)
    ppermute x16, starting transfers between devices, swapped(): found.append(lax.ppermute(v, axis, pairs) if pairs else jnp.zeros_like(v))  62.6 us
    all_to_all x1, blocking collectives, exchanged(): lax.all_to_all(lines, ('gx', 'gy'), split_axis=0, concat_axis=0, tiled=True)  31.3 us
    pallas_call x12, Pallas kernels, call(): pl.pallas_call(kernel, out_shape=[jax.ShapeDtypeStruct(s, t) for s, t in...  26.5 us
    ppermute x16, waiting for transfers between devices, swapped(): found.append(lax.ppermute(v, axis, pairs) if pairs else jnp.zeros_like(v))  17.1 us
    all_to_all x1, starting transfers between devices, exchanged(): lax.all_to_all(lines, ('gx', 'gy'), split_axis=0, concat_axis=0, tiled=True)  11.6 us
  transfers between devices with their start and end apart: 17, of which 6 were waited for; matrix products, arithmetic and copies ran while one was open for 0% of the time, Pallas kernels for 5%

profile of v4, /device:TPU:1, one launch (start us, length us, event | category | flops | bytes accessed | tf_op | source)
XLA Modules:
  0.0 150.2 jit_solution(868825045794919004)
XLA Ops:
  0.7 3.3 %dispatch.1 = f32[1088,128]{1,0:T(8,128)} custom-call(f32[3,512,128]{2,1,0:T(8,128)} %bitcast.25, f32[512,128]{1,0:T(8,128)} %bitcast.36, f32[512,128]{1,0:T(8,128)} %bitcast.28, s32[1,512]{1,0:T(1,128)} %bitcast.32, s32[1,512]{1,0:T(1,128)} %bitcast.37, s32[1,512]{1,0:T(1,128)} %bitcast.38), custom_call_target="tpu_custom_call" | custom-call | flops 100000000 | bytes 1873920 | tf_op jit(solution)/shard_map/dispatch/pallas_call | solution.py:71
  3.9 11.6 %all-to-all-start = ((f32[1088,1,128]{2,1,0:T(1,128)}), f32[1088,1,128]{2,1,0:T(1,128)S(1)}, u32[]{:S(2)}, u32[]{:S(2)}) async-start(f32[1088,1,128]{2,1,0:T(1,128)} %bitcast.35), calls=%async_computation | async-start | bytes 1114112 | tf_op jit(solution)/shard_map/all_to_all | solution.py:479
  15.6 0.1 pad_add_fusion.place
  15.7 0.6 start_z.1
  16.3 5.8 %collective-permute-start = (f32[264,128]{1,0:T(8,128)S(1)}, f32[264,128]{1,0:T(8,128)S(1)}, u32[]{:S(2)}, u32[]{:S(2)}) collective-permute-start(f32[264,128]{1,0:T(8,128)S(1)} %get-tuple-element.63), channel_id=1, source_target_pairs={{0,2},{2,0},{1,3},{3,1},{4,6},{6,4},{5,7},{7,5},{8,10},{10,8},{9,1... | collective-permute-start | bytes 405512 | tf_op jit(solution)/shard_map/ppermute | solution.py:473
  22.1 0.7 collective-permute-start.1
  22.8 5.8 %collective-permute-done.far_a = f32[264,128]{1,0:T(8,128)S(1)} collective-permute-done((f32[264,128]{1,0:T(8,128)S(1)}, f32[264,128]{1,0:T(8,128)S(1)}, u32[]{:S(2)}, u32[]{:S(2)}) %collective-permute-start) | collective-permute-done | bytes 135200 | tf_op jit(solution)/shard_map/ppermute | solution.py:473
  28.6 0.0 collective-permute-done.1.far_b
  28.6 0.8 collective-permute-start.3
  29.4 10.4 %collective-permute-start.2 = (f32[520,128]{1,0:T(8,128)S(1)}, f32[520,128]{1,0:T(8,128)S(1)}, u32[]{:S(2)}, u32[]{:S(2)}) collective-permute-start(f32[520,128]{1,0:T(8,128)S(1)} %get-tuple-element.67.own), channel_id=1, source_target_pairs={{0,1},{1,0},{2,3},{3,2},{4,5},{5,4},{6,7},{7,6},{8,9},{9,8},{10,11... | collective-permute-start | bytes 798728 | tf_op jit(solution)/shard_map/ppermute | solution.py:473
  39.8 0.0 collective-permute-done.3.near_b
  39.8 5.1 %collective-permute-done.2.near_a = f32[520,128]{1,0:T(8,128)S(1)} collective-permute-done((f32[520,128]{1,0:T(8,128)S(1)}, f32[520,128]{1,0:T(8,128)S(1)}, u32[]{:S(2)}, u32[]{:S(2)}) %collective-permute-start.2) | collective-permute-done | bytes 266272 | tf_op jit(solution)/shard_map/ppermute | solution.py:473
  44.9 0.6 start_x.1
  45.6 3.5 %collective-permute-start.4 = (f32[144,128]{1,0:T(8,128)S(1)}, f32[144,128]{1,0:T(8,128)S(1)}, u32[]{:S(2)}, u32[]{:S(2)}) collective-permute-start(f32[144,128]{1,0:T(8,128)S(1)} %get-tuple-element.70), channel_id=1, source_target_pairs={{0,32},{32,0},{64,96},{96,64},{128,160},{160,128},{192,224},{224,1... | collective-permute-start | bytes 221192 | tf_op jit(solution)/shard_map/ppermute | solution.py:473
  49.1 0.7 collective-permute-start.5
  49.7 1.1 collective-permute-done.4.xa
  50.8 0.0 collective-permute-done.5.xb
  50.8 1.3 combine.1
  52.1 4.7 %collective-permute-start.6 = (f32[128,128]{1,0:T(8,128)S(1)}, f32[128,128]{1,0:T(8,128)S(1)}, u32[]{:S(2)}, u32[]{:S(2)}) collective-permute-start(f32[128,128]{1,0:T(8,128)S(1)} %get-tuple-element.77), channel_id=1, source_target_pairs={{0,2},{2,0},{1,3},{3,1},{4,6},{6,4},{5,7},{7,5},{8,10},{10,8},{9,1... | collective-permute-start | bytes 196616 | tf_op jit(solution)/shard_map/ppermute | solution.py:473
  56.8 0.7 collective-permute-start.7
  57.5 1.0 collective-permute-done.6.far_a
  58.5 0.0 collective-permute-done.7.far_b
  58.5 0.7 collective-permute-start.9
  59.2 13.3 %collective-permute-start.8 = (f32[512,128]{1,0:T(8,128)S(1)}, f32[512,128]{1,0:T(8,128)S(1)}, u32[]{:S(2)}, u32[]{:S(2)}) collective-permute-start(f32[512,128]{1,0:T(8,128)S(1)} %get-tuple-element.81.own), channel_id=1, source_target_pairs={{0,1},{1,0},{2,3},{3,2},{4,5},{5,4},{6,7},{7,6},{8,9},{9,8},{10,11... | collective-permute-start | bytes 786440 | tf_op jit(solution)/shard_map/ppermute | solution.py:473
  72.5 1.2 start_y.1
  73.7 6.2 %collective-permute-start.10 = (f32[16,2304]{1,0:T(8,128)S(1)}, f32[16,2304]{1,0:T(8,128)S(1)}, u32[]{:S(2)}, u32[]{:S(2)}) collective-permute-start(f32[16,2304]{1,0:T(8,128)S(1)} %get-tuple-element.82), channel_id=1, source_target_pairs={{0,8},{8,0},{16,24},{24,16},{1,9},{9,1},{17,25},{25,17},{2,10},{10... | collective-permute-start | bytes 442376 | tf_op jit(solution)/shard_map/ppermute | solution.py:473
  79.8 3.2 %collective-permute-start.11 = (f32[16,2304]{1,0:T(8,128)S(1)}, f32[16,2304]{1,0:T(8,128)S(1)}, u32[]{:S(2)}, u32[]{:S(2)}) collective-permute-start(f32[16,2304]{1,0:T(8,128)S(1)} %get-tuple-element.83), channel_id=1, source_target_pairs={{8,16},{16,8},{9,17},{17,9},{10,18},{18,10},{11,19},{19,11},{12,20... | collective-permute-start | bytes 442376 | tf_op jit(solution)/shard_map/ppermute | solution.py:473
  83.0 1.0 gain.1
  84.1 0.0 copy-start.5
  84.1 0.0 copy-start.6
  84.1 0.0 copy-start.7
  84.1 0.4 ids.1
  84.5 1.8 %collective-permute-done.11.yb = f32[16,2304]{1,0:T(8,128)S(1)} collective-permute-done((f32[16,2304]{1,0:T(8,128)S(1)}, f32[16,2304]{1,0:T(8,128)S(1)}, u32[]{:S(2)}, u32[]{:S(2)}) %collective-permute-start.11) | collective-permute-done | bytes 147488 | tf_op jit(solution)/shard_map/ppermute | solution.py:473
  86.3 0.0 collective-permute-done.9.near_b
  86.3 0.0 collective-permute-done.8.near_a
  86.3 0.6 source_x.1
  86.9 6.1 %collective-permute-start.12 = (f32[112,128]{1,0:T(8,128)S(1)}, f32[112,128]{1,0:T(8,128)S(1)}, u32[]{:S(2)}, u32[]{:S(2)}) collective-permute-start(f32[112,128]{1,0:T(8,128)S(1)} %get-tuple-element.86), channel_id=1, source_target_pairs={{0,32},{32,0},{64,96},{96,64},{128,160},{160,128},{192,224},{224,1... | collective-permute-start | bytes 172040 | tf_op jit(solution)/shard_map/ppermute | solution.py:473
  93.0 0.7 collective-permute-start.13
  93.7 4.0 %weights.1 = (f32[16,144,128]{2,1,0:T(8,128)S(1)}, f32[16,160,128]{2,1,0:T(8,128)S(1)}, f32[16,144,128]{2,1,0:T(8,128)S(1)}, f32[16,144,128]{2,1,0:T(8,128)S(1)}...) custom-call(s32[4]{0:T(128)S(1)} %pad_add_fusion.place, f32[8]{0:T(128)S(1)} %copy-done.5, ...), custom_call_target="tpu_custom_call" | custom-call | flops 1000000000 | bytes 11690096 | tf_op jit(solution)/shard_map/weights/pallas_call | solution.py:71
  97.7 0.0 collective-permute-done.13.xb
  97.7 1.0 source_y.1
  98.7 1.9 %collective-permute-start.14 = (f32[8,2304]{1,0:T(8,128)S(1)}, f32[8,2304]{1,0:T(8,128)S(1)}, u32[]{:S(2)}, u32[]{:S(2)}) collective-permute-start(f32[8,2304]{1,0:T(8,128)S(1)} %get-tuple-element.112), channel_id=1, source_target_pairs={{0,8},{8,0},{16,24},{24,16},{1,9},{9,1},{17,25},{25,17},{2,10},{10... | collective-permute-start | bytes 221192 | tf_op jit(solution)/shard_map/ppermute | solution.py:473
  100.6 3.3 %collective-permute-start.15 = (f32[8,2304]{1,0:T(8,128)S(1)}, f32[8,2304]{1,0:T(8,128)S(1)}, u32[]{:S(2)}, u32[]{:S(2)}) collective-permute-start(f32[8,2304]{1,0:T(8,128)S(1)} %get-tuple-element.113), channel_id=1, source_target_pairs={{8,16},{16,8},{9,17},{17,9},{10,18},{18,10},{11,19},{19,11},{12,20... | collective-permute-start | bytes 221192 | tf_op jit(solution)/shard_map/ppermute | solution.py:473
  103.9 0.0 collective-permute-done.14.ya
  103.9 2.4 %collective-permute-done.15.yb = f32[8,2304]{1,0:T(8,128)S(1)} collective-permute-done((f32[8,2304]{1,0:T(8,128)S(1)}, f32[8,2304]{1,0:T(8,128)S(1)}, u32[]{:S(2)}, u32[]{:S(2)}) %collective-permute-start.15) | collective-permute-done | bytes 73760 | tf_op jit(solution)/shard_map/ppermute | solution.py:473
  106.3 11.4 %sweeps.1 = (f32[512,128]{1,0:T(8,128)}, f32[1024,128]{1,0:T(8,128)S(1)}) custom-call(s32[4]{0:T(128)S(1)} %pad_add_fusion.place, f32[16,160,128]{2,1,0:T(8,128)S(1)} %get-tuple-element.74.xm, f32[16,144,128]{2,1,0:T(8,128)S(1)} %get-tuple-element.101.wz, f32[16,160,128]{2,1,0:T(8,128)S(1)} %get-tuple-element.102.wx, ...), custom_call_target="tpu_custom_call" | custom-call | flops 100000000 | bytes 13959184 | tf_op jit(solution)/shard_map/sweeps/pallas_call | solution.py:71
  117.7 31.3 %all_to_all.10 = f32[1024,1,128]{2,1,0:T(1,128)S(1)} all-to-all(f32[1024,1,128]{2,1,0:T(1,128)S(1)} %bitcast.30), channel_id=1, replica_groups=mesh['gx'=16,'gy'=4,'gz'=8] {'gx','gy'}, dimensions={0} | all-to-all | bytes 1048576 | tf_op jit(solution)/shard_map/all_to_all | solution.py:479
  149.0 1.2 finish.1
  (16 shorter events, 0.0 us)
Async XLA Ops:
  0.6 15.1 %copy-start.2 = (f32[4,128,128]{2,1,0:T(8,128)S(1)}, f32[4,128,128]{2,1,0:T(8,128)}, u32[]{:S(2)}) copy-start(f32[4,128,128]{2,1,0:T(8,128)} %param.14) | copy-start | bytes 786436
  0.6 15.1 %copy-start.4 = (s32[1,1,1,512]{3,2,1,0:T(1,128)S(1)}, s32[1,1,1,512]{3,2,1,0:T(1,128)}, u32[]{:S(2)}) copy-start(s32[1,1,1,512]{3,2,1,0:T(1,128)} %param.18) | copy-start | bytes 6148
  3.9 46.9 %all-to-all-start = ((f32[1088,1,128]{2,1,0:T(1,128)}), f32[1088,1,128]{2,1,0:T(1,128)S(1)}, u32[]{:S(2)}, u32[]{:S(2)}) async-start(f32[1088,1,128]{2,1,0:T(1,128)} %bitcast.35), calls=%async_computation | async-start | bytes 1114112 | tf_op jit(solution)/shard_map/all_to_all | solution.py:479
  16.3 12.3 %collective-permute-start = (f32[264,128]{1,0:T(8,128)S(1)}, f32[264,128]{1,0:T(8,128)S(1)}, u32[]{:S(2)}, u32[]{:S(2)}) collective-permute-start(f32[264,128]{1,0:T(8,128)S(1)} %get-tuple-element.63), channel_id=1, source_target_pairs={{0,2},{2,0},{1,3},{3,1},{4,6},{6,4},{5,7},{7,5},{8,10},{10,8},{9,1... | collective-permute-start | bytes 405512 | tf_op jit(solution)/shard_map/ppermute | solution.py:473
  22.1 6.4 %collective-permute-start.1 = (f32[264,128]{1,0:T(8,128)S(1)}, f32[264,128]{1,0:T(8,128)S(1)}, u32[]{:S(2)}, u32[]{:S(2)}) collective-permute-start(f32[264,128]{1,0:T(8,128)S(1)} %get-tuple-element.64), channel_id=1, source_target_pairs={{2,4},{4,2},{3,5},{5,3},{10,12},{12,10},{11,13},{13,11},{18,20},{2... | collective-permute-start | bytes 405512 | tf_op jit(solution)/shard_map/ppermute | solution.py:473
  28.6 54.5 %copy-start = (f32[3,4,128,128]{3,2,1,0:T(8,128)S(1)}, f32[3,4,128,128]{3,2,1,0:T(8,128)}, u32[]{:S(2)}) copy-start(f32[3,4,128,128]{3,2,1,0:T(8,128)} %param.11) | copy-start | bytes 2359300
  28.6 54.5 %copy-start.3 = (s32[1,1,1,512,1]{3,4,2,1,0:T(1,128)S(1)}, s32[1,1,1,512,1]{3,4,2,1,0:T(1,128)}, u32[]{:S(2)}) copy-start(s32[1,1,1,512,1]{3,4,2,1,0:T(1,128)} %param.15) | copy-start | bytes 6148
  28.6 11.3 %collective-permute-start.3 = (f32[520,128]{1,0:T(8,128)S(1)}, f32[520,128]{1,0:T(8,128)S(1)}, u32[]{:S(2)}, u32[]{:S(2)}) collective-permute-start(f32[520,128]{1,0:T(8,128)S(1)} %get-tuple-element.67.own), channel_id=1, source_target_pairs={{1,2},{2,1},{3,4},{4,3},{5,6},{6,5},{9,10},{10,9},{11,12},{12,11},... | collective-permute-start | bytes 798728 | tf_op jit(solution)/shard_map/ppermute | solution.py:473
  29.4 15.6 %collective-permute-start.2 = (f32[520,128]{1,0:T(8,128)S(1)}, f32[520,128]{1,0:T(8,128)S(1)}, u32[]{:S(2)}, u32[]{:S(2)}) collective-permute-start(f32[520,128]{1,0:T(8,128)S(1)} %get-tuple-element.67.own), channel_id=1, source_target_pairs={{0,1},{1,0},{2,3},{3,2},{4,5},{5,4},{6,7},{7,6},{8,9},{9,8},{10,11... | collective-permute-start | bytes 798728 | tf_op jit(solution)/shard_map/ppermute | solution.py:473
  45.6 5.2 %collective-permute-start.4 = (f32[144,128]{1,0:T(8,128)S(1)}, f32[144,128]{1,0:T(8,128)S(1)}, u32[]{:S(2)}, u32[]{:S(2)}) collective-permute-start(f32[144,128]{1,0:T(8,128)S(1)} %get-tuple-element.70), channel_id=1, source_target_pairs={{0,32},{32,0},{64,96},{96,64},{128,160},{160,128},{192,224},{224,1... | collective-permute-start | bytes 221192 | tf_op jit(solution)/shard_map/ppermute | solution.py:473
  49.1 1.7 %collective-permute-start.5 = (f32[144,128]{1,0:T(8,128)S(1)}, f32[144,128]{1,0:T(8,128)S(1)}, u32[]{:S(2)}, u32[]{:S(2)}) collective-permute-start(f32[144,128]{1,0:T(8,128)S(1)} %get-tuple-element.71), channel_id=1, source_target_pairs={{32,64},{64,32},{96,128},{128,96},{160,192},{192,160},{224,256},{2... | collective-permute-start | bytes 221192 | tf_op jit(solution)/shard_map/ppermute | solution.py:473
  52.1 6.4 %collective-permute-start.6 = (f32[128,128]{1,0:T(8,128)S(1)}, f32[128,128]{1,0:T(8,128)S(1)}, u32[]{:S(2)}, u32[]{:S(2)}) collective-permute-start(f32[128,128]{1,0:T(8,128)S(1)} %get-tuple-element.77), channel_id=1, source_target_pairs={{0,2},{2,0},{1,3},{3,1},{4,6},{6,4},{5,7},{7,5},{8,10},{10,8},{9,1... | collective-permute-start | bytes 196616 | tf_op jit(solution)/shard_map/ppermute | solution.py:473
  56.8 1.6 %collective-permute-start.7 = (f32[128,128]{1,0:T(8,128)S(1)}, f32[128,128]{1,0:T(8,128)S(1)}, u32[]{:S(2)}, u32[]{:S(2)}) collective-permute-start(f32[128,128]{1,0:T(8,128)S(1)} %get-tuple-element.78), channel_id=1, source_target_pairs={{2,4},{4,2},{3,5},{5,3},{10,12},{12,10},{11,13},{13,11},{18,20},{2... | collective-permute-start | bytes 196616 | tf_op jit(solution)/shard_map/ppermute | solution.py:473
  58.5 27.8 %collective-permute-start.9 = (f32[512,128]{1,0:T(8,128)S(1)}, f32[512,128]{1,0:T(8,128)S(1)}, u32[]{:S(2)}, u32[]{:S(2)}) collective-permute-start(f32[512,128]{1,0:T(8,128)S(1)} %get-tuple-element.81.own), channel_id=1, source_target_pairs={{1,2},{2,1},{3,4},{4,3},{5,6},{6,5},{9,10},{10,9},{11,12},{12,11},... | collective-permute-start | bytes 786440 | tf_op jit(solution)/shard_map/ppermute | solution.py:473
  59.2 27.1 %collective-permute-start.8 = (f32[512,128]{1,0:T(8,128)S(1)}, f32[512,128]{1,0:T(8,128)S(1)}, u32[]{:S(2)}, u32[]{:S(2)}) collective-permute-start(f32[512,128]{1,0:T(8,128)S(1)} %get-tuple-element.81.own), channel_id=1, source_target_pairs={{0,1},{1,0},{2,3},{3,2},{4,5},{5,4},{6,7},{7,6},{8,9},{9,8},{10,11... | collective-permute-start | bytes 786440 | tf_op jit(solution)/shard_map/ppermute | solution.py:473
  73.7 10.8 %collective-permute-start.10 = (f32[16,2304]{1,0:T(8,128)S(1)}, f32[16,2304]{1,0:T(8,128)S(1)}, u32[]{:S(2)}, u32[]{:S(2)}) collective-permute-start(f32[16,2304]{1,0:T(8,128)S(1)} %get-tuple-element.82), channel_id=1, source_target_pairs={{0,8},{8,0},{16,24},{24,16},{1,9},{9,1},{17,25},{25,17},{2,10},{10... | collective-permute-start | bytes 442376 | tf_op jit(solution)/shard_map/ppermute | solution.py:473
  79.8 6.5 %collective-permute-start.11 = (f32[16,2304]{1,0:T(8,128)S(1)}, f32[16,2304]{1,0:T(8,128)S(1)}, u32[]{:S(2)}, u32[]{:S(2)}) collective-permute-start(f32[16,2304]{1,0:T(8,128)S(1)} %get-tuple-element.83), channel_id=1, source_target_pairs={{8,16},{16,8},{9,17},{17,9},{10,18},{18,10},{11,19},{19,11},{12,20... | collective-permute-start | bytes 442376 | tf_op jit(solution)/shard_map/ppermute | solution.py:473
  84.1 9.6 %copy-start.5 = (f32[8]{0:T(128)S(1)}, f32[8]{0:T(128)}, u32[]{:S(2)}) copy-start(f32[8]{0:T(128)} %base.1) | copy-start | bytes 100
  84.1 9.6 %copy-start.6 = (f32[8]{0:T(128)S(1)}, f32[8]{0:T(128)}, u32[]{:S(2)}) copy-start(f32[8]{0:T(128)} %soft.1) | copy-start | bytes 100
  84.1 9.6 %copy-start.7 = (f32[8]{0:T(128)S(1)}, f32[8]{0:T(128)}, u32[]{:S(2)}) copy-start(f32[8]{0:T(128)} %heat.1) | copy-start | bytes 100
  86.9 10.9 %collective-permute-start.12 = (f32[112,128]{1,0:T(8,128)S(1)}, f32[112,128]{1,0:T(8,128)S(1)}, u32[]{:S(2)}, u32[]{:S(2)}) collective-permute-start(f32[112,128]{1,0:T(8,128)S(1)} %get-tuple-element.86), channel_id=1, source_target_pairs={{0,32},{32,0},{64,96},{96,64},{128,160},{160,128},{192,224},{224,1... | collective-permute-start | bytes 172040 | tf_op jit(solution)/shard_map/ppermute | solution.py:473
  93.0 4.7 %collective-permute-start.13 = (f32[112,128]{1,0:T(8,128)S(1)}, f32[112,128]{1,0:T(8,128)S(1)}, u32[]{:S(2)}, u32[]{:S(2)}) collective-permute-start(f32[112,128]{1,0:T(8,128)S(1)} %get-tuple-element.87), channel_id=1, source_target_pairs={{32,64},{64,32},{96,128},{128,96},{160,192},{192,160},{224,256},{2... | collective-permute-start | bytes 172040 | tf_op jit(solution)/shard_map/ppermute | solution.py:473
  98.7 5.2 %collective-permute-start.14 = (f32[8,2304]{1,0:T(8,128)S(1)}, f32[8,2304]{1,0:T(8,128)S(1)}, u32[]{:S(2)}, u32[]{:S(2)}) collective-permute-start(f32[8,2304]{1,0:T(8,128)S(1)} %get-tuple-element.112), channel_id=1, source_target_pairs={{0,8},{8,0},{16,24},{24,16},{1,9},{9,1},{17,25},{25,17},{2,10},{10... | collective-permute-start | bytes 221192 | tf_op jit(solution)/shard_map/ppermute | solution.py:473
  100.6 5.7 %collective-permute-start.15 = (f32[8,2304]{1,0:T(8,128)S(1)}, f32[8,2304]{1,0:T(8,128)S(1)}, u32[]{:S(2)}, u32[]{:S(2)}) collective-permute-start(f32[8,2304]{1,0:T(8,128)S(1)} %get-tuple-element.113), channel_id=1, source_target_pairs={{8,16},{16,8},{9,17},{17,9},{10,18},{18,10},{11,19},{19,11},{12,20... | collective-permute-start | bytes 221192 | tf_op jit(solution)/shard_map/ppermute | solution.py:473
  117.7 31.3 %copy-start.1 = (f32[4,128,128]{2,1,0:T(8,128)S(1)}, f32[4,128,128]{2,1,0:T(8,128)}, u32[]{:S(2)}) copy-start(f32[4,128,128]{2,1,0:T(8,128)} %param.13) | copy-start | bytes 786436

commit v5 on v4

--- a/solution.py
+++ b/solution.py
@@ -138,7 +138,7 @@
     return high.astype(BF16), (got - 32.0 * high).astype(BF16)
 
 
-def combine_kernel(peers, slots, far, place, received, source, far_a, far_b):
+def combine_kernel(peers, slots, received, source, first, last):
     n = source.shape[0]
     total = received.shape[0]
     high, low = labels_of(received, peers, slots)
@@ -149,11 +149,8 @@
     ids = jnp.sum(jnp.where(mine, named, 0.0), axis=0, keepdims=True).astype(I32)
     picks = hot_of(iota((n, total), 0) + 1 == ids)
     source[...] = pick_rows(picks, received[...])
-    rows = far * (n // 4)
-    first, last = source[pl.ds(0, rows), :], source[pl.ds(n - rows, rows), :]
-    even = place[3] == 0
-    far_a[...] = jnp.where(even, last, first)
-    far_b[...] = jnp.where(even, first, last)
+    first[...] = source[pl.ds(0, LANES), :]
+    last[...] = source[pl.ds(n - LANES, LANES), :]
 
 
 def ids_kernel(peers, slots, received, ids):
@@ -167,7 +164,7 @@
     ids[...] = jnp.broadcast_to(found, (total, LANES)).astype(I32)
 
 
-def start_z_kernel(far, place, x0, material, near, far_a, far_b):
+def start_z_kernel(far, x0, material, near, up, down):
     layers, xcells = material.shape
     n = layers * xcells
     mat = (material[...] + 1).astype(F32)
@@ -175,48 +172,40 @@
     zeros = lambda k: jnp.zeros((k, LANES), F32)
     near[pl.ds(0, n), :] = x0[...]
     near[pl.ds(n, EDGE), :] = jnp.concatenate([mat, zeros(EDGE - layers)], axis=0)
-    up, down = x0[pl.ds(n - rows, rows), :], x0[pl.ds(0, rows), :]
-    mat_up = jnp.concatenate([mat[layers - far :], zeros(EDGE - far)], axis=0)
-    mat_down = jnp.concatenate([mat[:far], zeros(EDGE - far)], axis=0)
-    even = place[3] == 0
-    far_a[pl.ds(0, rows), :] = jnp.where(even, up, down)
-    far_b[pl.ds(0, rows), :] = jnp.where(even, down, up)
-    far_a[pl.ds(rows, EDGE), :] = jnp.where(even, mat_up, mat_down)
-    far_b[pl.ds(rows, EDGE), :] = jnp.where(even, mat_down, mat_up)
-
-
-def layer_readers(far, place, far_a, far_b, near_a, near_b, own):
-    even, even2 = place[2] == 0, place[3] == 0
-
-    def one(k, ref):
-        return lambda at, size: ref[pl.ds(k * LANES + at, size), :]
-
-    def either(k, cond, yes, no):
-        return lambda at, size: jnp.where(cond, one(k, yes)(at, size), one(k, no)(at, size))
-
-    found = [either(k, even2, far_b, far_a) for k in range(far)]
-    found += [either(k, even, near_b, near_a) for k in range(4)]
-    found += [one(k, own) for k in range(4)]
-    found += [either(k, even, near_a, near_b) for k in range(4)]
-    return found + [either(k, even2, far_a, far_b) for k in range(far)]
-
-
-def start_x_kernel(far, place, far_a, far_b, near_a, near_b, own, xz, mats, xa, xb):
-    readers = layer_readers(far, place, far_a, far_b, near_a, near_b, own)
-    count = len(readers)
-    even = place[0] == 0
-    for k, read in enumerate(readers):
-        piece = read(0, LANES)
+    up[pl.ds(0, rows), :] = x0[pl.ds(n - rows, rows), :]
+    up[pl.ds(rows, EDGE), :] = jnp.concatenate([mat[layers - far :], zeros(EDGE - far)], axis=0)
+    down[pl.ds(0, rows), :] = x0[pl.ds(0, rows), :]
+    down[pl.ds(rows, EDGE), :] = jnp.concatenate([mat[:far], zeros(EDGE - far)], axis=0)
+
+
+def start_x_kernel(far, low2, low, own, high, high2, xz, mats, xlow, xhigh):
+    found = [(low2, k) for k in range(far)]
+    for ref in (low, own, high):
+        found += [(ref, k) for k in range(4)]
+    found += [(high2, k) for k in range(far)]
+    count = len(found)
+    for k, (ref, at) in enumerate(found):
+        piece = ref[pl.ds(at * LANES, LANES), :]
         xz[k] = piece
-        low, high = piece[:EDGE], piece[LANES - EDGE :]
-        xa[pl.ds(k * EDGE, EDGE), :] = jnp.where(even, high, low)
-        xb[pl.ds(k * EDGE, EDGE), :] = jnp.where(even, low, high)
-    tail = [far * LANES] * far + [4 * LANES] * 12 + [far * LANES] * far
-    at = list(range(far)) + list(range(4)) * 3 + list(range(far))
-    for k, read in enumerate(readers):
-        mats[pl.ds(k, 1), :] = read(tail[k] + at[k] - at[k] * LANES, 1)
-    xa[pl.ds(count * EDGE, count), :] = mats[...]
-    xb[pl.ds(count * EDGE, count), :] = mats[...]
+        xlow[pl.ds(k * EDGE, EDGE), :] = piece[:EDGE]
+        xhigh[pl.ds(k * EDGE, EDGE), :] = piece[LANES - EDGE :]
+        mats[pl.ds(k, 1), :] = ref[pl.ds(ref.shape[0] - EDGE + at, 1), :]
+    xlow[pl.ds(count * EDGE, count), :] = mats[...]
+    xhigh[pl.ds(count * EDGE, count), :] = mats[...]
+
+
+def near_layers(low, own, high):
+    return [(ref, k) for ref in (low, own, high) for k in range(4)]
+
+
+def pack_x_kernel(low, own, high, start_low, start_high, xlow, xhigh):
+    top = start_low.shape[0]
+    xlow[pl.ds(0, top), :] = start_low[...]
+    xhigh[pl.ds(0, top), :] = start_high[...]
+    for k, (ref, at) in enumerate(near_layers(low, own, high)):
+        to = pl.ds(top + k * EDGE, EDGE)
+        xlow[to, :] = ref[pl.ds(at * LANES, EDGE), :]
+        xhigh[to, :] = ref[pl.ds((at + 1) * LANES - EDGE, EDGE), :]
 
 
 def flat_sides(rows):
@@ -225,23 +214,33 @@
     return dot(edges, high, 1, 1) + dot(edges, low, 1, 1)
 
 
-def start_y_kernel(place, xz, mats, xa, xb, xm, sides, flat_mat, ya, yb):
+def pack_y_kernel(xz, mats, low, own, high, after, before, xm, full, sides, heat_sides, flat_mat, ylow, yhigh):
     count = xz.shape[0]
-    even = place[0] == 0
-    after, before = jnp.where(even, xa[...], xb[...]), jnp.where(even, xb[...], xa[...])
     blank = jnp.zeros((EDGE, LANES), F32)
     for k in range(count):
-        part = slice(k * EDGE, (k + 1) * EDGE)
+        part = pl.ds(k * EDGE, EDGE)
         xm[k, pl.ds(0, EDGE)] = blank
-        xm[k, pl.ds(EDGE, EDGE)] = before[part]
+        xm[k, pl.ds(EDGE, EDGE)] = before[part, :]
         xm[k, pl.ds(2 * EDGE, LANES)] = xz[k]
-        xm[k, pl.ds(LANES + 2 * EDGE, EDGE)] = after[part]
+        xm[k, pl.ds(LANES + 2 * EDGE, EDGE)] = after[part, :]
         xm[k, pl.ds(LANES + 3 * EDGE, EDGE)] = blank
+    found = near_layers(low, own, high)
+    skip = (count - len(found)) // 2
+    top = count * (EDGE + 1)
+    for k in range(skip):
+        full[k] = jnp.zeros(full.shape[1:], F32)
+        full[count - 1 - k] = jnp.zeros(full.shape[1:], F32)
+    for k, (ref, at) in enumerate(found):
+        part = pl.ds(top + k * EDGE, EDGE)
+        full[skip + k, pl.ds(0, EDGE)] = before[part, :]
+        full[skip + k, pl.ds(EDGE, LANES)] = ref[pl.ds(at * LANES, LANES), :]
+        full[skip + k, pl.ds(EDGE + LANES, EDGE)] = after[part, :]
     rows = LANES + 2 * EDGE
     total = count * rows
     found = flat_sides(xm[:, EDGE : EDGE + rows].reshape(total, LANES))
     sides[...] = found
-    around = jnp.concatenate([before[count * EDGE :], mats[...], after[count * EDGE :]], axis=0)
+    beside = pl.ds(count * EDGE, count)
+    around = jnp.concatenate([before[beside, :], mats[...], after[beside, :]], axis=0)
     q = iota((1, total), 1)
     layer = lax.div(q, rows)
     row = q - layer * rows
@@ -251,13 +250,15 @@
     named = dot(around.astype(BF16), spread, 1, 0)
     mine = iota((3 * count, total), 0) == tile * count + layer
     mat = jnp.sum(jnp.where(mine, named, 0.0), axis=0, keepdims=True)
-    mat = jnp.where(iota((EDGE, total), 0) == 0, mat, 0.0)
-    flat_mat[...] = mat
-    even = place[1] == 0
-    ya[pl.ds(0, EDGE), :] = jnp.where(even, found[EDGE:], found[:EDGE])
-    yb[pl.ds(0, EDGE), :] = jnp.where(even, found[:EDGE], found[EDGE:])
-    ya[pl.ds(EDGE, EDGE), :] = mat
-    yb[pl.ds(EDGE, EDGE), :] = mat
+    flat_mat[...] = jnp.broadcast_to(mat, (EDGE, total))
+    heat_found = flat_sides(full[...].reshape(total, LANES))
+    heat_sides[...] = heat_found
+    ylow[pl.ds(0, EDGE), :] = found[:EDGE]
+    yhigh[pl.ds(0, EDGE), :] = found[EDGE:]
+    ylow[pl.ds(EDGE, EDGE), :] = heat_found[:EDGE]
+    yhigh[pl.ds(EDGE, EDGE), :] = heat_found[EDGE:]
+    ylow[pl.ds(2 * EDGE - 1, 1), :] = mat
+    yhigh[pl.ds(EDGE, 1), :] = mat
 
 
 def three_parts(v):
@@ -286,12 +287,12 @@
     return jnp.concatenate([before, sides, after], axis=0)
 
 
-def weights_kernel(place, base, soft, heat, xm, sides, flat_mat, ya, yb, wz, wx, wy, wyw, inv, b0, strips, cond, cols, ends):
+def weights_kernel(base, soft, heat, xm, sides, flat_mat, before, after, wz, wx, wy, wyw, inv, b0, strips, cond, cols, ends):
     count, rows = inv.shape[0], inv.shape[1]
     total = count * rows
-    even = place[1] == 0
-    after, before = jnp.where(even, ya[...], yb[...]), jnp.where(even, yb[...], ya[...])
-    mat = jnp.concatenate([flat_mat[0:1], before[EDGE : EDGE + 1], after[EDGE : EDGE + 1]], axis=0)
+    mat = jnp.concatenate(
+        [flat_mat[0:1], before[pl.ds(EDGE, 1), :], after[pl.ds(2 * EDGE - 1, 1), :]], axis=0
+    )
     tables = []
     for values in (base, soft, heat):
         found = jnp.zeros(mat.shape, F32)
@@ -360,39 +361,13 @@
             b0[k, to] = cf * xm[k, here] * i
 
 
-def source_x_kernel(far, place, far_a, far_b, near_a, near_b, own, xa, xb):
-    even = place[0] == 0
-    for k, read in enumerate(layer_readers(far, place, far_a, far_b, near_a, near_b, own)):
-        low, high = read(0, EDGE), read(LANES - EDGE, EDGE)
-        xa[pl.ds(k * EDGE, EDGE), :] = jnp.where(even, high, low)
-        xb[pl.ds(k * EDGE, EDGE), :] = jnp.where(even, low, high)
-
-
-def source_y_kernel(far, place, far_a, far_b, near_a, near_b, own, xa, xb, full, sides, ya, yb):
-    count, rows, _ = full.shape
-    even = place[0] == 0
-    full[0] = jnp.zeros((rows, LANES), F32)
-    full[count - 1] = jnp.zeros((rows, LANES), F32)
-    for k, read in enumerate(layer_readers(far, place, far_a, far_b, near_a, near_b, own)):
-        a, b = xa[pl.ds(k * EDGE, EDGE), :], xb[pl.ds(k * EDGE, EDGE), :]
-        full[k + 1, pl.ds(0, EDGE)] = jnp.where(even, b, a)
-        full[k + 1, pl.ds(EDGE, LANES)] = read(0, LANES)
-        full[k + 1, pl.ds(EDGE + LANES, EDGE)] = jnp.where(even, a, b)
-    found = flat_sides(full[...].reshape(count * rows, LANES))
-    sides[...] = found
-    even = place[1] == 0
-    ya[...] = jnp.where(even, found[EDGE:], found[:EDGE])
-    yb[...] = jnp.where(even, found[:EDGE], found[EDGE:])
-
-
-def sweep_kernel(place, xm, wz, wx, wy, wyw, inv, b0, strips, full, sides, ya, yb, ids, out, replies, b, d, xa, xb, ends):
+def sweep_kernel(xm, wz, wx, wy, wyw, inv, b0, strips, full, sides, before, after, low2, high2, ids,
+                 out, replies, b, d, xa, xb, ends):
     count, rows, _ = inv.shape
     total = count * rows
-    even = place[1] == 0
-    after, before = jnp.where(even, ya[...], yb[...]), jnp.where(even, yb[...], ya[...])
     factors = steps()
 
-    sb = strips[7] + strip_of(sides[...], before, after) * strips[6]
+    sb = strips[7] + strip_of(sides[...], before[EDGE:], after[EDGE:]) * strips[6]
     sx, sd = strips[8], None
     kept = [ends_of(sx)]
     for keep, add in factors[:-1]:
@@ -447,6 +422,17 @@
     final = xb if SWEEPS % 2 == 0 else xa
     for k in range(4):
         out[pl.ds(k * LANES, LANES), :] = final[SWEEPS + k, pl.ds(2 * EDGE, LANES)]
+    scale = 1.0
+    for _, add in factors:
+        scale = scale * add
+    tile = pl.ds(EDGE, LANES)
+    for ref, start, way, k in ((low2, 1, 1, 0), (high2, count - 2, -1, 3)):
+        gain = scale * inv[start, tile] * ref[...]
+        for j in range(1, SWEEPS):
+            at = start + way * j
+            gain = gain * inv[at, tile] * wz[at - 1 if way > 0 else at, tile]
+        to = pl.ds(k * LANES, LANES)
+        out[to, :] = out[to, :] + gain
     n = out.shape[0]
     name = ids[...]
     hot = jnp.concatenate([hot_of(name == iota(name.shape, 1) + at) for at in range(0, n, LANES)], axis=1)
@@ -462,16 +448,10 @@
     ionization[...] = jnp.exp(gain[...] * (1.0 + 0.3 * back))
 
 
-def swapped(a, b, axis, apart=1):
+def shifted(v, axis, by):
     count = lax.axis_size(axis)
-    found = []
-    for v, odd in ((a, 0), (b, 1)):
-        pairs = []
-        for i in range(count - apart):
-            if (i // apart) % 2 == odd:
-                pairs += [(i, i + apart), (i + apart, i)]
-        found.append(lax.ppermute(v, axis, pairs) if pairs else jnp.zeros_like(v))
-    return found
+    pairs = [(i, i + by) for i in range(count) if 0 <= i + by < count]
+    return lax.ppermute(v, axis, pairs) if pairs else jnp.zeros_like(v)
 
 
 def exchanged(v):
@@ -501,62 +481,51 @@
         scratch=[pltpu.VMEM(a.shape, a.dtype) for a in given] + [pltpu.SemaphoreType.DMA((len(given),))])
     received = exchanged(sent)
 
-    spot = [lax.axis_index(a) for a in ("gx", "gy", "gz")]
-    place = jnp.stack([spot[0] % 2, spot[1] % 2, spot[2] % 2, spot[2] // 2 % 2])
     far = SWEEPS - layers
     count = layers + 2 * SWEEPS
     rows = xcells + 2 * EDGE
     total = count * rows
     aside = sized(far * xcells + EDGE, width)
-    near, far_a, far_b = call(
-        functools.partial(start_z_kernel, far), [sized(n + EDGE, width), aside, aside],
-        [place, x0, mat], "start_z", smem=(0,))
-    far_a, far_b = swapped(far_a, far_b, "gz", 2)
-    near, far_a, far_b = lax.optimization_barrier((near, far_a, far_b))
-    near_a, near_b = swapped(near, near, "gz")
-    xz, mats, xa, xb = call(
-        functools.partial(start_x_kernel, far),
-        [sized(count, xcells, width), sized(count, width)] + [sized(count * (EDGE + 1), width)] * 2,
-        [place, far_a, far_b, near_a, near_b, near], "start_x", smem=(0,))
-    xa, xb = swapped(xa, xb, "gx")
-    received, xa, xb = lax.optimization_barrier((received, xa, xb))
-    tall = sized(count, rows + 2 * EDGE, width)
-    xm, sides, flat_mat, ya, yb = call(
-        start_y_kernel,
-        [tall, sized(2 * EDGE, total), sized(EDGE, total), sized(2 * EDGE, total), sized(2 * EDGE, total)],
-        [place, xz, mats, xa, xb], "start_y", smem=(0,))
-    ya, yb = swapped(ya, yb, "gy")
+    near, up, down = call(
+        functools.partial(start_z_kernel, far), [sized(n + EDGE, width), aside, aside], [x0, mat], "start_z")
+    low, high = shifted(near, "gz", 1), shifted(near, "gz", -1)
+    low2, high2 = shifted(up, "gz", 2), shifted(down, "gz", -2)
+    received, low, high, low2, high2 = lax.optimization_barrier((received, low, high, low2, high2))
+    edge = sized(count * (EDGE + 1), width)
+    xz, mats, start_low, start_high = call(
+        functools.partial(start_x_kernel, far), [sized(count, xcells, width), sized(count, width), edge, edge],
+        [low2, low, near, high, high2], "start_x")
     gain, dest = call(functools.partial(after_kernel, slots), [sized(n, width), ((n, LANES), I32)], [ef, own], "gain")
-    far -= 1
-    source, far_a, far_b = call(
-        functools.partial(combine_kernel, peers, slots, far),
-        [sized(n, width)] + [sized(far * xcells, width)] * 2, [place, received], "combine", flops=10**8, smem=(0,))
+
+    source, first, last = call(
+        functools.partial(combine_kernel, peers, slots), [sized(n, width)] + [sized(xcells, width)] * 2,
+        [received], "combine", flops=10**8)
     [ids] = call(functools.partial(ids_kernel, peers, slots), [((peers * slots, LANES), I32)], [received], "ids")
-    far_a, far_b = swapped(far_a, far_b, "gz", 2)
-    source, far_a, far_b = lax.optimization_barrier((source, far_a, far_b))
-    near_a, near_b = swapped(source, source, "gz")
-    near_a, near_b, ya, yb = lax.optimization_barrier((near_a, near_b, ya, yb))
-    tile = sized(count, rows, width)
+    low, high = shifted(source, "gz", 1), shifted(source, "gz", -1)
+    low, high, start_low, start_high = lax.optimization_barrier((low, high, start_low, start_high))
+    edge = sized(count * (EDGE + 1) + 3 * layers * EDGE, width)
+    xlow, xhigh = call(pack_x_kernel, [edge, edge], [low, source, high, start_low, start_high], "pack_x")
+    before, after = shifted(xhigh, "gx", 1), shifted(xlow, "gx", -1)
+    before, after, ids, gain, dest = lax.optimization_barrier((before, after, ids, gain, dest))
+    tall, tile, flat_edge = sized(count, rows + 2 * EDGE, width), sized(count, rows, width), sized(2 * EDGE, total)
+    xm, full, sides, heat_sides, flat_mat, ylow, yhigh = call(
+        pack_y_kernel, [tall, tile, flat_edge, flat_edge, sized(EDGE, total), flat_edge, flat_edge],
+        [xz, mats, low, source, high, after, before], "pack_y")
+    ylow, yhigh, first, last = lax.optimization_barrier((ylow, yhigh, first, last))
+    before, after = shifted(yhigh, "gy", 1), shifted(ylow, "gy", -1)
+    low2, high2 = shifted(last, "gz", 2), shifted(first, "gz", -2)
     weights = call(
         weights_kernel, [tile, tall, tile, tile, tile, tile, sized(9, 4 * EDGE, total)],
-        [place, mat_conductivity, mat_softening, mat_capacity, xm, sides, flat_mat, ya, yb], "weights",
+        [mat_conductivity, mat_softening, mat_capacity, xm, sides, flat_mat, before, after], "weights",
         scratch=[pltpu.VMEM((count, rows + 2 * EDGE, width), F32), pltpu.VMEM((total, 3 * width), F32),
                  pltpu.VMEM((total, width), F32)],
-        limit=32, flops=10**9, smem=(0, 1, 2, 3))
-    above = [place, far_a, far_b, near_a, near_b, source]
-    xa, xb = call(functools.partial(source_x_kernel, far), [sized((count - 2) * EDGE, width)] * 2, above, "source_x", smem=(0,))
-    xa, xb = swapped(xa, xb, "gx")
-    xa, xb, weights, ids, gain, dest = lax.optimization_barrier((xa, xb, weights, ids, gain, dest))
-    full, sides, ya, yb = call(
-        functools.partial(source_y_kernel, far),
-        [tile, sized(2 * EDGE, total), sized(EDGE, total), sized(EDGE, total)], above + [xa, xb], "source_y", smem=(0,))
-    ya, yb = swapped(ya, yb, "gy")
+        limit=32, flops=10**9, smem=(0, 1, 2))
     x, replies = call(
         sweep_kernel, [sized(n, width), sized(peers * slots, width)],
-        [place, xm] + list(weights) + [full, sides, ya, yb, ids], "sweeps",
+        [xm] + list(weights) + [full, heat_sides, before, after, low2, high2, ids], "sweeps",
         scratch=[pltpu.VMEM((count, rows, width), F32)] * 2 + [pltpu.VMEM((count, rows + 2 * EDGE, width), F32)] * 2
         + [pltpu.VMEM((total, SWEEPS * width), F32)],
-        limit=36, flops=10**8, smem=(0,))
+        limit=36, flops=10**8)
     returned = exchanged(replies)
     mobility, ionization = call(final_kernel, [sized(n, width)] * 2, [returned, dest, gain, mob], "finish", flops=10**8)
     shape = density.shape

time: 151 us -> 125 us (0.83)
  starting transfers between devices: 74.2 us -> 50.9 us
  Pallas kernels: 26.5 us -> 22.7 us
  waiting for transfers between devices: 17.1 us -> 20.3 us
  blocking collectives: 31.3 us -> 29.6 us
    ppermute x16 -> x12, starting transfers between devices: 62.6 us -> 39.2 us  [shifted(): return lax.ppermute(v, axis, pairs) if pairs else jnp.zeros_like(v)]
    pallas_call x12 -> x11, Pallas kernels: 26.5 us -> 22.7 us  [call(): pl.pallas_call(kernel, out_shape=[jax.ShapeDtypeStruct(s, t) for s, t in...]
    ppermute x16 -> x12, waiting for transfers between devices: 17.1 us -> 20.3 us  [shifted(): return lax.ppermute(v, axis, pairs) if pairs else jnp.zeros_like(v)]
    all_to_all x1, blocking collectives: 31.3 us -> 29.6 us  [exchanged(): lax.all_to_all(lines, ('gx', 'gy'), split_axis=0, concat_axis=0, tiled=True)]
  transfers between devices with their start and end apart: 17 -> 13, of which waited for: 6 -> 6; matrix products, arithmetic and copies ran while one was open for 0% -> 0% of each run, Pallas kernels for 5% -> 4%
where the time goes in v5:
time: 125 us; the launch traced here: 124 us
  starting transfers between devices  50.9 us (41%)
  blocking collectives  29.6 us (24%)
  Pallas kernels  22.7 us (18%)
  waiting for transfers between devices  20.3 us (16%)
    ppermute x12, starting transfers between devices, shifted(): return lax.ppermute(v, axis, pairs) if pairs else jnp.zeros_like(v)  39.2 us
    all_to_all x1, blocking collectives, exchanged(): lax.all_to_all(lines, ('gx', 'gy'), split_axis=0, concat_axis=0, tiled=True)  29.6 us
    pallas_call x11, Pallas kernels, call(): pl.pallas_call(kernel, out_shape=[jax.ShapeDtypeStruct(s, t) for s, t in...  22.7 us
    ppermute x12, waiting for transfers between devices, shifted(): return lax.ppermute(v, axis, pairs) if pairs else jnp.zeros_like(v)  20.3 us
    all_to_all x1, starting transfers between devices, exchanged(): lax.all_to_all(lines, ('gx', 'gy'), split_axis=0, concat_axis=0, tiled=True)  11.6 us
  transfers between devices with their start and end apart: 13, of which 6 were waited for; matrix products, arithmetic and copies ran while one was open for 0% of the time, Pallas kernels for 4%

profile of v5, /device:TPU:1, one launch (start us, length us, event | category | flops | bytes accessed | tf_op | source)
XLA Modules:
  0.0 124.4 jit_solution(3221980468189156025)
XLA Ops:
  0.6 0.0 copy-start.2
  0.6 0.0 copy-start.4
  0.7 3.3 %dispatch.1 = f32[1088,128]{1,0:T(8,128)} custom-call(f32[3,512,128]{2,1,0:T(8,128)} %bitcast.21, f32[512,128]{1,0:T(8,128)} %bitcast.32, f32[512,128]{1,0:T(8,128)} %bitcast.24, s32[1,512]{1,0:T(1,128)} %bitcast.28, s32[1,512]{1,0:T(1,128)} %bitcast.33, s32[1,512]{1,0:T(1,128)} %bitcast.34), custom_call_target="tpu_custom_call" | custom-call | flops 100000000 | bytes 1873920 | tf_op jit(solution)/shard_map/dispatch/pallas_call | solution.py:71
  4.0 11.6 %all-to-all-start = ((f32[1088,1,128]{2,1,0:T(1,128)}), f32[1088,1,128]{2,1,0:T(1,128)S(1)}, u32[]{:S(2)}, u32[]{:S(2)}) async-start(f32[1088,1,128]{2,1,0:T(1,128)} %bitcast.31), calls=%async_computation | async-start | bytes 1114112 | tf_op jit(solution)/shard_map/all_to_all | solution.py:459
  15.7 1.3 %collective-permute-start.1 = (f32[520,128]{1,0:T(8,128)S(1)}, f32[520,128]{1,0:T(8,128)S(1)}, u32[]{:S(2)}, u32[]{:S(2)}) collective-permute-start(f32[520,128]{1,0:T(8,128)S(1)} %get-tuple-element.53.own), channel_id=1, source_target_pairs={{1,0},{2,1},{3,2},{4,3},{5,4},{6,5},{7,6},{9,8},{10,9},{11,10},{12... | collective-permute-start | bytes 798728 | tf_op jit(solution)/shard_map/ppermute | solution.py:454
  17.0 4.6 %collective-permute-start = (f32[520,128]{1,0:T(8,128)S(1)}, f32[520,128]{1,0:T(8,128)S(1)}, u32[]{:S(2)}, u32[]{:S(2)}) collective-permute-start(f32[520,128]{1,0:T(8,128)S(1)} %get-tuple-element.53.own), channel_id=1, source_target_pairs={{0,1},{1,2},{2,3},{3,4},{4,5},{5,6},{6,7},{8,9},{9,10},{10,11},{11... | collective-permute-start | bytes 798728 | tf_op jit(solution)/shard_map/ppermute | solution.py:454
  21.6 5.8 %collective-permute-start.2 = (f32[264,128]{1,0:T(8,128)S(1)}, f32[264,128]{1,0:T(8,128)S(1)}, u32[]{:S(2)}, u32[]{:S(2)}) collective-permute-start(f32[264,128]{1,0:T(8,128)S(1)} %get-tuple-element.54), channel_id=1, source_target_pairs={{0,2},{1,3},{2,4},{3,5},{4,6},{5,7},{8,10},{9,11},{10,12},{11,13},... | collective-permute-start | bytes 405512 | tf_op jit(solution)/shard_map/ppermute | solution.py:454
  27.4 1.3 %collective-permute-start.3 = (f32[264,128]{1,0:T(8,128)S(1)}, f32[264,128]{1,0:T(8,128)S(1)}, u32[]{:S(2)}, u32[]{:S(2)}) collective-permute-start(f32[264,128]{1,0:T(8,128)S(1)} %get-tuple-element.55), channel_id=1, source_target_pairs={{2,0},{3,1},{4,2},{5,3},{6,4},{7,5},{10,8},{11,9},{12,10},{13,11},... | collective-permute-start | bytes 405512 | tf_op jit(solution)/shard_map/ppermute | solution.py:454
  28.7 0.9 collective-permute-done.2.low2
  29.7 9.6 %collective-permute-done.3.high2 = f32[264,128]{1,0:T(8,128)S(1)} collective-permute-done((f32[264,128]{1,0:T(8,128)S(1)}, f32[264,128]{1,0:T(8,128)S(1)}, u32[]{:S(2)}, u32[]{:S(2)}) %collective-permute-start.3) | collective-permute-done | bytes 135200 | tf_op jit(solution)/shard_map/ppermute | solution.py:454
  39.3 0.0 collective-permute-done.1.high
  39.3 0.0 collective-permute-done.low
  39.3 0.0 all-to-all-done
  39.3 0.0 copy-start
  39.3 0.0 copy-start.3
  39.3 0.7 combine.1
  40.1 1.3 %collective-permute-start.5 = (f32[512,128]{1,0:T(8,128)S(1)}, f32[512,128]{1,0:T(8,128)S(1)}, u32[]{:S(2)}, u32[]{:S(2)}) collective-permute-start(f32[512,128]{1,0:T(8,128)S(1)} %get-tuple-element.63.own), channel_id=1, source_target_pairs={{1,0},{2,1},{3,2},{4,3},{5,4},{6,5},{7,6},{9,8},{10,9},{11,10},{12... | collective-permute-start | bytes 786440 | tf_op jit(solution)/shard_map/ppermute | solution.py:454
  41.4 4.0 %collective-permute-start.4 = (f32[512,128]{1,0:T(8,128)S(1)}, f32[512,128]{1,0:T(8,128)S(1)}, u32[]{:S(2)}, u32[]{:S(2)}) collective-permute-start(f32[512,128]{1,0:T(8,128)S(1)} %get-tuple-element.63.own), channel_id=1, source_target_pairs={{0,1},{1,2},{2,3},{3,4},{4,5},{5,6},{6,7},{8,9},{9,10},{10,11},{11... | collective-permute-start | bytes 786440 | tf_op jit(solution)/shard_map/ppermute | solution.py:454
  45.4 0.1 start_x.1
  45.5 2.3 %collective-permute-done.5.high = f32[512,128]{1,0:T(8,128)S(1)} collective-permute-done((f32[512,128]{1,0:T(8,128)S(1)}, f32[512,128]{1,0:T(8,128)S(1)}, u32[]{:S(2)}, u32[]{:S(2)}) %collective-permute-start.5) | collective-permute-done | bytes 262176 | tf_op jit(solution)/shard_map/ppermute | solution.py:454
  47.8 0.9 collective-permute-done.4.low
  48.7 3.3 %collective-permute-start.6 = (f32[240,128]{1,0:T(8,128)S(1)}, f32[240,128]{1,0:T(8,128)S(1)}, u32[]{:S(2)}, u32[]{:S(2)}) collective-permute-start(f32[240,128]{1,0:T(8,128)S(1)} %get-tuple-element.70), channel_id=1, source_target_pairs={{0,32},{32,64},{64,96},{96,128},{128,160},{160,192},{192,224},{224... | collective-permute-start | bytes 368648 | tf_op jit(solution)/shard_map/ppermute | solution.py:454
  52.0 1.3 %collective-permute-start.7 = (f32[240,128]{1,0:T(8,128)S(1)}, f32[240,128]{1,0:T(8,128)S(1)}, u32[]{:S(2)}, u32[]{:S(2)}) collective-permute-start(f32[240,128]{1,0:T(8,128)S(1)} %get-tuple-element.71), channel_id=1, source_target_pairs={{32,0},{64,32},{96,64},{128,96},{160,128},{192,160},{224,192},{256... | collective-permute-start | bytes 368648 | tf_op jit(solution)/shard_map/ppermute | solution.py:454
  53.3 0.0 copy-done
  53.3 0.0 copy-done.3
  53.3 1.0 gain.1
  54.3 0.4 ids.1
  54.7 0.0 copy-start.5
  54.7 0.0 copy-start.6
  54.8 0.0 copy-start.7
  54.8 0.0 collective-permute-done.6.before
  54.8 2.8 %collective-permute-done.7.after = f32[240,128]{1,0:T(8,128)S(1)} collective-permute-done((f32[240,128]{1,0:T(8,128)S(1)}, f32[240,128]{1,0:T(8,128)S(1)}, u32[]{:S(2)}, u32[]{:S(2)}) %collective-permute-start.7) | collective-permute-done | bytes 122912 | tf_op jit(solution)/shard_map/ppermute | solution.py:454
  57.6 0.9 pack_y.1
  58.6 7.6 %collective-permute-start.8 = (f32[16,2304]{1,0:T(8,128)S(1)}, f32[16,2304]{1,0:T(8,128)S(1)}, u32[]{:S(2)}, u32[]{:S(2)}) collective-permute-start(f32[16,2304]{1,0:T(8,128)S(1)} %get-tuple-element.83), channel_id=1, source_target_pairs={{0,8},{8,16},{16,24},{1,9},{9,17},{17,25},{2,10},{10,18},{18,26},{... | collective-permute-start | bytes 442376 | tf_op jit(solution)/shard_map/ppermute | solution.py:454
  66.2 1.9 %collective-permute-start.9 = (f32[16,2304]{1,0:T(8,128)S(1)}, f32[16,2304]{1,0:T(8,128)S(1)}, u32[]{:S(2)}, u32[]{:S(2)}) collective-permute-start(f32[16,2304]{1,0:T(8,128)S(1)} %get-tuple-element.84), channel_id=1, source_target_pairs={{8,0},{16,8},{24,16},{9,1},{17,9},{25,17},{10,2},{18,10},{26,18},{... | collective-permute-start | bytes 442376 | tf_op jit(solution)/shard_map/ppermute | solution.py:454
  68.1 5.5 %collective-permute-start.10 = (f32[128,128]{1,0:T(8,128)S(1)}, f32[128,128]{1,0:T(8,128)S(1)}, u32[]{:S(2)}, u32[]{:S(2)}) collective-permute-start(f32[128,128]{1,0:T(8,128)S(1)} %get-tuple-element.94), channel_id=1, source_target_pairs={{0,2},{1,3},{2,4},{3,5},{4,6},{5,7},{8,10},{9,11},{10,12},{11,13},... | collective-permute-start | bytes 196616 | tf_op jit(solution)/shard_map/ppermute | solution.py:454
  73.6 1.3 %collective-permute-start.11 = (f32[128,128]{1,0:T(8,128)S(1)}, f32[128,128]{1,0:T(8,128)S(1)}, u32[]{:S(2)}, u32[]{:S(2)}) collective-permute-start(f32[128,128]{1,0:T(8,128)S(1)} %get-tuple-element.95), channel_id=1, source_target_pairs={{2,0},{3,1},{4,2},{5,3},{6,4},{7,5},{10,8},{11,9},{12,10},{13,11},... | collective-permute-start | bytes 196616 | tf_op jit(solution)/shard_map/ppermute | solution.py:454
  74.9 0.0 collective-permute-done.8.before
  74.9 0.0 collective-permute-done.9.after
  74.9 0.0 copy-done.5
  74.9 0.0 copy-done.6
  74.9 0.0 copy-done.7
  75.0 4.0 %weights.1 = (f32[16,144,128]{2,1,0:T(8,128)S(1)}, f32[16,160,128]{2,1,0:T(8,128)S(1)}, f32[16,144,128]{2,1,0:T(8,128)S(1)}, f32[16,144,128]{2,1,0:T(8,128)S(1)}...) custom-call(f32[8]{0:T(128)S(1)} %copy-done.5, f32[8]{0:T(128)S(1)} %copy-done.6, ...), custom_call_target="tpu_custom_call" | custom-call | flops 1000000000 | bytes 11690080 | tf_op jit(solution)/shard_map/weights/pallas_call | solution.py:71
  79.0 0.0 collective-permute-done.10.low2
  79.0 3.7 %collective-permute-done.11.high2 = f32[128,128]{1,0:T(8,128)S(1)} collective-permute-done((f32[128,128]{1,0:T(8,128)S(1)}, f32[128,128]{1,0:T(8,128)S(1)}, u32[]{:S(2)}, u32[]{:S(2)}) %collective-permute-start.11) | collective-permute-done | bytes 65568 | tf_op jit(solution)/shard_map/ppermute | solution.py:454
  82.7 11.0 %sweeps.1 = (f32[512,128]{1,0:T(8,128)}, f32[1024,128]{1,0:T(8,128)S(1)}) custom-call(f32[16,160,128]{2,1,0:T(8,128)S(1)} %get-tuple-element.76.xm, f32[16,144,128]{2,1,0:T(8,128)S(1)} %get-tuple-element.85.wz, f32[16,160,128]{2,1,0:T(8,128)S(1)} %get-tuple-element.86.wx, f32[16,144,128]{2,1,0:T(8,128)S(1)} %get-tuple-element.87.wy, ...), custom_call_target="tpu_custom_call" | custom-call | flops 100000000 | bytes 14237696 | tf_op jit(solution)/shard_map/sweeps/pallas_call | solution.py:71
  93.6 29.6 %all_to_all.10 = f32[1024,1,128]{2,1,0:T(1,128)S(1)} all-to-all(f32[1024,1,128]{2,1,0:T(1,128)S(1)} %bitcast.26), channel_id=1, replica_groups=mesh['gx'=16,'gy'=4,'gz'=8] {'gx','gy'}, dimensions={0} | all-to-all | bytes 1048576 | tf_op jit(solution)/shard_map/all_to_all | solution.py:459
  123.2 1.2 finish.1
  (6 shorter events, 0.1 us)
Async XLA Ops:
  0.6 15.0 %copy-start.2 = (f32[4,128,128]{2,1,0:T(8,128)S(1)}, f32[4,128,128]{2,1,0:T(8,128)}, u32[]{:S(2)}) copy-start(f32[4,128,128]{2,1,0:T(8,128)} %param.14) | copy-start | bytes 786436
  0.6 15.0 %copy-start.4 = (s32[1,1,1,512]{3,2,1,0:T(1,128)S(1)}, s32[1,1,1,512]{3,2,1,0:T(1,128)}, u32[]{:S(2)}) copy-start(s32[1,1,1,512]{3,2,1,0:T(1,128)} %param.18) | copy-start | bytes 6148
  4.0 35.3 %all-to-all-start = ((f32[1088,1,128]{2,1,0:T(1,128)}), f32[1088,1,128]{2,1,0:T(1,128)S(1)}, u32[]{:S(2)}, u32[]{:S(2)}) async-start(f32[1088,1,128]{2,1,0:T(1,128)} %bitcast.31), calls=%async_computation | async-start | bytes 1114112 | tf_op jit(solution)/shard_map/all_to_all | solution.py:459
  15.7 23.6 %collective-permute-start.1 = (f32[520,128]{1,0:T(8,128)S(1)}, f32[520,128]{1,0:T(8,128)S(1)}, u32[]{:S(2)}, u32[]{:S(2)}) collective-permute-start(f32[520,128]{1,0:T(8,128)S(1)} %get-tuple-element.53.own), channel_id=1, source_target_pairs={{1,0},{2,1},{3,2},{4,3},{5,4},{6,5},{7,6},{9,8},{10,9},{11,10},{12... | collective-permute-start | bytes 798728 | tf_op jit(solution)/shard_map/ppermute | solution.py:454
  17.0 22.3 %collective-permute-start = (f32[520,128]{1,0:T(8,128)S(1)}, f32[520,128]{1,0:T(8,128)S(1)}, u32[]{:S(2)}, u32[]{:S(2)}) collective-permute-start(f32[520,128]{1,0:T(8,128)S(1)} %get-tuple-element.53.own), channel_id=1, source_target_pairs={{0,1},{1,2},{2,3},{3,4},{4,5},{5,6},{6,7},{8,9},{9,10},{10,11},{11... | collective-permute-start | bytes 798728 | tf_op jit(solution)/shard_map/ppermute | solution.py:454
  21.6 8.1 %collective-permute-start.2 = (f32[264,128]{1,0:T(8,128)S(1)}, f32[264,128]{1,0:T(8,128)S(1)}, u32[]{:S(2)}, u32[]{:S(2)}) collective-permute-start(f32[264,128]{1,0:T(8,128)S(1)} %get-tuple-element.54), channel_id=1, source_target_pairs={{0,2},{1,3},{2,4},{3,5},{4,6},{5,7},{8,10},{9,11},{10,12},{11,13},... | collective-permute-start | bytes 405512 | tf_op jit(solution)/shard_map/ppermute | solution.py:454
  27.4 11.9 %collective-permute-start.3 = (f32[264,128]{1,0:T(8,128)S(1)}, f32[264,128]{1,0:T(8,128)S(1)}, u32[]{:S(2)}, u32[]{:S(2)}) collective-permute-start(f32[264,128]{1,0:T(8,128)S(1)} %get-tuple-element.55), channel_id=1, source_target_pairs={{2,0},{3,1},{4,2},{5,3},{6,4},{7,5},{10,8},{11,9},{12,10},{13,11},... | collective-permute-start | bytes 405512 | tf_op jit(solution)/shard_map/ppermute | solution.py:454
  39.3 14.0 %copy-start = (f32[3,4,128,128]{3,2,1,0:T(8,128)S(1)}, f32[3,4,128,128]{3,2,1,0:T(8,128)}, u32[]{:S(2)}) copy-start(f32[3,4,128,128]{3,2,1,0:T(8,128)} %param.11) | copy-start | bytes 2359300
  39.3 14.0 %copy-start.3 = (s32[1,1,1,512,1]{3,4,2,1,0:T(1,128)S(1)}, s32[1,1,1,512,1]{3,4,2,1,0:T(1,128)}, u32[]{:S(2)}) copy-start(s32[1,1,1,512,1]{3,4,2,1,0:T(1,128)} %param.15) | copy-start | bytes 6148
  40.1 7.7 %collective-permute-start.5 = (f32[512,128]{1,0:T(8,128)S(1)}, f32[512,128]{1,0:T(8,128)S(1)}, u32[]{:S(2)}, u32[]{:S(2)}) collective-permute-start(f32[512,128]{1,0:T(8,128)S(1)} %get-tuple-element.63.own), channel_id=1, source_target_pairs={{1,0},{2,1},{3,2},{4,3},{5,4},{6,5},{7,6},{9,8},{10,9},{11,10},{12... | collective-permute-start | bytes 786440 | tf_op jit(solution)/shard_map/ppermute | solution.py:454
  41.4 7.3 %collective-permute-start.4 = (f32[512,128]{1,0:T(8,128)S(1)}, f32[512,128]{1,0:T(8,128)S(1)}, u32[]{:S(2)}, u32[]{:S(2)}) collective-permute-start(f32[512,128]{1,0:T(8,128)S(1)} %get-tuple-element.63.own), channel_id=1, source_target_pairs={{0,1},{1,2},{2,3},{3,4},{4,5},{5,6},{6,7},{8,9},{9,10},{10,11},{11... | collective-permute-start | bytes 786440 | tf_op jit(solution)/shard_map/ppermute | solution.py:454
  48.7 6.1 %collective-permute-start.6 = (f32[240,128]{1,0:T(8,128)S(1)}, f32[240,128]{1,0:T(8,128)S(1)}, u32[]{:S(2)}, u32[]{:S(2)}) collective-permute-start(f32[240,128]{1,0:T(8,128)S(1)} %get-tuple-element.70), channel_id=1, source_target_pairs={{0,32},{32,64},{64,96},{96,128},{128,160},{160,192},{192,224},{224... | collective-permute-start | bytes 368648 | tf_op jit(solution)/shard_map/ppermute | solution.py:454
  52.0 5.6 %collective-permute-start.7 = (f32[240,128]{1,0:T(8,128)S(1)}, f32[240,128]{1,0:T(8,128)S(1)}, u32[]{:S(2)}, u32[]{:S(2)}) collective-permute-start(f32[240,128]{1,0:T(8,128)S(1)} %get-tuple-element.71), channel_id=1, source_target_pairs={{32,0},{64,32},{96,64},{128,96},{160,128},{192,160},{224,192},{256... | collective-permute-start | bytes 368648 | tf_op jit(solution)/shard_map/ppermute | solution.py:454
  54.7 20.2 %copy-start.5 = (f32[8]{0:T(128)S(1)}, f32[8]{0:T(128)}, u32[]{:S(2)}) copy-start(f32[8]{0:T(128)} %base.1) | copy-start | bytes 100
  54.7 20.2 %copy-start.6 = (f32[8]{0:T(128)S(1)}, f32[8]{0:T(128)}, u32[]{:S(2)}) copy-start(f32[8]{0:T(128)} %soft.1) | copy-start | bytes 100
  54.8 20.2 %copy-start.7 = (f32[8]{0:T(128)S(1)}, f32[8]{0:T(128)}, u32[]{:S(2)}) copy-start(f32[8]{0:T(128)} %heat.1) | copy-start | bytes 100
  58.6 16.3 %collective-permute-start.8 = (f32[16,2304]{1,0:T(8,128)S(1)}, f32[16,2304]{1,0:T(8,128)S(1)}, u32[]{:S(2)}, u32[]{:S(2)}) collective-permute-start(f32[16,2304]{1,0:T(8,128)S(1)} %get-tuple-element.83), channel_id=1, source_target_pairs={{0,8},{8,16},{16,24},{1,9},{9,17},{17,25},{2,10},{10,18},{18,26},{... | collective-permute-start | bytes 442376 | tf_op jit(solution)/shard_map/ppermute | solution.py:454
  66.2 8.7 %collective-permute-start.9 = (f32[16,2304]{1,0:T(8,128)S(1)}, f32[16,2304]{1,0:T(8,128)S(1)}, u32[]{:S(2)}, u32[]{:S(2)}) collective-permute-start(f32[16,2304]{1,0:T(8,128)S(1)} %get-tuple-element.84), channel_id=1, source_target_pairs={{8,0},{16,8},{24,16},{9,1},{17,9},{25,17},{10,2},{18,10},{26,18},{... | collective-permute-start | bytes 442376 | tf_op jit(solution)/shard_map/ppermute | solution.py:454
  68.1 10.8 %collective-permute-start.10 = (f32[128,128]{1,0:T(8,128)S(1)}, f32[128,128]{1,0:T(8,128)S(1)}, u32[]{:S(2)}, u32[]{:S(2)}) collective-permute-start(f32[128,128]{1,0:T(8,128)S(1)} %get-tuple-element.94), channel_id=1, source_target_pairs={{0,2},{1,3},{2,4},{3,5},{4,6},{5,7},{8,10},{9,11},{10,12},{11,13},... | collective-permute-start | bytes 196616 | tf_op jit(solution)/shard_map/ppermute | solution.py:454
  73.6 9.1 %collective-permute-start.11 = (f32[128,128]{1,0:T(8,128)S(1)}, f32[128,128]{1,0:T(8,128)S(1)}, u32[]{:S(2)}, u32[]{:S(2)}) collective-permute-start(f32[128,128]{1,0:T(8,128)S(1)} %get-tuple-element.95), channel_id=1, source_target_pairs={{2,0},{3,1},{4,2},{5,3},{6,4},{7,5},{10,8},{11,9},{12,10},{13,11},... | collective-permute-start | bytes 196616 | tf_op jit(solution)/shard_map/ppermute | solution.py:454
  93.6 29.6 %copy-start.1 = (f32[4,128,128]{2,1,0:T(8,128)S(1)}, f32[4,128,128]{2,1,0:T(8,128)}, u32[]{:S(2)}) copy-start(f32[4,128,128]{2,1,0:T(8,128)} %param.13) | copy-start | bytes 786436

commit v6 on v5

--- a/solution.py
+++ b/solution.py
@@ -361,8 +361,8 @@
             b0[k, to] = cf * xm[k, here] * i
 
 
-def sweep_kernel(xm, wz, wx, wy, wyw, inv, b0, strips, full, sides, before, after, low2, high2, ids,
-                 out, replies, b, d, xa, xb, ends):
+def sweep_kernel(xm, wz, wx, wy, wyw, inv, b0, strips, full, sides, before, after,
+                 out, pull, b, d, xa, xb, ends):
     count, rows, _ = inv.shape
     total = count * rows
     factors = steps()
@@ -378,9 +378,13 @@
         sd = step if sd is None else step + keep * sd
         sx = sx + sd
         kept.append(ends_of(sx))
-    place_in = end_lanes(2 * SWEEPS, SWEEPS)
-    kept = jnp.concatenate(parts(jnp.concatenate(kept, axis=0)), axis=0)
-    ends[...] = dot(kept, jnp.concatenate([place_in, place_in], axis=0), 0, 0)
+    place_in = end_lanes(2, 1)
+    place_in = jnp.concatenate([place_in, place_in], axis=0)
+    for s, pair in enumerate(kept):
+        start = (1 + s) * rows // LANES * LANES
+        stop = -(-(count - 1 - s) * rows // LANES) * LANES
+        ends[start:stop, s * LANES : (s + 1) * LANES] = dot(
+            jnp.concatenate(parts(pair[:, start:stop]), axis=0), place_in, 0, 0)
 
     piece = 24
     first, last = iota((piece, LANES), 1) == 0, iota((piece, LANES), 1) == LANES - 1
@@ -426,14 +430,20 @@
     for _, add in factors:
         scale = scale * add
     tile = pl.ds(EDGE, LANES)
-    for ref, start, way, k in ((low2, 1, 1, 0), (high2, count - 2, -1, 3)):
-        gain = scale * inv[start, tile] * ref[...]
+    for i, (start, way) in enumerate(((1, 1), (count - 2, -1))):
+        gain = scale * inv[start, tile]
         for j in range(1, SWEEPS):
             at = start + way * j
             gain = gain * inv[at, tile] * wz[at - 1 if way > 0 else at, tile]
-        to = pl.ds(k * LANES, LANES)
-        out[to, :] = out[to, :] + gain
+        pull[pl.ds(i * LANES, LANES), :] = gain
+
+
+def reply_kernel(x, pull, low2, high2, ids, out, replies):
     n = out.shape[0]
+    first, last = pl.ds(0, LANES), pl.ds(n - LANES, LANES)
+    out[...] = x[...]
+    out[first, :] = x[first, :] + pull[pl.ds(0, LANES), :] * low2[...]
+    out[last, :] = x[last, :] + pull[pl.ds(LANES, LANES), :] * high2[...]
     name = ids[...]
     hot = jnp.concatenate([hot_of(name == iota(name.shape, 1) + at) for at in range(0, n, LANES)], axis=1)
     replies[...] = pick_rows(hot, out[...])
@@ -520,12 +530,15 @@
         scratch=[pltpu.VMEM((count, rows + 2 * EDGE, width), F32), pltpu.VMEM((total, 3 * width), F32),
                  pltpu.VMEM((total, width), F32)],
         limit=32, flops=10**9, smem=(0, 1, 2))
-    x, replies = call(
-        sweep_kernel, [sized(n, width), sized(peers * slots, width)],
-        [xm] + list(weights) + [full, heat_sides, before, after, low2, high2, ids], "sweeps",
+    x, pull = call(
+        sweep_kernel, [sized(n, width), sized(2 * xcells, width)],
+        [xm] + list(weights) + [full, heat_sides, before, after], "sweeps",
         scratch=[pltpu.VMEM((count, rows, width), F32)] * 2 + [pltpu.VMEM((count, rows + 2 * EDGE, width), F32)] * 2
         + [pltpu.VMEM((total, SWEEPS * width), F32)],
         limit=36, flops=10**8)
+    x, pull, low2, high2 = lax.optimization_barrier((x, pull, low2, high2))
+    x, replies = call(
+        reply_kernel, [sized(n, width), sized(peers * slots, width)], [x, pull, low2, high2, ids], "reply", flops=10**8)
     returned = exchanged(replies)
     mobility, ionization = call(final_kernel, [sized(n, width)] * 2, [returned, dest, gain, mob], "finish", flops=10**8)
     shape = density.shape

time: 125 us -> 121 us (0.968); the launches traced: 124 us -> 119 us
  waiting for transfers between devices: 20.3 us -> 16.6 us
    ppermute x12, waiting for transfers between devices: 20.3 us -> 16.6 us  [shifted(): return lax.ppermute(v, axis, pairs) if pairs else jnp.zeros_like(v)]
    pallas_call x11 -> x12, Pallas kernels: 22.7 us -> 21.8 us  [call(): pl.pallas_call(kernel, out_shape=[jax.ShapeDtypeStruct(s, t) for s, t in...]
  transfers between devices with their start and end apart: 13 -> 13, of which waited for: 6 -> 5; matrix products, arithmetic and copies ran while one was open for 0% -> 0% of each run, Pallas kernels for 4% -> 12%
where the time goes in v6:
time: 121 us; the launch traced here: 119 us
  starting transfers between devices  50.9 us (42%)
  blocking collectives  28.5 us (24%)
  Pallas kernels  21.8 us (18%)
  waiting for transfers between devices  16.6 us (14%)
    ppermute x12, starting transfers between devices, shifted(): return lax.ppermute(v, axis, pairs) if pairs else jnp.zeros_like(v)  39.2 us
    all_to_all x1, blocking collectives, exchanged(): lax.all_to_all(lines, ('gx', 'gy'), split_axis=0, concat_axis=0, tiled=True)  28.5 us
    pallas_call x12, Pallas kernels, call(): pl.pallas_call(kernel, out_shape=[jax.ShapeDtypeStruct(s, t) for s, t in...  21.8 us
    ppermute x12, waiting for transfers between devices, shifted(): return lax.ppermute(v, axis, pairs) if pairs else jnp.zeros_like(v)  16.6 us
    all_to_all x1, starting transfers between devices, exchanged(): lax.all_to_all(lines, ('gx', 'gy'), split_axis=0, concat_axis=0, tiled=True)  11.6 us
  transfers between devices with their start and end apart: 13, of which 5 were waited for; matrix products, arithmetic and copies ran while one was open for 0% of the time, Pallas kernels for 12%

profile of v6, /device:TPU:1, one launch (start us, length us, event | category | flops | bytes accessed | tf_op | source)
XLA Modules:
  0.0 118.9 jit_solution(5991706203121435208)
XLA Ops:
  0.6 0.0 copy-start.2
  0.6 0.0 copy-start.4
  0.7 3.3 %dispatch.1 = f32[1088,128]{1,0:T(8,128)} custom-call(f32[3,512,128]{2,1,0:T(8,128)} %bitcast.21, f32[512,128]{1,0:T(8,128)} %bitcast.32, f32[512,128]{1,0:T(8,128)} %bitcast.24, s32[1,512]{1,0:T(1,128)} %bitcast.28, s32[1,512]{1,0:T(1,128)} %bitcast.33, s32[1,512]{1,0:T(1,128)} %bitcast.34), custom_call_target="tpu_custom_call" | custom-call | flops 100000000 | bytes 1873920 | tf_op jit(solution)/shard_map/dispatch/pallas_call | solution.py:71
  3.9 11.6 %all-to-all-start = ((f32[1088,1,128]{2,1,0:T(1,128)}), f32[1088,1,128]{2,1,0:T(1,128)S(1)}, u32[]{:S(2)}, u32[]{:S(2)}) async-start(f32[1088,1,128]{2,1,0:T(1,128)} %bitcast.31), calls=%async_computation | async-start | bytes 1114112 | tf_op jit(solution)/shard_map/all_to_all | solution.py:469
  15.6 0.0 copy-done.2
  15.6 0.0 copy-done.4
  15.7 1.3 %collective-permute-start.1 = (f32[520,128]{1,0:T(8,128)S(1)}, f32[520,128]{1,0:T(8,128)S(1)}, u32[]{:S(2)}, u32[]{:S(2)}) collective-permute-start(f32[520,128]{1,0:T(8,128)S(1)} %get-tuple-element.59.own), channel_id=1, source_target_pairs={{1,0},{2,1},{3,2},{4,3},{5,4},{6,5},{7,6},{9,8},{10,9},{11,10},{12... | collective-permute-start | bytes 798728 | tf_op jit(solution)/shard_map/ppermute | solution.py:464
  17.0 4.6 %collective-permute-start = (f32[520,128]{1,0:T(8,128)S(1)}, f32[520,128]{1,0:T(8,128)S(1)}, u32[]{:S(2)}, u32[]{:S(2)}) collective-permute-start(f32[520,128]{1,0:T(8,128)S(1)} %get-tuple-element.59.own), channel_id=1, source_target_pairs={{0,1},{1,2},{2,3},{3,4},{4,5},{5,6},{6,7},{8,9},{9,10},{10,11},{11... | collective-permute-start | bytes 798728 | tf_op jit(solution)/shard_map/ppermute | solution.py:464
  21.6 5.8 %collective-permute-start.2 = (f32[264,128]{1,0:T(8,128)S(1)}, f32[264,128]{1,0:T(8,128)S(1)}, u32[]{:S(2)}, u32[]{:S(2)}) collective-permute-start(f32[264,128]{1,0:T(8,128)S(1)} %get-tuple-element.60), channel_id=1, source_target_pairs={{0,2},{1,3},{2,4},{3,5},{4,6},{5,7},{8,10},{9,11},{10,12},{11,13},... | collective-permute-start | bytes 405512 | tf_op jit(solution)/shard_map/ppermute | solution.py:464
  27.4 1.3 %collective-permute-start.3 = (f32[264,128]{1,0:T(8,128)S(1)}, f32[264,128]{1,0:T(8,128)S(1)}, u32[]{:S(2)}, u32[]{:S(2)}) collective-permute-start(f32[264,128]{1,0:T(8,128)S(1)} %get-tuple-element.61), channel_id=1, source_target_pairs={{2,0},{3,1},{4,2},{5,3},{6,4},{7,5},{10,8},{11,9},{12,10},{13,11},... | collective-permute-start | bytes 405512 | tf_op jit(solution)/shard_map/ppermute | solution.py:464
  28.7 0.9 collective-permute-done.2.low2
  29.7 9.6 %collective-permute-done.3.high2 = f32[264,128]{1,0:T(8,128)S(1)} collective-permute-done((f32[264,128]{1,0:T(8,128)S(1)}, f32[264,128]{1,0:T(8,128)S(1)}, u32[]{:S(2)}, u32[]{:S(2)}) %collective-permute-start.3) | collective-permute-done | bytes 135200 | tf_op jit(solution)/shard_map/ppermute | solution.py:464
  39.3 0.0 collective-permute-done.1.high
  39.3 0.0 collective-permute-done.low
  39.3 0.0 all-to-all-done
  39.3 0.0 copy-start
  39.3 0.0 copy-start.3
  39.3 0.7 combine.1
  40.0 1.3 %collective-permute-start.5 = (f32[512,128]{1,0:T(8,128)S(1)}, f32[512,128]{1,0:T(8,128)S(1)}, u32[]{:S(2)}, u32[]{:S(2)}) collective-permute-start(f32[512,128]{1,0:T(8,128)S(1)} %get-tuple-element.69.own), channel_id=1, source_target_pairs={{1,0},{2,1},{3,2},{4,3},{5,4},{6,5},{7,6},{9,8},{10,9},{11,10},{12... | collective-permute-start | bytes 786440 | tf_op jit(solution)/shard_map/ppermute | solution.py:464
  41.3 4.0 %collective-permute-start.4 = (f32[512,128]{1,0:T(8,128)S(1)}, f32[512,128]{1,0:T(8,128)S(1)}, u32[]{:S(2)}, u32[]{:S(2)}) collective-permute-start(f32[512,128]{1,0:T(8,128)S(1)} %get-tuple-element.69.own), channel_id=1, source_target_pairs={{0,1},{1,2},{2,3},{3,4},{4,5},{5,6},{6,7},{8,9},{9,10},{10,11},{11... | collective-permute-start | bytes 786440 | tf_op jit(solution)/shard_map/ppermute | solution.py:464
  45.4 0.1 start_x.1
  45.4 2.3 %collective-permute-done.5.high = f32[512,128]{1,0:T(8,128)S(1)} collective-permute-done((f32[512,128]{1,0:T(8,128)S(1)}, f32[512,128]{1,0:T(8,128)S(1)}, u32[]{:S(2)}, u32[]{:S(2)}) %collective-permute-start.5) | collective-permute-done | bytes 262176 | tf_op jit(solution)/shard_map/ppermute | solution.py:464
  47.8 0.9 collective-permute-done.4.low
  48.7 3.3 %collective-permute-start.6 = (f32[240,128]{1,0:T(8,128)S(1)}, f32[240,128]{1,0:T(8,128)S(1)}, u32[]{:S(2)}, u32[]{:S(2)}) collective-permute-start(f32[240,128]{1,0:T(8,128)S(1)} %get-tuple-element.76), channel_id=1, source_target_pairs={{0,32},{32,64},{64,96},{96,128},{128,160},{160,192},{192,224},{224... | collective-permute-start | bytes 368648 | tf_op jit(solution)/shard_map/ppermute | solution.py:464
  52.0 1.3 %collective-permute-start.7 = (f32[240,128]{1,0:T(8,128)S(1)}, f32[240,128]{1,0:T(8,128)S(1)}, u32[]{:S(2)}, u32[]{:S(2)}) collective-permute-start(f32[240,128]{1,0:T(8,128)S(1)} %get-tuple-element.77), channel_id=1, source_target_pairs={{32,0},{64,32},{96,64},{128,96},{160,128},{192,160},{224,192},{256... | collective-permute-start | bytes 368648 | tf_op jit(solution)/shard_map/ppermute | solution.py:464
  53.3 0.0 copy-done
  53.3 1.0 gain.1
  54.3 0.4 ids.1
  54.7 0.0 copy-start.5
  54.7 0.0 copy-start.6
  54.7 0.0 copy-start.7
  54.7 0.0 collective-permute-done.6.before
  54.8 2.8 %collective-permute-done.7.after = f32[240,128]{1,0:T(8,128)S(1)} collective-permute-done((f32[240,128]{1,0:T(8,128)S(1)}, f32[240,128]{1,0:T(8,128)S(1)}, u32[]{:S(2)}, u32[]{:S(2)}) %collective-permute-start.7) | collective-permute-done | bytes 122912 | tf_op jit(solution)/shard_map/ppermute | solution.py:464
  57.6 0.9 pack_y.1
  58.6 7.6 %collective-permute-start.8 = (f32[16,2304]{1,0:T(8,128)S(1)}, f32[16,2304]{1,0:T(8,128)S(1)}, u32[]{:S(2)}, u32[]{:S(2)}) collective-permute-start(f32[16,2304]{1,0:T(8,128)S(1)} %get-tuple-element.89), channel_id=1, source_target_pairs={{0,8},{8,16},{16,24},{1,9},{9,17},{17,25},{2,10},{10,18},{18,26},{... | collective-permute-start | bytes 442376 | tf_op jit(solution)/shard_map/ppermute | solution.py:464
  66.2 1.9 %collective-permute-start.9 = (f32[16,2304]{1,0:T(8,128)S(1)}, f32[16,2304]{1,0:T(8,128)S(1)}, u32[]{:S(2)}, u32[]{:S(2)}) collective-permute-start(f32[16,2304]{1,0:T(8,128)S(1)} %get-tuple-element.90), channel_id=1, source_target_pairs={{8,0},{16,8},{24,16},{9,1},{17,9},{25,17},{10,2},{18,10},{26,18},{... | collective-permute-start | bytes 442376 | tf_op jit(solution)/shard_map/ppermute | solution.py:464
  68.1 5.5 %collective-permute-start.10 = (f32[128,128]{1,0:T(8,128)S(1)}, f32[128,128]{1,0:T(8,128)S(1)}, u32[]{:S(2)}, u32[]{:S(2)}) collective-permute-start(f32[128,128]{1,0:T(8,128)S(1)} %get-tuple-element.102), channel_id=1, source_target_pairs={{0,2},{1,3},{2,4},{3,5},{4,6},{5,7},{8,10},{9,11},{10,12},{11,13},... | collective-permute-start | bytes 196616 | tf_op jit(solution)/shard_map/ppermute | solution.py:464
  73.6 1.3 %collective-permute-start.11 = (f32[128,128]{1,0:T(8,128)S(1)}, f32[128,128]{1,0:T(8,128)S(1)}, u32[]{:S(2)}, u32[]{:S(2)}) collective-permute-start(f32[128,128]{1,0:T(8,128)S(1)} %get-tuple-element.103), channel_id=1, source_target_pairs={{2,0},{3,1},{4,2},{5,3},{6,4},{7,5},{10,8},{11,9},{12,10},{13,11},... | collective-permute-start | bytes 196616 | tf_op jit(solution)/shard_map/ppermute | solution.py:464
  74.9 0.0 collective-permute-done.8.before
  74.9 0.0 collective-permute-done.9.after
  74.9 4.0 %weights.1 = (f32[16,144,128]{2,1,0:T(8,128)S(1)}, f32[16,160,128]{2,1,0:T(8,128)S(1)}, f32[16,144,128]{2,1,0:T(8,128)S(1)}, f32[16,144,128]{2,1,0:T(8,128)S(1)}...) custom-call(f32[8]{0:T(128)S(1)} %copy-done.5, f32[8]{0:T(128)S(1)} %copy-done.6, ...), custom_call_target="tpu_custom_call" | custom-call | flops 1000000000 | bytes 11690080 | tf_op jit(solution)/shard_map/weights/pallas_call | solution.py:71
  78.9 9.1 %sweeps.1 = (f32[512,128]{1,0:T(8,128)S(1)}, f32[256,128]{1,0:T(8,128)S(1)}) custom-call(f32[16,160,128]{2,1,0:T(8,128)S(1)} %get-tuple-element.82.xm, f32[16,144,128]{2,1,0:T(8,128)S(1)} %get-tuple-element.91.wz, f32[16,160,128]{2,1,0:T(8,128)S(1)} %get-tuple-element.92.wx, f32[16,144,128]{2,1,0:T(8,128)S(1)} %get-tuple-element.93.wy, ...), custom_call_target="tpu_custom_call" | custom-call | flops 100000000 | bytes 13189120 | tf_op jit(solution)/shard_map/sweeps/pallas_call | solution.py:71
  88.0 0.0 copy-start.1
  88.0 0.0 collective-permute-done.10.low2
  88.0 0.0 collective-permute-done.11.high2
  88.1 1.0 reply.1
  89.1 28.5 %all_to_all.10 = f32[1024,1,128]{2,1,0:T(1,128)S(1)} all-to-all(f32[1024,1,128]{2,1,0:T(1,128)S(1)} %bitcast.26), channel_id=1, replica_groups=mesh['gx'=16,'gy'=4,'gz'=8] {'gx','gy'}, dimensions={0} | all-to-all | bytes 1048576 | tf_op jit(solution)/shard_map/all_to_all | solution.py:469
  117.6 1.2 %finish.1 = (f32[512,128]{1,0:T(8,128)}, f32[512,128]{1,0:T(8,128)}) custom-call(f32[1024,128]{1,0:T(8,128)S(1)} %bitcast.23, s32[512,128]{1,0:T(8,128)S(1)} %get-tuple-element.111.dest, f32[512,128]{1,0:T(8,128)S(1)} %get-tuple-element.112.gain, f32[512,128]{1,0:T(8,128)S(1)} %bitcast.25), custom_call_target="tpu_custom_call" | custom-call | flops 100000000 | bytes 1835008 | tf_op jit(solution)/shard_map/finish/pallas_call | solution.py:71
  (7 shorter events, 0.1 us)
Async XLA Ops:
  0.6 15.0 %copy-start.2 = (f32[4,128,128]{2,1,0:T(8,128)S(1)}, f32[4,128,128]{2,1,0:T(8,128)}, u32[]{:S(2)}) copy-start(f32[4,128,128]{2,1,0:T(8,128)} %param.14) | copy-start | bytes 786436
  0.6 15.0 %copy-start.4 = (s32[1,1,1,512]{3,2,1,0:T(1,128)S(1)}, s32[1,1,1,512]{3,2,1,0:T(1,128)}, u32[]{:S(2)}) copy-start(s32[1,1,1,512]{3,2,1,0:T(1,128)} %param.18) | copy-start | bytes 6148
  3.9 35.3 %all-to-all-start = ((f32[1088,1,128]{2,1,0:T(1,128)}), f32[1088,1,128]{2,1,0:T(1,128)S(1)}, u32[]{:S(2)}, u32[]{:S(2)}) async-start(f32[1088,1,128]{2,1,0:T(1,128)} %bitcast.31), calls=%async_computation | async-start | bytes 1114112 | tf_op jit(solution)/shard_map/all_to_all | solution.py:469
  15.7 23.6 %collective-permute-start.1 = (f32[520,128]{1,0:T(8,128)S(1)}, f32[520,128]{1,0:T(8,128)S(1)}, u32[]{:S(2)}, u32[]{:S(2)}) collective-permute-start(f32[520,128]{1,0:T(8,128)S(1)} %get-tuple-element.59.own), channel_id=1, source_target_pairs={{1,0},{2,1},{3,2},{4,3},{5,4},{6,5},{7,6},{9,8},{10,9},{11,10},{12... | collective-permute-start | bytes 798728 | tf_op jit(solution)/shard_map/ppermute | solution.py:464
  17.0 22.3 %collective-permute-start = (f32[520,128]{1,0:T(8,128)S(1)}, f32[520,128]{1,0:T(8,128)S(1)}, u32[]{:S(2)}, u32[]{:S(2)}) collective-permute-start(f32[520,128]{1,0:T(8,128)S(1)} %get-tuple-element.59.own), channel_id=1, source_target_pairs={{0,1},{1,2},{2,3},{3,4},{4,5},{5,6},{6,7},{8,9},{9,10},{10,11},{11... | collective-permute-start | bytes 798728 | tf_op jit(solution)/shard_map/ppermute | solution.py:464
  21.6 8.1 %collective-permute-start.2 = (f32[264,128]{1,0:T(8,128)S(1)}, f32[264,128]{1,0:T(8,128)S(1)}, u32[]{:S(2)}, u32[]{:S(2)}) collective-permute-start(f32[264,128]{1,0:T(8,128)S(1)} %get-tuple-element.60), channel_id=1, source_target_pairs={{0,2},{1,3},{2,4},{3,5},{4,6},{5,7},{8,10},{9,11},{10,12},{11,13},... | collective-permute-start | bytes 405512 | tf_op jit(solution)/shard_map/ppermute | solution.py:464
  27.4 11.9 %collective-permute-start.3 = (f32[264,128]{1,0:T(8,128)S(1)}, f32[264,128]{1,0:T(8,128)S(1)}, u32[]{:S(2)}, u32[]{:S(2)}) collective-permute-start(f32[264,128]{1,0:T(8,128)S(1)} %get-tuple-element.61), channel_id=1, source_target_pairs={{2,0},{3,1},{4,2},{5,3},{6,4},{7,5},{10,8},{11,9},{12,10},{13,11},... | collective-permute-start | bytes 405512 | tf_op jit(solution)/shard_map/ppermute | solution.py:464
  39.3 14.0 %copy-start = (f32[3,4,128,128]{3,2,1,0:T(8,128)S(1)}, f32[3,4,128,128]{3,2,1,0:T(8,128)}, u32[]{:S(2)}) copy-start(f32[3,4,128,128]{3,2,1,0:T(8,128)} %param.11) | copy-start | bytes 2359300
  39.3 14.0 %copy-start.3 = (s32[1,1,1,512,1]{3,4,2,1,0:T(1,128)S(1)}, s32[1,1,1,512,1]{3,4,2,1,0:T(1,128)}, u32[]{:S(2)}) copy-start(s32[1,1,1,512,1]{3,4,2,1,0:T(1,128)} %param.15) | copy-start | bytes 6148
  40.0 7.7 %collective-permute-start.5 = (f32[512,128]{1,0:T(8,128)S(1)}, f32[512,128]{1,0:T(8,128)S(1)}, u32[]{:S(2)}, u32[]{:S(2)}) collective-permute-start(f32[512,128]{1,0:T(8,128)S(1)} %get-tuple-element.69.own), channel_id=1, source_target_pairs={{1,0},{2,1},{3,2},{4,3},{5,4},{6,5},{7,6},{9,8},{10,9},{11,10},{12... | collective-permute-start | bytes 786440 | tf_op jit(solution)/shard_map/ppermute | solution.py:464
  41.3 7.3 %collective-permute-start.4 = (f32[512,128]{1,0:T(8,128)S(1)}, f32[512,128]{1,0:T(8,128)S(1)}, u32[]{:S(2)}, u32[]{:S(2)}) collective-permute-start(f32[512,128]{1,0:T(8,128)S(1)} %get-tuple-element.69.own), channel_id=1, source_target_pairs={{0,1},{1,2},{2,3},{3,4},{4,5},{5,6},{6,7},{8,9},{9,10},{10,11},{11... | collective-permute-start | bytes 786440 | tf_op jit(solution)/shard_map/ppermute | solution.py:464
  48.7 6.1 %collective-permute-start.6 = (f32[240,128]{1,0:T(8,128)S(1)}, f32[240,128]{1,0:T(8,128)S(1)}, u32[]{:S(2)}, u32[]{:S(2)}) collective-permute-start(f32[240,128]{1,0:T(8,128)S(1)} %get-tuple-element.76), channel_id=1, source_target_pairs={{0,32},{32,64},{64,96},{96,128},{128,160},{160,192},{192,224},{224... | collective-permute-start | bytes 368648 | tf_op jit(solution)/shard_map/ppermute | solution.py:464
  52.0 5.6 %collective-permute-start.7 = (f32[240,128]{1,0:T(8,128)S(1)}, f32[240,128]{1,0:T(8,128)S(1)}, u32[]{:S(2)}, u32[]{:S(2)}) collective-permute-start(f32[240,128]{1,0:T(8,128)S(1)} %get-tuple-element.77), channel_id=1, source_target_pairs={{32,0},{64,32},{96,64},{128,96},{160,128},{192,160},{224,192},{256... | collective-permute-start | bytes 368648 | tf_op jit(solution)/shard_map/ppermute | solution.py:464
  54.7 20.2 %copy-start.5 = (f32[8]{0:T(128)S(1)}, f32[8]{0:T(128)}, u32[]{:S(2)}) copy-start(f32[8]{0:T(128)} %base.1) | copy-start | bytes 100
  54.7 20.2 %copy-start.6 = (f32[8]{0:T(128)S(1)}, f32[8]{0:T(128)}, u32[]{:S(2)}) copy-start(f32[8]{0:T(128)} %soft.1) | copy-start | bytes 100
  54.7 20.2 %copy-start.7 = (f32[8]{0:T(128)S(1)}, f32[8]{0:T(128)}, u32[]{:S(2)}) copy-start(f32[8]{0:T(128)} %heat.1) | copy-start | bytes 100
  58.6 16.3 %collective-permute-start.8 = (f32[16,2304]{1,0:T(8,128)S(1)}, f32[16,2304]{1,0:T(8,128)S(1)}, u32[]{:S(2)}, u32[]{:S(2)}) collective-permute-start(f32[16,2304]{1,0:T(8,128)S(1)} %get-tuple-element.89), channel_id=1, source_target_pairs={{0,8},{8,16},{16,24},{1,9},{9,17},{17,25},{2,10},{10,18},{18,26},{... | collective-permute-start | bytes 442376 | tf_op jit(solution)/shard_map/ppermute | solution.py:464
  66.2 8.7 %collective-permute-start.9 = (f32[16,2304]{1,0:T(8,128)S(1)}, f32[16,2304]{1,0:T(8,128)S(1)}, u32[]{:S(2)}, u32[]{:S(2)}) collective-permute-start(f32[16,2304]{1,0:T(8,128)S(1)} %get-tuple-element.90), channel_id=1, source_target_pairs={{8,0},{16,8},{24,16},{9,1},{17,9},{25,17},{10,2},{18,10},{26,18},{... | collective-permute-start | bytes 442376 | tf_op jit(solution)/shard_map/ppermute | solution.py:464
  68.1 19.9 %collective-permute-start.10 = (f32[128,128]{1,0:T(8,128)S(1)}, f32[128,128]{1,0:T(8,128)S(1)}, u32[]{:S(2)}, u32[]{:S(2)}) collective-permute-start(f32[128,128]{1,0:T(8,128)S(1)} %get-tuple-element.102), channel_id=1, source_target_pairs={{0,2},{1,3},{2,4},{3,5},{4,6},{5,7},{8,10},{9,11},{10,12},{11,13},... | collective-permute-start | bytes 196616 | tf_op jit(solution)/shard_map/ppermute | solution.py:464
  73.6 14.5 %collective-permute-start.11 = (f32[128,128]{1,0:T(8,128)S(1)}, f32[128,128]{1,0:T(8,128)S(1)}, u32[]{:S(2)}, u32[]{:S(2)}) collective-permute-start(f32[128,128]{1,0:T(8,128)S(1)} %get-tuple-element.103), channel_id=1, source_target_pairs={{2,0},{3,1},{4,2},{5,3},{6,4},{7,5},{10,8},{11,9},{12,10},{13,11},... | collective-permute-start | bytes 196616 | tf_op jit(solution)/shard_map/ppermute | solution.py:464
  88.0 29.6 %copy-start.1 = (f32[4,128,128]{2,1,0:T(8,128)S(1)}, f32[4,128,128]{2,1,0:T(8,128)}, u32[]{:S(2)}) copy-start(f32[4,128,128]{2,1,0:T(8,128)} %param.13) | copy-start | bytes 786436

commit v7 on v6

--- a/solution.py
+++ b/solution.py
@@ -91,15 +91,12 @@
 def dispatch_kernel(peers, slots, *refs):
     far, out, near, sems = refs[:6], refs[6], refs[7:13], refs[13]
     copies = [pltpu.make_async_copy(a, b, sems.at[i]) for i, (a, b) in enumerate(zip(far, near))]
-    for copy in copies:
+    for copy in copies[3:] + copies[:3]:
         copy.start()
-    for copy in copies:
+    for copy in copies[3:]:
         copy.wait()
     ef, den, mob, owner, block, live = near
     n = owner.shape[1]
-    esq = ef[0] * ef[0] + ef[1] * ef[1] + ef[2] * ef[2]
-    heat = 0.2 * den[...] * mob[...] * esq
-    heat = jnp.where(iota(heat.shape, 1) < column(live[...]), heat, F32(0.0))
     own = owner[...]
     own_col = column(own)
     pos = jnp.zeros((1, n), I32)
@@ -109,16 +106,23 @@
         pos = pos + jnp.sum(jnp.where(earlier, 1, 0), axis=0, keepdims=True)
     dest = own * (slots + 1) + pos
     hot = hot_of(iota((peers * (slots + 1), n), 0) == dest)
-    out[...] = pick_rows(hot, heat)
     named = hot_of(iota((peers, n), 0) == own)
     at_slot = iota((LANES, n), 0) == pos
     code = block[...] + 1
     high = jnp.where(at_slot, code // 32, 0).astype(F32).astype(BF16)
     low = jnp.where(at_slot, code % 32, 0).astype(F32).astype(BF16)
-    out[pl.ds(slots, peers, stride=slots + 1), :] = dot(named, high, 1, 1) * 32.0 + dot(named, low, 1, 1)
-
-
-def after_kernel(slots, ef, owner, gain, dest):
+    labels = dot(named, high, 1, 1) * 32.0 + dot(named, low, 1, 1)
+    live_col = column(live[...])
+    for copy in copies[:3]:
+        copy.wait()
+    esq = ef[0] * ef[0] + ef[1] * ef[1] + ef[2] * ef[2]
+    heat = 0.2 * den[...] * mob[...] * esq
+    heat = jnp.where(iota(heat.shape, 1) < live_col, heat, F32(0.0))
+    out[...] = pick_rows(hot, heat)
+    out[pl.ds(slots, peers, stride=slots + 1), :] = labels
+
+
+def after_kernel(slots, ef, owner, gain, hot):
     n = owner.shape[1]
     esq = ef[0] * ef[0] + ef[1] * ef[1] + ef[2] * ef[2]
     gain[...] = -2.0 * lax.rsqrt(esq + 1.0)
@@ -129,7 +133,8 @@
         piece = own_col[at : at + LANES]
         earlier = (piece == own) & (iota((LANES, n), 1) < r)
         pos = jnp.sum(jnp.where(earlier, 1, 0), axis=1, keepdims=True)
-        dest[pl.ds(at, LANES), :] = jnp.broadcast_to(piece * slots + pos, (LANES, LANES))
+        size = (LANES, hot.shape[1])
+        hot[pl.ds(at, LANES), :] = hot_of(jnp.broadcast_to(piece * slots + pos, size) == iota(size, 1))
 
 
 def labels_of(received, peers, slots):
@@ -153,7 +158,7 @@
     last[...] = source[pl.ds(n - LANES, LANES), :]
 
 
-def ids_kernel(peers, slots, received, ids):
+def ids_kernel(peers, slots, received, hot):
     total = peers * slots
     high, low = labels_of(received, peers, slots)
     own = hot_of(lax.div(iota((total, peers), 0), slots) == iota((total, peers), 1))
@@ -161,7 +166,7 @@
     i = iota((total, LANES), 0)
     mine = iota((total, LANES), 1) == i - slots * lax.div(i, slots)
     found = jnp.sum(jnp.where(mine, named, 0.0), axis=1, keepdims=True) - 1.0
-    ids[...] = jnp.broadcast_to(found, (total, LANES)).astype(I32)
+    hot[...] = hot_of(jnp.broadcast_to(found.astype(I32), hot.shape) == iota(hot.shape, 1))
 
 
 def start_z_kernel(far, x0, material, near, up, down):
@@ -261,6 +266,12 @@
     yhigh[pl.ds(EDGE, 1), :] = mat
 
 
+def inverse(v):
+    guess = pl.reciprocal(v, approx=True)
+    guess = guess * (2.0 - v * guess)
+    return guess * (2.0 - v * guess)
+
+
 def three_parts(v):
     high = v.astype(BF16)
     rest = v - high.astype(F32)
@@ -287,7 +298,7 @@
     return jnp.concatenate([before, sides, after], axis=0)
 
 
-def weights_kernel(base, soft, heat, xm, sides, flat_mat, before, after, wz, wx, wy, wyw, inv, b0, strips, cond, cols, ends):
+def weights_kernel(base, soft, heat, xm, sides, flat_mat, before, after, wz, wx, wxl, wy, wyw, inv, b0, strips, cond, cols, ends):
     count, rows = inv.shape[0], inv.shape[1]
     total = count * rows
     mat = jnp.concatenate(
@@ -305,13 +316,13 @@
     wide = lambda t, i: jnp.broadcast_to(t[i : i + 1], (EDGE, total))
     kb, ks, cf = (jnp.concatenate([wide(t, 1), wide(t, 0), wide(t, 0), wide(t, 2)], axis=0) for t in tables)
     sx = strip_of(sides[...], before[:EDGE], after[:EDGE])
-    sc = kb / (1.0 + ks * sx)
+    sc = kb * inverse(1.0 + ks * sx)
     down = lambda by, axis: 0.5 * (sc + turned(sc, by, axis))
     around = [down(rows, 1), down(-rows, 1), down(1, 1), down(-1, 1), down(1, 0), down(-1, 0)]
     diag = cf
     for w in around:
         diag = diag + w
-    si = jnp.where(cf > 0.0, 1.0 / diag, 0.0)
+    si = jnp.where(cf > 0.0, inverse(diag), 0.0)
     for i, w in enumerate(around):
         strips[i] = w * si
     strips[6] = si
@@ -327,12 +338,10 @@
     def _(k):
         cond[k, pl.ds(0, EDGE)] = blank
         cond[k, pl.ds(rows + EDGE, EDGE)] = blank
-        wx[k, pl.ds(0, EDGE)] = blank
-        wx[k, pl.ds(rows + EDGE, EDGE)] = blank
         for at in range(0, rows, piece):
             part = pl.ds(pl.multiple_of(k * rows + at, 8), piece)
             x = xm[k, pl.ds(EDGE + at, piece)]
-            cond[k, pl.ds(EDGE + at, piece)] = cols[part, 0:LANES] / (1.0 + cols[part, LANES : 2 * LANES] * x)
+            cond[k, pl.ds(EDGE + at, piece)] = cols[part, 0:LANES] * inverse(1.0 + cols[part, LANES : 2 * LANES] * x)
 
     first, last = iota((piece, LANES), 1) == 0, iota((piece, LANES), 1) == LANES - 1
     wz[0] = 0.5 * (cond[0, pl.ds(EDGE, rows)] + cond[1, pl.ds(EDGE, rows)])
@@ -352,16 +361,17 @@
             w = 0.5 * (c + jnp.where(first, end, turned(c, 1, 1)))
             cf = cols[part, 2 * LANES : 3 * LANES]
             diag = cf + up + low + right + left + e + w
-            i = jnp.where(cf > 0.0, 1.0 / diag, 0.0)
+            i = jnp.where(cf > 0.0, inverse(diag), 0.0)
             wz[k, to] = up
-            wx[k, here] = right
+            wx[k, to] = right
+            wxl[k, to] = left
             wy[k, to] = e
             wyw[k, to] = w
             inv[k, to] = i
             b0[k, to] = cf * xm[k, here] * i
 
 
-def sweep_kernel(xm, wz, wx, wy, wyw, inv, b0, strips, full, sides, before, after,
+def sweep_kernel(xm, wz, wx, wxl, wy, wyw, inv, b0, strips, full, sides, before, after,
                  out, pull, b, d, xa, xb, ends):
     count, rows, _ = inv.shape
     total = count * rows
@@ -408,8 +418,8 @@
                 e = jnp.where(last, end, turned(x, -1, 1))
                 w = jnp.where(first, end, turned(x, 1, 1))
                 near = wz[k, to] * src[k + 1, here] + wz[k - 1, to] * src[k - 1, here]
-                near += wx[k, here] * src[k, pl.ds(EDGE + at + 1, piece)]
-                near += wx[k, pl.ds(EDGE + at - 1, piece)] * src[k, pl.ds(EDGE + at - 1, piece)]
+                near += wx[k, to] * src[k, pl.ds(EDGE + at + 1, piece)]
+                near += wxl[k, to] * src[k, pl.ds(EDGE + at - 1, piece)]
                 near += wy[k, to] * e + wyw[k, to] * w
                 if s == 0:
                     rhs = b0[k, to] + full[k, to] * inv[k, to]
@@ -438,22 +448,17 @@
         pull[pl.ds(i * LANES, LANES), :] = gain
 
 
-def reply_kernel(x, pull, low2, high2, ids, out, replies):
+def reply_kernel(x, pull, low2, high2, hot, out, replies):
     n = out.shape[0]
     first, last = pl.ds(0, LANES), pl.ds(n - LANES, LANES)
     out[...] = x[...]
     out[first, :] = x[first, :] + pull[pl.ds(0, LANES), :] * low2[...]
     out[last, :] = x[last, :] + pull[pl.ds(LANES, LANES), :] * high2[...]
-    name = ids[...]
-    hot = jnp.concatenate([hot_of(name == iota(name.shape, 1) + at) for at in range(0, n, LANES)], axis=1)
-    replies[...] = pick_rows(hot, out[...])
-
-
-def final_kernel(returned, dest, gain, mob, mobility, ionization):
-    total = returned.shape[0]
-    name = dest[...]
-    hot = jnp.concatenate([hot_of(name == iota(name.shape, 1) + at) for at in range(0, total, LANES)], axis=1)
-    back = pick_rows(hot, returned[...])
+    replies[...] = pick_rows(hot[...], out[...])
+
+
+def final_kernel(returned, hot, gain, mob, mobility, ionization):
+    back = pick_rows(hot[...], returned[...])
     mobility[...] = mob[...] * jnp.exp(-0.7 * back)
     ionization[...] = jnp.exp(gain[...] * (1.0 + 0.3 * back))
 
@@ -500,23 +505,23 @@
         functools.partial(start_z_kernel, far), [sized(n + EDGE, width), aside, aside], [x0, mat], "start_z")
     low, high = shifted(near, "gz", 1), shifted(near, "gz", -1)
     low2, high2 = shifted(up, "gz", 2), shifted(down, "gz", -2)
-    received, low, high, low2, high2 = lax.optimization_barrier((received, low, high, low2, high2))
+    gain, dest = call(functools.partial(after_kernel, slots), [sized(n, width), ((n, peers * slots), BF16)], [ef, own], "gain")
+    received, low, high, low2, high2, gain, dest = lax.optimization_barrier(
+        (received, low, high, low2, high2, gain, dest))
     edge = sized(count * (EDGE + 1), width)
     xz, mats, start_low, start_high = call(
         functools.partial(start_x_kernel, far), [sized(count, xcells, width), sized(count, width), edge, edge],
         [low2, low, near, high, high2], "start_x")
-    gain, dest = call(functools.partial(after_kernel, slots), [sized(n, width), ((n, LANES), I32)], [ef, own], "gain")
 
     source, first, last = call(
         functools.partial(combine_kernel, peers, slots), [sized(n, width)] + [sized(xcells, width)] * 2,
         [received], "combine", flops=10**8)
-    [ids] = call(functools.partial(ids_kernel, peers, slots), [((peers * slots, LANES), I32)], [received], "ids")
+    [ids] = call(functools.partial(ids_kernel, peers, slots), [((peers * slots, n), BF16)], [received], "ids")
     low, high = shifted(source, "gz", 1), shifted(source, "gz", -1)
-    low, high, start_low, start_high = lax.optimization_barrier((low, high, start_low, start_high))
+    low, high, start_low, start_high, ids = lax.optimization_barrier((low, high, start_low, start_high, ids))
     edge = sized(count * (EDGE + 1) + 3 * layers * EDGE, width)
     xlow, xhigh = call(pack_x_kernel, [edge, edge], [low, source, high, start_low, start_high], "pack_x")
     before, after = shifted(xhigh, "gx", 1), shifted(xlow, "gx", -1)
-    before, after, ids, gain, dest = lax.optimization_barrier((before, after, ids, gain, dest))
     tall, tile, flat_edge = sized(count, rows + 2 * EDGE, width), sized(count, rows, width), sized(2 * EDGE, total)
     xm, full, sides, heat_sides, flat_mat, ylow, yhigh = call(
         pack_y_kernel, [tall, tile, flat_edge, flat_edge, sized(EDGE, total), flat_edge, flat_edge],
@@ -525,7 +530,7 @@
     before, after = shifted(yhigh, "gy", 1), shifted(ylow, "gy", -1)
     low2, high2 = shifted(last, "gz", 2), shifted(first, "gz", -2)
     weights = call(
-        weights_kernel, [tile, tall, tile, tile, tile, tile, sized(9, 4 * EDGE, total)],
+        weights_kernel, [tile] * 7 + [sized(9, 4 * EDGE, total)],
         [mat_conductivity, mat_softening, mat_capacity, xm, sides, flat_mat, before, after], "weights",
         scratch=[pltpu.VMEM((count, rows + 2 * EDGE, width), F32), pltpu.VMEM((total, 3 * width), F32),
                  pltpu.VMEM((total, width), F32)],

time: 121 us -> 123 us (1.017)
  waiting for transfers between devices: 16.6 us -> 13.2 us
  blocking collectives: 28.5 us -> 30.9 us
  local copies, waits for them, and re-layouts: 0.05 us -> 1.36 us
    ppermute x12, waiting for transfers between devices: 16.6 us -> 13.2 us  [shifted(): return lax.ppermute(v, axis, pairs) if pairs else jnp.zeros_like(v)]
    all_to_all x1, blocking collectives: 28.5 us -> 30.9 us  [exchanged(): lax.all_to_all(lines, ('gx', 'gy'), split_axis=0, concat_axis=0, tiled=True)]
    unnamed x16 -> x24, local copies, waits for them, and re-layouts: 0.05 us -> 1.36 us
  transfers between devices with their start and end apart: 13 -> 13, of which waited for: 5 -> 5; matrix products, arithmetic and copies ran while one was open for 0% -> 0% of each run, Pallas kernels for 12% -> 13%
where the time goes in v7:
time: 123 us; the launch traced here: 121 us
  starting transfers between devices  51.6 us (42%)
  blocking collectives  30.9 us (25%)
  Pallas kernels  22.5 us (18%)
  waiting for transfers between devices  13.2 us (11%)
  local copies, waits for them, and re-layouts  1.36 us (1%)
    ppermute x12, starting transfers between devices, shifted(): return lax.ppermute(v, axis, pairs) if pairs else jnp.zeros_like(v)  40 us
    all_to_all x1, blocking collectives, exchanged(): lax.all_to_all(lines, ('gx', 'gy'), split_axis=0, concat_axis=0, tiled=True)  30.9 us
    pallas_call x12, Pallas kernels, call(): pl.pallas_call(kernel, out_shape=[jax.ShapeDtypeStruct(s, t) for s, t in...  22.5 us
    ppermute x12, waiting for transfers between devices, shifted(): return lax.ppermute(v, axis, pairs) if pairs else jnp.zeros_like(v)  13.2 us
    all_to_all x1, starting transfers between devices, exchanged(): lax.all_to_all(lines, ('gx', 'gy'), split_axis=0, concat_axis=0, tiled=True)  11.6 us
  transfers between devices with their start and end apart: 13, of which 5 were waited for; matrix products, arithmetic and copies ran while one was open for 0% of the time, Pallas kernels for 13%

profile of v7, /device:TPU:1, one launch (start us, length us, event | category | flops | bytes accessed | tf_op | source)
XLA Modules:
  0.0 120.5 jit_solution(17345185921691637744)
XLA Ops:
  0.6 0.0 copy-start.2
  0.6 0.0 copy-start.8
  0.7 0.0 copy-start
  0.7 0.0 copy-start.7
  0.7 3.0 %dispatch.1 = f32[1088,128]{1,0:T(8,128)} custom-call(f32[3,512,128]{2,1,0:T(8,128)} %bitcast.21, f32[512,128]{1,0:T(8,128)} %bitcast.32, f32[512,128]{1,0:T(8,128)} %bitcast.24, s32[1,512]{1,0:T(1,128)} %bitcast.28, s32[1,512]{1,0:T(1,128)} %bitcast.33, s32[1,512]{1,0:T(1,128)} %bitcast.34), custom_call_target="tpu_custom_call" | custom-call | flops 100000000 | bytes 1873920 | tf_op jit(solution)/shard_map/dispatch/pallas_call | solution.py:71
  3.7 11.6 %all-to-all-start = ((f32[1088,1,128]{2,1,0:T(1,128)}), f32[1088,1,128]{2,1,0:T(1,128)S(1)}, u32[]{:S(2)}, u32[]{:S(2)}) async-start(f32[1088,1,128]{2,1,0:T(1,128)} %bitcast.31), calls=%async_computation | async-start | bytes 1114112 | tf_op jit(solution)/shard_map/all_to_all | solution.py:474
  15.4 1.3 %collective-permute-start.1 = (f32[520,128]{1,0:T(8,128)S(1)}, f32[520,128]{1,0:T(8,128)S(1)}, u32[]{:S(2)}, u32[]{:S(2)}) collective-permute-start(f32[520,128]{1,0:T(8,128)S(1)} %get-tuple-element.58.own), channel_id=1, source_target_pairs={{1,0},{2,1},{3,2},{4,3},{5,4},{6,5},{7,6},{9,8},{10,9},{11,10},{12... | collective-permute-start | bytes 798728 | tf_op jit(solution)/shard_map/ppermute | solution.py:469
  16.7 4.6 %collective-permute-start = (f32[520,128]{1,0:T(8,128)S(1)}, f32[520,128]{1,0:T(8,128)S(1)}, u32[]{:S(2)}, u32[]{:S(2)}) collective-permute-start(f32[520,128]{1,0:T(8,128)S(1)} %get-tuple-element.58.own), channel_id=1, source_target_pairs={{0,1},{1,2},{2,3},{3,4},{4,5},{5,6},{6,7},{8,9},{9,10},{10,11},{11... | collective-permute-start | bytes 798728 | tf_op jit(solution)/shard_map/ppermute | solution.py:469
  21.4 5.8 %collective-permute-start.2 = (f32[264,128]{1,0:T(8,128)S(1)}, f32[264,128]{1,0:T(8,128)S(1)}, u32[]{:S(2)}, u32[]{:S(2)}) collective-permute-start(f32[264,128]{1,0:T(8,128)S(1)} %get-tuple-element.59), channel_id=1, source_target_pairs={{0,2},{1,3},{2,4},{3,5},{4,6},{5,7},{8,10},{9,11},{10,12},{11,13},... | collective-permute-start | bytes 405512 | tf_op jit(solution)/shard_map/ppermute | solution.py:469
  27.2 1.3 %collective-permute-start.3 = (f32[264,128]{1,0:T(8,128)S(1)}, f32[264,128]{1,0:T(8,128)S(1)}, u32[]{:S(2)}, u32[]{:S(2)}) collective-permute-start(f32[264,128]{1,0:T(8,128)S(1)} %get-tuple-element.60), channel_id=1, source_target_pairs={{2,0},{3,1},{4,2},{5,3},{6,4},{7,5},{10,8},{11,9},{12,10},{13,11},... | collective-permute-start | bytes 405512 | tf_op jit(solution)/shard_map/ppermute | solution.py:469
  28.5 1.1 gain.1
  29.6 0.0 collective-permute-done.2.low2
  29.7 0.0 copy-start.3
  29.7 0.6 copy-done.3
  30.3 8.7 %collective-permute-done.3.high2 = f32[264,128]{1,0:T(8,128)S(1)} collective-permute-done((f32[264,128]{1,0:T(8,128)S(1)}, f32[264,128]{1,0:T(8,128)S(1)}, u32[]{:S(2)}, u32[]{:S(2)}) %collective-permute-start.3) | collective-permute-done | bytes 135200 | tf_op jit(solution)/shard_map/ppermute | solution.py:469
  39.0 0.7 copy-done.5
  39.7 0.0 collective-permute-done.1.high
  39.7 0.0 collective-permute-done.low
  39.7 0.0 all-to-all-done
  39.7 0.7 combine.1
  40.5 1.3 %collective-permute-start.5 = (f32[512,128]{1,0:T(8,128)S(1)}, f32[512,128]{1,0:T(8,128)S(1)}, u32[]{:S(2)}, u32[]{:S(2)}) collective-permute-start(f32[512,128]{1,0:T(8,128)S(1)} %get-tuple-element.70.own), channel_id=1, source_target_pairs={{1,0},{2,1},{3,2},{4,3},{5,4},{6,5},{7,6},{9,8},{10,9},{11,10},{12... | collective-permute-start | bytes 786440 | tf_op jit(solution)/shard_map/ppermute | solution.py:469
  41.8 4.0 %collective-permute-start.4 = (f32[512,128]{1,0:T(8,128)S(1)}, f32[512,128]{1,0:T(8,128)S(1)}, u32[]{:S(2)}, u32[]{:S(2)}) collective-permute-start(f32[512,128]{1,0:T(8,128)S(1)} %get-tuple-element.70.own), channel_id=1, source_target_pairs={{0,1},{1,2},{2,3},{3,4},{4,5},{5,6},{6,7},{8,9},{9,10},{10,11},{11... | collective-permute-start | bytes 786440 | tf_op jit(solution)/shard_map/ppermute | solution.py:469
  45.8 0.5 ids.1.hot
  46.4 0.1 start_x.1
  46.4 1.8 %collective-permute-done.5.high = f32[512,128]{1,0:T(8,128)S(1)} collective-permute-done((f32[512,128]{1,0:T(8,128)S(1)}, f32[512,128]{1,0:T(8,128)S(1)}, u32[]{:S(2)}, u32[]{:S(2)}) %collective-permute-start.5) | collective-permute-done | bytes 262176 | tf_op jit(solution)/shard_map/ppermute | solution.py:469
  48.2 0.9 collective-permute-done.4.low
  49.1 0.0 copy-start.9
  49.1 0.0 copy-start.10
  49.1 0.0 copy-start.11
  49.1 1.4 %collective-permute-start.6 = (f32[240,128]{1,0:T(8,128)S(1)}, f32[240,128]{1,0:T(8,128)S(1)}, u32[]{:S(2)}, u32[]{:S(2)}) collective-permute-start(f32[240,128]{1,0:T(8,128)S(1)} %get-tuple-element.77), channel_id=1, source_target_pairs={{32,0},{64,32},{96,64},{128,96},{160,128},{192,160},{224,192},{256... | collective-permute-start | bytes 368648 | tf_op jit(solution)/shard_map/ppermute | solution.py:469
  50.6 4.0 %collective-permute-start.7 = (f32[240,128]{1,0:T(8,128)S(1)}, f32[240,128]{1,0:T(8,128)S(1)}, u32[]{:S(2)}, u32[]{:S(2)}) collective-permute-start(f32[240,128]{1,0:T(8,128)S(1)} %get-tuple-element.78), channel_id=1, source_target_pairs={{0,32},{32,64},{64,96},{96,128},{128,160},{160,192},{192,224},{224... | collective-permute-start | bytes 368648 | tf_op jit(solution)/shard_map/ppermute | solution.py:469
  54.6 0.3 collective-permute-done.6.after
  54.9 1.5 %collective-permute-done.7.before = f32[240,128]{1,0:T(8,128)S(1)} collective-permute-done((f32[240,128]{1,0:T(8,128)S(1)}, f32[240,128]{1,0:T(8,128)S(1)}, u32[]{:S(2)}, u32[]{:S(2)}) %collective-permute-start.7) | collective-permute-done | bytes 122912 | tf_op jit(solution)/shard_map/ppermute | solution.py:469
  56.4 0.9 pack_y.1
  57.4 7.5 %collective-permute-start.8 = (f32[16,2304]{1,0:T(8,128)S(1)}, f32[16,2304]{1,0:T(8,128)S(1)}, u32[]{:S(2)}, u32[]{:S(2)}) collective-permute-start(f32[16,2304]{1,0:T(8,128)S(1)} %get-tuple-element.86), channel_id=1, source_target_pairs={{0,8},{8,16},{16,24},{1,9},{9,17},{17,25},{2,10},{10,18},{18,26},{... | collective-permute-start | bytes 442376 | tf_op jit(solution)/shard_map/ppermute | solution.py:469
  64.9 1.9 %collective-permute-start.9 = (f32[16,2304]{1,0:T(8,128)S(1)}, f32[16,2304]{1,0:T(8,128)S(1)}, u32[]{:S(2)}, u32[]{:S(2)}) collective-permute-start(f32[16,2304]{1,0:T(8,128)S(1)} %get-tuple-element.87), channel_id=1, source_target_pairs={{8,0},{16,8},{24,16},{9,1},{17,9},{25,17},{10,2},{18,10},{26,18},{... | collective-permute-start | bytes 442376 | tf_op jit(solution)/shard_map/ppermute | solution.py:469
  66.8 5.5 %collective-permute-start.10 = (f32[128,128]{1,0:T(8,128)S(1)}, f32[128,128]{1,0:T(8,128)S(1)}, u32[]{:S(2)}, u32[]{:S(2)}) collective-permute-start(f32[128,128]{1,0:T(8,128)S(1)} %get-tuple-element.100), channel_id=1, source_target_pairs={{0,2},{1,3},{2,4},{3,5},{4,6},{5,7},{8,10},{9,11},{10,12},{11,13},... | collective-permute-start | bytes 196616 | tf_op jit(solution)/shard_map/ppermute | solution.py:469
  72.3 1.3 %collective-permute-start.11 = (f32[128,128]{1,0:T(8,128)S(1)}, f32[128,128]{1,0:T(8,128)S(1)}, u32[]{:S(2)}, u32[]{:S(2)}) collective-permute-start(f32[128,128]{1,0:T(8,128)S(1)} %get-tuple-element.101), channel_id=1, source_target_pairs={{2,0},{3,1},{4,2},{5,3},{6,4},{7,5},{10,8},{11,9},{12,10},{13,11},... | collective-permute-start | bytes 196616 | tf_op jit(solution)/shard_map/ppermute | solution.py:469
  73.6 0.0 collective-permute-done.8.before
  73.6 0.0 collective-permute-done.9.after
  73.7 4.6 %weights.1 = (f32[16,144,128]{2,1,0:T(8,128)S(1)}, f32[16,144,128]{2,1,0:T(8,128)S(1)}, f32[16,144,128]{2,1,0:T(8,128)S(1)}, f32[16,144,128]{2,1,0:T(8,128)S(1)}...) custom-call(f32[8]{0:T(128)S(1)} %copy-done.9, ...), custom_call_target="tpu_custom_call" | custom-call | flops 1000000000 | bytes 12738656 | tf_op jit(solution)/shard_map/weights/pallas_call | solution.py:71
  78.3 9.3 %sweeps.1 = (f32[512,128]{1,0:T(8,128)S(1)}, f32[256,128]{1,0:T(8,128)S(1)}) custom-call(f32[16,160,128]{2,1,0:T(8,128)S(1)} %get-tuple-element.79.xm, f32[16,144,128]{2,1,0:T(8,128)S(1)} %get-tuple-element.88.wz, f32[16,144,128]{2,1,0:T(8,128)S(1)} %get-tuple-element.89.wx, f32[16,144,128]{2,1,0:T(8,128)S(1)} %get-tuple-element.90.wxl, ...), custom_call_target="tpu_custom_call" | custom-call | flops 100000000 | bytes 14237696 | tf_op jit(solution)/shard_map/sweeps/pallas_call | solution.py:71
  87.5 0.0 collective-permute-done.10.low2
  87.6 0.0 collective-permute-done.11.high2
  87.6 0.0 copy-start.1
  87.6 0.8 reply.1
  88.4 30.9 %all_to_all.10 = f32[1024,1,128]{2,1,0:T(1,128)S(1)} all-to-all(f32[1024,1,128]{2,1,0:T(1,128)S(1)} %bitcast.26), channel_id=1, replica_groups=mesh['gx'=16,'gy'=4,'gz'=8] {'gx','gy'}, dimensions={0} | all-to-all | bytes 1048576 | tf_op jit(solution)/shard_map/all_to_all | solution.py:474
  119.3 1.2 %finish.1 = (f32[512,128]{1,0:T(8,128)}, f32[512,128]{1,0:T(8,128)}) custom-call(f32[1024,128]{1,0:T(8,128)S(1)} %bitcast.23, bf16[512,1024]{1,0:T(8,128)(2,1)S(1)} %get-tuple-element.109.hot, f32[512,128]{1,0:T(8,128)S(1)} %get-tuple-element.110.gain, f32[512,128]{1,0:T(8,128)S(1)} %bitcast.25), custom_call_target="tpu_custom_call" | custom-call | flops 100000000 | bytes 2621440 | tf_op jit(solution)/shard_map/finish/pallas_call | solution.py:71
  (15 shorter events, 0.1 us)
Async XLA Ops:
  0.6 14.7 %copy-start.2 = (f32[4,128,128]{2,1,0:T(8,128)S(1)}, f32[4,128,128]{2,1,0:T(8,128)}, u32[]{:S(2)}) copy-start(f32[4,128,128]{2,1,0:T(8,128)} %param.14) | copy-start | bytes 786436
  0.6 14.7 %copy-start.8 = (s32[1,1,1,512]{3,2,1,0:T(1,128)S(1)}, s32[1,1,1,512]{3,2,1,0:T(1,128)}, u32[]{:S(2)}) copy-start(s32[1,1,1,512]{3,2,1,0:T(1,128)} %param.18) | copy-start | bytes 6148
  0.7 27.8 %copy-start = (f32[3,4,128,128]{3,2,1,0:T(8,128)S(1)}, f32[3,4,128,128]{3,2,1,0:T(8,128)}, u32[]{:S(2)}) copy-start(f32[3,4,128,128]{3,2,1,0:T(8,128)} %param.11) | copy-start | bytes 2359300
  0.7 27.8 %copy-start.7 = (s32[1,1,1,512,1]{3,4,2,1,0:T(1,128)S(1)}, s32[1,1,1,512,1]{3,4,2,1,0:T(1,128)}, u32[]{:S(2)}) copy-start(s32[1,1,1,512,1]{3,4,2,1,0:T(1,128)} %param.15) | copy-start | bytes 6148
  3.7 36.0 %all-to-all-start = ((f32[1088,1,128]{2,1,0:T(1,128)}), f32[1088,1,128]{2,1,0:T(1,128)S(1)}, u32[]{:S(2)}, u32[]{:S(2)}) async-start(f32[1088,1,128]{2,1,0:T(1,128)} %bitcast.31), calls=%async_computation | async-start | bytes 1114112 | tf_op jit(solution)/shard_map/all_to_all | solution.py:474
  15.4 24.3 %collective-permute-start.1 = (f32[520,128]{1,0:T(8,128)S(1)}, f32[520,128]{1,0:T(8,128)S(1)}, u32[]{:S(2)}, u32[]{:S(2)}) collective-permute-start(f32[520,128]{1,0:T(8,128)S(1)} %get-tuple-element.58.own), channel_id=1, source_target_pairs={{1,0},{2,1},{3,2},{4,3},{5,4},{6,5},{7,6},{9,8},{10,9},{11,10},{12... | collective-permute-start | bytes 798728 | tf_op jit(solution)/shard_map/ppermute | solution.py:469
  16.7 23.0 %collective-permute-start = (f32[520,128]{1,0:T(8,128)S(1)}, f32[520,128]{1,0:T(8,128)S(1)}, u32[]{:S(2)}, u32[]{:S(2)}) collective-permute-start(f32[520,128]{1,0:T(8,128)S(1)} %get-tuple-element.58.own), channel_id=1, source_target_pairs={{0,1},{1,2},{2,3},{3,4},{4,5},{5,6},{6,7},{8,9},{9,10},{10,11},{11... | collective-permute-start | bytes 798728 | tf_op jit(solution)/shard_map/ppermute | solution.py:469
  21.4 8.3 %collective-permute-start.2 = (f32[264,128]{1,0:T(8,128)S(1)}, f32[264,128]{1,0:T(8,128)S(1)}, u32[]{:S(2)}, u32[]{:S(2)}) collective-permute-start(f32[264,128]{1,0:T(8,128)S(1)} %get-tuple-element.59), channel_id=1, source_target_pairs={{0,2},{1,3},{2,4},{3,5},{4,6},{5,7},{8,10},{9,11},{10,12},{11,13},... | collective-permute-start | bytes 405512 | tf_op jit(solution)/shard_map/ppermute | solution.py:469
  27.2 11.9 %collective-permute-start.3 = (f32[264,128]{1,0:T(8,128)S(1)}, f32[264,128]{1,0:T(8,128)S(1)}, u32[]{:S(2)}, u32[]{:S(2)}) collective-permute-start(f32[264,128]{1,0:T(8,128)S(1)} %get-tuple-element.60), channel_id=1, source_target_pairs={{2,0},{3,1},{4,2},{5,3},{6,4},{7,5},{10,8},{11,9},{12,10},{13,11},... | collective-permute-start | bytes 405512 | tf_op jit(solution)/shard_map/ppermute | solution.py:469
  29.7 0.7 copy-start.3
  39.0 0.7 copy-start.5
  39.7 6.6 %copy-start.4 = (f32[264,128]{1,0:T(8,128)S(1)}, f32[264,128]{1,0:T(8,128)}, u32[]{:S(2)}) copy-start(f32[264,128]{1,0:T(8,128)} %copy-done.3) | copy-start | bytes 405508
  39.7 6.6 %copy-start.6 = (f32[264,128]{1,0:T(8,128)S(1)}, f32[264,128]{1,0:T(8,128)}, u32[]{:S(2)}) copy-start(f32[264,128]{1,0:T(8,128)} %copy-done.5) | copy-start | bytes 405508
  40.5 7.7 %collective-permute-start.5 = (f32[512,128]{1,0:T(8,128)S(1)}, f32[512,128]{1,0:T(8,128)S(1)}, u32[]{:S(2)}, u32[]{:S(2)}) collective-permute-start(f32[512,128]{1,0:T(8,128)S(1)} %get-tuple-element.70.own), channel_id=1, source_target_pairs={{1,0},{2,1},{3,2},{4,3},{5,4},{6,5},{7,6},{9,8},{10,9},{11,10},{12... | collective-permute-start | bytes 786440 | tf_op jit(solution)/shard_map/ppermute | solution.py:469
  41.8 7.3 %collective-permute-start.4 = (f32[512,128]{1,0:T(8,128)S(1)}, f32[512,128]{1,0:T(8,128)S(1)}, u32[]{:S(2)}, u32[]{:S(2)}) collective-permute-start(f32[512,128]{1,0:T(8,128)S(1)} %get-tuple-element.70.own), channel_id=1, source_target_pairs={{0,1},{1,2},{2,3},{3,4},{4,5},{5,6},{6,7},{8,9},{9,10},{10,11},{11... | collective-permute-start | bytes 786440 | tf_op jit(solution)/shard_map/ppermute | solution.py:469
  49.1 24.5 %copy-start.9 = (f32[8]{0:T(128)S(1)}, f32[8]{0:T(128)}, u32[]{:S(2)}) copy-start(f32[8]{0:T(128)} %base.1) | copy-start | bytes 100
  49.1 24.5 %copy-start.10 = (f32[8]{0:T(128)S(1)}, f32[8]{0:T(128)}, u32[]{:S(2)}) copy-start(f32[8]{0:T(128)} %soft.1) | copy-start | bytes 100
  49.1 24.5 %copy-start.11 = (f32[8]{0:T(128)S(1)}, f32[8]{0:T(128)}, u32[]{:S(2)}) copy-start(f32[8]{0:T(128)} %heat.1) | copy-start | bytes 100
  49.1 5.8 %collective-permute-start.6 = (f32[240,128]{1,0:T(8,128)S(1)}, f32[240,128]{1,0:T(8,128)S(1)}, u32[]{:S(2)}, u32[]{:S(2)}) collective-permute-start(f32[240,128]{1,0:T(8,128)S(1)} %get-tuple-element.77), channel_id=1, source_target_pairs={{32,0},{64,32},{96,64},{128,96},{160,128},{192,160},{224,192},{256... | collective-permute-start | bytes 368648 | tf_op jit(solution)/shard_map/ppermute | solution.py:469
  50.6 5.8 %collective-permute-start.7 = (f32[240,128]{1,0:T(8,128)S(1)}, f32[240,128]{1,0:T(8,128)S(1)}, u32[]{:S(2)}, u32[]{:S(2)}) collective-permute-start(f32[240,128]{1,0:T(8,128)S(1)} %get-tuple-element.78), channel_id=1, source_target_pairs={{0,32},{32,64},{64,96},{96,128},{128,160},{160,192},{192,224},{224... | collective-permute-start | bytes 368648 | tf_op jit(solution)/shard_map/ppermute | solution.py:469
  57.4 16.3 %collective-permute-start.8 = (f32[16,2304]{1,0:T(8,128)S(1)}, f32[16,2304]{1,0:T(8,128)S(1)}, u32[]{:S(2)}, u32[]{:S(2)}) collective-permute-start(f32[16,2304]{1,0:T(8,128)S(1)} %get-tuple-element.86), channel_id=1, source_target_pairs={{0,8},{8,16},{16,24},{1,9},{9,17},{17,25},{2,10},{10,18},{18,26},{... | collective-permute-start | bytes 442376 | tf_op jit(solution)/shard_map/ppermute | solution.py:469
  64.9 8.7 %collective-permute-start.9 = (f32[16,2304]{1,0:T(8,128)S(1)}, f32[16,2304]{1,0:T(8,128)S(1)}, u32[]{:S(2)}, u32[]{:S(2)}) collective-permute-start(f32[16,2304]{1,0:T(8,128)S(1)} %get-tuple-element.87), channel_id=1, source_target_pairs={{8,0},{16,8},{24,16},{9,1},{17,9},{25,17},{10,2},{18,10},{26,18},{... | collective-permute-start | bytes 442376 | tf_op jit(solution)/shard_map/ppermute | solution.py:469
  66.8 20.7 %collective-permute-start.10 = (f32[128,128]{1,0:T(8,128)S(1)}, f32[128,128]{1,0:T(8,128)S(1)}, u32[]{:S(2)}, u32[]{:S(2)}) collective-permute-start(f32[128,128]{1,0:T(8,128)S(1)} %get-tuple-element.100), channel_id=1, source_target_pairs={{0,2},{1,3},{2,4},{3,5},{4,6},{5,7},{8,10},{9,11},{10,12},{11,13},... | collective-permute-start | bytes 196616 | tf_op jit(solution)/shard_map/ppermute | solution.py:469
  72.3 15.2 %collective-permute-start.11 = (f32[128,128]{1,0:T(8,128)S(1)}, f32[128,128]{1,0:T(8,128)S(1)}, u32[]{:S(2)}, u32[]{:S(2)}) collective-permute-start(f32[128,128]{1,0:T(8,128)S(1)} %get-tuple-element.101), channel_id=1, source_target_pairs={{2,0},{3,1},{4,2},{5,3},{6,4},{7,5},{10,8},{11,9},{12,10},{13,11},... | collective-permute-start | bytes 196616 | tf_op jit(solution)/shard_map/ppermute | solution.py:469
  87.6 31.7 %copy-start.1 = (f32[4,128,128]{2,1,0:T(8,128)S(1)}, f32[4,128,128]{2,1,0:T(8,128)}, u32[]{:S(2)}) copy-start(f32[4,128,128]{2,1,0:T(8,128)} %param.13) | copy-start | bytes 786436

commit v8 on v7

--- a/solution.py
+++ b/solution.py
@@ -199,18 +199,14 @@
     xhigh[pl.ds(count * EDGE, count), :] = mats[...]
 
 
-def near_layers(low, own, high):
-    return [(ref, k) for ref in (low, own, high) for k in range(4)]
-
-
-def pack_x_kernel(low, own, high, start_low, start_high, xlow, xhigh):
+def pack_x_kernel(source, start_low, start_high, xlow, xhigh):
     top = start_low.shape[0]
     xlow[pl.ds(0, top), :] = start_low[...]
     xhigh[pl.ds(0, top), :] = start_high[...]
-    for k, (ref, at) in enumerate(near_layers(low, own, high)):
+    for k in range(source.shape[0] // LANES):
         to = pl.ds(top + k * EDGE, EDGE)
-        xlow[to, :] = ref[pl.ds(at * LANES, EDGE), :]
-        xhigh[to, :] = ref[pl.ds((at + 1) * LANES - EDGE, EDGE), :]
+        xlow[to, :] = source[pl.ds(k * LANES, EDGE), :]
+        xhigh[to, :] = source[pl.ds((k + 1) * LANES - EDGE, EDGE), :]
 
 
 def flat_sides(rows):
@@ -219,7 +215,7 @@
     return dot(edges, high, 1, 1) + dot(edges, low, 1, 1)
 
 
-def pack_y_kernel(xz, mats, low, own, high, after, before, xm, full, sides, heat_sides, flat_mat, ylow, yhigh):
+def pack_y_kernel(xz, mats, own, after, before, xm, full, sides, heat_sides, flat_mat, ylow, yhigh):
     count = xz.shape[0]
     blank = jnp.zeros((EDGE, LANES), F32)
     for k in range(count):
@@ -229,17 +225,14 @@
         xm[k, pl.ds(2 * EDGE, LANES)] = xz[k]
         xm[k, pl.ds(LANES + 2 * EDGE, EDGE)] = after[part, :]
         xm[k, pl.ds(LANES + 3 * EDGE, EDGE)] = blank
-    found = near_layers(low, own, high)
-    skip = (count - len(found)) // 2
     top = count * (EDGE + 1)
-    for k in range(skip):
-        full[k] = jnp.zeros(full.shape[1:], F32)
-        full[count - 1 - k] = jnp.zeros(full.shape[1:], F32)
-    for k, (ref, at) in enumerate(found):
+    size = LANES + 2 * EDGE
+    layers = own.shape[0] // LANES
+    for k in range(layers):
         part = pl.ds(top + k * EDGE, EDGE)
-        full[skip + k, pl.ds(0, EDGE)] = before[part, :]
-        full[skip + k, pl.ds(EDGE, LANES)] = ref[pl.ds(at * LANES, LANES), :]
-        full[skip + k, pl.ds(EDGE + LANES, EDGE)] = after[part, :]
+        full[pl.ds(k * size, EDGE), :] = before[part, :]
+        full[pl.ds(k * size + EDGE, LANES), :] = own[pl.ds(k * LANES, LANES), :]
+        full[pl.ds(k * size + EDGE + LANES, EDGE), :] = after[part, :]
     rows = LANES + 2 * EDGE
     total = count * rows
     found = flat_sides(xm[:, EDGE : EDGE + rows].reshape(total, LANES))
@@ -256,20 +249,18 @@
     mine = iota((3 * count, total), 0) == tile * count + layer
     mat = jnp.sum(jnp.where(mine, named, 0.0), axis=0, keepdims=True)
     flat_mat[...] = jnp.broadcast_to(mat, (EDGE, total))
-    heat_found = flat_sides(full[...].reshape(total, LANES))
+    heat_found = flat_sides(full[...])
+    inner = pl.ds(0, layers * rows)
+    beyond = jnp.zeros((EDGE, total), F32)
     heat_sides[...] = heat_found
     ylow[pl.ds(0, EDGE), :] = found[:EDGE]
     yhigh[pl.ds(0, EDGE), :] = found[EDGE:]
-    ylow[pl.ds(EDGE, EDGE), :] = heat_found[:EDGE]
-    yhigh[pl.ds(EDGE, EDGE), :] = heat_found[EDGE:]
+    ylow[pl.ds(EDGE, EDGE), :] = beyond
+    yhigh[pl.ds(EDGE, EDGE), :] = beyond
+    ylow[pl.ds(EDGE, EDGE), inner] = heat_found[:EDGE]
+    yhigh[pl.ds(EDGE, EDGE), inner] = heat_found[EDGE:]
     ylow[pl.ds(2 * EDGE - 1, 1), :] = mat
     yhigh[pl.ds(EDGE, 1), :] = mat
-
-
-def inverse(v):
-    guess = pl.reciprocal(v, approx=True)
-    guess = guess * (2.0 - v * guess)
-    return guess * (2.0 - v * guess)
 
 
 def three_parts(v):
@@ -298,7 +289,17 @@
     return jnp.concatenate([before, sides, after], axis=0)
 
 
-def weights_kernel(base, soft, heat, xm, sides, flat_mat, before, after, wz, wx, wxl, wy, wyw, inv, b0, strips, cond, cols, ends):
+def pack_z_kernel(full, sides, before, after, out):
+    n = full.shape[0]
+    out[pl.ds(0, n), :] = full[...]
+    strip = strip_of(sides[...], before[pl.ds(EDGE, EDGE), 0:n], after[pl.ds(EDGE, EDGE), 0:n])
+    blocks = -(-n // LANES)
+    strip = jnp.concatenate([strip, jnp.zeros((4 * EDGE, blocks * LANES - n), F32)], axis=1)
+    for i in range(blocks):
+        out[pl.ds(n + 4 * EDGE * i, 4 * EDGE), :] = strip[:, i * LANES : (i + 1) * LANES]
+
+
+def weights_kernel(base, soft, heat, xm, sides, flat_mat, before, after, wz, wx, wy, wyw, inv, b0, strips, cond, cols, ends):
     count, rows = inv.shape[0], inv.shape[1]
     total = count * rows
     mat = jnp.concatenate(
@@ -316,13 +317,13 @@
     wide = lambda t, i: jnp.broadcast_to(t[i : i + 1], (EDGE, total))
     kb, ks, cf = (jnp.concatenate([wide(t, 1), wide(t, 0), wide(t, 0), wide(t, 2)], axis=0) for t in tables)
     sx = strip_of(sides[...], before[:EDGE], after[:EDGE])
-    sc = kb * inverse(1.0 + ks * sx)
+    sc = kb / (1.0 + ks * sx)
     down = lambda by, axis: 0.5 * (sc + turned(sc, by, axis))
     around = [down(rows, 1), down(-rows, 1), down(1, 1), down(-1, 1), down(1, 0), down(-1, 0)]
     diag = cf
     for w in around:
         diag = diag + w
-    si = jnp.where(cf > 0.0, inverse(diag), 0.0)
+    si = jnp.where(cf > 0.0, 1.0 / diag, 0.0)
     for i, w in enumerate(around):
         strips[i] = w * si
     strips[6] = si
@@ -338,10 +339,12 @@
     def _(k):
         cond[k, pl.ds(0, EDGE)] = blank
         cond[k, pl.ds(rows + EDGE, EDGE)] = blank
+        wx[k, pl.ds(0, EDGE)] = blank
+        wx[k, pl.ds(rows + EDGE, EDGE)] = blank
         for at in range(0, rows, piece):
             part = pl.ds(pl.multiple_of(k * rows + at, 8), piece)
             x = xm[k, pl.ds(EDGE + at, piece)]
-            cond[k, pl.ds(EDGE + at, piece)] = cols[part, 0:LANES] * inverse(1.0 + cols[part, LANES : 2 * LANES] * x)
+            cond[k, pl.ds(EDGE + at, piece)] = cols[part, 0:LANES] / (1.0 + cols[part, LANES : 2 * LANES] * x)
 
     first, last = iota((piece, LANES), 1) == 0, iota((piece, LANES), 1) == LANES - 1
     wz[0] = 0.5 * (cond[0, pl.ds(EDGE, rows)] + cond[1, pl.ds(EDGE, rows)])
@@ -361,23 +364,37 @@
             w = 0.5 * (c + jnp.where(first, end, turned(c, 1, 1)))
             cf = cols[part, 2 * LANES : 3 * LANES]
             diag = cf + up + low + right + left + e + w
-            i = jnp.where(cf > 0.0, inverse(diag), 0.0)
+            i = jnp.where(cf > 0.0, 1.0 / diag, 0.0)
             wz[k, to] = up
-            wx[k, to] = right
-            wxl[k, to] = left
+            wx[k, here] = right
             wy[k, to] = e
             wyw[k, to] = w
             inv[k, to] = i
             b0[k, to] = cf * xm[k, here] * i
 
 
-def sweep_kernel(xm, wz, wx, wxl, wy, wyw, inv, b0, strips, full, sides, before, after,
-                 out, pull, b, d, xa, xb, ends):
+def sweep_kernel(xm, wz, wx, wy, wyw, inv, b0, strips, low, own, high,
+                 out, pull, full, b, d, xa, xb, ends):
     count, rows, _ = inv.shape
     total = count * rows
     factors = steps()
 
-    sb = strips[7] + strip_of(sides[...], before[EDGE:], after[EDGE:]) * strips[6]
+    layers = out.shape[0] // LANES
+    n = layers * rows
+    skip = (count - 3 * layers) // 2
+    sb = jnp.zeros((4 * EDGE, total), F32)
+    blocks = -(-n // LANES)
+    blank = jnp.zeros((4 * EDGE, total - blocks * LANES), F32)
+    for i, ref in enumerate((low, own, high)):
+        start = skip + i * layers
+        for k in range(layers):
+            full[start + k] = ref[pl.ds(k * rows, rows), :]
+        cells = [ref[pl.ds(n + 4 * EDGE * j, 4 * EDGE), :] for j in range(blocks)]
+        sb = sb + turned(jnp.concatenate(cells + [blank], axis=1), start * rows, 1)
+    for k in range(skip):
+        full[k] = jnp.zeros((rows, LANES), F32)
+        full[count - 1 - k] = jnp.zeros((rows, LANES), F32)
+    sb = strips[7] + sb * strips[6]
     sx, sd = strips[8], None
     kept = [ends_of(sx)]
     for keep, add in factors[:-1]:
@@ -418,8 +435,8 @@
                 e = jnp.where(last, end, turned(x, -1, 1))
                 w = jnp.where(first, end, turned(x, 1, 1))
                 near = wz[k, to] * src[k + 1, here] + wz[k - 1, to] * src[k - 1, here]
-                near += wx[k, to] * src[k, pl.ds(EDGE + at + 1, piece)]
-                near += wxl[k, to] * src[k, pl.ds(EDGE + at - 1, piece)]
+                near += wx[k, here] * src[k, pl.ds(EDGE + at + 1, piece)]
+                near += wx[k, pl.ds(EDGE + at - 1, piece)] * src[k, pl.ds(EDGE + at - 1, piece)]
                 near += wy[k, to] * e + wyw[k, to] * w
                 if s == 0:
                     rhs = b0[k, to] + full[k, to] * inv[k, to]
@@ -506,39 +523,45 @@
     low, high = shifted(near, "gz", 1), shifted(near, "gz", -1)
     low2, high2 = shifted(up, "gz", 2), shifted(down, "gz", -2)
     gain, dest = call(functools.partial(after_kernel, slots), [sized(n, width), ((n, peers * slots), BF16)], [ef, own], "gain")
-    received, low, high, low2, high2, gain, dest = lax.optimization_barrier(
-        (received, low, high, low2, high2, gain, dest))
     edge = sized(count * (EDGE + 1), width)
     xz, mats, start_low, start_high = call(
         functools.partial(start_x_kernel, far), [sized(count, xcells, width), sized(count, width), edge, edge],
         [low2, low, near, high, high2], "start_x")
+    received, start_low, start_high, gain, dest = lax.optimization_barrier(
+        (received, start_low, start_high, gain, dest))
 
     source, first, last = call(
         functools.partial(combine_kernel, peers, slots), [sized(n, width)] + [sized(xcells, width)] * 2,
         [received], "combine", flops=10**8)
     [ids] = call(functools.partial(ids_kernel, peers, slots), [((peers * slots, n), BF16)], [received], "ids")
-    low, high = shifted(source, "gz", 1), shifted(source, "gz", -1)
-    low, high, start_low, start_high, ids = lax.optimization_barrier((low, high, start_low, start_high, ids))
-    edge = sized(count * (EDGE + 1) + 3 * layers * EDGE, width)
-    xlow, xhigh = call(pack_x_kernel, [edge, edge], [low, source, high, start_low, start_high], "pack_x")
+    edge = sized(count * (EDGE + 1) + layers * EDGE, width)
+    xlow, xhigh = call(pack_x_kernel, [edge, edge], [source, start_low, start_high], "pack_x")
     before, after = shifted(xhigh, "gx", 1), shifted(xlow, "gx", -1)
+    before, after, ids = lax.optimization_barrier((before, after, ids))
     tall, tile, flat_edge = sized(count, rows + 2 * EDGE, width), sized(count, rows, width), sized(2 * EDGE, total)
+    inner = layers * rows
     xm, full, sides, heat_sides, flat_mat, ylow, yhigh = call(
-        pack_y_kernel, [tall, tile, flat_edge, flat_edge, sized(EDGE, total), flat_edge, flat_edge],
-        [xz, mats, low, source, high, after, before], "pack_y")
-    ylow, yhigh, first, last = lax.optimization_barrier((ylow, yhigh, first, last))
+        pack_y_kernel,
+        [tall, sized(inner, width), flat_edge, sized(2 * EDGE, inner), sized(EDGE, total), flat_edge, flat_edge],
+        [xz, mats, source, after, before], "pack_y")
     before, after = shifted(yhigh, "gy", 1), shifted(ylow, "gy", -1)
+    blocks = -(-inner // LANES)
+    [around] = call(
+        pack_z_kernel, [sized(inner + 4 * EDGE * blocks, width)], [full, heat_sides, before, after], "pack_z")
+    around, first, last = lax.optimization_barrier((around, first, last))
+    low, high = shifted(around, "gz", 1), shifted(around, "gz", -1)
     low2, high2 = shifted(last, "gz", 2), shifted(first, "gz", -2)
     weights = call(
-        weights_kernel, [tile] * 7 + [sized(9, 4 * EDGE, total)],
+        weights_kernel, [tile, tall, tile, tile, tile, tile, sized(9, 4 * EDGE, total)],
         [mat_conductivity, mat_softening, mat_capacity, xm, sides, flat_mat, before, after], "weights",
         scratch=[pltpu.VMEM((count, rows + 2 * EDGE, width), F32), pltpu.VMEM((total, 3 * width), F32),
                  pltpu.VMEM((total, width), F32)],
         limit=32, flops=10**9, smem=(0, 1, 2))
+    low, high, weights = lax.optimization_barrier((low, high, weights))
     x, pull = call(
         sweep_kernel, [sized(n, width), sized(2 * xcells, width)],
-        [xm] + list(weights) + [full, heat_sides, before, after], "sweeps",
-        scratch=[pltpu.VMEM((count, rows, width), F32)] * 2 + [pltpu.VMEM((count, rows + 2 * EDGE, width), F32)] * 2
+        [xm] + list(weights) + [low, around, high], "sweeps",
+        scratch=[pltpu.VMEM((count, rows, width), F32)] * 3 + [pltpu.VMEM((count, rows + 2 * EDGE, width), F32)] * 2
         + [pltpu.VMEM((total, SWEEPS * width), F32)],
         limit=36, flops=10**8)
     x, pull, low2, high2 = lax.optimization_barrier((x, pull, low2, high2))

time: 123 us -> 119 us (0.967); the launches traced: 121 us -> 118 us
  waiting for transfers between devices: 13.2 us -> 19 us
  starting transfers between devices: 51.6 us -> 48.4 us
  blocking collectives: 30.9 us -> 27.7 us
    ppermute x12, waiting for transfers between devices: 13.2 us -> 19 us  [shifted(): return lax.ppermute(v, axis, pairs) if pairs else jnp.zeros_like(v)]
    ppermute x12, starting transfers between devices: 40 us -> 36.7 us  [shifted(): return lax.ppermute(v, axis, pairs) if pairs else jnp.zeros_like(v)]
    all_to_all x1, blocking collectives: 30.9 us -> 27.7 us  [exchanged(): lax.all_to_all(lines, ('gx', 'gy'), split_axis=0, concat_axis=0, tiled=True)]
    pallas_call x12 -> x13, Pallas kernels: 22.5 us -> 21.6 us  [call(): pl.pallas_call(kernel, out_shape=[jax.ShapeDtypeStruct(s, t) for s, t in...]
  transfers between devices with their start and end apart: 13 -> 13, of which waited for: 5 -> 4; matrix products, arithmetic and copies ran while one was open for 0% -> 0% of each run, Pallas kernels for 13% -> 13%
where the time goes in v8:
time: 119 us; the launch traced here: 118 us
  starting transfers between devices  48.4 us (41%)
  blocking collectives  27.7 us (23%)
  Pallas kernels  21.6 us (18%)
  waiting for transfers between devices  19 us (16%)
    ppermute x12, starting transfers between devices, shifted(): return lax.ppermute(v, axis, pairs) if pairs else jnp.zeros_like(v)  36.7 us
    all_to_all x1, blocking collectives, exchanged(): lax.all_to_all(lines, ('gx', 'gy'), split_axis=0, concat_axis=0, tiled=True)  27.7 us
    pallas_call x13, Pallas kernels, call(): pl.pallas_call(kernel, out_shape=[jax.ShapeDtypeStruct(s, t) for s, t in...  21.6 us
    ppermute x12, waiting for transfers between devices, shifted(): return lax.ppermute(v, axis, pairs) if pairs else jnp.zeros_like(v)  19 us
    all_to_all x1, starting transfers between devices, exchanged(): lax.all_to_all(lines, ('gx', 'gy'), split_axis=0, concat_axis=0, tiled=True)  11.6 us
  transfers between devices with their start and end apart: 13, of which 4 were waited for; matrix products, arithmetic and copies ran while one was open for 0% of the time, Pallas kernels for 13%

profile of v8, /device:TPU:1, one launch (start us, length us, event | category | flops | bytes accessed | tf_op | source)
XLA Modules:
  0.0 118.4 jit_solution(5210425387079626111)
XLA Ops:
  0.6 0.0 copy-start.2
  0.6 0.0 copy-start.6
  0.7 0.0 copy-start
  0.7 0.0 copy-start.5
  0.7 3.0 %dispatch.1 = f32[1088,128]{1,0:T(8,128)} custom-call(f32[3,512,128]{2,1,0:T(8,128)} %bitcast.21, f32[512,128]{1,0:T(8,128)} %bitcast.32, f32[512,128]{1,0:T(8,128)} %bitcast.24, s32[1,512]{1,0:T(1,128)} %bitcast.28, s32[1,512]{1,0:T(1,128)} %bitcast.33, s32[1,512]{1,0:T(1,128)} %bitcast.34), custom_call_target="tpu_custom_call" | custom-call | flops 100000000 | bytes 1873920 | tf_op jit(solution)/shard_map/dispatch/pallas_call | solution.py:71
  3.7 11.6 %all-to-all-start = ((f32[1088,1,128]{2,1,0:T(1,128)}), f32[1088,1,128]{2,1,0:T(1,128)S(1)}, u32[]{:S(2)}, u32[]{:S(2)}) async-start(f32[1088,1,128]{2,1,0:T(1,128)} %bitcast.31), calls=%async_computation | async-start | bytes 1114112 | tf_op jit(solution)/shard_map/all_to_all | solution.py:491
  15.4 0.0 copy-done.2
  15.4 0.0 copy-done.6
  15.4 4.0 %collective-permute-start.1 = (f32[520,128]{1,0:T(8,128)S(1)}, f32[520,128]{1,0:T(8,128)S(1)}, u32[]{:S(2)}, u32[]{:S(2)}) collective-permute-start(f32[520,128]{1,0:T(8,128)S(1)} %get-tuple-element.62.own), channel_id=1, source_target_pairs={{0,1},{1,2},{2,3},{3,4},{4,5},{5,6},{6,7},{8,9},{9,10},{10,11},{11... | collective-permute-start | bytes 798728 | tf_op jit(solution)/shard_map/ppermute | solution.py:486
  19.4 1.3 %collective-permute-start.2 = (f32[520,128]{1,0:T(8,128)S(1)}, f32[520,128]{1,0:T(8,128)S(1)}, u32[]{:S(2)}, u32[]{:S(2)}) collective-permute-start(f32[520,128]{1,0:T(8,128)S(1)} %get-tuple-element.62.own), channel_id=1, source_target_pairs={{1,0},{2,1},{3,2},{4,3},{5,4},{6,5},{7,6},{9,8},{10,9},{11,10},{12... | collective-permute-start | bytes 798728 | tf_op jit(solution)/shard_map/ppermute | solution.py:486
  20.7 6.4 %collective-permute-start = (f32[264,128]{1,0:T(8,128)S(1)}, f32[264,128]{1,0:T(8,128)S(1)}, u32[]{:S(2)}, u32[]{:S(2)}) collective-permute-start(f32[264,128]{1,0:T(8,128)S(1)} %get-tuple-element.61), channel_id=1, source_target_pairs={{0,2},{1,3},{2,4},{3,5},{4,6},{5,7},{8,10},{9,11},{10,12},{11,13},... | collective-permute-start | bytes 405512 | tf_op jit(solution)/shard_map/ppermute | solution.py:486
  27.2 1.3 %collective-permute-start.3 = (f32[264,128]{1,0:T(8,128)S(1)}, f32[264,128]{1,0:T(8,128)S(1)}, u32[]{:S(2)}, u32[]{:S(2)}) collective-permute-start(f32[264,128]{1,0:T(8,128)S(1)} %get-tuple-element.63), channel_id=1, source_target_pairs={{2,0},{3,1},{4,2},{5,3},{6,4},{7,5},{10,8},{11,9},{12,10},{13,11},... | collective-permute-start | bytes 405512 | tf_op jit(solution)/shard_map/ppermute | solution.py:486
  28.5 1.1 gain.1
  29.6 0.0 copy-start.3
  29.6 0.7 copy-done.3
  30.3 0.0 collective-permute-done.low2
  30.3 11.1 %collective-permute-done.3.high2 = f32[264,128]{1,0:T(8,128)S(1)} collective-permute-done((f32[264,128]{1,0:T(8,128)S(1)}, f32[264,128]{1,0:T(8,128)S(1)}, u32[]{:S(2)}, u32[]{:S(2)}) %collective-permute-start.3) | collective-permute-done | bytes 135200 | tf_op jit(solution)/shard_map/ppermute | solution.py:486
  41.4 0.0 collective-permute-done.1.low
  41.4 0.0 collective-permute-done.2.high
  41.4 0.1 start_x.1
  41.5 0.0 all-to-all-done
  41.5 0.7 combine.1
  42.3 3.3 %collective-permute-start.4 = (f32[176,128]{1,0:T(8,128)S(1)}, f32[176,128]{1,0:T(8,128)S(1)}, u32[]{:S(2)}, u32[]{:S(2)}) collective-permute-start(f32[176,128]{1,0:T(8,128)S(1)} %get-tuple-element.74), channel_id=1, source_target_pairs={{0,32},{32,64},{64,96},{96,128},{128,160},{160,192},{192,224},{224... | collective-permute-start | bytes 270344 | tf_op jit(solution)/shard_map/ppermute | solution.py:486
  45.6 1.3 %collective-permute-start.5 = (f32[176,128]{1,0:T(8,128)S(1)}, f32[176,128]{1,0:T(8,128)S(1)}, u32[]{:S(2)}, u32[]{:S(2)}) collective-permute-start(f32[176,128]{1,0:T(8,128)S(1)} %get-tuple-element.75), channel_id=1, source_target_pairs={{32,0},{64,32},{96,64},{128,96},{160,128},{192,160},{224,192},{256... | collective-permute-start | bytes 270344 | tf_op jit(solution)/shard_map/ppermute | solution.py:486
  46.9 0.5 ids.1.hot
  47.4 0.0 collective-permute-done.4.before
  47.4 3.4 %collective-permute-done.5.after = f32[176,128]{1,0:T(8,128)S(1)} collective-permute-done((f32[176,128]{1,0:T(8,128)S(1)}, f32[176,128]{1,0:T(8,128)S(1)}, u32[]{:S(2)}, u32[]{:S(2)}) %collective-permute-start.5) | collective-permute-done | bytes 90144 | tf_op jit(solution)/shard_map/ppermute | solution.py:486
  50.9 0.7 pack_y.1
  51.6 4.9 %collective-permute-start.6 = (f32[16,2304]{1,0:T(8,128)S(1)}, f32[16,2304]{1,0:T(8,128)S(1)}, u32[]{:S(2)}, u32[]{:S(2)}) collective-permute-start(f32[16,2304]{1,0:T(8,128)S(1)} %get-tuple-element.81), channel_id=1, source_target_pairs={{0,8},{8,16},{16,24},{1,9},{9,17},{17,25},{2,10},{10,18},{18,26},{... | collective-permute-start | bytes 442376 | tf_op jit(solution)/shard_map/ppermute | solution.py:486
  56.5 1.9 %collective-permute-start.7 = (f32[16,2304]{1,0:T(8,128)S(1)}, f32[16,2304]{1,0:T(8,128)S(1)}, u32[]{:S(2)}, u32[]{:S(2)}) collective-permute-start(f32[16,2304]{1,0:T(8,128)S(1)} %get-tuple-element.82), channel_id=1, source_target_pairs={{8,0},{16,8},{24,16},{9,1},{17,9},{25,17},{10,2},{18,10},{26,18},{... | collective-permute-start | bytes 442376 | tf_op jit(solution)/shard_map/ppermute | solution.py:486
  58.4 0.2 collective-permute-done.6.before
  58.6 4.4 %collective-permute-done.7.after = f32[16,2304]{1,0:T(8,128)S(1)} collective-permute-done((f32[16,2304]{1,0:T(8,128)S(1)}, f32[16,2304]{1,0:T(8,128)S(1)}, u32[]{:S(2)}, u32[]{:S(2)}) %collective-permute-start.7) | collective-permute-done | bytes 147488 | tf_op jit(solution)/shard_map/ppermute | solution.py:486
  63.0 1.3 %collective-permute-start.8 = (f32[736,128]{1,0:T(8,128)S(1)}, f32[736,128]{1,0:T(8,128)S(1)}, u32[]{:S(2)}, u32[]{:S(2)}) collective-permute-start(f32[736,128]{1,0:T(8,128)S(1)} %pack_z.1.own), channel_id=1, source_target_pairs={{0,1},{1,2},{2,3},{3,4},{4,5},{5,6},{6,7},{8,9},{9,10},{10,11},{11... | collective-permute-start | bytes 1130504 | tf_op jit(solution)/shard_map/ppermute | solution.py:486
  64.3 1.3 %collective-permute-start.9 = (f32[736,128]{1,0:T(8,128)S(1)}, f32[736,128]{1,0:T(8,128)S(1)}, u32[]{:S(2)}, u32[]{:S(2)}) collective-permute-start(f32[736,128]{1,0:T(8,128)S(1)} %pack_z.1.own), channel_id=1, source_target_pairs={{1,0},{2,1},{3,2},{4,3},{5,4},{6,5},{7,6},{9,8},{10,9},{11,10},{12... | collective-permute-start | bytes 1130504 | tf_op jit(solution)/shard_map/ppermute | solution.py:486
  65.6 8.4 %collective-permute-start.10 = (f32[128,128]{1,0:T(8,128)S(1)}, f32[128,128]{1,0:T(8,128)S(1)}, u32[]{:S(2)}, u32[]{:S(2)}) collective-permute-start(f32[128,128]{1,0:T(8,128)S(1)} %get-tuple-element.106), channel_id=1, source_target_pairs={{0,2},{1,3},{2,4},{3,5},{4,6},{5,7},{8,10},{9,11},{10,12},{11,13},... | collective-permute-start | bytes 196616 | tf_op jit(solution)/shard_map/ppermute | solution.py:486
  74.0 1.3 %collective-permute-start.11 = (f32[128,128]{1,0:T(8,128)S(1)}, f32[128,128]{1,0:T(8,128)S(1)}, u32[]{:S(2)}, u32[]{:S(2)}) collective-permute-start(f32[128,128]{1,0:T(8,128)S(1)} %get-tuple-element.107), channel_id=1, source_target_pairs={{2,0},{3,1},{4,2},{5,3},{6,4},{7,5},{10,8},{11,9},{12,10},{13,11},... | collective-permute-start | bytes 196616 | tf_op jit(solution)/shard_map/ppermute | solution.py:486
  75.4 4.0 %weights.1 = (f32[16,144,128]{2,1,0:T(8,128)S(1)}, f32[16,160,128]{2,1,0:T(8,128)S(1)}, f32[16,144,128]{2,1,0:T(8,128)S(1)}, f32[16,144,128]{2,1,0:T(8,128)S(1)}...) custom-call(f32[8]{0:T(128)S(1)} %copy-done.7, f32[8]{0:T(128)S(1)} %copy-done.8, ...), custom_call_target="tpu_custom_call" | custom-call | flops 1000000000 | bytes 11690080 | tf_op jit(solution)/shard_map/weights/pallas_call | solution.py:71
  79.4 0.0 collective-permute-done.8.low
  79.4 0.0 collective-permute-done.9.high
  79.4 9.2 %sweeps.1 = (f32[512,128]{1,0:T(8,128)S(1)}, f32[256,128]{1,0:T(8,128)S(1)}) custom-call(f32[16,160,128]{2,1,0:T(8,128)S(1)} %get-tuple-element.78.xm, f32[16,144,128]{2,1,0:T(8,128)S(1)} %get-tuple-element.95.wz, f32[16,160,128]{2,1,0:T(8,128)S(1)} %get-tuple-element.96.wx, f32[16,144,128]{2,1,0:T(8,128)S(1)} %get-tuple-element.97.wy, ...), custom_call_target="tpu_custom_call" | custom-call | flops 100000000 | bytes 12697600 | tf_op jit(solution)/shard_map/sweeps/pallas_call | solution.py:71
  88.5 0.0 collective-permute-done.10.low2
  88.6 0.0 collective-permute-done.11.high2
  88.6 0.0 copy-start.1
  88.6 0.0 copy-start.4
  88.6 0.8 reply.1
  89.4 27.7 %all_to_all.10 = f32[1024,1,128]{2,1,0:T(1,128)S(1)} all-to-all(f32[1024,1,128]{2,1,0:T(1,128)S(1)} %bitcast.26), channel_id=1, replica_groups=mesh['gx'=16,'gy'=4,'gz'=8] {'gx','gy'}, dimensions={0} | all-to-all | bytes 1048576 | tf_op jit(solution)/shard_map/all_to_all | solution.py:491
  117.1 0.0 copy-done.4
  117.1 1.2 %finish.1 = (f32[512,128]{1,0:T(8,128)}, f32[512,128]{1,0:T(8,128)}) custom-call(f32[1024,128]{1,0:T(8,128)S(1)} %bitcast.23, bf16[512,1024]{1,0:T(8,128)(2,1)S(1)} %get-tuple-element.115.hot, f32[512,128]{1,0:T(8,128)S(1)} %copy-done.4, f32[512,128]{1,0:T(8,128)S(1)} %bitcast.25), custom_call_target="tpu_custom_call" | custom-call | flops 100000000 | bytes 2621440 | tf_op jit(solution)/shard_map/finish/pallas_call | solution.py:71
  (12 shorter events, 0.1 us)
Async XLA Ops:
  0.6 14.7 %copy-start.2 = (f32[4,128,128]{2,1,0:T(8,128)S(1)}, f32[4,128,128]{2,1,0:T(8,128)}, u32[]{:S(2)}) copy-start(f32[4,128,128]{2,1,0:T(8,128)} %param.14) | copy-start | bytes 786436
  0.6 14.7 %copy-start.6 = (s32[1,1,1,512]{3,2,1,0:T(1,128)S(1)}, s32[1,1,1,512]{3,2,1,0:T(1,128)}, u32[]{:S(2)}) copy-start(s32[1,1,1,512]{3,2,1,0:T(1,128)} %param.18) | copy-start | bytes 6148
  0.7 27.8 %copy-start = (f32[3,4,128,128]{3,2,1,0:T(8,128)S(1)}, f32[3,4,128,128]{3,2,1,0:T(8,128)}, u32[]{:S(2)}) copy-start(f32[3,4,128,128]{3,2,1,0:T(8,128)} %param.11) | copy-start | bytes 2359300
  0.7 27.8 %copy-start.5 = (s32[1,1,1,512,1]{3,4,2,1,0:T(1,128)S(1)}, s32[1,1,1,512,1]{3,4,2,1,0:T(1,128)}, u32[]{:S(2)}) copy-start(s32[1,1,1,512,1]{3,4,2,1,0:T(1,128)} %param.15) | copy-start | bytes 6148
  3.7 37.8 %all-to-all-start = ((f32[1088,1,128]{2,1,0:T(1,128)}), f32[1088,1,128]{2,1,0:T(1,128)S(1)}, u32[]{:S(2)}, u32[]{:S(2)}) async-start(f32[1088,1,128]{2,1,0:T(1,128)} %bitcast.31), calls=%async_computation | async-start | bytes 1114112 | tf_op jit(solution)/shard_map/all_to_all | solution.py:491
  15.4 26.0 %collective-permute-start.1 = (f32[520,128]{1,0:T(8,128)S(1)}, f32[520,128]{1,0:T(8,128)S(1)}, u32[]{:S(2)}, u32[]{:S(2)}) collective-permute-start(f32[520,128]{1,0:T(8,128)S(1)} %get-tuple-element.62.own), channel_id=1, source_target_pairs={{0,1},{1,2},{2,3},{3,4},{4,5},{5,6},{6,7},{8,9},{9,10},{10,11},{11... | collective-permute-start | bytes 798728 | tf_op jit(solution)/shard_map/ppermute | solution.py:486
  19.4 22.0 %collective-permute-start.2 = (f32[520,128]{1,0:T(8,128)S(1)}, f32[520,128]{1,0:T(8,128)S(1)}, u32[]{:S(2)}, u32[]{:S(2)}) collective-permute-start(f32[520,128]{1,0:T(8,128)S(1)} %get-tuple-element.62.own), channel_id=1, source_target_pairs={{1,0},{2,1},{3,2},{4,3},{5,4},{6,5},{7,6},{9,8},{10,9},{11,10},{12... | collective-permute-start | bytes 798728 | tf_op jit(solution)/shard_map/ppermute | solution.py:486
  20.7 9.6 %collective-permute-start = (f32[264,128]{1,0:T(8,128)S(1)}, f32[264,128]{1,0:T(8,128)S(1)}, u32[]{:S(2)}, u32[]{:S(2)}) collective-permute-start(f32[264,128]{1,0:T(8,128)S(1)} %get-tuple-element.61), channel_id=1, source_target_pairs={{0,2},{1,3},{2,4},{3,5},{4,6},{5,7},{8,10},{9,11},{10,12},{11,13},... | collective-permute-start | bytes 405512 | tf_op jit(solution)/shard_map/ppermute | solution.py:486
  27.2 14.2 %collective-permute-start.3 = (f32[264,128]{1,0:T(8,128)S(1)}, f32[264,128]{1,0:T(8,128)S(1)}, u32[]{:S(2)}, u32[]{:S(2)}) collective-permute-start(f32[264,128]{1,0:T(8,128)S(1)} %get-tuple-element.63), channel_id=1, source_target_pairs={{2,0},{3,1},{4,2},{5,3},{6,4},{7,5},{10,8},{11,9},{12,10},{13,11},... | collective-permute-start | bytes 405512 | tf_op jit(solution)/shard_map/ppermute | solution.py:486
  29.6 0.7 copy-start.3
  42.3 5.2 %collective-permute-start.4 = (f32[176,128]{1,0:T(8,128)S(1)}, f32[176,128]{1,0:T(8,128)S(1)}, u32[]{:S(2)}, u32[]{:S(2)}) collective-permute-start(f32[176,128]{1,0:T(8,128)S(1)} %get-tuple-element.74), channel_id=1, source_target_pairs={{0,32},{32,64},{64,96},{96,128},{128,160},{160,192},{192,224},{224... | collective-permute-start | bytes 270344 | tf_op jit(solution)/shard_map/ppermute | solution.py:486
  45.6 5.3 %collective-permute-start.5 = (f32[176,128]{1,0:T(8,128)S(1)}, f32[176,128]{1,0:T(8,128)S(1)}, u32[]{:S(2)}, u32[]{:S(2)}) collective-permute-start(f32[176,128]{1,0:T(8,128)S(1)} %get-tuple-element.75), channel_id=1, source_target_pairs={{32,0},{64,32},{96,64},{128,96},{160,128},{192,160},{224,192},{256... | collective-permute-start | bytes 270344 | tf_op jit(solution)/shard_map/ppermute | solution.py:486
  50.9 24.5 %copy-start.7 = (f32[8]{0:T(128)S(1)}, f32[8]{0:T(128)}, u32[]{:S(2)}) copy-start(f32[8]{0:T(128)} %base.1) | copy-start | bytes 100
  50.9 24.5 %copy-start.8 = (f32[8]{0:T(128)S(1)}, f32[8]{0:T(128)}, u32[]{:S(2)}) copy-start(f32[8]{0:T(128)} %soft.1) | copy-start | bytes 100
  50.9 24.5 %copy-start.9 = (f32[8]{0:T(128)S(1)}, f32[8]{0:T(128)}, u32[]{:S(2)}) copy-start(f32[8]{0:T(128)} %heat.1) | copy-start | bytes 100
  51.6 7.0 %collective-permute-start.6 = (f32[16,2304]{1,0:T(8,128)S(1)}, f32[16,2304]{1,0:T(8,128)S(1)}, u32[]{:S(2)}, u32[]{:S(2)}) collective-permute-start(f32[16,2304]{1,0:T(8,128)S(1)} %get-tuple-element.81), channel_id=1, source_target_pairs={{0,8},{8,16},{16,24},{1,9},{9,17},{17,25},{2,10},{10,18},{18,26},{... | collective-permute-start | bytes 442376 | tf_op jit(solution)/shard_map/ppermute | solution.py:486
  56.5 6.5 %collective-permute-start.7 = (f32[16,2304]{1,0:T(8,128)S(1)}, f32[16,2304]{1,0:T(8,128)S(1)}, u32[]{:S(2)}, u32[]{:S(2)}) collective-permute-start(f32[16,2304]{1,0:T(8,128)S(1)} %get-tuple-element.82), channel_id=1, source_target_pairs={{8,0},{16,8},{24,16},{9,1},{17,9},{25,17},{10,2},{18,10},{26,18},{... | collective-permute-start | bytes 442376 | tf_op jit(solution)/shard_map/ppermute | solution.py:486
  63.0 16.4 %collective-permute-start.8 = (f32[736,128]{1,0:T(8,128)S(1)}, f32[736,128]{1,0:T(8,128)S(1)}, u32[]{:S(2)}, u32[]{:S(2)}) collective-permute-start(f32[736,128]{1,0:T(8,128)S(1)} %pack_z.1.own), channel_id=1, source_target_pairs={{0,1},{1,2},{2,3},{3,4},{4,5},{5,6},{6,7},{8,9},{9,10},{10,11},{11... | collective-permute-start | bytes 1130504 | tf_op jit(solution)/shard_map/ppermute | solution.py:486
  64.3 15.1 %collective-permute-start.9 = (f32[736,128]{1,0:T(8,128)S(1)}, f32[736,128]{1,0:T(8,128)S(1)}, u32[]{:S(2)}, u32[]{:S(2)}) collective-permute-start(f32[736,128]{1,0:T(8,128)S(1)} %pack_z.1.own), channel_id=1, source_target_pairs={{1,0},{2,1},{3,2},{4,3},{5,4},{6,5},{7,6},{9,8},{10,9},{11,10},{12... | collective-permute-start | bytes 1130504 | tf_op jit(solution)/shard_map/ppermute | solution.py:486
  65.6 22.9 %collective-permute-start.10 = (f32[128,128]{1,0:T(8,128)S(1)}, f32[128,128]{1,0:T(8,128)S(1)}, u32[]{:S(2)}, u32[]{:S(2)}) collective-permute-start(f32[128,128]{1,0:T(8,128)S(1)} %get-tuple-element.106), channel_id=1, source_target_pairs={{0,2},{1,3},{2,4},{3,5},{4,6},{5,7},{8,10},{9,11},{10,12},{11,13},... | collective-permute-start | bytes 196616 | tf_op jit(solution)/shard_map/ppermute | solution.py:486
  74.0 14.5 %collective-permute-start.11 = (f32[128,128]{1,0:T(8,128)S(1)}, f32[128,128]{1,0:T(8,128)S(1)}, u32[]{:S(2)}, u32[]{:S(2)}) collective-permute-start(f32[128,128]{1,0:T(8,128)S(1)} %get-tuple-element.107), channel_id=1, source_target_pairs={{2,0},{3,1},{4,2},{5,3},{6,4},{7,5},{10,8},{11,9},{12,10},{13,11},... | collective-permute-start | bytes 196616 | tf_op jit(solution)/shard_map/ppermute | solution.py:486
  88.6 28.6 %copy-start.1 = (f32[4,128,128]{2,1,0:T(8,128)S(1)}, f32[4,128,128]{2,1,0:T(8,128)}, u32[]{:S(2)}) copy-start(f32[4,128,128]{2,1,0:T(8,128)} %param.13) | copy-start | bytes 786436
  88.6 28.6 %copy-start.4 = (f32[512,128]{1,0:T(8,128)S(1)}, f32[512,128]{1,0:T(8,128)}, u32[]{:S(2)}) copy-start(f32[512,128]{1,0:T(8,128)} %copy-done.3) | copy-start | bytes 786436

commit v9 on v8

--- a/solution.py
+++ b/solution.py
@@ -544,13 +544,14 @@
         pack_y_kernel,
         [tall, sized(inner, width), flat_edge, sized(2 * EDGE, inner), sized(EDGE, total), flat_edge, flat_edge],
         [xz, mats, source, after, before], "pack_y")
+    ylow, yhigh, first, last = lax.optimization_barrier((ylow, yhigh, first, last))
     before, after = shifted(yhigh, "gy", 1), shifted(ylow, "gy", -1)
+    low2, high2 = shifted(last, "gz", 2), shifted(first, "gz", -2)
     blocks = -(-inner // LANES)
     [around] = call(
         pack_z_kernel, [sized(inner + 4 * EDGE * blocks, width)], [full, heat_sides, before, after], "pack_z")
-    around, first, last = lax.optimization_barrier((around, first, last))
+    around, low2, high2 = lax.optimization_barrier((around, low2, high2))
     low, high = shifted(around, "gz", 1), shifted(around, "gz", -1)
-    low2, high2 = shifted(last, "gz", 2), shifted(first, "gz", -2)
     weights = call(
         weights_kernel, [tile, tall, tile, tile, tile, tile, sized(9, 4 * EDGE, total)],
         [mat_conductivity, mat_softening, mat_capacity, xm, sides, flat_mat, before, after], "weights",

time: 119 us -> 125 us (1.050)
  waiting for transfers between devices: 19 us -> 27 us
  starting transfers between devices: 48.4 us -> 45.7 us
    ppermute x12, waiting for transfers between devices: 19 us -> 27 us  [shifted(): return lax.ppermute(v, axis, pairs) if pairs else jnp.zeros_like(v)]
    ppermute x12, starting transfers between devices: 36.7 us -> 34.1 us  [shifted(): return lax.ppermute(v, axis, pairs) if pairs else jnp.zeros_like(v)]
  transfers between devices with their start and end apart: 13 -> 13, of which waited for: 4 -> 5; matrix products, arithmetic and copies ran while one was open for 0% -> 0% of each run, Pallas kernels for 13% -> 5%
where the time goes in v9:
time: 125 us; the launch traced here: 124 us
  starting transfers between devices  45.7 us (37%)
  blocking collectives  28 us (22%)
  waiting for transfers between devices  27 us (22%)
  Pallas kernels  21.6 us (17%)
    ppermute x12, starting transfers between devices, shifted(): return lax.ppermute(v, axis, pairs) if pairs else jnp.zeros_like(v)  34.1 us
    all_to_all x1, blocking collectives, exchanged(): lax.all_to_all(lines, ('gx', 'gy'), split_axis=0, concat_axis=0, tiled=True)  28 us
    ppermute x12, waiting for transfers between devices, shifted(): return lax.ppermute(v, axis, pairs) if pairs else jnp.zeros_like(v)  27 us
    pallas_call x13, Pallas kernels, call(): pl.pallas_call(kernel, out_shape=[jax.ShapeDtypeStruct(s, t) for s, t in...  21.6 us
    all_to_all x1, starting transfers between devices, exchanged(): lax.all_to_all(lines, ('gx', 'gy'), split_axis=0, concat_axis=0, tiled=True)  11.6 us
  transfers between devices with their start and end apart: 13, of which 5 were waited for; matrix products, arithmetic and copies ran while one was open for 0% of the time, Pallas kernels for 5%

profile of v9, /device:TPU:1, one launch (start us, length us, event | category | flops | bytes accessed | tf_op | source)
XLA Modules:
  0.0 124.0 jit_solution(2051895048755653840)
XLA Ops:
  0.6 0.0 copy-start.2
  0.6 0.0 copy-start.6
  0.7 0.0 copy-start
  0.7 0.0 copy-start.5
  0.7 3.0 %dispatch.1 = f32[1088,128]{1,0:T(8,128)} custom-call(f32[3,512,128]{2,1,0:T(8,128)} %bitcast.21, f32[512,128]{1,0:T(8,128)} %bitcast.32, f32[512,128]{1,0:T(8,128)} %bitcast.24, s32[1,512]{1,0:T(1,128)} %bitcast.28, s32[1,512]{1,0:T(1,128)} %bitcast.33, s32[1,512]{1,0:T(1,128)} %bitcast.34), custom_call_target="tpu_custom_call" | custom-call | flops 100000000 | bytes 1873920 | tf_op jit(solution)/shard_map/dispatch/pallas_call | solution.py:71
  3.7 11.6 %all-to-all-start = ((f32[1088,1,128]{2,1,0:T(1,128)}), f32[1088,1,128]{2,1,0:T(1,128)S(1)}, u32[]{:S(2)}, u32[]{:S(2)}) async-start(f32[1088,1,128]{2,1,0:T(1,128)} %bitcast.31), calls=%async_computation | async-start | bytes 1114112 | tf_op jit(solution)/shard_map/all_to_all | solution.py:491
  15.4 4.0 %collective-permute-start.1 = (f32[520,128]{1,0:T(8,128)S(1)}, f32[520,128]{1,0:T(8,128)S(1)}, u32[]{:S(2)}, u32[]{:S(2)}) collective-permute-start(f32[520,128]{1,0:T(8,128)S(1)} %get-tuple-element.66.own), channel_id=1, source_target_pairs={{0,1},{1,2},{2,3},{3,4},{4,5},{5,6},{6,7},{8,9},{9,10},{10,11},{11... | collective-permute-start | bytes 798728 | tf_op jit(solution)/shard_map/ppermute | solution.py:486
  19.4 1.3 %collective-permute-start.2 = (f32[520,128]{1,0:T(8,128)S(1)}, f32[520,128]{1,0:T(8,128)S(1)}, u32[]{:S(2)}, u32[]{:S(2)}) collective-permute-start(f32[520,128]{1,0:T(8,128)S(1)} %get-tuple-element.66.own), channel_id=1, source_target_pairs={{1,0},{2,1},{3,2},{4,3},{5,4},{6,5},{7,6},{9,8},{10,9},{11,10},{12... | collective-permute-start | bytes 798728 | tf_op jit(solution)/shard_map/ppermute | solution.py:486
  20.7 6.4 %collective-permute-start = (f32[264,128]{1,0:T(8,128)S(1)}, f32[264,128]{1,0:T(8,128)S(1)}, u32[]{:S(2)}, u32[]{:S(2)}) collective-permute-start(f32[264,128]{1,0:T(8,128)S(1)} %get-tuple-element.65), channel_id=1, source_target_pairs={{0,2},{1,3},{2,4},{3,5},{4,6},{5,7},{8,10},{9,11},{10,12},{11,13},... | collective-permute-start | bytes 405512 | tf_op jit(solution)/shard_map/ppermute | solution.py:486
  27.2 1.3 %collective-permute-start.3 = (f32[264,128]{1,0:T(8,128)S(1)}, f32[264,128]{1,0:T(8,128)S(1)}, u32[]{:S(2)}, u32[]{:S(2)}) collective-permute-start(f32[264,128]{1,0:T(8,128)S(1)} %get-tuple-element.67), channel_id=1, source_target_pairs={{2,0},{3,1},{4,2},{5,3},{6,4},{7,5},{10,8},{11,9},{12,10},{13,11},... | collective-permute-start | bytes 405512 | tf_op jit(solution)/shard_map/ppermute | solution.py:486
  28.5 1.1 gain.1
  29.6 0.0 copy-start.3
  29.6 0.7 copy-done.3
  30.3 0.0 collective-permute-done.low2
  30.3 11.1 %collective-permute-done.3.high2 = f32[264,128]{1,0:T(8,128)S(1)} collective-permute-done((f32[264,128]{1,0:T(8,128)S(1)}, f32[264,128]{1,0:T(8,128)S(1)}, u32[]{:S(2)}, u32[]{:S(2)}) %collective-permute-start.3) | collective-permute-done | bytes 135200 | tf_op jit(solution)/shard_map/ppermute | solution.py:486
  41.4 0.0 collective-permute-done.1.low
  41.4 0.0 collective-permute-done.2.high
  41.4 0.1 start_x.1
  41.5 0.0 all-to-all-done
  41.5 0.7 combine.1
  42.3 3.3 %collective-permute-start.4 = (f32[176,128]{1,0:T(8,128)S(1)}, f32[176,128]{1,0:T(8,128)S(1)}, u32[]{:S(2)}, u32[]{:S(2)}) collective-permute-start(f32[176,128]{1,0:T(8,128)S(1)} %get-tuple-element.78), channel_id=1, source_target_pairs={{0,32},{32,64},{64,96},{96,128},{128,160},{160,192},{192,224},{224... | collective-permute-start | bytes 270344 | tf_op jit(solution)/shard_map/ppermute | solution.py:486
  45.6 1.3 %collective-permute-start.5 = (f32[176,128]{1,0:T(8,128)S(1)}, f32[176,128]{1,0:T(8,128)S(1)}, u32[]{:S(2)}, u32[]{:S(2)}) collective-permute-start(f32[176,128]{1,0:T(8,128)S(1)} %get-tuple-element.79), channel_id=1, source_target_pairs={{32,0},{64,32},{96,64},{128,96},{160,128},{192,160},{224,192},{256... | collective-permute-start | bytes 270344 | tf_op jit(solution)/shard_map/ppermute | solution.py:486
  46.9 0.5 ids.1.hot
  47.4 0.0 collective-permute-done.4.before
  47.4 3.4 %collective-permute-done.5.after = f32[176,128]{1,0:T(8,128)S(1)} collective-permute-done((f32[176,128]{1,0:T(8,128)S(1)}, f32[176,128]{1,0:T(8,128)S(1)}, u32[]{:S(2)}, u32[]{:S(2)}) %collective-permute-start.5) | collective-permute-done | bytes 90144 | tf_op jit(solution)/shard_map/ppermute | solution.py:486
  50.9 0.7 pack_y.1
  51.6 4.9 %collective-permute-start.6 = (f32[16,2304]{1,0:T(8,128)S(1)}, f32[16,2304]{1,0:T(8,128)S(1)}, u32[]{:S(2)}, u32[]{:S(2)}) collective-permute-start(f32[16,2304]{1,0:T(8,128)S(1)} %get-tuple-element.89), channel_id=1, source_target_pairs={{0,8},{8,16},{16,24},{1,9},{9,17},{17,25},{2,10},{10,18},{18,26},{... | collective-permute-start | bytes 442376 | tf_op jit(solution)/shard_map/ppermute | solution.py:486
  56.5 1.9 %collective-permute-start.7 = (f32[16,2304]{1,0:T(8,128)S(1)}, f32[16,2304]{1,0:T(8,128)S(1)}, u32[]{:S(2)}, u32[]{:S(2)}) collective-permute-start(f32[16,2304]{1,0:T(8,128)S(1)} %get-tuple-element.90), channel_id=1, source_target_pairs={{8,0},{16,8},{24,16},{9,1},{17,9},{25,17},{10,2},{18,10},{26,18},{... | collective-permute-start | bytes 442376 | tf_op jit(solution)/shard_map/ppermute | solution.py:486
  58.4 5.7 %collective-permute-start.8 = (f32[128,128]{1,0:T(8,128)S(1)}, f32[128,128]{1,0:T(8,128)S(1)}, u32[]{:S(2)}, u32[]{:S(2)}) collective-permute-start(f32[128,128]{1,0:T(8,128)S(1)} %get-tuple-element.91), channel_id=1, source_target_pairs={{0,2},{1,3},{2,4},{3,5},{4,6},{5,7},{8,10},{9,11},{10,12},{11,13},... | collective-permute-start | bytes 196616 | tf_op jit(solution)/shard_map/ppermute | solution.py:486
  64.2 1.3 %collective-permute-start.9 = (f32[128,128]{1,0:T(8,128)S(1)}, f32[128,128]{1,0:T(8,128)S(1)}, u32[]{:S(2)}, u32[]{:S(2)}) collective-permute-start(f32[128,128]{1,0:T(8,128)S(1)} %get-tuple-element.92), channel_id=1, source_target_pairs={{2,0},{3,1},{4,2},{5,3},{6,4},{7,5},{10,8},{11,9},{12,10},{13,11},... | collective-permute-start | bytes 196616 | tf_op jit(solution)/shard_map/ppermute | solution.py:486
  65.5 0.0 collective-permute-done.6.before
  65.5 0.0 collective-permute-done.7.after
  65.5 0.0 collective-permute-done.8.low2
  65.5 4.5 %collective-permute-done.9.high2 = f32[128,128]{1,0:T(8,128)S(1)} collective-permute-done((f32[128,128]{1,0:T(8,128)S(1)}, f32[128,128]{1,0:T(8,128)S(1)}, u32[]{:S(2)}, u32[]{:S(2)}) %collective-permute-start.9) | collective-permute-done | bytes 65568 | tf_op jit(solution)/shard_map/ppermute | solution.py:486
  70.1 1.3 %collective-permute-start.10 = (f32[736,128]{1,0:T(8,128)S(1)}, f32[736,128]{1,0:T(8,128)S(1)}, u32[]{:S(2)}, u32[]{:S(2)}) collective-permute-start(f32[736,128]{1,0:T(8,128)S(1)} %pack_z.1.own), channel_id=1, source_target_pairs={{0,1},{1,2},{2,3},{3,4},{4,5},{5,6},{6,7},{8,9},{9,10},{10,11},{11... | collective-permute-start | bytes 1130504 | tf_op jit(solution)/shard_map/ppermute | solution.py:486
  71.4 1.3 %collective-permute-start.11 = (f32[736,128]{1,0:T(8,128)S(1)}, f32[736,128]{1,0:T(8,128)S(1)}, u32[]{:S(2)}, u32[]{:S(2)}) collective-permute-start(f32[736,128]{1,0:T(8,128)S(1)} %pack_z.1.own), channel_id=1, source_target_pairs={{1,0},{2,1},{3,2},{4,3},{5,4},{6,5},{7,6},{9,8},{10,9},{11,10},{12... | collective-permute-start | bytes 1130504 | tf_op jit(solution)/shard_map/ppermute | solution.py:486
  72.7 0.0 copy-done.7
  72.7 0.0 copy-done.8
  72.7 0.0 copy-done.9
  72.7 4.0 %weights.1 = (f32[16,144,128]{2,1,0:T(8,128)S(1)}, f32[16,160,128]{2,1,0:T(8,128)S(1)}, f32[16,144,128]{2,1,0:T(8,128)S(1)}, f32[16,144,128]{2,1,0:T(8,128)S(1)}...) custom-call(f32[8]{0:T(128)S(1)} %copy-done.7, f32[8]{0:T(128)S(1)} %copy-done.8, ...), custom_call_target="tpu_custom_call" | custom-call | flops 1000000000 | bytes 11690080 | tf_op jit(solution)/shard_map/weights/pallas_call | solution.py:71
  76.7 2.5 %collective-permute-done.10.low = f32[736,128]{1,0:T(8,128)S(1)} collective-permute-done((f32[736,128]{1,0:T(8,128)S(1)}, f32[736,128]{1,0:T(8,128)S(1)}, u32[]{:S(2)}, u32[]{:S(2)}) %collective-permute-start.10) | collective-permute-done | bytes 376864 | tf_op jit(solution)/shard_map/ppermute | solution.py:486
  79.2 5.5 %collective-permute-done.11.high = f32[736,128]{1,0:T(8,128)S(1)} collective-permute-done((f32[736,128]{1,0:T(8,128)S(1)}, f32[736,128]{1,0:T(8,128)S(1)}, u32[]{:S(2)}, u32[]{:S(2)}) %collective-permute-start.11) | collective-permute-done | bytes 376864 | tf_op jit(solution)/shard_map/ppermute | solution.py:486
  84.7 9.2 %sweeps.1 = (f32[512,128]{1,0:T(8,128)S(1)}, f32[256,128]{1,0:T(8,128)S(1)}) custom-call(f32[16,160,128]{2,1,0:T(8,128)S(1)} %get-tuple-element.82.xm, f32[16,144,128]{2,1,0:T(8,128)S(1)} %get-tuple-element.103.wz, f32[16,160,128]{2,1,0:T(8,128)S(1)} %get-tuple-element.104.wx, f32[16,144,128]{2,1,0:T(8,128)S(1)} %get-tuple-element.105.wy, ...), custom_call_target="tpu_custom_call" | custom-call | flops 100000000 | bytes 12697600 | tf_op jit(solution)/shard_map/sweeps/pallas_call | solution.py:71
  93.9 0.0 copy-start.1
  93.9 0.0 copy-start.4
  93.9 0.8 reply.1
  94.7 28.0 %all_to_all.10 = f32[1024,1,128]{2,1,0:T(1,128)S(1)} all-to-all(f32[1024,1,128]{2,1,0:T(1,128)S(1)} %bitcast.26), channel_id=1, replica_groups=mesh['gx'=16,'gy'=4,'gz'=8] {'gx','gy'}, dimensions={0} | all-to-all | bytes 1048576 | tf_op jit(solution)/shard_map/all_to_all | solution.py:491
  122.7 1.2 %finish.1 = (f32[512,128]{1,0:T(8,128)}, f32[512,128]{1,0:T(8,128)}) custom-call(f32[1024,128]{1,0:T(8,128)S(1)} %bitcast.23, bf16[512,1024]{1,0:T(8,128)(2,1)S(1)} %get-tuple-element.123.hot, f32[512,128]{1,0:T(8,128)S(1)} %copy-done.4, f32[512,128]{1,0:T(8,128)S(1)} %bitcast.25), custom_call_target="tpu_custom_call" | custom-call | flops 100000000 | bytes 2621440 | tf_op jit(solution)/shard_map/finish/pallas_call | solution.py:71
  (12 shorter events, 0.1 us)
Async XLA Ops:
  0.6 14.7 %copy-start.2 = (f32[4,128,128]{2,1,0:T(8,128)S(1)}, f32[4,128,128]{2,1,0:T(8,128)}, u32[]{:S(2)}) copy-start(f32[4,128,128]{2,1,0:T(8,128)} %param.14) | copy-start | bytes 786436
  0.6 14.7 %copy-start.6 = (s32[1,1,1,512]{3,2,1,0:T(1,128)S(1)}, s32[1,1,1,512]{3,2,1,0:T(1,128)}, u32[]{:S(2)}) copy-start(s32[1,1,1,512]{3,2,1,0:T(1,128)} %param.18) | copy-start | bytes 6148
  0.7 27.8 %copy-start = (f32[3,4,128,128]{3,2,1,0:T(8,128)S(1)}, f32[3,4,128,128]{3,2,1,0:T(8,128)}, u32[]{:S(2)}) copy-start(f32[3,4,128,128]{3,2,1,0:T(8,128)} %param.11) | copy-start | bytes 2359300
  0.7 27.8 %copy-start.5 = (s32[1,1,1,512,1]{3,4,2,1,0:T(1,128)S(1)}, s32[1,1,1,512,1]{3,4,2,1,0:T(1,128)}, u32[]{:S(2)}) copy-start(s32[1,1,1,512,1]{3,4,2,1,0:T(1,128)} %param.15) | copy-start | bytes 6148
  3.7 37.8 %all-to-all-start = ((f32[1088,1,128]{2,1,0:T(1,128)}), f32[1088,1,128]{2,1,0:T(1,128)S(1)}, u32[]{:S(2)}, u32[]{:S(2)}) async-start(f32[1088,1,128]{2,1,0:T(1,128)} %bitcast.31), calls=%async_computation | async-start | bytes 1114112 | tf_op jit(solution)/shard_map/all_to_all | solution.py:491
  15.4 26.0 %collective-permute-start.1 = (f32[520,128]{1,0:T(8,128)S(1)}, f32[520,128]{1,0:T(8,128)S(1)}, u32[]{:S(2)}, u32[]{:S(2)}) collective-permute-start(f32[520,128]{1,0:T(8,128)S(1)} %get-tuple-element.66.own), channel_id=1, source_target_pairs={{0,1},{1,2},{2,3},{3,4},{4,5},{5,6},{6,7},{8,9},{9,10},{10,11},{11... | collective-permute-start | bytes 798728 | tf_op jit(solution)/shard_map/ppermute | solution.py:486
  19.4 22.0 %collective-permute-start.2 = (f32[520,128]{1,0:T(8,128)S(1)}, f32[520,128]{1,0:T(8,128)S(1)}, u32[]{:S(2)}, u32[]{:S(2)}) collective-permute-start(f32[520,128]{1,0:T(8,128)S(1)} %get-tuple-element.66.own), channel_id=1, source_target_pairs={{1,0},{2,1},{3,2},{4,3},{5,4},{6,5},{7,6},{9,8},{10,9},{11,10},{12... | collective-permute-start | bytes 798728 | tf_op jit(solution)/shard_map/ppermute | solution.py:486
  20.7 9.6 %collective-permute-start = (f32[264,128]{1,0:T(8,128)S(1)}, f32[264,128]{1,0:T(8,128)S(1)}, u32[]{:S(2)}, u32[]{:S(2)}) collective-permute-start(f32[264,128]{1,0:T(8,128)S(1)} %get-tuple-element.65), channel_id=1, source_target_pairs={{0,2},{1,3},{2,4},{3,5},{4,6},{5,7},{8,10},{9,11},{10,12},{11,13},... | collective-permute-start | bytes 405512 | tf_op jit(solution)/shard_map/ppermute | solution.py:486
  27.2 14.2 %collective-permute-start.3 = (f32[264,128]{1,0:T(8,128)S(1)}, f32[264,128]{1,0:T(8,128)S(1)}, u32[]{:S(2)}, u32[]{:S(2)}) collective-permute-start(f32[264,128]{1,0:T(8,128)S(1)} %get-tuple-element.67), channel_id=1, source_target_pairs={{2,0},{3,1},{4,2},{5,3},{6,4},{7,5},{10,8},{11,9},{12,10},{13,11},... | collective-permute-start | bytes 405512 | tf_op jit(solution)/shard_map/ppermute | solution.py:486
  29.6 0.7 copy-start.3
  42.3 5.2 %collective-permute-start.4 = (f32[176,128]{1,0:T(8,128)S(1)}, f32[176,128]{1,0:T(8,128)S(1)}, u32[]{:S(2)}, u32[]{:S(2)}) collective-permute-start(f32[176,128]{1,0:T(8,128)S(1)} %get-tuple-element.78), channel_id=1, source_target_pairs={{0,32},{32,64},{64,96},{96,128},{128,160},{160,192},{192,224},{224... | collective-permute-start | bytes 270344 | tf_op jit(solution)/shard_map/ppermute | solution.py:486
  45.6 5.3 %collective-permute-start.5 = (f32[176,128]{1,0:T(8,128)S(1)}, f32[176,128]{1,0:T(8,128)S(1)}, u32[]{:S(2)}, u32[]{:S(2)}) collective-permute-start(f32[176,128]{1,0:T(8,128)S(1)} %get-tuple-element.79), channel_id=1, source_target_pairs={{32,0},{64,32},{96,64},{128,96},{160,128},{192,160},{224,192},{256... | collective-permute-start | bytes 270344 | tf_op jit(solution)/shard_map/ppermute | solution.py:486
  50.9 21.8 %copy-start.7 = (f32[8]{0:T(128)S(1)}, f32[8]{0:T(128)}, u32[]{:S(2)}) copy-start(f32[8]{0:T(128)} %base.1) | copy-start | bytes 100
  50.9 21.8 %copy-start.8 = (f32[8]{0:T(128)S(1)}, f32[8]{0:T(128)}, u32[]{:S(2)}) copy-start(f32[8]{0:T(128)} %soft.1) | copy-start | bytes 100
  50.9 21.8 %copy-start.9 = (f32[8]{0:T(128)S(1)}, f32[8]{0:T(128)}, u32[]{:S(2)}) copy-start(f32[8]{0:T(128)} %heat.1) | copy-start | bytes 100
  51.6 13.9 %collective-permute-start.6 = (f32[16,2304]{1,0:T(8,128)S(1)}, f32[16,2304]{1,0:T(8,128)S(1)}, u32[]{:S(2)}, u32[]{:S(2)}) collective-permute-start(f32[16,2304]{1,0:T(8,128)S(1)} %get-tuple-element.89), channel_id=1, source_target_pairs={{0,8},{8,16},{16,24},{1,9},{9,17},{17,25},{2,10},{10,18},{18,26},{... | collective-permute-start | bytes 442376 | tf_op jit(solution)/shard_map/ppermute | solution.py:486
  56.5 9.0 %collective-permute-start.7 = (f32[16,2304]{1,0:T(8,128)S(1)}, f32[16,2304]{1,0:T(8,128)S(1)}, u32[]{:S(2)}, u32[]{:S(2)}) collective-permute-start(f32[16,2304]{1,0:T(8,128)S(1)} %get-tuple-element.90), channel_id=1, source_target_pairs={{8,0},{16,8},{24,16},{9,1},{17,9},{25,17},{10,2},{18,10},{26,18},{... | collective-permute-start | bytes 442376 | tf_op jit(solution)/shard_map/ppermute | solution.py:486
  58.4 7.1 %collective-permute-start.8 = (f32[128,128]{1,0:T(8,128)S(1)}, f32[128,128]{1,0:T(8,128)S(1)}, u32[]{:S(2)}, u32[]{:S(2)}) collective-permute-start(f32[128,128]{1,0:T(8,128)S(1)} %get-tuple-element.91), channel_id=1, source_target_pairs={{0,2},{1,3},{2,4},{3,5},{4,6},{5,7},{8,10},{9,11},{10,12},{11,13},... | collective-permute-start | bytes 196616 | tf_op jit(solution)/shard_map/ppermute | solution.py:486
  64.2 5.9 %collective-permute-start.9 = (f32[128,128]{1,0:T(8,128)S(1)}, f32[128,128]{1,0:T(8,128)S(1)}, u32[]{:S(2)}, u32[]{:S(2)}) collective-permute-start(f32[128,128]{1,0:T(8,128)S(1)} %get-tuple-element.92), channel_id=1, source_target_pairs={{2,0},{3,1},{4,2},{5,3},{6,4},{7,5},{10,8},{11,9},{12,10},{13,11},... | collective-permute-start | bytes 196616 | tf_op jit(solution)/shard_map/ppermute | solution.py:486
  70.1 9.2 %collective-permute-start.10 = (f32[736,128]{1,0:T(8,128)S(1)}, f32[736,128]{1,0:T(8,128)S(1)}, u32[]{:S(2)}, u32[]{:S(2)}) collective-permute-start(f32[736,128]{1,0:T(8,128)S(1)} %pack_z.1.own), channel_id=1, source_target_pairs={{0,1},{1,2},{2,3},{3,4},{4,5},{5,6},{6,7},{8,9},{9,10},{10,11},{11... | collective-permute-start | bytes 1130504 | tf_op jit(solution)/shard_map/ppermute | solution.py:486
  71.4 13.3 %collective-permute-start.11 = (f32[736,128]{1,0:T(8,128)S(1)}, f32[736,128]{1,0:T(8,128)S(1)}, u32[]{:S(2)}, u32[]{:S(2)}) collective-permute-start(f32[736,128]{1,0:T(8,128)S(1)} %pack_z.1.own), channel_id=1, source_target_pairs={{1,0},{2,1},{3,2},{4,3},{5,4},{6,5},{7,6},{9,8},{10,9},{11,10},{12... | collective-permute-start | bytes 1130504 | tf_op jit(solution)/shard_map/ppermute | solution.py:486
  93.9 28.9 %copy-start.1 = (f32[4,128,128]{2,1,0:T(8,128)S(1)}, f32[4,128,128]{2,1,0:T(8,128)}, u32[]{:S(2)}) copy-start(f32[4,128,128]{2,1,0:T(8,128)} %param.13) | copy-start | bytes 786436
  93.9 28.9 %copy-start.4 = (f32[512,128]{1,0:T(8,128)S(1)}, f32[512,128]{1,0:T(8,128)}, u32[]{:S(2)}) copy-start(f32[512,128]{1,0:T(8,128)} %copy-done.3) | copy-start | bytes 786436

commit v10 on v8

--- a/solution.py
+++ b/solution.py
@@ -548,16 +548,15 @@
     blocks = -(-inner // LANES)
     [around] = call(
         pack_z_kernel, [sized(inner + 4 * EDGE * blocks, width)], [full, heat_sides, before, after], "pack_z")
-    around, first, last = lax.optimization_barrier((around, first, last))
     low, high = shifted(around, "gz", 1), shifted(around, "gz", -1)
-    low2, high2 = shifted(last, "gz", 2), shifted(first, "gz", -2)
     weights = call(
         weights_kernel, [tile, tall, tile, tile, tile, tile, sized(9, 4 * EDGE, total)],
         [mat_conductivity, mat_softening, mat_capacity, xm, sides, flat_mat, before, after], "weights",
         scratch=[pltpu.VMEM((count, rows + 2 * EDGE, width), F32), pltpu.VMEM((total, 3 * width), F32),
                  pltpu.VMEM((total, width), F32)],
         limit=32, flops=10**9, smem=(0, 1, 2))
-    low, high, weights = lax.optimization_barrier((low, high, weights))
+    first, last, weights = lax.optimization_barrier((first, last, weights))
+    low2, high2 = shifted(last, "gz", 2), shifted(first, "gz", -2)
     x, pull = call(
         sweep_kernel, [sized(n, width), sized(2 * xcells, width)],
         [xm] + list(weights) + [low, around, high], "sweeps",

time: 119 us -> 119 us (level)
  no operation moved by 1% of the time
where the time goes in v10:
time: 119 us; the launch traced here: 118 us
  starting transfers between devices  48.4 us (41%)
  blocking collectives  27.7 us (23%)
  Pallas kernels  21.6 us (18%)
  waiting for transfers between devices  19 us (16%)
    ppermute x12, starting transfers between devices, shifted(): return lax.ppermute(v, axis, pairs) if pairs else jnp.zeros_like(v)  36.7 us
    all_to_all x1, blocking collectives, exchanged(): lax.all_to_all(lines, ('gx', 'gy'), split_axis=0, concat_axis=0, tiled=True)  27.7 us
    pallas_call x13, Pallas kernels, call(): pl.pallas_call(kernel, out_shape=[jax.ShapeDtypeStruct(s, t) for s, t in...  21.6 us
    ppermute x12, waiting for transfers between devices, shifted(): return lax.ppermute(v, axis, pairs) if pairs else jnp.zeros_like(v)  19 us
    all_to_all x1, starting transfers between devices, exchanged(): lax.all_to_all(lines, ('gx', 'gy'), split_axis=0, concat_axis=0, tiled=True)  11.6 us
  transfers between devices with their start and end apart: 13, of which 4 were waited for; matrix products, arithmetic and copies ran while one was open for 0% of the time, Pallas kernels for 13%

profile of v10, /device:TPU:1, one launch (start us, length us, event | category | flops | bytes accessed | tf_op | source)
XLA Modules:
  0.0 118.4 jit_solution(2410899097730534763)
XLA Ops:
  0.6 0.0 copy-start.2
  0.6 0.0 copy-start.6
  0.7 0.0 copy-start
  0.7 0.0 copy-start.5
  0.7 3.0 %dispatch.1 = f32[1088,128]{1,0:T(8,128)} custom-call(f32[3,512,128]{2,1,0:T(8,128)} %bitcast.21, f32[512,128]{1,0:T(8,128)} %bitcast.32, f32[512,128]{1,0:T(8,128)} %bitcast.24, s32[1,512]{1,0:T(1,128)} %bitcast.28, s32[1,512]{1,0:T(1,128)} %bitcast.33, s32[1,512]{1,0:T(1,128)} %bitcast.34), custom_call_target="tpu_custom_call" | custom-call | flops 100000000 | bytes 1873920 | tf_op jit(solution)/shard_map/dispatch/pallas_call | solution.py:71
  3.7 11.6 %all-to-all-start = ((f32[1088,1,128]{2,1,0:T(1,128)}), f32[1088,1,128]{2,1,0:T(1,128)S(1)}, u32[]{:S(2)}, u32[]{:S(2)}) async-start(f32[1088,1,128]{2,1,0:T(1,128)} %bitcast.31), calls=%async_computation | async-start | bytes 1114112 | tf_op jit(solution)/shard_map/all_to_all | solution.py:491
  15.4 0.0 copy-done.2
  15.4 0.0 copy-done.6
  15.4 4.0 %collective-permute-start.1 = (f32[520,128]{1,0:T(8,128)S(1)}, f32[520,128]{1,0:T(8,128)S(1)}, u32[]{:S(2)}, u32[]{:S(2)}) collective-permute-start(f32[520,128]{1,0:T(8,128)S(1)} %get-tuple-element.59.own), channel_id=1, source_target_pairs={{0,1},{1,2},{2,3},{3,4},{4,5},{5,6},{6,7},{8,9},{9,10},{10,11},{11... | collective-permute-start | bytes 798728 | tf_op jit(solution)/shard_map/ppermute | solution.py:486
  19.4 1.3 %collective-permute-start.2 = (f32[520,128]{1,0:T(8,128)S(1)}, f32[520,128]{1,0:T(8,128)S(1)}, u32[]{:S(2)}, u32[]{:S(2)}) collective-permute-start(f32[520,128]{1,0:T(8,128)S(1)} %get-tuple-element.59.own), channel_id=1, source_target_pairs={{1,0},{2,1},{3,2},{4,3},{5,4},{6,5},{7,6},{9,8},{10,9},{11,10},{12... | collective-permute-start | bytes 798728 | tf_op jit(solution)/shard_map/ppermute | solution.py:486
  20.7 6.4 %collective-permute-start = (f32[264,128]{1,0:T(8,128)S(1)}, f32[264,128]{1,0:T(8,128)S(1)}, u32[]{:S(2)}, u32[]{:S(2)}) collective-permute-start(f32[264,128]{1,0:T(8,128)S(1)} %get-tuple-element.58), channel_id=1, source_target_pairs={{0,2},{1,3},{2,4},{3,5},{4,6},{5,7},{8,10},{9,11},{10,12},{11,13},... | collective-permute-start | bytes 405512 | tf_op jit(solution)/shard_map/ppermute | solution.py:486
  27.2 1.3 %collective-permute-start.3 = (f32[264,128]{1,0:T(8,128)S(1)}, f32[264,128]{1,0:T(8,128)S(1)}, u32[]{:S(2)}, u32[]{:S(2)}) collective-permute-start(f32[264,128]{1,0:T(8,128)S(1)} %get-tuple-element.60), channel_id=1, source_target_pairs={{2,0},{3,1},{4,2},{5,3},{6,4},{7,5},{10,8},{11,9},{12,10},{13,11},... | collective-permute-start | bytes 405512 | tf_op jit(solution)/shard_map/ppermute | solution.py:486
  28.5 1.1 gain.1
  29.6 0.0 copy-start.3
  29.6 0.7 copy-done.3
  30.3 0.0 collective-permute-done.low2
  30.3 11.1 %collective-permute-done.3.high2 = f32[264,128]{1,0:T(8,128)S(1)} collective-permute-done((f32[264,128]{1,0:T(8,128)S(1)}, f32[264,128]{1,0:T(8,128)S(1)}, u32[]{:S(2)}, u32[]{:S(2)}) %collective-permute-start.3) | collective-permute-done | bytes 135200 | tf_op jit(solution)/shard_map/ppermute | solution.py:486
  41.4 0.0 collective-permute-done.1.low
  41.4 0.0 collective-permute-done.2.high
  41.4 0.1 start_x.1
  41.5 0.0 all-to-all-done
  41.5 0.7 combine.1
  42.3 3.3 %collective-permute-start.4 = (f32[176,128]{1,0:T(8,128)S(1)}, f32[176,128]{1,0:T(8,128)S(1)}, u32[]{:S(2)}, u32[]{:S(2)}) collective-permute-start(f32[176,128]{1,0:T(8,128)S(1)} %get-tuple-element.71), channel_id=1, source_target_pairs={{0,32},{32,64},{64,96},{96,128},{128,160},{160,192},{192,224},{224... | collective-permute-start | bytes 270344 | tf_op jit(solution)/shard_map/ppermute | solution.py:486
  45.6 1.3 %collective-permute-start.5 = (f32[176,128]{1,0:T(8,128)S(1)}, f32[176,128]{1,0:T(8,128)S(1)}, u32[]{:S(2)}, u32[]{:S(2)}) collective-permute-start(f32[176,128]{1,0:T(8,128)S(1)} %get-tuple-element.72), channel_id=1, source_target_pairs={{32,0},{64,32},{96,64},{128,96},{160,128},{192,160},{224,192},{256... | collective-permute-start | bytes 270344 | tf_op jit(solution)/shard_map/ppermute | solution.py:486
  46.9 0.5 ids.1.hot
  47.4 0.0 collective-permute-done.4.before
  47.4 3.4 %collective-permute-done.5.after = f32[176,128]{1,0:T(8,128)S(1)} collective-permute-done((f32[176,128]{1,0:T(8,128)S(1)}, f32[176,128]{1,0:T(8,128)S(1)}, u32[]{:S(2)}, u32[]{:S(2)}) %collective-permute-start.5) | collective-permute-done | bytes 90144 | tf_op jit(solution)/shard_map/ppermute | solution.py:486
  50.9 0.7 pack_y.1
  51.6 4.9 %collective-permute-start.6 = (f32[16,2304]{1,0:T(8,128)S(1)}, f32[16,2304]{1,0:T(8,128)S(1)}, u32[]{:S(2)}, u32[]{:S(2)}) collective-permute-start(f32[16,2304]{1,0:T(8,128)S(1)} %get-tuple-element.80), channel_id=1, source_target_pairs={{0,8},{8,16},{16,24},{1,9},{9,17},{17,25},{2,10},{10,18},{18,26},{... | collective-permute-start | bytes 442376 | tf_op jit(solution)/shard_map/ppermute | solution.py:486
  56.5 1.9 %collective-permute-start.7 = (f32[16,2304]{1,0:T(8,128)S(1)}, f32[16,2304]{1,0:T(8,128)S(1)}, u32[]{:S(2)}, u32[]{:S(2)}) collective-permute-start(f32[16,2304]{1,0:T(8,128)S(1)} %get-tuple-element.81), channel_id=1, source_target_pairs={{8,0},{16,8},{24,16},{9,1},{17,9},{25,17},{10,2},{18,10},{26,18},{... | collective-permute-start | bytes 442376 | tf_op jit(solution)/shard_map/ppermute | solution.py:486
  58.4 0.2 collective-permute-done.6.before
  58.6 4.4 %collective-permute-done.7.after = f32[16,2304]{1,0:T(8,128)S(1)} collective-permute-done((f32[16,2304]{1,0:T(8,128)S(1)}, f32[16,2304]{1,0:T(8,128)S(1)}, u32[]{:S(2)}, u32[]{:S(2)}) %collective-permute-start.7) | collective-permute-done | bytes 147488 | tf_op jit(solution)/shard_map/ppermute | solution.py:486
  63.0 1.3 %collective-permute-start.8 = (f32[736,128]{1,0:T(8,128)S(1)}, f32[736,128]{1,0:T(8,128)S(1)}, u32[]{:S(2)}, u32[]{:S(2)}) collective-permute-start(f32[736,128]{1,0:T(8,128)S(1)} %pack_z.1.own), channel_id=1, source_target_pairs={{0,1},{1,2},{2,3},{3,4},{4,5},{5,6},{6,7},{8,9},{9,10},{10,11},{11... | collective-permute-start | bytes 1130504 | tf_op jit(solution)/shard_map/ppermute | solution.py:486
  64.3 1.3 %collective-permute-start.9 = (f32[736,128]{1,0:T(8,128)S(1)}, f32[736,128]{1,0:T(8,128)S(1)}, u32[]{:S(2)}, u32[]{:S(2)}) collective-permute-start(f32[736,128]{1,0:T(8,128)S(1)} %pack_z.1.own), channel_id=1, source_target_pairs={{1,0},{2,1},{3,2},{4,3},{5,4},{6,5},{7,6},{9,8},{10,9},{11,10},{12... | collective-permute-start | bytes 1130504 | tf_op jit(solution)/shard_map/ppermute | solution.py:486
  65.6 4.0 %weights.1 = (f32[16,144,128]{2,1,0:T(8,128)S(1)}, f32[16,160,128]{2,1,0:T(8,128)S(1)}, f32[16,144,128]{2,1,0:T(8,128)S(1)}, f32[16,144,128]{2,1,0:T(8,128)S(1)}...) custom-call(f32[8]{0:T(128)S(1)} %copy-done.7, f32[8]{0:T(128)S(1)} %copy-done.8, ...), custom_call_target="tpu_custom_call" | custom-call | flops 1000000000 | bytes 11690080 | tf_op jit(solution)/shard_map/weights/pallas_call | solution.py:71
  69.6 8.4 %collective-permute-start.10 = (f32[128,128]{1,0:T(8,128)S(1)}, f32[128,128]{1,0:T(8,128)S(1)}, u32[]{:S(2)}, u32[]{:S(2)}) collective-permute-start(f32[128,128]{1,0:T(8,128)S(1)} %get-tuple-element.100), channel_id=1, source_target_pairs={{0,2},{1,3},{2,4},{3,5},{4,6},{5,7},{8,10},{9,11},{10,12},{11,13},... | collective-permute-start | bytes 196616 | tf_op jit(solution)/shard_map/ppermute | solution.py:486
  78.1 1.3 %collective-permute-start.11 = (f32[128,128]{1,0:T(8,128)S(1)}, f32[128,128]{1,0:T(8,128)S(1)}, u32[]{:S(2)}, u32[]{:S(2)}) collective-permute-start(f32[128,128]{1,0:T(8,128)S(1)} %get-tuple-element.101), channel_id=1, source_target_pairs={{2,0},{3,1},{4,2},{5,3},{6,4},{7,5},{10,8},{11,9},{12,10},{13,11},... | collective-permute-start | bytes 196616 | tf_op jit(solution)/shard_map/ppermute | solution.py:486
  79.4 0.0 collective-permute-done.8.low
  79.4 0.0 collective-permute-done.9.high
  79.4 9.2 %sweeps.1 = (f32[512,128]{1,0:T(8,128)S(1)}, f32[256,128]{1,0:T(8,128)S(1)}) custom-call(f32[16,160,128]{2,1,0:T(8,128)S(1)} %get-tuple-element.75.xm, f32[16,144,128]{2,1,0:T(8,128)S(1)} %get-tuple-element.89.wz, f32[16,160,128]{2,1,0:T(8,128)S(1)} %get-tuple-element.90.wx, f32[16,144,128]{2,1,0:T(8,128)S(1)} %get-tuple-element.91.wy, ...), custom_call_target="tpu_custom_call" | custom-call | flops 100000000 | bytes 12697600 | tf_op jit(solution)/shard_map/sweeps/pallas_call | solution.py:71
  88.5 0.0 collective-permute-done.10.low2
  88.6 0.0 collective-permute-done.11.high2
  88.6 0.0 copy-start.1
  88.6 0.0 copy-start.4
  88.6 0.8 reply.1
  89.4 27.7 %all_to_all.10 = f32[1024,1,128]{2,1,0:T(1,128)S(1)} all-to-all(f32[1024,1,128]{2,1,0:T(1,128)S(1)} %bitcast.26), channel_id=1, replica_groups=mesh['gx'=16,'gy'=4,'gz'=8] {'gx','gy'}, dimensions={0} | all-to-all | bytes 1048576 | tf_op jit(solution)/shard_map/all_to_all | solution.py:491
  117.1 0.0 copy-done.4
  117.1 1.2 %finish.1 = (f32[512,128]{1,0:T(8,128)}, f32[512,128]{1,0:T(8,128)}) custom-call(f32[1024,128]{1,0:T(8,128)S(1)} %bitcast.23, bf16[512,1024]{1,0:T(8,128)(2,1)S(1)} %get-tuple-element.109.hot, f32[512,128]{1,0:T(8,128)S(1)} %copy-done.4, f32[512,128]{1,0:T(8,128)S(1)} %bitcast.25), custom_call_target="tpu_custom_call" | custom-call | flops 100000000 | bytes 2621440 | tf_op jit(solution)/shard_map/finish/pallas_call | solution.py:71
  (12 shorter events, 0.1 us)
Async XLA Ops:
  0.6 14.7 %copy-start.2 = (f32[4,128,128]{2,1,0:T(8,128)S(1)}, f32[4,128,128]{2,1,0:T(8,128)}, u32[]{:S(2)}) copy-start(f32[4,128,128]{2,1,0:T(8,128)} %param.14) | copy-start | bytes 786436
  0.6 14.7 %copy-start.6 = (s32[1,1,1,512]{3,2,1,0:T(1,128)S(1)}, s32[1,1,1,512]{3,2,1,0:T(1,128)}, u32[]{:S(2)}) copy-start(s32[1,1,1,512]{3,2,1,0:T(1,128)} %param.18) | copy-start | bytes 6148
  0.7 27.8 %copy-start = (f32[3,4,128,128]{3,2,1,0:T(8,128)S(1)}, f32[3,4,128,128]{3,2,1,0:T(8,128)}, u32[]{:S(2)}) copy-start(f32[3,4,128,128]{3,2,1,0:T(8,128)} %param.11) | copy-start | bytes 2359300
  0.7 27.8 %copy-start.5 = (s32[1,1,1,512,1]{3,4,2,1,0:T(1,128)S(1)}, s32[1,1,1,512,1]{3,4,2,1,0:T(1,128)}, u32[]{:S(2)}) copy-start(s32[1,1,1,512,1]{3,4,2,1,0:T(1,128)} %param.15) | copy-start | bytes 6148
  3.7 37.8 %all-to-all-start = ((f32[1088,1,128]{2,1,0:T(1,128)}), f32[1088,1,128]{2,1,0:T(1,128)S(1)}, u32[]{:S(2)}, u32[]{:S(2)}) async-start(f32[1088,1,128]{2,1,0:T(1,128)} %bitcast.31), calls=%async_computation | async-start | bytes 1114112 | tf_op jit(solution)/shard_map/all_to_all | solution.py:491
  15.4 26.0 %collective-permute-start.1 = (f32[520,128]{1,0:T(8,128)S(1)}, f32[520,128]{1,0:T(8,128)S(1)}, u32[]{:S(2)}, u32[]{:S(2)}) collective-permute-start(f32[520,128]{1,0:T(8,128)S(1)} %get-tuple-element.59.own), channel_id=1, source_target_pairs={{0,1},{1,2},{2,3},{3,4},{4,5},{5,6},{6,7},{8,9},{9,10},{10,11},{11... | collective-permute-start | bytes 798728 | tf_op jit(solution)/shard_map/ppermute | solution.py:486
  19.4 22.0 %collective-permute-start.2 = (f32[520,128]{1,0:T(8,128)S(1)}, f32[520,128]{1,0:T(8,128)S(1)}, u32[]{:S(2)}, u32[]{:S(2)}) collective-permute-start(f32[520,128]{1,0:T(8,128)S(1)} %get-tuple-element.59.own), channel_id=1, source_target_pairs={{1,0},{2,1},{3,2},{4,3},{5,4},{6,5},{7,6},{9,8},{10,9},{11,10},{12... | collective-permute-start | bytes 798728 | tf_op jit(solution)/shard_map/ppermute | solution.py:486
  20.7 9.6 %collective-permute-start = (f32[264,128]{1,0:T(8,128)S(1)}, f32[264,128]{1,0:T(8,128)S(1)}, u32[]{:S(2)}, u32[]{:S(2)}) collective-permute-start(f32[264,128]{1,0:T(8,128)S(1)} %get-tuple-element.58), channel_id=1, source_target_pairs={{0,2},{1,3},{2,4},{3,5},{4,6},{5,7},{8,10},{9,11},{10,12},{11,13},... | collective-permute-start | bytes 405512 | tf_op jit(solution)/shard_map/ppermute | solution.py:486
  27.2 14.2 %collective-permute-start.3 = (f32[264,128]{1,0:T(8,128)S(1)}, f32[264,128]{1,0:T(8,128)S(1)}, u32[]{:S(2)}, u32[]{:S(2)}) collective-permute-start(f32[264,128]{1,0:T(8,128)S(1)} %get-tuple-element.60), channel_id=1, source_target_pairs={{2,0},{3,1},{4,2},{5,3},{6,4},{7,5},{10,8},{11,9},{12,10},{13,11},... | collective-permute-start | bytes 405512 | tf_op jit(solution)/shard_map/ppermute | solution.py:486
  29.6 0.7 copy-start.3
  42.3 5.2 %collective-permute-start.4 = (f32[176,128]{1,0:T(8,128)S(1)}, f32[176,128]{1,0:T(8,128)S(1)}, u32[]{:S(2)}, u32[]{:S(2)}) collective-permute-start(f32[176,128]{1,0:T(8,128)S(1)} %get-tuple-element.71), channel_id=1, source_target_pairs={{0,32},{32,64},{64,96},{96,128},{128,160},{160,192},{192,224},{224... | collective-permute-start | bytes 270344 | tf_op jit(solution)/shard_map/ppermute | solution.py:486
  45.6 5.3 %collective-permute-start.5 = (f32[176,128]{1,0:T(8,128)S(1)}, f32[176,128]{1,0:T(8,128)S(1)}, u32[]{:S(2)}, u32[]{:S(2)}) collective-permute-start(f32[176,128]{1,0:T(8,128)S(1)} %get-tuple-element.72), channel_id=1, source_target_pairs={{32,0},{64,32},{96,64},{128,96},{160,128},{192,160},{224,192},{256... | collective-permute-start | bytes 270344 | tf_op jit(solution)/shard_map/ppermute | solution.py:486
  50.9 14.8 %copy-start.7 = (f32[8]{0:T(128)S(1)}, f32[8]{0:T(128)}, u32[]{:S(2)}) copy-start(f32[8]{0:T(128)} %base.1) | copy-start | bytes 100
  50.9 14.8 %copy-start.8 = (f32[8]{0:T(128)S(1)}, f32[8]{0:T(128)}, u32[]{:S(2)}) copy-start(f32[8]{0:T(128)} %soft.1) | copy-start | bytes 100
  50.9 14.8 %copy-start.9 = (f32[8]{0:T(128)S(1)}, f32[8]{0:T(128)}, u32[]{:S(2)}) copy-start(f32[8]{0:T(128)} %heat.1) | copy-start | bytes 100
  51.6 7.0 %collective-permute-start.6 = (f32[16,2304]{1,0:T(8,128)S(1)}, f32[16,2304]{1,0:T(8,128)S(1)}, u32[]{:S(2)}, u32[]{:S(2)}) collective-permute-start(f32[16,2304]{1,0:T(8,128)S(1)} %get-tuple-element.80), channel_id=1, source_target_pairs={{0,8},{8,16},{16,24},{1,9},{9,17},{17,25},{2,10},{10,18},{18,26},{... | collective-permute-start | bytes 442376 | tf_op jit(solution)/shard_map/ppermute | solution.py:486
  56.5 6.5 %collective-permute-start.7 = (f32[16,2304]{1,0:T(8,128)S(1)}, f32[16,2304]{1,0:T(8,128)S(1)}, u32[]{:S(2)}, u32[]{:S(2)}) collective-permute-start(f32[16,2304]{1,0:T(8,128)S(1)} %get-tuple-element.81), channel_id=1, source_target_pairs={{8,0},{16,8},{24,16},{9,1},{17,9},{25,17},{10,2},{18,10},{26,18},{... | collective-permute-start | bytes 442376 | tf_op jit(solution)/shard_map/ppermute | solution.py:486
  63.0 16.4 %collective-permute-start.8 = (f32[736,128]{1,0:T(8,128)S(1)}, f32[736,128]{1,0:T(8,128)S(1)}, u32[]{:S(2)}, u32[]{:S(2)}) collective-permute-start(f32[736,128]{1,0:T(8,128)S(1)} %pack_z.1.own), channel_id=1, source_target_pairs={{0,1},{1,2},{2,3},{3,4},{4,5},{5,6},{6,7},{8,9},{9,10},{10,11},{11... | collective-permute-start | bytes 1130504 | tf_op jit(solution)/shard_map/ppermute | solution.py:486
  64.3 15.1 %collective-permute-start.9 = (f32[736,128]{1,0:T(8,128)S(1)}, f32[736,128]{1,0:T(8,128)S(1)}, u32[]{:S(2)}, u32[]{:S(2)}) collective-permute-start(f32[736,128]{1,0:T(8,128)S(1)} %pack_z.1.own), channel_id=1, source_target_pairs={{1,0},{2,1},{3,2},{4,3},{5,4},{6,5},{7,6},{9,8},{10,9},{11,10},{12... | collective-permute-start | bytes 1130504 | tf_op jit(solution)/shard_map/ppermute | solution.py:486
  69.6 18.9 %collective-permute-start.10 = (f32[128,128]{1,0:T(8,128)S(1)}, f32[128,128]{1,0:T(8,128)S(1)}, u32[]{:S(2)}, u32[]{:S(2)}) collective-permute-start(f32[128,128]{1,0:T(8,128)S(1)} %get-tuple-element.100), channel_id=1, source_target_pairs={{0,2},{1,3},{2,4},{3,5},{4,6},{5,7},{8,10},{9,11},{10,12},{11,13},... | collective-permute-start | bytes 196616 | tf_op jit(solution)/shard_map/ppermute | solution.py:486
  78.1 10.5 %collective-permute-start.11 = (f32[128,128]{1,0:T(8,128)S(1)}, f32[128,128]{1,0:T(8,128)S(1)}, u32[]{:S(2)}, u32[]{:S(2)}) collective-permute-start(f32[128,128]{1,0:T(8,128)S(1)} %get-tuple-element.101), channel_id=1, source_target_pairs={{2,0},{3,1},{4,2},{5,3},{6,4},{7,5},{10,8},{11,9},{12,10},{13,11},... | collective-permute-start | bytes 196616 | tf_op jit(solution)/shard_map/ppermute | solution.py:486
  88.6 28.6 %copy-start.1 = (f32[4,128,128]{2,1,0:T(8,128)S(1)}, f32[4,128,128]{2,1,0:T(8,128)}, u32[]{:S(2)}) copy-start(f32[4,128,128]{2,1,0:T(8,128)} %param.13) | copy-start | bytes 786436
  88.6 28.6 %copy-start.4 = (f32[512,128]{1,0:T(8,128)S(1)}, f32[512,128]{1,0:T(8,128)}, u32[]{:S(2)}) copy-start(f32[512,128]{1,0:T(8,128)} %copy-done.3) | copy-start | bytes 786436

commit v11 on v10

--- a/solution.py
+++ b/solution.py
@@ -250,17 +250,17 @@
     mat = jnp.sum(jnp.where(mine, named, 0.0), axis=0, keepdims=True)
     flat_mat[...] = jnp.broadcast_to(mat, (EDGE, total))
     heat_found = flat_sides(full[...])
-    inner = pl.ds(0, layers * rows)
-    beyond = jnp.zeros((EDGE, total), F32)
     heat_sides[...] = heat_found
-    ylow[pl.ds(0, EDGE), :] = found[:EDGE]
-    yhigh[pl.ds(0, EDGE), :] = found[EDGE:]
-    ylow[pl.ds(EDGE, EDGE), :] = beyond
-    yhigh[pl.ds(EDGE, EDGE), :] = beyond
-    ylow[pl.ds(EDGE, EDGE), inner] = heat_found[:EDGE]
-    yhigh[pl.ds(EDGE, EDGE), inner] = heat_found[EDGE:]
-    ylow[pl.ds(2 * EDGE - 1, 1), :] = mat
-    yhigh[pl.ds(EDGE, 1), :] = mat
+    third = total // 3
+    ylow[:, pl.ds(0, total)] = found[:EDGE]
+    yhigh[:, pl.ds(0, total)] = found[EDGE:]
+    rest = jnp.zeros((2 * EDGE, third - layers * rows), F32)
+    block = jnp.concatenate([heat_found, rest], axis=1)
+    ylow[:, pl.ds(total, third)] = block[:EDGE]
+    yhigh[:, pl.ds(total, third)] = block[EDGE:]
+    for i in range(3):
+        ylow[pl.ds(EDGE - 3 + i, 1), pl.ds(total, third)] = mat[:, i * third : (i + 1) * third]
+        yhigh[pl.ds(i, 1), pl.ds(total, third)] = mat[:, i * third : (i + 1) * third]
 
 
 def three_parts(v):
@@ -292,7 +292,8 @@
 def pack_z_kernel(full, sides, before, after, out):
     n = full.shape[0]
     out[pl.ds(0, n), :] = full[...]
-    strip = strip_of(sides[...], before[pl.ds(EDGE, EDGE), 0:n], after[pl.ds(EDGE, EDGE), 0:n])
+    at = before.shape[1] * 3 // 4
+    strip = strip_of(sides[...], before[:, at : at + n], after[:, at : at + n])
     blocks = -(-n // LANES)
     strip = jnp.concatenate([strip, jnp.zeros((4 * EDGE, blocks * LANES - n), F32)], axis=1)
     for i in range(blocks):
@@ -302,8 +303,14 @@
 def weights_kernel(base, soft, heat, xm, sides, flat_mat, before, after, wz, wx, wy, wyw, inv, b0, strips, cond, cols, ends):
     count, rows = inv.shape[0], inv.shape[1]
     total = count * rows
+    third = pl.ds(total, total // 3)
     mat = jnp.concatenate(
-        [flat_mat[0:1], before[pl.ds(EDGE, 1), :], after[pl.ds(2 * EDGE - 1, 1), :]], axis=0
+        [
+            flat_mat[0:1],
+            jnp.concatenate([before[pl.ds(i, 1), third] for i in range(3)], axis=1),
+            jnp.concatenate([after[pl.ds(EDGE - 3 + i, 1), third] for i in range(3)], axis=1),
+        ],
+        axis=0,
     )
     tables = []
     for values in (base, soft, heat):
@@ -316,7 +323,7 @@
     cols[...] = dot(jnp.concatenate(own, axis=0), hot_of(lax.div(r, 3) == lax.div(y, LANES)), 0, 0)
     wide = lambda t, i: jnp.broadcast_to(t[i : i + 1], (EDGE, total))
     kb, ks, cf = (jnp.concatenate([wide(t, 1), wide(t, 0), wide(t, 0), wide(t, 2)], axis=0) for t in tables)
-    sx = strip_of(sides[...], before[:EDGE], after[:EDGE])
+    sx = strip_of(sides[...], before[:, :total], after[:, :total])
     sc = kb / (1.0 + ks * sx)
     down = lambda by, axis: 0.5 * (sc + turned(sc, by, axis))
     around = [down(rows, 1), down(-rows, 1), down(1, 1), down(-1, 1), down(1, 0), down(-1, 0)]
@@ -397,13 +404,15 @@
     sb = strips[7] + sb * strips[6]
     sx, sd = strips[8], None
     kept = [ends_of(sx)]
-    for keep, add in factors[:-1]:
-        near = strips[0] * turned(sx, rows, 1) + strips[1] * turned(sx, -rows, 1)
-        near += strips[2] * turned(sx, 1, 1) + strips[3] * turned(sx, -1, 1)
-        near += strips[4] * turned(sx, 1, 0) + strips[5] * turned(sx, -1, 0)
-        step = add * (sb - sx + near)
+    for s, (keep, add) in enumerate(factors[:-1]):
+        lanes = slice(s * LANES, total - s * LANES)
+        part = lambda i: strips[i, :, lanes]
+        near = part(0) * turned(sx, rows, 1) + part(1) * turned(sx, -rows, 1)
+        near += part(2) * turned(sx, 1, 1) + part(3) * turned(sx, -1, 1)
+        near += part(4) * turned(sx, 1, 0) + part(5) * turned(sx, -1, 0)
+        step = add * (sb[:, lanes] - sx + near)
         sd = step if sd is None else step + keep * sd
-        sx = sx + sd
+        sx, sd = (sx + sd)[:, LANES:-LANES], sd[:, LANES:-LANES]
         kept.append(ends_of(sx))
     place_in = end_lanes(2, 1)
     place_in = jnp.concatenate([place_in, place_in], axis=0)
@@ -411,7 +420,7 @@
         start = (1 + s) * rows // LANES * LANES
         stop = -(-(count - 1 - s) * rows // LANES) * LANES
         ends[start:stop, s * LANES : (s + 1) * LANES] = dot(
-            jnp.concatenate(parts(pair[:, start:stop]), axis=0), place_in, 0, 0)
+            jnp.concatenate(parts(pair[:, start - s * LANES : stop - s * LANES]), axis=0), place_in, 0, 0)
 
     piece = 24
     first, last = iota((piece, LANES), 1) == 0, iota((piece, LANES), 1) == LANES - 1
@@ -540,9 +549,10 @@
     before, after, ids = lax.optimization_barrier((before, after, ids))
     tall, tile, flat_edge = sized(count, rows + 2 * EDGE, width), sized(count, rows, width), sized(2 * EDGE, total)
     inner = layers * rows
+    y_edge = sized(EDGE, total + total // 3)
     xm, full, sides, heat_sides, flat_mat, ylow, yhigh = call(
         pack_y_kernel,
-        [tall, sized(inner, width), flat_edge, sized(2 * EDGE, inner), sized(EDGE, total), flat_edge, flat_edge],
+        [tall, sized(inner, width), flat_edge, sized(2 * EDGE, inner), sized(EDGE, total), y_edge, y_edge],
         [xz, mats, source, after, before], "pack_y")
     before, after = shifted(yhigh, "gy", 1), shifted(ylow, "gy", -1)
     blocks = -(-inner // LANES)

time: 119 us -> 118 us (level)
  transfers between devices with their start and end apart: 13 -> 13, of which waited for: 4 -> 3; matrix products, arithmetic and copies ran while one was open for 0% -> 0% of each run, Pallas kernels for 13% -> 13%
where the time goes in v11:
time: 118 us
  starting transfers between devices  48.4 us (41%)
  blocking collectives  27.7 us (23%)
  Pallas kernels  21.5 us (18%)
  waiting for transfers between devices  18.5 us (16%)
    ppermute x12, starting transfers between devices, shifted(): return lax.ppermute(v, axis, pairs) if pairs else jnp.zeros_like(v)  36.7 us
    all_to_all x1, blocking collectives, exchanged(): lax.all_to_all(lines, ('gx', 'gy'), split_axis=0, concat_axis=0, tiled=True)  27.7 us
    pallas_call x13, Pallas kernels, call(): pl.pallas_call(kernel, out_shape=[jax.ShapeDtypeStruct(s, t) for s, t in...  21.5 us
    ppermute x12, waiting for transfers between devices, shifted(): return lax.ppermute(v, axis, pairs) if pairs else jnp.zeros_like(v)  18.5 us
    all_to_all x1, starting transfers between devices, exchanged(): lax.all_to_all(lines, ('gx', 'gy'), split_axis=0, concat_axis=0, tiled=True)  11.6 us
  transfers between devices with their start and end apart: 13, of which 3 were waited for; matrix products, arithmetic and copies ran while one was open for 0% of the time, Pallas kernels for 13%

profile of v11, /device:TPU:1, one launch (start us, length us, event | category | flops | bytes accessed | tf_op | source)
XLA Modules:
  0.0 117.8 jit_solution(5621272388729564050)
XLA Ops:
  0.6 0.0 copy-start.2
  0.6 0.0 copy-start.6
  0.7 0.0 copy-start
  0.7 0.0 copy-start.5
  0.7 3.0 %dispatch.1 = f32[1088,128]{1,0:T(8,128)} custom-call(f32[3,512,128]{2,1,0:T(8,128)} %bitcast.21, f32[512,128]{1,0:T(8,128)} %bitcast.32, f32[512,128]{1,0:T(8,128)} %bitcast.24, s32[1,512]{1,0:T(1,128)} %bitcast.28, s32[1,512]{1,0:T(1,128)} %bitcast.33, s32[1,512]{1,0:T(1,128)} %bitcast.34), custom_call_target="tpu_custom_call" | custom-call | flops 100000000 | bytes 1873920 | tf_op jit(solution)/shard_map/dispatch/pallas_call | solution.py:71
  3.7 11.6 %all-to-all-start = ((f32[1088,1,128]{2,1,0:T(1,128)}), f32[1088,1,128]{2,1,0:T(1,128)S(1)}, u32[]{:S(2)}, u32[]{:S(2)}) async-start(f32[1088,1,128]{2,1,0:T(1,128)} %bitcast.31), calls=%async_computation | async-start | bytes 1114112 | tf_op jit(solution)/shard_map/all_to_all | solution.py:500
  15.4 0.0 copy-done.2
  15.4 0.0 copy-done.6
  15.4 4.0 %collective-permute-start.1 = (f32[520,128]{1,0:T(8,128)S(1)}, f32[520,128]{1,0:T(8,128)S(1)}, u32[]{:S(2)}, u32[]{:S(2)}) collective-permute-start(f32[520,128]{1,0:T(8,128)S(1)} %get-tuple-element.59.own), channel_id=1, source_target_pairs={{0,1},{1,2},{2,3},{3,4},{4,5},{5,6},{6,7},{8,9},{9,10},{10,11},{11... | collective-permute-start | bytes 798728 | tf_op jit(solution)/shard_map/ppermute | solution.py:495
  19.4 1.3 %collective-permute-start.2 = (f32[520,128]{1,0:T(8,128)S(1)}, f32[520,128]{1,0:T(8,128)S(1)}, u32[]{:S(2)}, u32[]{:S(2)}) collective-permute-start(f32[520,128]{1,0:T(8,128)S(1)} %get-tuple-element.59.own), channel_id=1, source_target_pairs={{1,0},{2,1},{3,2},{4,3},{5,4},{6,5},{7,6},{9,8},{10,9},{11,10},{12... | collective-permute-start | bytes 798728 | tf_op jit(solution)/shard_map/ppermute | solution.py:495
  20.7 6.4 %collective-permute-start = (f32[264,128]{1,0:T(8,128)S(1)}, f32[264,128]{1,0:T(8,128)S(1)}, u32[]{:S(2)}, u32[]{:S(2)}) collective-permute-start(f32[264,128]{1,0:T(8,128)S(1)} %get-tuple-element.58), channel_id=1, source_target_pairs={{0,2},{1,3},{2,4},{3,5},{4,6},{5,7},{8,10},{9,11},{10,12},{11,13},... | collective-permute-start | bytes 405512 | tf_op jit(solution)/shard_map/ppermute | solution.py:495
  27.2 1.3 %collective-permute-start.3 = (f32[264,128]{1,0:T(8,128)S(1)}, f32[264,128]{1,0:T(8,128)S(1)}, u32[]{:S(2)}, u32[]{:S(2)}) collective-permute-start(f32[264,128]{1,0:T(8,128)S(1)} %get-tuple-element.60), channel_id=1, source_target_pairs={{2,0},{3,1},{4,2},{5,3},{6,4},{7,5},{10,8},{11,9},{12,10},{13,11},... | collective-permute-start | bytes 405512 | tf_op jit(solution)/shard_map/ppermute | solution.py:495
  28.5 1.1 gain.1
  29.6 0.0 copy-start.3
  29.6 0.7 copy-done.3
  30.3 0.0 collective-permute-done.low2
  30.3 11.1 %collective-permute-done.3.high2 = f32[264,128]{1,0:T(8,128)S(1)} collective-permute-done((f32[264,128]{1,0:T(8,128)S(1)}, f32[264,128]{1,0:T(8,128)S(1)}, u32[]{:S(2)}, u32[]{:S(2)}) %collective-permute-start.3) | collective-permute-done | bytes 135200 | tf_op jit(solution)/shard_map/ppermute | solution.py:495
  41.4 0.0 collective-permute-done.1.low
  41.4 0.0 collective-permute-done.2.high
  41.4 0.1 start_x.1
  41.5 0.0 all-to-all-done
  41.5 0.7 combine.1
  42.3 3.3 %collective-permute-start.4 = (f32[176,128]{1,0:T(8,128)S(1)}, f32[176,128]{1,0:T(8,128)S(1)}, u32[]{:S(2)}, u32[]{:S(2)}) collective-permute-start(f32[176,128]{1,0:T(8,128)S(1)} %get-tuple-element.71), channel_id=1, source_target_pairs={{0,32},{32,64},{64,96},{96,128},{128,160},{160,192},{192,224},{224... | collective-permute-start | bytes 270344 | tf_op jit(solution)/shard_map/ppermute | solution.py:495
  45.6 1.3 %collective-permute-start.5 = (f32[176,128]{1,0:T(8,128)S(1)}, f32[176,128]{1,0:T(8,128)S(1)}, u32[]{:S(2)}, u32[]{:S(2)}) collective-permute-start(f32[176,128]{1,0:T(8,128)S(1)} %get-tuple-element.72), channel_id=1, source_target_pairs={{32,0},{64,32},{96,64},{128,96},{160,128},{192,160},{224,192},{256... | collective-permute-start | bytes 270344 | tf_op jit(solution)/shard_map/ppermute | solution.py:495
  46.9 0.5 ids.1.hot
  47.4 0.0 collective-permute-done.4.before
  47.4 3.4 %collective-permute-done.5.after = f32[176,128]{1,0:T(8,128)S(1)} collective-permute-done((f32[176,128]{1,0:T(8,128)S(1)}, f32[176,128]{1,0:T(8,128)S(1)}, u32[]{:S(2)}, u32[]{:S(2)}) %collective-permute-start.5) | collective-permute-done | bytes 90144 | tf_op jit(solution)/shard_map/ppermute | solution.py:495
  50.9 0.7 pack_y.1
  51.6 4.9 %collective-permute-start.6 = (f32[8,3072]{1,0:T(8,128)S(1)}, f32[8,3072]{1,0:T(8,128)S(1)}, u32[]{:S(2)}, u32[]{:S(2)}) collective-permute-start(f32[8,3072]{1,0:T(8,128)S(1)} %get-tuple-element.80), channel_id=1, source_target_pairs={{0,8},{8,16},{16,24},{1,9},{9,17},{17,25},{2,10},{10,18},{18,26},{... | collective-permute-start | bytes 294920 | tf_op jit(solution)/shard_map/ppermute | solution.py:495
  56.5 1.9 %collective-permute-start.7 = (f32[8,3072]{1,0:T(8,128)S(1)}, f32[8,3072]{1,0:T(8,128)S(1)}, u32[]{:S(2)}, u32[]{:S(2)}) collective-permute-start(f32[8,3072]{1,0:T(8,128)S(1)} %get-tuple-element.81), channel_id=1, source_target_pairs={{8,0},{16,8},{24,16},{9,1},{17,9},{25,17},{10,2},{18,10},{26,18},{... | collective-permute-start | bytes 294920 | tf_op jit(solution)/shard_map/ppermute | solution.py:495
  58.4 0.0 collective-permute-done.6.before
  58.4 4.0 %collective-permute-done.7.after = f32[8,3072]{1,0:T(8,128)S(1)} collective-permute-done((f32[8,3072]{1,0:T(8,128)S(1)}, f32[8,3072]{1,0:T(8,128)S(1)}, u32[]{:S(2)}, u32[]{:S(2)}) %collective-permute-start.7) | collective-permute-done | bytes 98336 | tf_op jit(solution)/shard_map/ppermute | solution.py:495
  62.5 1.3 %collective-permute-start.8 = (f32[736,128]{1,0:T(8,128)S(1)}, f32[736,128]{1,0:T(8,128)S(1)}, u32[]{:S(2)}, u32[]{:S(2)}) collective-permute-start(f32[736,128]{1,0:T(8,128)S(1)} %pack_z.1.own), channel_id=1, source_target_pairs={{0,1},{1,2},{2,3},{3,4},{4,5},{5,6},{6,7},{8,9},{9,10},{10,11},{11... | collective-permute-start | bytes 1130504 | tf_op jit(solution)/shard_map/ppermute | solution.py:495
  63.8 1.3 %collective-permute-start.9 = (f32[736,128]{1,0:T(8,128)S(1)}, f32[736,128]{1,0:T(8,128)S(1)}, u32[]{:S(2)}, u32[]{:S(2)}) collective-permute-start(f32[736,128]{1,0:T(8,128)S(1)} %pack_z.1.own), channel_id=1, source_target_pairs={{1,0},{2,1},{3,2},{4,3},{5,4},{6,5},{7,6},{9,8},{10,9},{11,10},{12... | collective-permute-start | bytes 1130504 | tf_op jit(solution)/shard_map/ppermute | solution.py:495
  65.1 4.0 %weights.1 = (f32[16,144,128]{2,1,0:T(8,128)S(1)}, f32[16,160,128]{2,1,0:T(8,128)S(1)}, f32[16,144,128]{2,1,0:T(8,128)S(1)}, f32[16,144,128]{2,1,0:T(8,128)S(1)}...) custom-call(f32[8]{0:T(128)S(1)} %copy-done.7, f32[8]{0:T(128)S(1)} %copy-done.8, ...), custom_call_target="tpu_custom_call" | custom-call | flops 1000000000 | bytes 11591776 | tf_op jit(solution)/shard_map/weights/pallas_call | solution.py:71
  69.1 8.4 %collective-permute-start.10 = (f32[128,128]{1,0:T(8,128)S(1)}, f32[128,128]{1,0:T(8,128)S(1)}, u32[]{:S(2)}, u32[]{:S(2)}) collective-permute-start(f32[128,128]{1,0:T(8,128)S(1)} %get-tuple-element.100), channel_id=1, source_target_pairs={{0,2},{1,3},{2,4},{3,5},{4,6},{5,7},{8,10},{9,11},{10,12},{11,13},... | collective-permute-start | bytes 196616 | tf_op jit(solution)/shard_map/ppermute | solution.py:495
  77.5 1.3 %collective-permute-start.11 = (f32[128,128]{1,0:T(8,128)S(1)}, f32[128,128]{1,0:T(8,128)S(1)}, u32[]{:S(2)}, u32[]{:S(2)}) collective-permute-start(f32[128,128]{1,0:T(8,128)S(1)} %get-tuple-element.101), channel_id=1, source_target_pairs={{2,0},{3,1},{4,2},{5,3},{6,4},{7,5},{10,8},{11,9},{12,10},{13,11},... | collective-permute-start | bytes 196616 | tf_op jit(solution)/shard_map/ppermute | solution.py:495
  78.8 0.0 collective-permute-done.8.low
  78.9 0.0 collective-permute-done.9.high
  78.9 9.1 %sweeps.1 = (f32[512,128]{1,0:T(8,128)S(1)}, f32[256,128]{1,0:T(8,128)S(1)}) custom-call(f32[16,160,128]{2,1,0:T(8,128)S(1)} %get-tuple-element.75.xm, f32[16,144,128]{2,1,0:T(8,128)S(1)} %get-tuple-element.89.wz, f32[16,160,128]{2,1,0:T(8,128)S(1)} %get-tuple-element.90.wx, f32[16,144,128]{2,1,0:T(8,128)S(1)} %get-tuple-element.91.wy, ...), custom_call_target="tpu_custom_call" | custom-call | flops 100000000 | bytes 12697600 | tf_op jit(solution)/shard_map/sweeps/pallas_call | solution.py:71
  87.9 0.0 collective-permute-done.10.low2
  88.0 0.0 collective-permute-done.11.high2
  88.0 0.0 copy-start.1
  88.0 0.0 copy-start.4
  88.0 0.8 reply.1
  88.8 27.7 %all_to_all.10 = f32[1024,1,128]{2,1,0:T(1,128)S(1)} all-to-all(f32[1024,1,128]{2,1,0:T(1,128)S(1)} %bitcast.26), channel_id=1, replica_groups=mesh['gx'=16,'gy'=4,'gz'=8] {'gx','gy'}, dimensions={0} | all-to-all | bytes 1048576 | tf_op jit(solution)/shard_map/all_to_all | solution.py:500
  116.5 0.0 copy-done.4
  116.5 1.2 %finish.1 = (f32[512,128]{1,0:T(8,128)}, f32[512,128]{1,0:T(8,128)}) custom-call(f32[1024,128]{1,0:T(8,128)S(1)} %bitcast.23, bf16[512,1024]{1,0:T(8,128)(2,1)S(1)} %get-tuple-element.109.hot, f32[512,128]{1,0:T(8,128)S(1)} %copy-done.4, f32[512,128]{1,0:T(8,128)S(1)} %bitcast.25), custom_call_target="tpu_custom_call" | custom-call | flops 100000000 | bytes 2621440 | tf_op jit(solution)/shard_map/finish/pallas_call | solution.py:71
  (12 shorter events, 0.1 us)
Async XLA Ops:
  0.6 14.7 %copy-start.2 = (f32[4,128,128]{2,1,0:T(8,128)S(1)}, f32[4,128,128]{2,1,0:T(8,128)}, u32[]{:S(2)}) copy-start(f32[4,128,128]{2,1,0:T(8,128)} %param.14) | copy-start | bytes 786436
  0.6 14.7 %copy-start.6 = (s32[1,1,1,512]{3,2,1,0:T(1,128)S(1)}, s32[1,1,1,512]{3,2,1,0:T(1,128)}, u32[]{:S(2)}) copy-start(s32[1,1,1,512]{3,2,1,0:T(1,128)} %param.18) | copy-start | bytes 6148
  0.7 27.8 %copy-start = (f32[3,4,128,128]{3,2,1,0:T(8,128)S(1)}, f32[3,4,128,128]{3,2,1,0:T(8,128)}, u32[]{:S(2)}) copy-start(f32[3,4,128,128]{3,2,1,0:T(8,128)} %param.11) | copy-start | bytes 2359300
  0.7 27.8 %copy-start.5 = (s32[1,1,1,512,1]{3,4,2,1,0:T(1,128)S(1)}, s32[1,1,1,512,1]{3,4,2,1,0:T(1,128)}, u32[]{:S(2)}) copy-start(s32[1,1,1,512,1]{3,4,2,1,0:T(1,128)} %param.15) | copy-start | bytes 6148
  3.7 37.8 %all-to-all-start = ((f32[1088,1,128]{2,1,0:T(1,128)}), f32[1088,1,128]{2,1,0:T(1,128)S(1)}, u32[]{:S(2)}, u32[]{:S(2)}) async-start(f32[1088,1,128]{2,1,0:T(1,128)} %bitcast.31), calls=%async_computation | async-start | bytes 1114112 | tf_op jit(solution)/shard_map/all_to_all | solution.py:500
  15.4 26.0 %collective-permute-start.1 = (f32[520,128]{1,0:T(8,128)S(1)}, f32[520,128]{1,0:T(8,128)S(1)}, u32[]{:S(2)}, u32[]{:S(2)}) collective-permute-start(f32[520,128]{1,0:T(8,128)S(1)} %get-tuple-element.59.own), channel_id=1, source_target_pairs={{0,1},{1,2},{2,3},{3,4},{4,5},{5,6},{6,7},{8,9},{9,10},{10,11},{11... | collective-permute-start | bytes 798728 | tf_op jit(solution)/shard_map/ppermute | solution.py:495
  19.4 22.0 %collective-permute-start.2 = (f32[520,128]{1,0:T(8,128)S(1)}, f32[520,128]{1,0:T(8,128)S(1)}, u32[]{:S(2)}, u32[]{:S(2)}) collective-permute-start(f32[520,128]{1,0:T(8,128)S(1)} %get-tuple-element.59.own), channel_id=1, source_target_pairs={{1,0},{2,1},{3,2},{4,3},{5,4},{6,5},{7,6},{9,8},{10,9},{11,10},{12... | collective-permute-start | bytes 798728 | tf_op jit(solution)/shard_map/ppermute | solution.py:495
  20.7 9.6 %collective-permute-start = (f32[264,128]{1,0:T(8,128)S(1)}, f32[264,128]{1,0:T(8,128)S(1)}, u32[]{:S(2)}, u32[]{:S(2)}) collective-permute-start(f32[264,128]{1,0:T(8,128)S(1)} %get-tuple-element.58), channel_id=1, source_target_pairs={{0,2},{1,3},{2,4},{3,5},{4,6},{5,7},{8,10},{9,11},{10,12},{11,13},... | collective-permute-start | bytes 405512 | tf_op jit(solution)/shard_map/ppermute | solution.py:495
  27.2 14.2 %collective-permute-start.3 = (f32[264,128]{1,0:T(8,128)S(1)}, f32[264,128]{1,0:T(8,128)S(1)}, u32[]{:S(2)}, u32[]{:S(2)}) collective-permute-start(f32[264,128]{1,0:T(8,128)S(1)} %get-tuple-element.60), channel_id=1, source_target_pairs={{2,0},{3,1},{4,2},{5,3},{6,4},{7,5},{10,8},{11,9},{12,10},{13,11},... | collective-permute-start | bytes 405512 | tf_op jit(solution)/shard_map/ppermute | solution.py:495
  29.6 0.7 copy-start.3
  42.3 5.2 %collective-permute-start.4 = (f32[176,128]{1,0:T(8,128)S(1)}, f32[176,128]{1,0:T(8,128)S(1)}, u32[]{:S(2)}, u32[]{:S(2)}) collective-permute-start(f32[176,128]{1,0:T(8,128)S(1)} %get-tuple-element.71), channel_id=1, source_target_pairs={{0,32},{32,64},{64,96},{96,128},{128,160},{160,192},{192,224},{224... | collective-permute-start | bytes 270344 | tf_op jit(solution)/shard_map/ppermute | solution.py:495
  45.6 5.3 %collective-permute-start.5 = (f32[176,128]{1,0:T(8,128)S(1)}, f32[176,128]{1,0:T(8,128)S(1)}, u32[]{:S(2)}, u32[]{:S(2)}) collective-permute-start(f32[176,128]{1,0:T(8,128)S(1)} %get-tuple-element.72), channel_id=1, source_target_pairs={{32,0},{64,32},{96,64},{128,96},{160,128},{192,160},{224,192},{256... | collective-permute-start | bytes 270344 | tf_op jit(solution)/shard_map/ppermute | solution.py:495
  50.9 14.2 %copy-start.7 = (f32[8]{0:T(128)S(1)}, f32[8]{0:T(128)}, u32[]{:S(2)}) copy-start(f32[8]{0:T(128)} %base.1) | copy-start | bytes 100
  50.9 14.2 %copy-start.8 = (f32[8]{0:T(128)S(1)}, f32[8]{0:T(128)}, u32[]{:S(2)}) copy-start(f32[8]{0:T(128)} %soft.1) | copy-start | bytes 100
  50.9 14.2 %copy-start.9 = (f32[8]{0:T(128)S(1)}, f32[8]{0:T(128)}, u32[]{:S(2)}) copy-start(f32[8]{0:T(128)} %heat.1) | copy-start | bytes 100
  51.6 6.8 %collective-permute-start.6 = (f32[8,3072]{1,0:T(8,128)S(1)}, f32[8,3072]{1,0:T(8,128)S(1)}, u32[]{:S(2)}, u32[]{:S(2)}) collective-permute-start(f32[8,3072]{1,0:T(8,128)S(1)} %get-tuple-element.80), channel_id=1, source_target_pairs={{0,8},{8,16},{16,24},{1,9},{9,17},{17,25},{2,10},{10,18},{18,26},{... | collective-permute-start | bytes 294920 | tf_op jit(solution)/shard_map/ppermute | solution.py:495
  56.5 5.9 %collective-permute-start.7 = (f32[8,3072]{1,0:T(8,128)S(1)}, f32[8,3072]{1,0:T(8,128)S(1)}, u32[]{:S(2)}, u32[]{:S(2)}) collective-permute-start(f32[8,3072]{1,0:T(8,128)S(1)} %get-tuple-element.81), channel_id=1, source_target_pairs={{8,0},{16,8},{24,16},{9,1},{17,9},{25,17},{10,2},{18,10},{26,18},{... | collective-permute-start | bytes 294920 | tf_op jit(solution)/shard_map/ppermute | solution.py:495
  62.5 16.4 %collective-permute-start.8 = (f32[736,128]{1,0:T(8,128)S(1)}, f32[736,128]{1,0:T(8,128)S(1)}, u32[]{:S(2)}, u32[]{:S(2)}) collective-permute-start(f32[736,128]{1,0:T(8,128)S(1)} %pack_z.1.own), channel_id=1, source_target_pairs={{0,1},{1,2},{2,3},{3,4},{4,5},{5,6},{6,7},{8,9},{9,10},{10,11},{11... | collective-permute-start | bytes 1130504 | tf_op jit(solution)/shard_map/ppermute | solution.py:495
  63.8 15.1 %collective-permute-start.9 = (f32[736,128]{1,0:T(8,128)S(1)}, f32[736,128]{1,0:T(8,128)S(1)}, u32[]{:S(2)}, u32[]{:S(2)}) collective-permute-start(f32[736,128]{1,0:T(8,128)S(1)} %pack_z.1.own), channel_id=1, source_target_pairs={{1,0},{2,1},{3,2},{4,3},{5,4},{6,5},{7,6},{9,8},{10,9},{11,10},{12... | collective-permute-start | bytes 1130504 | tf_op jit(solution)/shard_map/ppermute | solution.py:495
  69.1 18.8 %collective-permute-start.10 = (f32[128,128]{1,0:T(8,128)S(1)}, f32[128,128]{1,0:T(8,128)S(1)}, u32[]{:S(2)}, u32[]{:S(2)}) collective-permute-start(f32[128,128]{1,0:T(8,128)S(1)} %get-tuple-element.100), channel_id=1, source_target_pairs={{0,2},{1,3},{2,4},{3,5},{4,6},{5,7},{8,10},{9,11},{10,12},{11,13},... | collective-permute-start | bytes 196616 | tf_op jit(solution)/shard_map/ppermute | solution.py:495
  77.5 10.4 %collective-permute-start.11 = (f32[128,128]{1,0:T(8,128)S(1)}, f32[128,128]{1,0:T(8,128)S(1)}, u32[]{:S(2)}, u32[]{:S(2)}) collective-permute-start(f32[128,128]{1,0:T(8,128)S(1)} %get-tuple-element.101), channel_id=1, source_target_pairs={{2,0},{3,1},{4,2},{5,3},{6,4},{7,5},{10,8},{11,9},{12,10},{13,11},... | collective-permute-start | bytes 196616 | tf_op jit(solution)/shard_map/ppermute | solution.py:495
  88.0 28.6 %copy-start.1 = (f32[4,128,128]{2,1,0:T(8,128)S(1)}, f32[4,128,128]{2,1,0:T(8,128)}, u32[]{:S(2)}) copy-start(f32[4,128,128]{2,1,0:T(8,128)} %param.13) | copy-start | bytes 786436
  88.0 28.6 %copy-start.4 = (f32[512,128]{1,0:T(8,128)S(1)}, f32[512,128]{1,0:T(8,128)}, u32[]{:S(2)}) copy-start(f32[512,128]{1,0:T(8,128)} %copy-done.3) | copy-start | bytes 786436

commit v12 on v11

--- a/solution.py
+++ b/solution.py
@@ -495,6 +495,15 @@
     return lax.ppermute(v, axis, pairs) if pairs else jnp.zeros_like(v)
 
 
+def swapped(a, b, axis):
+    count = lax.axis_size(axis)
+    found = []
+    for v, odd in ((a, 0), (b, 1)):
+        pairs = [p for i in range(odd, count - 1, 2) for p in ((i, i + 1), (i + 1, i))]
+        found.append(lax.ppermute(v, axis, pairs) if pairs else jnp.zeros_like(v))
+    return found
+
+
 def exchanged(v):
     lines = v.reshape(v.shape[0], 1, v.shape[1])
     return lax.all_to_all(lines, ("gx", "gy"), split_axis=0, concat_axis=0, tiled=True).reshape(v.shape)
@@ -554,7 +563,9 @@
         pack_y_kernel,
         [tall, sized(inner, width), flat_edge, sized(2 * EDGE, inner), sized(EDGE, total), y_edge, y_edge],
         [xz, mats, source, after, before], "pack_y")
-    before, after = shifted(yhigh, "gy", 1), shifted(ylow, "gy", -1)
+    even = lax.axis_index("gy") % 2 == 0
+    one, two = swapped(jnp.where(even, yhigh, ylow), jnp.where(even, ylow, yhigh), "gy")
+    before, after = jnp.where(even, two, one), jnp.where(even, one, two)
     blocks = -(-inner // LANES)
     [around] = call(
         pack_z_kernel, [sized(inner + 4 * EDGE * blocks, width)], [full, heat_sides, before, after], "pack_z")

time: 118 us -> 118 us (level)
    ppermute x0 -> x2, starting transfers between devices: none -> 6.82 us  [swapped(): found.append(lax.ppermute(v, axis, pairs) if pairs else jnp.zeros_like(v))]
    ppermute x12 -> x10, starting transfers between devices: 36.7 us -> 29.9 us  [shifted(): return lax.ppermute(v, axis, pairs) if pairs else jnp.zeros_like(v)]
    ppermute x12 -> x10, waiting for transfers between devices: 18.5 us -> 14.5 us  [shifted(): return lax.ppermute(v, axis, pairs) if pairs else jnp.zeros_like(v)]
    ppermute x0 -> x2, waiting for transfers between devices: none -> 2.93 us  [swapped(): found.append(lax.ppermute(v, axis, pairs) if pairs else jnp.zeros_like(v))]
where the time goes in v12:
time: 118 us
  starting transfers between devices  48.4 us (41%)
  blocking collectives  28.5 us (24%)
  Pallas kernels  21.5 us (18%)
  waiting for transfers between devices  17.4 us (15%)
    ppermute x10, starting transfers between devices, shifted(): return lax.ppermute(v, axis, pairs) if pairs else jnp.zeros_like(v)  29.9 us
    all_to_all x1, blocking collectives, exchanged(): lax.all_to_all(lines, ('gx', 'gy'), split_axis=0, concat_axis=0, tiled=True)  28.5 us
    pallas_call x13, Pallas kernels, call(): pl.pallas_call(kernel, out_shape=[jax.ShapeDtypeStruct(s, t) for s, t in...  21.5 us
    ppermute x10, waiting for transfers between devices, shifted(): return lax.ppermute(v, axis, pairs) if pairs else jnp.zeros_like(v)  14.5 us
    all_to_all x1, starting transfers between devices, exchanged(): lax.all_to_all(lines, ('gx', 'gy'), split_axis=0, concat_axis=0, tiled=True)  11.6 us
    ppermute x2, starting transfers between devices, swapped(): found.append(lax.ppermute(v, axis, pairs) if pairs else jnp.zeros_like(v))  6.82 us
    ppermute x2, waiting for transfers between devices, swapped(): found.append(lax.ppermute(v, axis, pairs) if pairs else jnp.zeros_like(v))  2.93 us
  transfers between devices with their start and end apart: 13, of which 3 were waited for; matrix products, arithmetic and copies ran while one was open for 0% of the time, Pallas kernels for 13%

profile of v12, /device:TPU:1, one launch (start us, length us, event | category | flops | bytes accessed | tf_op | source)
XLA Modules:
  0.0 117.5 jit_solution(60300596061158083)
XLA Ops:
  0.6 0.0 copy-start.2
  0.6 0.0 copy-start.6
  0.7 0.0 copy-start
  0.7 0.0 copy-start.5
  0.7 3.0 %dispatch.1 = f32[1088,128]{1,0:T(8,128)} custom-call(f32[3,512,128]{2,1,0:T(8,128)} %bitcast.21, f32[512,128]{1,0:T(8,128)} %bitcast.32, f32[512,128]{1,0:T(8,128)} %bitcast.24, s32[1,512]{1,0:T(1,128)} %bitcast.28, s32[1,512]{1,0:T(1,128)} %bitcast.33, s32[1,512]{1,0:T(1,128)} %bitcast.34), custom_call_target="tpu_custom_call" | custom-call | flops 100000000 | bytes 1873920 | tf_op jit(solution)/shard_map/dispatch/pallas_call | solution.py:71
  3.7 11.6 %all-to-all-start = ((f32[1088,1,128]{2,1,0:T(1,128)}), f32[1088,1,128]{2,1,0:T(1,128)S(1)}, u32[]{:S(2)}, u32[]{:S(2)}) async-start(f32[1088,1,128]{2,1,0:T(1,128)} %bitcast.31), calls=%async_computation | async-start | bytes 1114112 | tf_op jit(solution)/shard_map/all_to_all | solution.py:509
  15.4 4.0 %collective-permute-start.1 = (f32[520,128]{1,0:T(8,128)S(1)}, f32[520,128]{1,0:T(8,128)S(1)}, u32[]{:S(2)}, u32[]{:S(2)}) collective-permute-start(f32[520,128]{1,0:T(8,128)S(1)} %get-tuple-element.59.own), channel_id=1, source_target_pairs={{0,1},{1,2},{2,3},{3,4},{4,5},{5,6},{6,7},{8,9},{9,10},{10,11},{11... | collective-permute-start | bytes 798728 | tf_op jit(solution)/shard_map/ppermute | solution.py:495
  19.5 1.3 %collective-permute-start.2 = (f32[520,128]{1,0:T(8,128)S(1)}, f32[520,128]{1,0:T(8,128)S(1)}, u32[]{:S(2)}, u32[]{:S(2)}) collective-permute-start(f32[520,128]{1,0:T(8,128)S(1)} %get-tuple-element.59.own), channel_id=1, source_target_pairs={{1,0},{2,1},{3,2},{4,3},{5,4},{6,5},{7,6},{9,8},{10,9},{11,10},{12... | collective-permute-start | bytes 798728 | tf_op jit(solution)/shard_map/ppermute | solution.py:495
  20.8 6.4 %collective-permute-start = (f32[264,128]{1,0:T(8,128)S(1)}, f32[264,128]{1,0:T(8,128)S(1)}, u32[]{:S(2)}, u32[]{:S(2)}) collective-permute-start(f32[264,128]{1,0:T(8,128)S(1)} %get-tuple-element.58), channel_id=1, source_target_pairs={{0,2},{1,3},{2,4},{3,5},{4,6},{5,7},{8,10},{9,11},{10,12},{11,13},... | collective-permute-start | bytes 405512 | tf_op jit(solution)/shard_map/ppermute | solution.py:495
  27.2 1.3 %collective-permute-start.3 = (f32[264,128]{1,0:T(8,128)S(1)}, f32[264,128]{1,0:T(8,128)S(1)}, u32[]{:S(2)}, u32[]{:S(2)}) collective-permute-start(f32[264,128]{1,0:T(8,128)S(1)} %get-tuple-element.60), channel_id=1, source_target_pairs={{2,0},{3,1},{4,2},{5,3},{6,4},{7,5},{10,8},{11,9},{12,10},{13,11},... | collective-permute-start | bytes 405512 | tf_op jit(solution)/shard_map/ppermute | solution.py:495
  28.5 1.1 gain.1
  29.6 0.0 copy-start.3
  29.7 0.7 copy-done.3
  30.3 0.0 collective-permute-done.low2
  30.4 11.1 %collective-permute-done.3.high2 = f32[264,128]{1,0:T(8,128)S(1)} collective-permute-done((f32[264,128]{1,0:T(8,128)S(1)}, f32[264,128]{1,0:T(8,128)S(1)}, u32[]{:S(2)}, u32[]{:S(2)}) %collective-permute-start.3) | collective-permute-done | bytes 135200 | tf_op jit(solution)/shard_map/ppermute | solution.py:495
  41.4 0.0 collective-permute-done.1.low
  41.4 0.0 collective-permute-done.2.high
  41.4 0.1 start_x.1
  41.5 0.0 all-to-all-done
  41.5 0.7 combine.1
  42.3 3.3 %collective-permute-start.4 = (f32[176,128]{1,0:T(8,128)S(1)}, f32[176,128]{1,0:T(8,128)S(1)}, u32[]{:S(2)}, u32[]{:S(2)}) collective-permute-start(f32[176,128]{1,0:T(8,128)S(1)} %get-tuple-element.71), channel_id=1, source_target_pairs={{0,32},{32,64},{64,96},{96,128},{128,160},{160,192},{192,224},{224... | collective-permute-start | bytes 270344 | tf_op jit(solution)/shard_map/ppermute | solution.py:495
  45.6 1.3 %collective-permute-start.5 = (f32[176,128]{1,0:T(8,128)S(1)}, f32[176,128]{1,0:T(8,128)S(1)}, u32[]{:S(2)}, u32[]{:S(2)}) collective-permute-start(f32[176,128]{1,0:T(8,128)S(1)} %get-tuple-element.72), channel_id=1, source_target_pairs={{32,0},{64,32},{96,64},{128,96},{160,128},{192,160},{224,192},{256... | collective-permute-start | bytes 270344 | tf_op jit(solution)/shard_map/ppermute | solution.py:495
  46.9 0.5 ids.1.hot
  47.4 0.0 collective-permute-done.4.before
  47.5 3.4 %collective-permute-done.5.after = f32[176,128]{1,0:T(8,128)S(1)} collective-permute-done((f32[176,128]{1,0:T(8,128)S(1)}, f32[176,128]{1,0:T(8,128)S(1)}, u32[]{:S(2)}, u32[]{:S(2)}) %collective-permute-start.5) | collective-permute-done | bytes 90144 | tf_op jit(solution)/shard_map/ppermute | solution.py:495
  50.9 0.7 pack_y.1
  51.6 0.0 copy-start.7
  51.6 0.0 copy-start.8
  51.6 0.0 copy-start.9
  51.6 3.8 %collective-permute-start.7 = (f32[8,3072]{1,0:T(8,128)S(1)}, f32[8,3072]{1,0:T(8,128)S(1)}, u32[]{:S(2)}, u32[]{:S(2)}) collective-permute-start(f32[8,3072]{1,0:T(8,128)S(1)} %get-tuple-element.115), channel_id=1, source_target_pairs={{0,8},{8,0},{16,24},{24,16},{1,9},{9,1},{17,25},{25,17},{2,10},{10... | collective-permute-start | bytes 294920 | tf_op jit(solution)/shard_map/ppermute | solution.py:503
  55.5 3.0 %collective-permute-start.6 = (f32[8,3072]{1,0:T(8,128)S(1)}, f32[8,3072]{1,0:T(8,128)S(1)}, u32[]{:S(2)}, u32[]{:S(2)}) collective-permute-start(f32[8,3072]{1,0:T(8,128)S(1)} %get-tuple-element.116), channel_id=1, source_target_pairs={{8,16},{16,8},{9,17},{17,9},{10,18},{18,10},{11,19},{19,11},{12,20... | collective-permute-start | bytes 294920 | tf_op jit(solution)/shard_map/ppermute | solution.py:503
  58.5 0.0 collective-permute-done.7
  58.5 2.9 %collective-permute-done.6 = f32[8,3072]{1,0:T(8,128)S(1)} collective-permute-done((f32[8,3072]{1,0:T(8,128)S(1)}, f32[8,3072]{1,0:T(8,128)S(1)}, u32[]{:S(2)}, u32[]{:S(2)}) %collective-permute-start.6) | collective-permute-done | bytes 98336 | tf_op jit(solution)/shard_map/ppermute | solution.py:503
  61.5 1.3 %collective-permute-start.8 = (f32[736,128]{1,0:T(8,128)S(1)}, f32[736,128]{1,0:T(8,128)S(1)}, u32[]{:S(2)}, u32[]{:S(2)}) collective-permute-start(f32[736,128]{1,0:T(8,128)S(1)} %pack_z.1.own), channel_id=1, source_target_pairs={{0,1},{1,2},{2,3},{3,4},{4,5},{5,6},{6,7},{8,9},{9,10},{10,11},{11... | collective-permute-start | bytes 1130504 | tf_op jit(solution)/shard_map/ppermute | solution.py:495
  62.8 1.3 %collective-permute-start.9 = (f32[736,128]{1,0:T(8,128)S(1)}, f32[736,128]{1,0:T(8,128)S(1)}, u32[]{:S(2)}, u32[]{:S(2)}) collective-permute-start(f32[736,128]{1,0:T(8,128)S(1)} %pack_z.1.own), channel_id=1, source_target_pairs={{1,0},{2,1},{3,2},{4,3},{5,4},{6,5},{7,6},{9,8},{10,9},{11,10},{12... | collective-permute-start | bytes 1130504 | tf_op jit(solution)/shard_map/ppermute | solution.py:495
  64.1 4.0 %weights.1 = (f32[16,144,128]{2,1,0:T(8,128)S(1)}, f32[16,160,128]{2,1,0:T(8,128)S(1)}, f32[16,144,128]{2,1,0:T(8,128)S(1)}, f32[16,144,128]{2,1,0:T(8,128)S(1)}...) custom-call(f32[8]{0:T(128)S(1)} %copy-done.7, f32[8]{0:T(128)S(1)} %copy-done.8, ...), custom_call_target="tpu_custom_call" | custom-call | flops 1000000000 | bytes 11591776 | tf_op jit(solution)/shard_map/weights/pallas_call | solution.py:71
  68.1 8.4 %collective-permute-start.10 = (f32[128,128]{1,0:T(8,128)S(1)}, f32[128,128]{1,0:T(8,128)S(1)}, u32[]{:S(2)}, u32[]{:S(2)}) collective-permute-start(f32[128,128]{1,0:T(8,128)S(1)} %get-tuple-element.100), channel_id=1, source_target_pairs={{0,2},{1,3},{2,4},{3,5},{4,6},{5,7},{8,10},{9,11},{10,12},{11,13},... | collective-permute-start | bytes 196616 | tf_op jit(solution)/shard_map/ppermute | solution.py:495
  76.6 1.3 %collective-permute-start.11 = (f32[128,128]{1,0:T(8,128)S(1)}, f32[128,128]{1,0:T(8,128)S(1)}, u32[]{:S(2)}, u32[]{:S(2)}) collective-permute-start(f32[128,128]{1,0:T(8,128)S(1)} %get-tuple-element.101), channel_id=1, source_target_pairs={{2,0},{3,1},{4,2},{5,3},{6,4},{7,5},{10,8},{11,9},{12,10},{13,11},... | collective-permute-start | bytes 196616 | tf_op jit(solution)/shard_map/ppermute | solution.py:495
  77.9 0.0 collective-permute-done.8.low
  77.9 0.0 collective-permute-done.9.high
  77.9 9.1 %sweeps.1 = (f32[512,128]{1,0:T(8,128)S(1)}, f32[256,128]{1,0:T(8,128)S(1)}) custom-call(f32[16,160,128]{2,1,0:T(8,128)S(1)} %get-tuple-element.75.xm, f32[16,144,128]{2,1,0:T(8,128)S(1)} %get-tuple-element.89.wz, f32[16,160,128]{2,1,0:T(8,128)S(1)} %get-tuple-element.90.wx, f32[16,144,128]{2,1,0:T(8,128)S(1)} %get-tuple-element.91.wy, ...), custom_call_target="tpu_custom_call" | custom-call | flops 100000000 | bytes 12697600 | tf_op jit(solution)/shard_map/sweeps/pallas_call | solution.py:71
  87.0 0.0 collective-permute-done.10.low2
  87.0 0.0 collective-permute-done.11.high2
  87.0 0.0 copy-start.1
  87.0 0.0 copy-start.4
  87.0 0.8 reply.1
  87.8 28.5 %all_to_all.10 = f32[1024,1,128]{2,1,0:T(1,128)S(1)} all-to-all(f32[1024,1,128]{2,1,0:T(1,128)S(1)} %bitcast.26), channel_id=1, replica_groups=mesh['gx'=16,'gy'=4,'gz'=8] {'gx','gy'}, dimensions={0} | all-to-all | bytes 1048576 | tf_op jit(solution)/shard_map/all_to_all | solution.py:509
  116.3 1.2 %finish.1 = (f32[512,128]{1,0:T(8,128)}, f32[512,128]{1,0:T(8,128)}) custom-call(f32[1024,128]{1,0:T(8,128)S(1)} %bitcast.23, bf16[512,1024]{1,0:T(8,128)(2,1)S(1)} %get-tuple-element.109.hot, f32[512,128]{1,0:T(8,128)S(1)} %copy-done.4, f32[512,128]{1,0:T(8,128)S(1)} %bitcast.25), custom_call_target="tpu_custom_call" | custom-call | flops 100000000 | bytes 2621440 | tf_op jit(solution)/shard_map/finish/pallas_call | solution.py:71
  (14 shorter events, 0.1 us)
Async XLA Ops:
  0.6 14.7 %copy-start.2 = (f32[4,128,128]{2,1,0:T(8,128)S(1)}, f32[4,128,128]{2,1,0:T(8,128)}, u32[]{:S(2)}) copy-start(f32[4,128,128]{2,1,0:T(8,128)} %param.14) | copy-start | bytes 786436
  0.6 14.7 %copy-start.6 = (s32[1,1,1,512]{3,2,1,0:T(1,128)S(1)}, s32[1,1,1,512]{3,2,1,0:T(1,128)}, u32[]{:S(2)}) copy-start(s32[1,1,1,512]{3,2,1,0:T(1,128)} %param.18) | copy-start | bytes 6148
  0.7 27.8 %copy-start = (f32[3,4,128,128]{3,2,1,0:T(8,128)S(1)}, f32[3,4,128,128]{3,2,1,0:T(8,128)}, u32[]{:S(2)}) copy-start(f32[3,4,128,128]{3,2,1,0:T(8,128)} %param.11) | copy-start | bytes 2359300
  0.7 27.8 %copy-start.5 = (s32[1,1,1,512,1]{3,4,2,1,0:T(1,128)S(1)}, s32[1,1,1,512,1]{3,4,2,1,0:T(1,128)}, u32[]{:S(2)}) copy-start(s32[1,1,1,512,1]{3,4,2,1,0:T(1,128)} %param.15) | copy-start | bytes 6148
  3.7 37.8 %all-to-all-start = ((f32[1088,1,128]{2,1,0:T(1,128)}), f32[1088,1,128]{2,1,0:T(1,128)S(1)}, u32[]{:S(2)}, u32[]{:S(2)}) async-start(f32[1088,1,128]{2,1,0:T(1,128)} %bitcast.31), calls=%async_computation | async-start | bytes 1114112 | tf_op jit(solution)/shard_map/all_to_all | solution.py:509
  15.4 26.0 %collective-permute-start.1 = (f32[520,128]{1,0:T(8,128)S(1)}, f32[520,128]{1,0:T(8,128)S(1)}, u32[]{:S(2)}, u32[]{:S(2)}) collective-permute-start(f32[520,128]{1,0:T(8,128)S(1)} %get-tuple-element.59.own), channel_id=1, source_target_pairs={{0,1},{1,2},{2,3},{3,4},{4,5},{5,6},{6,7},{8,9},{9,10},{10,11},{11... | collective-permute-start | bytes 798728 | tf_op jit(solution)/shard_map/ppermute | solution.py:495
  19.5 22.0 %collective-permute-start.2 = (f32[520,128]{1,0:T(8,128)S(1)}, f32[520,128]{1,0:T(8,128)S(1)}, u32[]{:S(2)}, u32[]{:S(2)}) collective-permute-start(f32[520,128]{1,0:T(8,128)S(1)} %get-tuple-element.59.own), channel_id=1, source_target_pairs={{1,0},{2,1},{3,2},{4,3},{5,4},{6,5},{7,6},{9,8},{10,9},{11,10},{12... | collective-permute-start | bytes 798728 | tf_op jit(solution)/shard_map/ppermute | solution.py:495
  20.8 9.6 %collective-permute-start = (f32[264,128]{1,0:T(8,128)S(1)}, f32[264,128]{1,0:T(8,128)S(1)}, u32[]{:S(2)}, u32[]{:S(2)}) collective-permute-start(f32[264,128]{1,0:T(8,128)S(1)} %get-tuple-element.58), channel_id=1, source_target_pairs={{0,2},{1,3},{2,4},{3,5},{4,6},{5,7},{8,10},{9,11},{10,12},{11,13},... | collective-permute-start | bytes 405512 | tf_op jit(solution)/shard_map/ppermute | solution.py:495
  27.2 14.2 %collective-permute-start.3 = (f32[264,128]{1,0:T(8,128)S(1)}, f32[264,128]{1,0:T(8,128)S(1)}, u32[]{:S(2)}, u32[]{:S(2)}) collective-permute-start(f32[264,128]{1,0:T(8,128)S(1)} %get-tuple-element.60), channel_id=1, source_target_pairs={{2,0},{3,1},{4,2},{5,3},{6,4},{7,5},{10,8},{11,9},{12,10},{13,11},... | collective-permute-start | bytes 405512 | tf_op jit(solution)/shard_map/ppermute | solution.py:495
  29.6 0.7 copy-start.3
  42.3 5.2 %collective-permute-start.4 = (f32[176,128]{1,0:T(8,128)S(1)}, f32[176,128]{1,0:T(8,128)S(1)}, u32[]{:S(2)}, u32[]{:S(2)}) collective-permute-start(f32[176,128]{1,0:T(8,128)S(1)} %get-tuple-element.71), channel_id=1, source_target_pairs={{0,32},{32,64},{64,96},{96,128},{128,160},{160,192},{192,224},{224... | collective-permute-start | bytes 270344 | tf_op jit(solution)/shard_map/ppermute | solution.py:495
  45.6 5.3 %collective-permute-start.5 = (f32[176,128]{1,0:T(8,128)S(1)}, f32[176,128]{1,0:T(8,128)S(1)}, u32[]{:S(2)}, u32[]{:S(2)}) collective-permute-start(f32[176,128]{1,0:T(8,128)S(1)} %get-tuple-element.72), channel_id=1, source_target_pairs={{32,0},{64,32},{96,64},{128,96},{160,128},{192,160},{224,192},{256... | collective-permute-start | bytes 270344 | tf_op jit(solution)/shard_map/ppermute | solution.py:495
  51.6 12.5 %copy-start.7 = (f32[8]{0:T(128)S(1)}, f32[8]{0:T(128)}, u32[]{:S(2)}) copy-start(f32[8]{0:T(128)} %base.1) | copy-start | bytes 100
  51.6 12.5 %copy-start.8 = (f32[8]{0:T(128)S(1)}, f32[8]{0:T(128)}, u32[]{:S(2)}) copy-start(f32[8]{0:T(128)} %soft.1) | copy-start | bytes 100
  51.6 12.5 %copy-start.9 = (f32[8]{0:T(128)S(1)}, f32[8]{0:T(128)}, u32[]{:S(2)}) copy-start(f32[8]{0:T(128)} %heat.1) | copy-start | bytes 100
  51.6 6.8 %collective-permute-start.7 = (f32[8,3072]{1,0:T(8,128)S(1)}, f32[8,3072]{1,0:T(8,128)S(1)}, u32[]{:S(2)}, u32[]{:S(2)}) collective-permute-start(f32[8,3072]{1,0:T(8,128)S(1)} %get-tuple-element.115), channel_id=1, source_target_pairs={{0,8},{8,0},{16,24},{24,16},{1,9},{9,1},{17,25},{25,17},{2,10},{10... | collective-permute-start | bytes 294920 | tf_op jit(solution)/shard_map/ppermute | solution.py:503
  55.5 5.9 %collective-permute-start.6 = (f32[8,3072]{1,0:T(8,128)S(1)}, f32[8,3072]{1,0:T(8,128)S(1)}, u32[]{:S(2)}, u32[]{:S(2)}) collective-permute-start(f32[8,3072]{1,0:T(8,128)S(1)} %get-tuple-element.116), channel_id=1, source_target_pairs={{8,16},{16,8},{9,17},{17,9},{10,18},{18,10},{11,19},{19,11},{12,20... | collective-permute-start | bytes 294920 | tf_op jit(solution)/shard_map/ppermute | solution.py:503
  61.5 16.4 %collective-permute-start.8 = (f32[736,128]{1,0:T(8,128)S(1)}, f32[736,128]{1,0:T(8,128)S(1)}, u32[]{:S(2)}, u32[]{:S(2)}) collective-permute-start(f32[736,128]{1,0:T(8,128)S(1)} %pack_z.1.own), channel_id=1, source_target_pairs={{0,1},{1,2},{2,3},{3,4},{4,5},{5,6},{6,7},{8,9},{9,10},{10,11},{11... | collective-permute-start | bytes 1130504 | tf_op jit(solution)/shard_map/ppermute | solution.py:495
  62.8 15.1 %collective-permute-start.9 = (f32[736,128]{1,0:T(8,128)S(1)}, f32[736,128]{1,0:T(8,128)S(1)}, u32[]{:S(2)}, u32[]{:S(2)}) collective-permute-start(f32[736,128]{1,0:T(8,128)S(1)} %pack_z.1.own), channel_id=1, source_target_pairs={{1,0},{2,1},{3,2},{4,3},{5,4},{6,5},{7,6},{9,8},{10,9},{11,10},{12... | collective-permute-start | bytes 1130504 | tf_op jit(solution)/shard_map/ppermute | solution.py:495
  68.1 18.8 %collective-permute-start.10 = (f32[128,128]{1,0:T(8,128)S(1)}, f32[128,128]{1,0:T(8,128)S(1)}, u32[]{:S(2)}, u32[]{:S(2)}) collective-permute-start(f32[128,128]{1,0:T(8,128)S(1)} %get-tuple-element.100), channel_id=1, source_target_pairs={{0,2},{1,3},{2,4},{3,5},{4,6},{5,7},{8,10},{9,11},{10,12},{11,13},... | collective-permute-start | bytes 196616 | tf_op jit(solution)/shard_map/ppermute | solution.py:495
  76.6 10.4 %collective-permute-start.11 = (f32[128,128]{1,0:T(8,128)S(1)}, f32[128,128]{1,0:T(8,128)S(1)}, u32[]{:S(2)}, u32[]{:S(2)}) collective-permute-start(f32[128,128]{1,0:T(8,128)S(1)} %get-tuple-element.101), channel_id=1, source_target_pairs={{2,0},{3,1},{4,2},{5,3},{6,4},{7,5},{10,8},{11,9},{12,10},{13,11},... | collective-permute-start | bytes 196616 | tf_op jit(solution)/shard_map/ppermute | solution.py:495
  87.0 29.3 %copy-start.1 = (f32[4,128,128]{2,1,0:T(8,128)S(1)}, f32[4,128,128]{2,1,0:T(8,128)}, u32[]{:S(2)}) copy-start(f32[4,128,128]{2,1,0:T(8,128)} %param.13) | copy-start | bytes 786436
  87.0 29.3 %copy-start.4 = (f32[512,128]{1,0:T(8,128)S(1)}, f32[512,128]{1,0:T(8,128)}, u32[]{:S(2)}) copy-start(f32[512,128]{1,0:T(8,128)} %copy-done.3) | copy-start | bytes 786436

commit v13 on v12

--- a/solution.py
+++ b/solution.py
@@ -422,7 +422,7 @@
         ends[start:stop, s * LANES : (s + 1) * LANES] = dot(
             jnp.concatenate(parts(pair[:, start - s * LANES : stop - s * LANES]), axis=0), place_in, 0, 0)
 
-    piece = 24
+    piece = 48
     first, last = iota((piece, LANES), 1) == 0, iota((piece, LANES), 1) == LANES - 1
     blank = jnp.zeros((EDGE, LANES), F32)
 

time: 118 us -> 118 us (level)
  no operation moved by 1% of the time
where the time goes in v13:
time: 118 us; the launch traced here: 117 us
  starting transfers between devices  48.4 us (41%)
  blocking collectives  28.5 us (24%)
  Pallas kernels  21.3 us (18%)
  waiting for transfers between devices  17.4 us (15%)
    ppermute x10, starting transfers between devices, shifted(): return lax.ppermute(v, axis, pairs) if pairs else jnp.zeros_like(v)  29.9 us
    all_to_all x1, blocking collectives, exchanged(): lax.all_to_all(lines, ('gx', 'gy'), split_axis=0, concat_axis=0, tiled=True)  28.5 us
    pallas_call x13, Pallas kernels, call(): pl.pallas_call(kernel, out_shape=[jax.ShapeDtypeStruct(s, t) for s, t in...  21.3 us
    ppermute x10, waiting for transfers between devices, shifted(): return lax.ppermute(v, axis, pairs) if pairs else jnp.zeros_like(v)  14.5 us
    all_to_all x1, starting transfers between devices, exchanged(): lax.all_to_all(lines, ('gx', 'gy'), split_axis=0, concat_axis=0, tiled=True)  11.6 us
    ppermute x2, starting transfers between devices, swapped(): found.append(lax.ppermute(v, axis, pairs) if pairs else jnp.zeros_like(v))  6.82 us
    ppermute x2, waiting for transfers between devices, swapped(): found.append(lax.ppermute(v, axis, pairs) if pairs else jnp.zeros_like(v))  2.93 us
  transfers between devices with their start and end apart: 13, of which 3 were waited for; matrix products, arithmetic and copies ran while one was open for 0% of the time, Pallas kernels for 13%

profile of v13, /device:TPU:1, one launch (start us, length us, event | category | flops | bytes accessed | tf_op | source)
XLA Modules:
  0.0 117.4 jit_solution(11797667150982555247)
XLA Ops:
  0.6 0.0 copy-start.2
  0.7 3.0 %dispatch.1 = f32[1088,128]{1,0:T(8,128)} custom-call(f32[3,512,128]{2,1,0:T(8,128)} %bitcast.21, f32[512,128]{1,0:T(8,128)} %bitcast.32, f32[512,128]{1,0:T(8,128)} %bitcast.24, s32[1,512]{1,0:T(1,128)} %bitcast.28, s32[1,512]{1,0:T(1,128)} %bitcast.33, s32[1,512]{1,0:T(1,128)} %bitcast.34), custom_call_target="tpu_custom_call" | custom-call | flops 100000000 | bytes 1873920 | tf_op jit(solution)/shard_map/dispatch/pallas_call | solution.py:71
  3.7 11.6 %all-to-all-start = ((f32[1088,1,128]{2,1,0:T(1,128)}), f32[1088,1,128]{2,1,0:T(1,128)S(1)}, u32[]{:S(2)}, u32[]{:S(2)}) async-start(f32[1088,1,128]{2,1,0:T(1,128)} %bitcast.31), calls=%async_computation | async-start | bytes 1114112 | tf_op jit(solution)/shard_map/all_to_all | solution.py:509
  15.4 4.0 %collective-permute-start.1 = (f32[520,128]{1,0:T(8,128)S(1)}, f32[520,128]{1,0:T(8,128)S(1)}, u32[]{:S(2)}, u32[]{:S(2)}) collective-permute-start(f32[520,128]{1,0:T(8,128)S(1)} %get-tuple-element.59.own), channel_id=1, source_target_pairs={{0,1},{1,2},{2,3},{3,4},{4,5},{5,6},{6,7},{8,9},{9,10},{10,11},{11... | collective-permute-start | bytes 798728 | tf_op jit(solution)/shard_map/ppermute | solution.py:495
  19.5 1.3 %collective-permute-start.2 = (f32[520,128]{1,0:T(8,128)S(1)}, f32[520,128]{1,0:T(8,128)S(1)}, u32[]{:S(2)}, u32[]{:S(2)}) collective-permute-start(f32[520,128]{1,0:T(8,128)S(1)} %get-tuple-element.59.own), channel_id=1, source_target_pairs={{1,0},{2,1},{3,2},{4,3},{5,4},{6,5},{7,6},{9,8},{10,9},{11,10},{12... | collective-permute-start | bytes 798728 | tf_op jit(solution)/shard_map/ppermute | solution.py:495
  20.8 6.4 %collective-permute-start = (f32[264,128]{1,0:T(8,128)S(1)}, f32[264,128]{1,0:T(8,128)S(1)}, u32[]{:S(2)}, u32[]{:S(2)}) collective-permute-start(f32[264,128]{1,0:T(8,128)S(1)} %get-tuple-element.58), channel_id=1, source_target_pairs={{0,2},{1,3},{2,4},{3,5},{4,6},{5,7},{8,10},{9,11},{10,12},{11,13},... | collective-permute-start | bytes 405512 | tf_op jit(solution)/shard_map/ppermute | solution.py:495
  27.2 1.3 %collective-permute-start.3 = (f32[264,128]{1,0:T(8,128)S(1)}, f32[264,128]{1,0:T(8,128)S(1)}, u32[]{:S(2)}, u32[]{:S(2)}) collective-permute-start(f32[264,128]{1,0:T(8,128)S(1)} %get-tuple-element.60), channel_id=1, source_target_pairs={{2,0},{3,1},{4,2},{5,3},{6,4},{7,5},{10,8},{11,9},{12,10},{13,11},... | collective-permute-start | bytes 405512 | tf_op jit(solution)/shard_map/ppermute | solution.py:495
  28.5 0.0 copy-done
  28.5 0.0 copy-done.5
  28.5 1.1 gain.1
  29.6 0.0 copy-start.3
  29.7 0.7 copy-done.3
  30.3 0.0 collective-permute-done.low2
  30.4 11.1 %collective-permute-done.3.high2 = f32[264,128]{1,0:T(8,128)S(1)} collective-permute-done((f32[264,128]{1,0:T(8,128)S(1)}, f32[264,128]{1,0:T(8,128)S(1)}, u32[]{:S(2)}, u32[]{:S(2)}) %collective-permute-start.3) | collective-permute-done | bytes 135200 | tf_op jit(solution)/shard_map/ppermute | solution.py:495
  41.4 0.0 collective-permute-done.1.low
  41.4 0.0 collective-permute-done.2.high
  41.4 0.1 start_x.1
  41.5 0.0 all-to-all-done
  41.5 0.7 combine.1
  42.3 3.3 %collective-permute-start.4 = (f32[176,128]{1,0:T(8,128)S(1)}, f32[176,128]{1,0:T(8,128)S(1)}, u32[]{:S(2)}, u32[]{:S(2)}) collective-permute-start(f32[176,128]{1,0:T(8,128)S(1)} %get-tuple-element.71), channel_id=1, source_target_pairs={{0,32},{32,64},{64,96},{96,128},{128,160},{160,192},{192,224},{224... | collective-permute-start | bytes 270344 | tf_op jit(solution)/shard_map/ppermute | solution.py:495
  45.6 1.3 %collective-permute-start.5 = (f32[176,128]{1,0:T(8,128)S(1)}, f32[176,128]{1,0:T(8,128)S(1)}, u32[]{:S(2)}, u32[]{:S(2)}) collective-permute-start(f32[176,128]{1,0:T(8,128)S(1)} %get-tuple-element.72), channel_id=1, source_target_pairs={{32,0},{64,32},{96,64},{128,96},{160,128},{192,160},{224,192},{256... | collective-permute-start | bytes 270344 | tf_op jit(solution)/shard_map/ppermute | solution.py:495
  46.9 0.5 ids.1.hot
  47.4 0.0 collective-permute-done.4.before
  47.5 3.4 %collective-permute-done.5.after = f32[176,128]{1,0:T(8,128)S(1)} collective-permute-done((f32[176,128]{1,0:T(8,128)S(1)}, f32[176,128]{1,0:T(8,128)S(1)}, u32[]{:S(2)}, u32[]{:S(2)}) %collective-permute-start.5) | collective-permute-done | bytes 90144 | tf_op jit(solution)/shard_map/ppermute | solution.py:495
  50.9 0.7 pack_y.1
  51.6 0.0 copy-start.7
  51.6 0.0 copy-start.8
  51.6 0.0 copy-start.9
  51.6 3.8 %collective-permute-start.7 = (f32[8,3072]{1,0:T(8,128)S(1)}, f32[8,3072]{1,0:T(8,128)S(1)}, u32[]{:S(2)}, u32[]{:S(2)}) collective-permute-start(f32[8,3072]{1,0:T(8,128)S(1)} %get-tuple-element.115), channel_id=1, source_target_pairs={{0,8},{8,0},{16,24},{24,16},{1,9},{9,1},{17,25},{25,17},{2,10},{10... | collective-permute-start | bytes 294920 | tf_op jit(solution)/shard_map/ppermute | solution.py:503
  55.5 3.0 %collective-permute-start.6 = (f32[8,3072]{1,0:T(8,128)S(1)}, f32[8,3072]{1,0:T(8,128)S(1)}, u32[]{:S(2)}, u32[]{:S(2)}) collective-permute-start(f32[8,3072]{1,0:T(8,128)S(1)} %get-tuple-element.116), channel_id=1, source_target_pairs={{8,16},{16,8},{9,17},{17,9},{10,18},{18,10},{11,19},{19,11},{12,20... | collective-permute-start | bytes 294920 | tf_op jit(solution)/shard_map/ppermute | solution.py:503
  58.5 0.0 collective-permute-done.7
  58.5 2.9 %collective-permute-done.6 = f32[8,3072]{1,0:T(8,128)S(1)} collective-permute-done((f32[8,3072]{1,0:T(8,128)S(1)}, f32[8,3072]{1,0:T(8,128)S(1)}, u32[]{:S(2)}, u32[]{:S(2)}) %collective-permute-start.6) | collective-permute-done | bytes 98336 | tf_op jit(solution)/shard_map/ppermute | solution.py:503
  61.5 1.3 %collective-permute-start.8 = (f32[736,128]{1,0:T(8,128)S(1)}, f32[736,128]{1,0:T(8,128)S(1)}, u32[]{:S(2)}, u32[]{:S(2)}) collective-permute-start(f32[736,128]{1,0:T(8,128)S(1)} %pack_z.1.own), channel_id=1, source_target_pairs={{0,1},{1,2},{2,3},{3,4},{4,5},{5,6},{6,7},{8,9},{9,10},{10,11},{11... | collective-permute-start | bytes 1130504 | tf_op jit(solution)/shard_map/ppermute | solution.py:495
  62.8 1.3 %collective-permute-start.9 = (f32[736,128]{1,0:T(8,128)S(1)}, f32[736,128]{1,0:T(8,128)S(1)}, u32[]{:S(2)}, u32[]{:S(2)}) collective-permute-start(f32[736,128]{1,0:T(8,128)S(1)} %pack_z.1.own), channel_id=1, source_target_pairs={{1,0},{2,1},{3,2},{4,3},{5,4},{6,5},{7,6},{9,8},{10,9},{11,10},{12... | collective-permute-start | bytes 1130504 | tf_op jit(solution)/shard_map/ppermute | solution.py:495
  64.1 4.0 %weights.1 = (f32[16,144,128]{2,1,0:T(8,128)S(1)}, f32[16,160,128]{2,1,0:T(8,128)S(1)}, f32[16,144,128]{2,1,0:T(8,128)S(1)}, f32[16,144,128]{2,1,0:T(8,128)S(1)}...) custom-call(f32[8]{0:T(128)S(1)} %copy-done.7, f32[8]{0:T(128)S(1)} %copy-done.8, ...), custom_call_target="tpu_custom_call" | custom-call | flops 1000000000 | bytes 11591776 | tf_op jit(solution)/shard_map/weights/pallas_call | solution.py:71
  68.1 8.4 %collective-permute-start.10 = (f32[128,128]{1,0:T(8,128)S(1)}, f32[128,128]{1,0:T(8,128)S(1)}, u32[]{:S(2)}, u32[]{:S(2)}) collective-permute-start(f32[128,128]{1,0:T(8,128)S(1)} %get-tuple-element.100), channel_id=1, source_target_pairs={{0,2},{1,3},{2,4},{3,5},{4,6},{5,7},{8,10},{9,11},{10,12},{11,13},... | collective-permute-start | bytes 196616 | tf_op jit(solution)/shard_map/ppermute | solution.py:495
  76.6 1.3 %collective-permute-start.11 = (f32[128,128]{1,0:T(8,128)S(1)}, f32[128,128]{1,0:T(8,128)S(1)}, u32[]{:S(2)}, u32[]{:S(2)}) collective-permute-start(f32[128,128]{1,0:T(8,128)S(1)} %get-tuple-element.101), channel_id=1, source_target_pairs={{2,0},{3,1},{4,2},{5,3},{6,4},{7,5},{10,8},{11,9},{12,10},{13,11},... | collective-permute-start | bytes 196616 | tf_op jit(solution)/shard_map/ppermute | solution.py:495
  77.9 0.0 collective-permute-done.8.low
  77.9 0.0 collective-permute-done.9.high
  77.9 8.9 %sweeps.1 = (f32[512,128]{1,0:T(8,128)S(1)}, f32[256,128]{1,0:T(8,128)S(1)}) custom-call(f32[16,160,128]{2,1,0:T(8,128)S(1)} %get-tuple-element.75.xm, f32[16,144,128]{2,1,0:T(8,128)S(1)} %get-tuple-element.89.wz, f32[16,160,128]{2,1,0:T(8,128)S(1)} %get-tuple-element.90.wx, f32[16,144,128]{2,1,0:T(8,128)S(1)} %get-tuple-element.91.wy, ...), custom_call_target="tpu_custom_call" | custom-call | flops 100000000 | bytes 12697600 | tf_op jit(solution)/shard_map/sweeps/pallas_call | solution.py:71
  86.8 0.0 collective-permute-done.10.low2
  86.8 0.0 collective-permute-done.11.high2
  86.8 0.0 copy-start.1
  86.8 0.0 copy-start.4
  86.8 0.8 reply.1
  87.7 28.5 %all_to_all.10 = f32[1024,1,128]{2,1,0:T(1,128)S(1)} all-to-all(f32[1024,1,128]{2,1,0:T(1,128)S(1)} %bitcast.26), channel_id=1, replica_groups=mesh['gx'=16,'gy'=4,'gz'=8] {'gx','gy'}, dimensions={0} | all-to-all | bytes 1048576 | tf_op jit(solution)/shard_map/all_to_all | solution.py:509
  116.1 0.0 copy-done.1
  116.1 1.2 %finish.1 = (f32[512,128]{1,0:T(8,128)}, f32[512,128]{1,0:T(8,128)}) custom-call(f32[1024,128]{1,0:T(8,128)S(1)} %bitcast.23, bf16[512,1024]{1,0:T(8,128)(2,1)S(1)} %get-tuple-element.109.hot, f32[512,128]{1,0:T(8,128)S(1)} %copy-done.4, f32[512,128]{1,0:T(8,128)S(1)} %bitcast.25), custom_call_target="tpu_custom_call" | custom-call | flops 100000000 | bytes 2621440 | tf_op jit(solution)/shard_map/finish/pallas_call | solution.py:71
  (14 shorter events, 0.1 us)
Async XLA Ops:
  0.6 14.7 %copy-start.2 = (f32[4,128,128]{2,1,0:T(8,128)S(1)}, f32[4,128,128]{2,1,0:T(8,128)}, u32[]{:S(2)}) copy-start(f32[4,128,128]{2,1,0:T(8,128)} %param.14) | copy-start | bytes 786436
  0.6 14.7 %copy-start.6 = (s32[1,1,1,512]{3,2,1,0:T(1,128)S(1)}, s32[1,1,1,512]{3,2,1,0:T(1,128)}, u32[]{:S(2)}) copy-start(s32[1,1,1,512]{3,2,1,0:T(1,128)} %param.18) | copy-start | bytes 6148
  0.7 27.8 %copy-start = (f32[3,4,128,128]{3,2,1,0:T(8,128)S(1)}, f32[3,4,128,128]{3,2,1,0:T(8,128)}, u32[]{:S(2)}) copy-start(f32[3,4,128,128]{3,2,1,0:T(8,128)} %param.11) | copy-start | bytes 2359300
  0.7 27.8 %copy-start.5 = (s32[1,1,1,512,1]{3,4,2,1,0:T(1,128)S(1)}, s32[1,1,1,512,1]{3,4,2,1,0:T(1,128)}, u32[]{:S(2)}) copy-start(s32[1,1,1,512,1]{3,4,2,1,0:T(1,128)} %param.15) | copy-start | bytes 6148
  3.7 37.8 %all-to-all-start = ((f32[1088,1,128]{2,1,0:T(1,128)}), f32[1088,1,128]{2,1,0:T(1,128)S(1)}, u32[]{:S(2)}, u32[]{:S(2)}) async-start(f32[1088,1,128]{2,1,0:T(1,128)} %bitcast.31), calls=%async_computation | async-start | bytes 1114112 | tf_op jit(solution)/shard_map/all_to_all | solution.py:509
  15.4 26.0 %collective-permute-start.1 = (f32[520,128]{1,0:T(8,128)S(1)}, f32[520,128]{1,0:T(8,128)S(1)}, u32[]{:S(2)}, u32[]{:S(2)}) collective-permute-start(f32[520,128]{1,0:T(8,128)S(1)} %get-tuple-element.59.own), channel_id=1, source_target_pairs={{0,1},{1,2},{2,3},{3,4},{4,5},{5,6},{6,7},{8,9},{9,10},{10,11},{11... | collective-permute-start | bytes 798728 | tf_op jit(solution)/shard_map/ppermute | solution.py:495
  19.5 22.0 %collective-permute-start.2 = (f32[520,128]{1,0:T(8,128)S(1)}, f32[520,128]{1,0:T(8,128)S(1)}, u32[]{:S(2)}, u32[]{:S(2)}) collective-permute-start(f32[520,128]{1,0:T(8,128)S(1)} %get-tuple-element.59.own), channel_id=1, source_target_pairs={{1,0},{2,1},{3,2},{4,3},{5,4},{6,5},{7,6},{9,8},{10,9},{11,10},{12... | collective-permute-start | bytes 798728 | tf_op jit(solution)/shard_map/ppermute | solution.py:495
  20.8 9.6 %collective-permute-start = (f32[264,128]{1,0:T(8,128)S(1)}, f32[264,128]{1,0:T(8,128)S(1)}, u32[]{:S(2)}, u32[]{:S(2)}) collective-permute-start(f32[264,128]{1,0:T(8,128)S(1)} %get-tuple-element.58), channel_id=1, source_target_pairs={{0,2},{1,3},{2,4},{3,5},{4,6},{5,7},{8,10},{9,11},{10,12},{11,13},... | collective-permute-start | bytes 405512 | tf_op jit(solution)/shard_map/ppermute | solution.py:495
  27.2 14.2 %collective-permute-start.3 = (f32[264,128]{1,0:T(8,128)S(1)}, f32[264,128]{1,0:T(8,128)S(1)}, u32[]{:S(2)}, u32[]{:S(2)}) collective-permute-start(f32[264,128]{1,0:T(8,128)S(1)} %get-tuple-element.60), channel_id=1, source_target_pairs={{2,0},{3,1},{4,2},{5,3},{6,4},{7,5},{10,8},{11,9},{12,10},{13,11},... | collective-permute-start | bytes 405512 | tf_op jit(solution)/shard_map/ppermute | solution.py:495
  29.6 0.7 copy-start.3
  42.3 5.2 %collective-permute-start.4 = (f32[176,128]{1,0:T(8,128)S(1)}, f32[176,128]{1,0:T(8,128)S(1)}, u32[]{:S(2)}, u32[]{:S(2)}) collective-permute-start(f32[176,128]{1,0:T(8,128)S(1)} %get-tuple-element.71), channel_id=1, source_target_pairs={{0,32},{32,64},{64,96},{96,128},{128,160},{160,192},{192,224},{224... | collective-permute-start | bytes 270344 | tf_op jit(solution)/shard_map/ppermute | solution.py:495
  45.6 5.3 %collective-permute-start.5 = (f32[176,128]{1,0:T(8,128)S(1)}, f32[176,128]{1,0:T(8,128)S(1)}, u32[]{:S(2)}, u32[]{:S(2)}) collective-permute-start(f32[176,128]{1,0:T(8,128)S(1)} %get-tuple-element.72), channel_id=1, source_target_pairs={{32,0},{64,32},{96,64},{128,96},{160,128},{192,160},{224,192},{256... | collective-permute-start | bytes 270344 | tf_op jit(solution)/shard_map/ppermute | solution.py:495
  51.6 12.5 %copy-start.7 = (f32[8]{0:T(128)S(1)}, f32[8]{0:T(128)}, u32[]{:S(2)}) copy-start(f32[8]{0:T(128)} %base.1) | copy-start | bytes 100
  51.6 12.5 %copy-start.8 = (f32[8]{0:T(128)S(1)}, f32[8]{0:T(128)}, u32[]{:S(2)}) copy-start(f32[8]{0:T(128)} %soft.1) | copy-start | bytes 100
  51.6 12.5 %copy-start.9 = (f32[8]{0:T(128)S(1)}, f32[8]{0:T(128)}, u32[]{:S(2)}) copy-start(f32[8]{0:T(128)} %heat.1) | copy-start | bytes 100
  51.6 6.8 %collective-permute-start.7 = (f32[8,3072]{1,0:T(8,128)S(1)}, f32[8,3072]{1,0:T(8,128)S(1)}, u32[]{:S(2)}, u32[]{:S(2)}) collective-permute-start(f32[8,3072]{1,0:T(8,128)S(1)} %get-tuple-element.115), channel_id=1, source_target_pairs={{0,8},{8,0},{16,24},{24,16},{1,9},{9,1},{17,25},{25,17},{2,10},{10... | collective-permute-start | bytes 294920 | tf_op jit(solution)/shard_map/ppermute | solution.py:503
  55.5 5.9 %collective-permute-start.6 = (f32[8,3072]{1,0:T(8,128)S(1)}, f32[8,3072]{1,0:T(8,128)S(1)}, u32[]{:S(2)}, u32[]{:S(2)}) collective-permute-start(f32[8,3072]{1,0:T(8,128)S(1)} %get-tuple-element.116), channel_id=1, source_target_pairs={{8,16},{16,8},{9,17},{17,9},{10,18},{18,10},{11,19},{19,11},{12,20... | collective-permute-start | bytes 294920 | tf_op jit(solution)/shard_map/ppermute | solution.py:503
  61.5 16.4 %collective-permute-start.8 = (f32[736,128]{1,0:T(8,128)S(1)}, f32[736,128]{1,0:T(8,128)S(1)}, u32[]{:S(2)}, u32[]{:S(2)}) collective-permute-start(f32[736,128]{1,0:T(8,128)S(1)} %pack_z.1.own), channel_id=1, source_target_pairs={{0,1},{1,2},{2,3},{3,4},{4,5},{5,6},{6,7},{8,9},{9,10},{10,11},{11... | collective-permute-start | bytes 1130504 | tf_op jit(solution)/shard_map/ppermute | solution.py:495
  62.8 15.1 %collective-permute-start.9 = (f32[736,128]{1,0:T(8,128)S(1)}, f32[736,128]{1,0:T(8,128)S(1)}, u32[]{:S(2)}, u32[]{:S(2)}) collective-permute-start(f32[736,128]{1,0:T(8,128)S(1)} %pack_z.1.own), channel_id=1, source_target_pairs={{1,0},{2,1},{3,2},{4,3},{5,4},{6,5},{7,6},{9,8},{10,9},{11,10},{12... | collective-permute-start | bytes 1130504 | tf_op jit(solution)/shard_map/ppermute | solution.py:495
  68.1 18.7 %collective-permute-start.10 = (f32[128,128]{1,0:T(8,128)S(1)}, f32[128,128]{1,0:T(8,128)S(1)}, u32[]{:S(2)}, u32[]{:S(2)}) collective-permute-start(f32[128,128]{1,0:T(8,128)S(1)} %get-tuple-element.100), channel_id=1, source_target_pairs={{0,2},{1,3},{2,4},{3,5},{4,6},{5,7},{8,10},{9,11},{10,12},{11,13},... | collective-permute-start | bytes 196616 | tf_op jit(solution)/shard_map/ppermute | solution.py:495
  76.6 10.3 %collective-permute-start.11 = (f32[128,128]{1,0:T(8,128)S(1)}, f32[128,128]{1,0:T(8,128)S(1)}, u32[]{:S(2)}, u32[]{:S(2)}) collective-permute-start(f32[128,128]{1,0:T(8,128)S(1)} %get-tuple-element.101), channel_id=1, source_target_pairs={{2,0},{3,1},{4,2},{5,3},{6,4},{7,5},{10,8},{11,9},{12,10},{13,11},... | collective-permute-start | bytes 196616 | tf_op jit(solution)/shard_map/ppermute | solution.py:495
  86.8 29.3 %copy-start.1 = (f32[4,128,128]{2,1,0:T(8,128)S(1)}, f32[4,128,128]{2,1,0:T(8,128)}, u32[]{:S(2)}) copy-start(f32[4,128,128]{2,1,0:T(8,128)} %param.13) | copy-start | bytes 786436
  86.8 29.3 %copy-start.4 = (f32[512,128]{1,0:T(8,128)S(1)}, f32[512,128]{1,0:T(8,128)}, u32[]{:S(2)}) copy-start(f32[512,128]{1,0:T(8,128)} %copy-done.3) | copy-start | bytes 786436
